TPU v7x, 32 devices: a whole 2x2x4 slice. The times are simulated.
32 devices in a mesh: basin: 2 (over y), row: 4 (over z), col: 2 (over x), sub: 2 (over core).
Axes of the slice: x: 2, y: 2, z: 4, core: 2. Of those that a mesh axis runs over, the one named last changes fastest.
Arguments:
- water_depth: float32 [256, 128, 128], P(('basin', 'row', 'col', 'sub')), parts along dimension 0, may hold values from 0.1 to 3
- flow_east: float32 [256, 128, 128], P(('basin', 'row', 'col', 'sub')), parts along dimension 0, may hold values from -3 to 3
- flow_south: float32 [256, 128, 128], P(('basin', 'row', 'col', 'sub')), parts along dimension 0, may hold values from -3 to 3
- bed_level: float32 [256, 128, 128], P(('basin', 'row', 'col', 'sub')), parts along dimension 0, may hold values from -2 to 2
- manning_n: float32 [256, 128, 128], P(('basin', 'row', 'col', 'sub')), parts along dimension 0, may hold values from 0.03 to 0.15
- placed_before: int32 [256], P('basin'), parts along dimension 0, may hold values from 0 to 127, as said below
- placed_after: int32 [256], P('basin'), parts along dimension 0, may hold values from 0 to 127, as said below
- wet_tiles: int32 [256], P('basin'), parts along dimension 0, may hold values 0 or 1
Outputs:
- new_depth: float32 [256, 128, 128], P(('basin', 'row', 'col', 'sub')), parts along dimension 0
- new_flow_east: float32 [256, 128, 128], P(('basin', 'row', 'col', 'sub')), parts along dimension 0
- new_flow_south: float32 [256, 128, 128], P(('basin', 'row', 'col', 'sub')), parts along dimension 0
There are 2 independent parts, one for each index of `basin`. A program takes and returns all parts, laid end to end along the dimension named above; each array names one. Nothing has to cross between parts.
Inputs may be any that keep to these rules, and one draw needn't show every extreme that they name: placed_before holds every tile once. Slot s lies on the device of index s // 8 over row, col and sub together; the tiles of tile row r sit on the devices of row index r. placed_after holds every tile once. A tile either keeps its slot of placed_before or goes to a slot on another device of the same row index. Each device gives up exactly 4 tiles and takes exactly 4, at most 2 of them from any one device.
All inputs are finite; a program needn't handle non-finite values.
Results may differ from a plain program's by a relative error of at most 0.00002.
Values sent between devices are 32-bit elements; how exact they have to be, the bound alone decides.
No kernel may reach another device: no remote copies, remote signals or barrier semaphores. Data moves between devices by JAX's collectives and lax.ppermute only.
A program may use at most 64 MiB of HBM per device.

v0:
```python
import jax
import jax.numpy as jnp
from jax import lax
from jax.sharding import PartitionSpec as P

STEPS = 6
FIRST = 3


GRAV = 9.81
STEP_TIME = 0.5
SPACING = 5.0
RATE = 0.1
DEPTH_FLOOR = 0.3


def padded(array, sides, width):
    for axis, dim in sides:
        size, length = (lax.axis_size(axis), array.shape[dim])
        up = [(i, (i + 1) % size) for i in range(size - 1)]
        down = [(j, i) for i, j in up]
        last = lax.slice_in_dim(array, length - width, length, axis=dim)
        first = lax.slice_in_dim(array, 0, width, axis=dim)
        before = lax.ppermute(last, axis, up)
        after = lax.ppermute(first, axis, down)
        array = jnp.concatenate([before, array, after], axis=dim)
    return array


def face_flow(discharge, surface, surface_next, ground, ground_next, manning):
    wetted = jnp.maximum(surface, surface_next) - jnp.maximum(ground, ground_next)
    pressure = GRAV * STEP_TIME * jnp.maximum(wetted, 0.0) * (surface_next - surface) / SPACING
    resistance = 1.0 + GRAV * STEP_TIME * manning * manning * jnp.abs(discharge) / jnp.power(
        jnp.maximum(wetted, DEPTH_FLOOR), 7.0 / 3.0
    )
    return (discharge - pressure) / resistance


def inverse(ordering):
    entries = ordering.shape[0]
    return jnp.zeros((entries,), jnp.int32).at[ordering].set(jnp.arange(entries, dtype=jnp.int32))


def shards(
    water_depth, flow_east, flow_south, bed_level, manning_n, placed_before, placed_after, wet_tiles
):
    tile_count = water_depth.shape[0]
    tile_side = water_depth.shape[1]
    lane_count = lax.axis_size(("col", "sub"))
    row_tiles = lane_count * tile_count
    slot_total = placed_before.shape[0]
    device_total = slot_total // tile_count
    row_total = slot_total // row_tiles
    my_row = lax.axis_index("row")
    my_device = my_row * lane_count + lax.axis_index(("col", "sub"))
    my_slots = my_device * tile_count + jnp.arange(tile_count, dtype=jnp.int32)
    where_before = inverse(placed_before)
    where_after = inverse(placed_after)
    wet_flags = wet_tiles == 1
    columns = jnp.arange(tile_side, dtype=jnp.int32)
    slot_ids = jnp.arange(tile_count, dtype=jnp.int32)

    def near_index(slot_list):
        return (slot_list // row_tiles - my_row + 1) * row_tiles + slot_list % row_tiles

    def share_edges(edge_rows):
        row_group = lax.all_gather(edge_rows[None], ("col", "sub"), axis=1, tiled=True)
        spread = padded(row_group, (("row", 0),), 1)
        return spread.reshape(3 * row_tiles, 2, tile_side)

    def tile_links(tile_ids, where_now):
        column = tile_ids % row_tiles
        tile_row = tile_ids // row_tiles
        has_east = column < row_tiles - 1
        has_west = column > 0
        has_south = tile_row < row_total - 1
        has_north = tile_row > 0
        east_tile = jnp.where(has_east, tile_ids + 1, tile_ids)
        west_tile = jnp.where(has_west, tile_ids - 1, tile_ids)
        south_tile = jnp.where(has_south, tile_ids + row_tiles, tile_ids)
        north_tile = jnp.where(has_north, tile_ids - row_tiles, tile_ids)
        mine_wet = wet_flags[tile_ids]
        return (
            mine_wet,
            mine_wet & has_east & wet_flags[east_tile],
            mine_wet & has_south & wet_flags[south_tile],
            mine_wet & has_west & wet_flags[west_tile],
            mine_wet & has_north & wet_flags[north_tile],
            near_index(where_now[east_tile]),
            near_index(where_now[south_tile]),
            near_index(where_now[west_tile]),
            near_index(where_now[north_tile]),
            near_index(where_before[east_tile]),
            near_index(where_before[south_tile]),
        )

    bed_near = share_edges(jnp.stack([bed_level[:, :, 0], bed_level[:, 0, :]], axis=1))
    layout = tile_links(placed_before[my_slots], where_before)
    fields = (water_depth, flow_east, flow_south, bed_level, manning_n)
    for step_index in range(STEPS):
        if step_index == FIRST:
            field_count = len(fields)
            stacked = jnp.stack(fields, axis=1)
            dest_device = where_after[placed_before] // tile_count
            home_device = jnp.arange(slot_total, dtype=jnp.int32) // tile_count
            grid_leave = (dest_device != home_device).reshape(device_total, tile_count)
            earlier = slot_ids[None, :] < slot_ids[:, None]
            source = where_before[placed_after[my_slots]]
            source_device = source // tile_count
            staying = source_device == my_device
            source_lane = source_device % lane_count
            kept_tiles = stacked[source % tile_count]
            mine_leave = grid_leave[my_device]
            move_out = min(tile_count // 2, 2 * (lane_count - 1))
            rank_out = jnp.sum((grid_leave[:, None, :] & earlier[None]).astype(jnp.int32), axis=2)
            mine_rank = rank_out[my_device]
            wanted = mine_leave[None, :] & (
                mine_rank[None, :] == jnp.arange(move_out, dtype=jnp.int32)[:, None]
            )
            chosen_slots = jnp.sum(jnp.where(wanted, slot_ids[None, :], 0), axis=1)
            position = source_lane * move_out + rank_out.reshape(-1)[source]
            block_piece = lax.all_gather(stacked[chosen_slots], ("col", "sub"), axis=0, tiled=True)
            piece_rows = block_piece.shape[0]
            inside = (position >= 0) & (position < piece_rows) & jnp.logical_not(staying)
            chosen = block_piece[jnp.clip(position, 0, piece_rows - 1)]
            arrived = jnp.where(inside[:, None, None, None], chosen, jnp.zeros_like(stacked))
            placed = jnp.where(staying[:, None, None, None], kept_tiles, arrived)
            fields = tuple((placed[:, field_index] for field_index in range(field_count)))
            layout = tile_links(placed_after[my_slots], where_after)
        depth_now, flow_x, flow_y, ground, manning = fields
        (
            advance_mine_wet,
            open_east,
            open_south,
            open_west,
            open_north,
            east_now,
            south_now,
            west_now,
            north_now,
            east_bed,
            south_bed,
        ) = layout
        edge_set = share_edges(jnp.stack([depth_now[:, :, 0], depth_now[:, 0, :]], axis=1))
        east_ground = bed_near[east_bed, 0]
        south_ground = bed_near[south_bed, 1]
        surface = depth_now + ground
        surface_east = jnp.concatenate(
            [surface[:, :, 1:], (edge_set[east_now, 0] + east_ground)[:, :, None]], axis=2
        )
        ground_east = jnp.concatenate([ground[:, :, 1:], east_ground[:, :, None]], axis=2)
        surface_south = jnp.concatenate(
            [surface[:, 1:, :], (edge_set[south_now, 1] + south_ground)[:, None, :]], axis=1
        )
        ground_south = jnp.concatenate([ground[:, 1:, :], south_ground[:, None, :]], axis=1)
        wet_cells = advance_mine_wet[:, None, None]
        interior = columns < tile_side - 1
        open_x = wet_cells & (interior[None, None, :] | open_east[:, None, None])
        open_y = wet_cells & (interior[None, :, None] | open_south[:, None, None])
        updated_x = face_flow(flow_x, surface, surface_east, ground, ground_east, manning)
        updated_y = face_flow(flow_y, surface, surface_south, ground, ground_south, manning)
        flow_x = jnp.where(wet_cells, jnp.where(open_x, updated_x, 0.0), flow_x)
        flow_y = jnp.where(wet_cells, jnp.where(open_y, updated_y, 0.0), flow_y)
        edge_flow = share_edges(
            jnp.stack([flow_x[:, :, tile_side - 1], flow_y[:, tile_side - 1, :]], axis=1)
        )
        west_in = jnp.where(open_west[:, None], edge_flow[west_now, 0], 0.0)
        north_in = jnp.where(open_north[:, None], edge_flow[north_now, 1], 0.0)
        inflow_x = jnp.concatenate([west_in[:, :, None], flow_x[:, :, :-1]], axis=2)
        inflow_y = jnp.concatenate([north_in[:, None, :], flow_y[:, :-1, :]], axis=1)
        depth_new = jnp.where(
            wet_cells, depth_now + RATE * (inflow_x - flow_x + inflow_y - flow_y), depth_now
        )
        depth_now, flow_x, flow_y = (depth_new, flow_x, flow_y)
        fields = (depth_now, flow_x, flow_y, fields[3], fields[4])
    return (fields[0], fields[1], fields[2])


def solution(mesh):
    placed = (
        P(("basin", "row", "col", "sub"), None, None),
        P(("basin", "row", "col", "sub"), None, None),
        P(("basin", "row", "col", "sub"), None, None),
        P(("basin", "row", "col", "sub"), None, None),
        P(("basin", "row", "col", "sub"), None, None),
        P("basin"),
        P("basin"),
        P("basin"),
    )
    return jax.shard_map(
        shards,
        mesh=mesh,
        in_specs=placed,
        out_specs=(
            P(("basin", "row", "col", "sub"), None, None),
            P(("basin", "row", "col", "sub"), None, None),
            P(("basin", "row", "col", "sub"), None, None),
        ),
        check_vma=False,
    )
```

profile of v0, /device:TPU:0, one launch (start us, length us, event | category | flops | bytes accessed | tf_op | source)
XLA Modules:
  0.0 334.3 jit_solution(3129552135304832213)
XLA Ops:
  9.2 6.2 %all-gather = f32[32,2,128]{2,1,0:T(2,128)S(1)} all-gather(f32[8,2,128]{2,1,0:T(2,128)S(1)} %copy.361), channel_id=2, replica_groups=mesh['basin'=2,'row'=4,'col'=2,'sub'=2] {'col','sub'}, dimensions={0}, use_global_device_ids=true | all-gather | bytes 40960 | tf_op jit(solution)/shard_map/all_gather | solution.py:67
  15.4 1.3 collective-permute-start.1
  16.7 4.6 %collective-permute-start = (f32[1,32,2,128]{3,2,1,0:T(2,128)S(1)}, f32[1,32,2,128]{3,2,1,0:T(2,128)S(1)}, u32[]{:S(2)}, u32[]{:S(2)}) collective-permute-start(f32[1,32,2,128]{3,2,1,0:T(2,128)S(1)} %bitcast.554), channel_id=1, source_target_pairs={{0,4},{4,8},{8,12},{1,5},{5,9},{9,13},{2,6},{6,10},{10,14},{3,7},{... | collective-permute-start | bytes 98312 | tf_op jit(solution)/shard_map/ppermute | solution.py:24
  23.3 5.2 %all-gather.1 = f32[32,2,128]{2,1,0:T(2,128)S(1)} all-gather(f32[8,2,128]{2,1,0:T(2,128)S(1)} %copy.364), channel_id=3, replica_groups=mesh['basin'=2,'row'=4,'col'=2,'sub'=2] {'col','sub'}, dimensions={0}, use_global_device_ids=true | all-gather | bytes 40960 | tf_op jit(solution)/shard_map/all_gather | solution.py:67
  28.5 1.3 collective-permute-start.3
  29.7 4.6 %collective-permute-start.2 = (f32[1,32,2,128]{3,2,1,0:T(2,128)S(1)}, f32[1,32,2,128]{3,2,1,0:T(2,128)S(1)}, u32[]{:S(2)}, u32[]{:S(2)}) collective-permute-start(f32[1,32,2,128]{3,2,1,0:T(2,128)S(1)} %bitcast.557), channel_id=1, source_target_pairs={{0,4},{4,8},{8,12},{1,5},{5,9},{9,13},{2,6},{6,10},{10,14},{3,7},{... | collective-permute-start | bytes 98312 | tf_op jit(solution)/shard_map/ppermute | solution.py:24
  35.0 1.3 gather_fusion.3
  36.3 1.3 gather_fusion
  58.7 3.6 %select_select_fusion.12 = (f32[8,128,128]{2,1,0:T(8,128)S(1)}, f32[8,128,128]{2,1,0:T(8,128)}, f32[8,128,128]{2,1,0:T(8,128)S(1)}, f32[8,128,128]{2,1,0:T(8,128)}) fusion(f32[8,128,128]{2,1,0:T(8,128)} %param.9, f32[8,128,128]{2,1,0:T(8,128)S(1)} %add.1217, f32[8,128,1]{2,1,0:T(8,128)} %copy.365, f32[8,128,127]{2,1,0:T(8,128)} %slice.356, ...), kind=kLoop, calls=%fused_computation.134 | loop fusion | flops 5242880 | bytes 6817800 | tf_op jit(solution)/shard_map/jit(_where)/select_n | solution.py:162
  62.7 5.2 %all-gather.2 = f32[32,2,128]{2,1,0:T(2,128)S(1)} all-gather(f32[8,2,128]{2,1,0:T(2,128)S(1)} %pad_maximum_fusion.27), channel_id=4, replica_groups=mesh['basin'=2,'row'=4,'col'=2,'sub'=2] {'col','sub'}, dimensions={0}, use_global_device_ids=true | all-gather | bytes 40960 | tf_op jit(solution)/shard_map/all_gather | solution.py:67
  67.9 1.3 collective-permute-start.5
  69.2 4.6 %collective-permute-start.4 = (f32[1,32,2,128]{3,2,1,0:T(2,128)S(1)}, f32[1,32,2,128]{3,2,1,0:T(2,128)S(1)}, u32[]{:S(2)}, u32[]{:S(2)}) collective-permute-start(f32[1,32,2,128]{3,2,1,0:T(2,128)S(1)} %bitcast.560), channel_id=1, source_target_pairs={{0,4},{4,8},{8,12},{1,5},{5,9},{9,13},{2,6},{6,10},{10,14},{3,7},{... | collective-permute-start | bytes 98312 | tf_op jit(solution)/shard_map/ppermute | solution.py:24
  73.8 1.5 collective-permute-done.4
  77.7 1.4 fusion.101
  79.4 5.2 %all-gather.3 = f32[32,2,128]{2,1,0:T(2,128)S(1)} all-gather(f32[8,2,128]{2,1,0:T(2,128)S(1)} %pad_maximum_fusion.28), channel_id=5, replica_groups=mesh['basin'=2,'row'=4,'col'=2,'sub'=2] {'col','sub'}, dimensions={0}, use_global_device_ids=true | all-gather | bytes 40960 | tf_op jit(solution)/shard_map/all_gather | solution.py:67
  84.6 1.3 collective-permute-start.7
  85.8 4.9 %collective-permute-start.6 = (f32[1,32,2,128]{3,2,1,0:T(2,128)S(1)}, f32[1,32,2,128]{3,2,1,0:T(2,128)S(1)}, u32[]{:S(2)}, u32[]{:S(2)}) collective-permute-start(f32[1,32,2,128]{3,2,1,0:T(2,128)S(1)} %bitcast.566), channel_id=1, source_target_pairs={{0,4},{4,8},{8,12},{1,5},{5,9},{9,13},{2,6},{6,10},{10,14},{3,7},{... | collective-permute-start | bytes 98312 | tf_op jit(solution)/shard_map/ppermute | solution.py:24
  95.0 3.1 select_select_fusion.10
  98.5 5.2 %all-gather.4 = f32[32,2,128]{2,1,0:T(2,128)S(1)} all-gather(f32[8,2,128]{2,1,0:T(2,128)S(1)} %pad_maximum_fusion.29), channel_id=6, replica_groups=mesh['basin'=2,'row'=4,'col'=2,'sub'=2] {'col','sub'}, dimensions={0}, use_global_device_ids=true | all-gather | bytes 40960 | tf_op jit(solution)/shard_map/all_gather | solution.py:67
  103.7 1.3 collective-permute-start.9
  105.0 4.6 %collective-permute-start.8 = (f32[1,32,2,128]{3,2,1,0:T(2,128)S(1)}, f32[1,32,2,128]{3,2,1,0:T(2,128)S(1)}, u32[]{:S(2)}, u32[]{:S(2)}) collective-permute-start(f32[1,32,2,128]{3,2,1,0:T(2,128)S(1)} %bitcast.572), channel_id=1, source_target_pairs={{0,4},{4,8},{8,12},{1,5},{5,9},{9,13},{2,6},{6,10},{10,14},{3,7},{... | collective-permute-start | bytes 98312 | tf_op jit(solution)/shard_map/ppermute | solution.py:24
  109.7 1.5 collective-permute-done.8
  112.8 1.4 fusion.100
  114.4 5.2 %all-gather.5 = f32[32,2,128]{2,1,0:T(2,128)S(1)} all-gather(f32[8,2,128]{2,1,0:T(2,128)S(1)} %pad_maximum_fusion.30), channel_id=7, replica_groups=mesh['basin'=2,'row'=4,'col'=2,'sub'=2] {'col','sub'}, dimensions={0}, use_global_device_ids=true | all-gather | bytes 40960 | tf_op jit(solution)/shard_map/all_gather | solution.py:67
  119.6 1.3 collective-permute-start.11
  120.9 5.0 %collective-permute-start.10 = (f32[1,32,2,128]{3,2,1,0:T(2,128)S(1)}, f32[1,32,2,128]{3,2,1,0:T(2,128)S(1)}, u32[]{:S(2)}, u32[]{:S(2)}) collective-permute-start(f32[1,32,2,128]{3,2,1,0:T(2,128)S(1)} %bitcast.569), channel_id=1, source_target_pairs={{0,4},{4,8},{8,12},{1,5},{5,9},{9,13},{2,6},{6,10},{10,14},{3,7},{... | collective-permute-start | bytes 98312 | tf_op jit(solution)/shard_map/ppermute | solution.py:24
  130.0 3.1 select_select_fusion.8
  133.6 5.2 %all-gather.6 = f32[32,2,128]{2,1,0:T(2,128)S(1)} all-gather(f32[8,2,128]{2,1,0:T(2,128)S(1)} %pad_maximum_fusion.31), channel_id=8, replica_groups=mesh['basin'=2,'row'=4,'col'=2,'sub'=2] {'col','sub'}, dimensions={0}, use_global_device_ids=true | all-gather | bytes 40960 | tf_op jit(solution)/shard_map/all_gather | solution.py:67
  138.7 1.3 collective-permute-start.13
  140.0 4.6 %collective-permute-start.12 = (f32[1,32,2,128]{3,2,1,0:T(2,128)S(1)}, f32[1,32,2,128]{3,2,1,0:T(2,128)S(1)}, u32[]{:S(2)}, u32[]{:S(2)}) collective-permute-start(f32[1,32,2,128]{3,2,1,0:T(2,128)S(1)} %bitcast.584), channel_id=1, source_target_pairs={{0,4},{4,8},{8,12},{1,5},{5,9},{9,13},{2,6},{6,10},{10,14},{3,7},{... | collective-permute-start | bytes 98312 | tf_op jit(solution)/shard_map/ppermute | solution.py:24
  144.6 1.6 collective-permute-done.12
  147.8 1.4 fusion.1
  149.7 1.8 gather_fusion.30
  159.2 2.2 gather_fusion.27
  161.5 33.9 %all-gather.16.cloned.1.call-done = f32[16,5,128,128]{3,2,1,0:T(8,128)} async-done(((f32[4,5,128,128]{3,2,1,0:T(8,128)}), f32[16,5,128,128]{3,2,1,0:T(8,128)}) %all-gather.16.cloned.1.call-update) | async-done | bytes 5242896 | tf_op jit(solution)/shard_map/all_gather | solution.py:122
  195.4 4.8 %gather_fusion.31 = f32[8,5,128,128]{3,2,1,0:T(8,128)} fusion(f32[16,5,128,128]{3,2,1,0:T(8,128)} %all-gather.16.cloned.1.call-done, s32[1024]{0:T(1024)S(1)} %pad_clamp_fusion.4), kind=kCustom, calls=%fused_computation.31 | custom fusion | bytes 5242912 | tf_op jit(solution)/shard_map/gather | solution.py:125
  200.1 3.1 select_select_fusion
  205.3 5.2 %all-gather.8 = f32[32,2,128]{2,1,0:T(2,128)S(1)} all-gather(f32[8,2,128]{2,1,0:T(2,128)S(1)} %pad_maximum_fusion.32), channel_id=10, replica_groups=mesh['basin'=2,'row'=4,'col'=2,'sub'=2] {'col','sub'}, dimensions={0}, use_global_device_ids=true | all-gather | bytes 40960 | tf_op jit(solution)/shard_map/all_gather | solution.py:67
  210.5 1.3 collective-permute-start.15
  211.8 4.5 %collective-permute-start.14 = (f32[1,32,2,128]{3,2,1,0:T(2,128)S(1)}, f32[1,32,2,128]{3,2,1,0:T(2,128)S(1)}, u32[]{:S(2)}, u32[]{:S(2)}) collective-permute-start(f32[1,32,2,128]{3,2,1,0:T(2,128)S(1)} %bitcast.563), channel_id=1, source_target_pairs={{0,4},{4,8},{8,12},{1,5},{5,9},{9,13},{2,6},{6,10},{10,14},{3,7},{... | collective-permute-start | bytes 98312 | tf_op jit(solution)/shard_map/ppermute | solution.py:24
  222.4 3.5 %select_select_fusion.6 = (f32[8,128,128]{2,1,0:T(8,128)S(1)}, f32[8,128,128]{2,1,0:T(8,128)}, f32[8,128,128]{2,1,0:T(8,128)S(1)}, f32[8,128,128]{2,1,0:T(8,128)}) fusion(f32[8,5,128,128]{3,2,1,0:T(8,128)S(1)} %select_select_fusion, f32[8,128,1]{2,1,0:T(8,128)} %copy.392, f32[8,128,127]{2,1,0:T(8,128)} %slice.381, pred[8]{0:T(512)(128)(4,1)S(1)} %gather_fusion.1, ...), kind=kLoop, calls=%fused_computation.128 | loop fusion | flops 5373952 | bytes 6817800 | tf_op jit(solution)/shard_map/jit(_where)/select_n | solution.py:162
  227.1 5.2 %all-gather.9 = f32[32,2,128]{2,1,0:T(2,128)S(1)} all-gather(f32[8,2,128]{2,1,0:T(2,128)S(1)} %pad_maximum_fusion.33), channel_id=11, replica_groups=mesh['basin'=2,'row'=4,'col'=2,'sub'=2] {'col','sub'}, dimensions={0}, use_global_device_ids=true | all-gather | bytes 40960 | tf_op jit(solution)/shard_map/all_gather | solution.py:67
  232.3 1.3 collective-permute-start.17
  233.6 4.5 %collective-permute-start.16 = (f32[1,32,2,128]{3,2,1,0:T(2,128)S(1)}, f32[1,32,2,128]{3,2,1,0:T(2,128)S(1)}, u32[]{:S(2)}, u32[]{:S(2)}) collective-permute-start(f32[1,32,2,128]{3,2,1,0:T(2,128)S(1)} %bitcast.575), channel_id=1, source_target_pairs={{0,4},{4,8},{8,12},{1,5},{5,9},{9,13},{2,6},{6,10},{10,14},{3,7},{... | collective-permute-start | bytes 98312 | tf_op jit(solution)/shard_map/ppermute | solution.py:24
  238.2 1.5 collective-permute-done.16
  242.1 2.5 fusion.99
  246.7 5.2 %all-gather.10 = f32[32,2,128]{2,1,0:T(2,128)S(1)} all-gather(f32[8,2,128]{2,1,0:T(2,128)S(1)} %pad_maximum_fusion.34), channel_id=12, replica_groups=mesh['basin'=2,'row'=4,'col'=2,'sub'=2] {'col','sub'}, dimensions={0}, use_global_device_ids=true | all-gather | bytes 40960 | tf_op jit(solution)/shard_map/all_gather | solution.py:67
  253.1 4.9 %collective-permute-start.18 = (f32[1,32,2,128]{3,2,1,0:T(2,128)S(1)}, f32[1,32,2,128]{3,2,1,0:T(2,128)S(1)}, u32[]{:S(2)}, u32[]{:S(2)}) collective-permute-start(f32[1,32,2,128]{3,2,1,0:T(2,128)S(1)} %bitcast.578), channel_id=1, source_target_pairs={{0,4},{4,8},{8,12},{1,5},{5,9},{9,13},{2,6},{6,10},{10,14},{3,7},{... | collective-permute-start | bytes 98312 | tf_op jit(solution)/shard_map/ppermute | solution.py:24
  258.0 2.1 slice.393
  260.1 1.9 slice.397
  264.2 3.4 %select_select_fusion.4 = (f32[8,128,128]{2,1,0:T(8,128)S(1)}, f32[8,128,128]{2,1,0:T(8,128)S(1)}) fusion(f32[8,128,128]{2,1,0:T(8,128)} %copy-done.1, f32[8,128,128]{2,1,0:T(8,128)} %get-tuple-element.8, f32[8,128,128]{2,1,0:T(8,128)} %get-tuple-element.14, f32[8,128,1]{2,1,0:T(8,128)} %copy.399, f32[8,128,127]{2,1,0:T(8,128)} %slice.393, ...), kind=kLoop, calls=%fused_computation.126 | loop fusion | flops 4718592 | bytes 5244936 | tf_op jit(solution)/shard_map/jit(_where)/select_n | solution.py:162
  268.8 5.2 %all-gather.11 = f32[32,2,128]{2,1,0:T(2,128)S(1)} all-gather(f32[8,2,128]{2,1,0:T(2,128)S(1)} %pad_maximum_fusion.35), channel_id=13, replica_groups=mesh['basin'=2,'row'=4,'col'=2,'sub'=2] {'col','sub'}, dimensions={0}, use_global_device_ids=true | all-gather | bytes 40960 | tf_op jit(solution)/shard_map/all_gather | solution.py:67
  275.3 4.8 %collective-permute-start.20 = (f32[1,32,2,128]{3,2,1,0:T(2,128)S(1)}, f32[1,32,2,128]{3,2,1,0:T(2,128)S(1)}, u32[]{:S(2)}, u32[]{:S(2)}) collective-permute-start(f32[1,32,2,128]{3,2,1,0:T(2,128)S(1)} %bitcast.587), channel_id=1, source_target_pairs={{0,4},{4,8},{8,12},{1,5},{5,9},{9,13},{2,6},{6,10},{10,14},{3,7},{... | collective-permute-start | bytes 98312 | tf_op jit(solution)/shard_map/ppermute | solution.py:24
  280.1 1.3 collective-permute-done.20
  283.8 2.6 fusion.98
  288.5 5.2 %all-gather.12 = f32[32,2,128]{2,1,0:T(2,128)S(1)} all-gather(f32[8,2,128]{2,1,0:T(2,128)S(1)} %pad_maximum_fusion.36), channel_id=14, replica_groups=mesh['basin'=2,'row'=4,'col'=2,'sub'=2] {'col','sub'}, dimensions={0}, use_global_device_ids=true | all-gather | bytes 40960 | tf_op jit(solution)/shard_map/all_gather | solution.py:67
  295.0 4.9 %collective-permute-start.22 = (f32[1,32,2,128]{3,2,1,0:T(2,128)S(1)}, f32[1,32,2,128]{3,2,1,0:T(2,128)S(1)}, u32[]{:S(2)}, u32[]{:S(2)}) collective-permute-start(f32[1,32,2,128]{3,2,1,0:T(2,128)S(1)} %bitcast.581), channel_id=1, source_target_pairs={{0,4},{4,8},{8,12},{1,5},{5,9},{9,13},{2,6},{6,10},{10,14},{3,7},{... | collective-permute-start | bytes 98312 | tf_op jit(solution)/shard_map/ppermute | solution.py:24
  299.9 2.0 slice.401
  301.9 1.9 slice.405
  306.0 3.3 select_select_fusion.2
  310.5 5.2 %all-gather.13 = f32[32,2,128]{2,1,0:T(2,128)S(1)} all-gather(f32[8,2,128]{2,1,0:T(2,128)S(1)} %pad_maximum_fusion.37), channel_id=15, replica_groups=mesh['basin'=2,'row'=4,'col'=2,'sub'=2] {'col','sub'}, dimensions={0}, use_global_device_ids=true | all-gather | bytes 40960 | tf_op jit(solution)/shard_map/all_gather | solution.py:67
  317.0 4.6 %collective-permute-start.24 = (f32[1,32,2,128]{3,2,1,0:T(2,128)S(1)}, f32[1,32,2,128]{3,2,1,0:T(2,128)S(1)}, u32[]{:S(2)}, u32[]{:S(2)}) collective-permute-start(f32[1,32,2,128]{3,2,1,0:T(2,128)S(1)} %bitcast.590), channel_id=1, source_target_pairs={{0,4},{4,8},{8,12},{1,5},{5,9},{9,13},{2,6},{6,10},{10,14},{3,7},{... | collective-permute-start | bytes 98312 | tf_op jit(solution)/shard_map/ppermute | solution.py:24
  321.6 1.6 collective-permute-done.24
  324.7 2.8 add_select_fusion
  (272 shorter events, 81.2 us)
Async XLA Ops:
  7.2 188.2 %all-gather.16.cloned.1.call-start = ((), (), s32[]{:S(2)}) async-start(), calls=%async_computation | async-start | bytes 6553600 | tf_op jit(solution)/shard_map/all_gather | solution.py:122
  15.4 38.8 %collective-permute-start.1 = (f32[1,32,2,128]{3,2,1,0:T(2,128)S(1)}, f32[1,32,2,128]{3,2,1,0:T(2,128)S(1)}, u32[]{:S(2)}, u32[]{:S(2)}) collective-permute-start(f32[1,32,2,128]{3,2,1,0:T(2,128)S(1)} %bitcast.553), channel_id=1, source_target_pairs={{4,0},{8,4},{12,8},{5,1},{9,5},{13,9},{6,2},{10,6},{14,10},{7,3},{... | collective-permute-start | bytes 98312 | tf_op jit(solution)/shard_map/ppermute | solution.py:25
  16.7 37.5 %collective-permute-start = (f32[1,32,2,128]{3,2,1,0:T(2,128)S(1)}, f32[1,32,2,128]{3,2,1,0:T(2,128)S(1)}, u32[]{:S(2)}, u32[]{:S(2)}) collective-permute-start(f32[1,32,2,128]{3,2,1,0:T(2,128)S(1)} %bitcast.554), channel_id=1, source_target_pairs={{0,4},{4,8},{8,12},{1,5},{5,9},{9,13},{2,6},{6,10},{10,14},{3,7},{... | collective-permute-start | bytes 98312 | tf_op jit(solution)/shard_map/ppermute | solution.py:24
  28.5 26.3 %collective-permute-start.3 = (f32[1,32,2,128]{3,2,1,0:T(2,128)S(1)}, f32[1,32,2,128]{3,2,1,0:T(2,128)S(1)}, u32[]{:S(2)}, u32[]{:S(2)}) collective-permute-start(f32[1,32,2,128]{3,2,1,0:T(2,128)S(1)} %bitcast.556), channel_id=1, source_target_pairs={{4,0},{8,4},{12,8},{5,1},{9,5},{13,9},{6,2},{10,6},{14,10},{7,3},{... | collective-permute-start | bytes 98312 | tf_op jit(solution)/shard_map/ppermute | solution.py:25
  29.7 25.1 %collective-permute-start.2 = (f32[1,32,2,128]{3,2,1,0:T(2,128)S(1)}, f32[1,32,2,128]{3,2,1,0:T(2,128)S(1)}, u32[]{:S(2)}, u32[]{:S(2)}) collective-permute-start(f32[1,32,2,128]{3,2,1,0:T(2,128)S(1)} %bitcast.557), channel_id=1, source_target_pairs={{0,4},{4,8},{8,12},{1,5},{5,9},{9,13},{2,6},{6,10},{10,14},{3,7},{... | collective-permute-start | bytes 98312 | tf_op jit(solution)/shard_map/ppermute | solution.py:24
  42.6 8.5 %copy-start = (f32[8,128,128]{2,1,0:T(8,128)S(1)}, f32[8,128,128]{2,1,0:T(8,128)}, u32[]{:S(2)}) copy-start(f32[8,128,128]{2,1,0:T(8,128)} %param.11) | copy-start | bytes 1572868
  42.6 8.5 %copy-start.8 = (f32[8,128,128]{2,1,0:T(8,128)S(1)}, f32[8,128,128]{2,1,0:T(8,128)}, u32[]{:S(2)}) copy-start(f32[8,128,128]{2,1,0:T(8,128)} %param.8) | copy-start | bytes 1572868
  51.4 7.3 %copy-start.5 = (f32[8,128,128]{2,1,0:T(8,128)S(1)}, f32[8,128,128]{2,1,0:T(8,128)}, u32[]{:S(2)}) copy-start(f32[8,128,128]{2,1,0:T(8,128)} %param.12) | copy-start | bytes 1572868
  62.3 15.5 %copy-start.9 = (f32[8,128,128]{2,1,0:T(8,128)S(1)}, f32[8,128,128]{2,1,0:T(8,128)}, u32[]{:S(2)}) copy-start(f32[8,128,128]{2,1,0:T(8,128)} %param.8) | copy-start | bytes 1572868
  67.9 5.9 %collective-permute-start.5 = (f32[1,32,2,128]{3,2,1,0:T(2,128)S(1)}, f32[1,32,2,128]{3,2,1,0:T(2,128)S(1)}, u32[]{:S(2)}, u32[]{:S(2)}) collective-permute-start(f32[1,32,2,128]{3,2,1,0:T(2,128)S(1)} %bitcast.559), channel_id=1, source_target_pairs={{4,0},{8,4},{12,8},{5,1},{9,5},{13,9},{6,2},{10,6},{14,10},{7,3},{... | collective-permute-start | bytes 98312 | tf_op jit(solution)/shard_map/ppermute | solution.py:25
  69.2 6.1 %collective-permute-start.4 = (f32[1,32,2,128]{3,2,1,0:T(2,128)S(1)}, f32[1,32,2,128]{3,2,1,0:T(2,128)S(1)}, u32[]{:S(2)}, u32[]{:S(2)}) collective-permute-start(f32[1,32,2,128]{3,2,1,0:T(2,128)S(1)} %bitcast.560), channel_id=1, source_target_pairs={{0,4},{4,8},{8,12},{1,5},{5,9},{9,13},{2,6},{6,10},{10,14},{3,7},{... | collective-permute-start | bytes 98312 | tf_op jit(solution)/shard_map/ppermute | solution.py:24
  79.1 15.9 %copy-start.12 = (f32[8,128,128]{2,1,0:T(8,128)}, f32[8,128,128]{2,1,0:T(8,128)S(1)}, u32[]{:S(2)}) copy-start(f32[8,128,128]{2,1,0:T(8,128)S(1)} %get-tuple-element.22) | copy-start | bytes 1572868
  84.6 8.2 %collective-permute-start.7 = (f32[1,32,2,128]{3,2,1,0:T(2,128)S(1)}, f32[1,32,2,128]{3,2,1,0:T(2,128)S(1)}, u32[]{:S(2)}, u32[]{:S(2)}) collective-permute-start(f32[1,32,2,128]{3,2,1,0:T(2,128)S(1)} %bitcast.565), channel_id=1, source_target_pairs={{4,0},{8,4},{12,8},{5,1},{9,5},{13,9},{6,2},{10,6},{14,10},{7,3},{... | collective-permute-start | bytes 98312 | tf_op jit(solution)/shard_map/ppermute | solution.py:25
  85.8 6.9 %collective-permute-start.6 = (f32[1,32,2,128]{3,2,1,0:T(2,128)S(1)}, f32[1,32,2,128]{3,2,1,0:T(2,128)S(1)}, u32[]{:S(2)}, u32[]{:S(2)}) collective-permute-start(f32[1,32,2,128]{3,2,1,0:T(2,128)S(1)} %bitcast.566), channel_id=1, source_target_pairs={{0,4},{4,8},{8,12},{1,5},{5,9},{9,13},{2,6},{6,10},{10,14},{3,7},{... | collective-permute-start | bytes 98312 | tf_op jit(solution)/shard_map/ppermute | solution.py:24
  103.7 6.0 %collective-permute-start.9 = (f32[1,32,2,128]{3,2,1,0:T(2,128)S(1)}, f32[1,32,2,128]{3,2,1,0:T(2,128)S(1)}, u32[]{:S(2)}, u32[]{:S(2)}) collective-permute-start(f32[1,32,2,128]{3,2,1,0:T(2,128)S(1)} %bitcast.571), channel_id=1, source_target_pairs={{4,0},{8,4},{12,8},{5,1},{9,5},{13,9},{6,2},{10,6},{14,10},{7,3},{... | collective-permute-start | bytes 98312 | tf_op jit(solution)/shard_map/ppermute | solution.py:25
  105.0 6.1 %collective-permute-start.8 = (f32[1,32,2,128]{3,2,1,0:T(2,128)S(1)}, f32[1,32,2,128]{3,2,1,0:T(2,128)S(1)}, u32[]{:S(2)}, u32[]{:S(2)}) collective-permute-start(f32[1,32,2,128]{3,2,1,0:T(2,128)S(1)} %bitcast.572), channel_id=1, source_target_pairs={{0,4},{4,8},{8,12},{1,5},{5,9},{9,13},{2,6},{6,10},{10,14},{3,7},{... | collective-permute-start | bytes 98312 | tf_op jit(solution)/shard_map/ppermute | solution.py:24
  114.1 15.9 %copy-start.10 = (f32[8,128,128]{2,1,0:T(8,128)}, f32[8,128,128]{2,1,0:T(8,128)S(1)}, u32[]{:S(2)}) copy-start(f32[8,128,128]{2,1,0:T(8,128)S(1)} %get-tuple-element.20) | copy-start | bytes 1572868
  119.6 8.2 %collective-permute-start.11 = (f32[1,32,2,128]{3,2,1,0:T(2,128)S(1)}, f32[1,32,2,128]{3,2,1,0:T(2,128)S(1)}, u32[]{:S(2)}, u32[]{:S(2)}) collective-permute-start(f32[1,32,2,128]{3,2,1,0:T(2,128)S(1)} %bitcast.568), channel_id=1, source_target_pairs={{4,0},{8,4},{12,8},{5,1},{9,5},{13,9},{6,2},{10,6},{14,10},{7,3},{... | collective-permute-start | bytes 98312 | tf_op jit(solution)/shard_map/ppermute | solution.py:25
  120.9 6.9 %collective-permute-start.10 = (f32[1,32,2,128]{3,2,1,0:T(2,128)S(1)}, f32[1,32,2,128]{3,2,1,0:T(2,128)S(1)}, u32[]{:S(2)}, u32[]{:S(2)}) collective-permute-start(f32[1,32,2,128]{3,2,1,0:T(2,128)S(1)} %bitcast.569), channel_id=1, source_target_pairs={{0,4},{4,8},{8,12},{1,5},{5,9},{9,13},{2,6},{6,10},{10,14},{3,7},{... | collective-permute-start | bytes 98312 | tf_op jit(solution)/shard_map/ppermute | solution.py:24
  138.7 5.9 %collective-permute-start.13 = (f32[1,32,2,128]{3,2,1,0:T(2,128)S(1)}, f32[1,32,2,128]{3,2,1,0:T(2,128)S(1)}, u32[]{:S(2)}, u32[]{:S(2)}) collective-permute-start(f32[1,32,2,128]{3,2,1,0:T(2,128)S(1)} %bitcast.583), channel_id=1, source_target_pairs={{4,0},{8,4},{12,8},{5,1},{9,5},{13,9},{6,2},{10,6},{14,10},{7,3},{... | collective-permute-start | bytes 98312 | tf_op jit(solution)/shard_map/ppermute | solution.py:25
  140.0 6.1 %collective-permute-start.12 = (f32[1,32,2,128]{3,2,1,0:T(2,128)S(1)}, f32[1,32,2,128]{3,2,1,0:T(2,128)S(1)}, u32[]{:S(2)}, u32[]{:S(2)}) collective-permute-start(f32[1,32,2,128]{3,2,1,0:T(2,128)S(1)} %bitcast.584), channel_id=1, source_target_pairs={{0,4},{4,8},{8,12},{1,5},{5,9},{9,13},{2,6},{6,10},{10,14},{3,7},{... | collective-permute-start | bytes 98312 | tf_op jit(solution)/shard_map/ppermute | solution.py:24
  147.8 1.6 copy-start.6
  203.3 0.8 copy-start.14
  210.5 9.6 %collective-permute-start.15 = (f32[1,32,2,128]{3,2,1,0:T(2,128)S(1)}, f32[1,32,2,128]{3,2,1,0:T(2,128)S(1)}, u32[]{:S(2)}, u32[]{:S(2)}) collective-permute-start(f32[1,32,2,128]{3,2,1,0:T(2,128)S(1)} %bitcast.562), channel_id=1, source_target_pairs={{4,0},{8,4},{12,8},{5,1},{9,5},{13,9},{6,2},{10,6},{14,10},{7,3},{... | collective-permute-start | bytes 98312 | tf_op jit(solution)/shard_map/ppermute | solution.py:25
  211.8 8.3 %collective-permute-start.14 = (f32[1,32,2,128]{3,2,1,0:T(2,128)S(1)}, f32[1,32,2,128]{3,2,1,0:T(2,128)S(1)}, u32[]{:S(2)}, u32[]{:S(2)}) collective-permute-start(f32[1,32,2,128]{3,2,1,0:T(2,128)S(1)} %bitcast.563), channel_id=1, source_target_pairs={{0,4},{4,8},{8,12},{1,5},{5,9},{9,13},{2,6},{6,10},{10,14},{3,7},{... | collective-permute-start | bytes 98312 | tf_op jit(solution)/shard_map/ppermute | solution.py:24
  225.9 0.8 copy-start.3
  225.9 18.7 %copy-start.1 = (f32[8,128,128]{2,1,0:T(8,128)}, f32[8,128,128]{2,1,0:T(8,128)S(1)}, u32[]{:S(2)}) copy-start(f32[8,128,128]{2,1,0:T(8,128)S(1)} %get-tuple-element.13) | copy-start | bytes 1572868
  232.3 5.9 %collective-permute-start.17 = (f32[1,32,2,128]{3,2,1,0:T(2,128)S(1)}, f32[1,32,2,128]{3,2,1,0:T(2,128)S(1)}, u32[]{:S(2)}, u32[]{:S(2)}) collective-permute-start(f32[1,32,2,128]{3,2,1,0:T(2,128)S(1)} %bitcast.574), channel_id=1, source_target_pairs={{4,0},{8,4},{12,8},{5,1},{9,5},{13,9},{6,2},{10,6},{14,10},{7,3},{... | collective-permute-start | bytes 98312 | tf_op jit(solution)/shard_map/ppermute | solution.py:25
  233.6 6.1 %collective-permute-start.16 = (f32[1,32,2,128]{3,2,1,0:T(2,128)S(1)}, f32[1,32,2,128]{3,2,1,0:T(2,128)S(1)}, u32[]{:S(2)}, u32[]{:S(2)}) collective-permute-start(f32[1,32,2,128]{3,2,1,0:T(2,128)S(1)} %bitcast.575), channel_id=1, source_target_pairs={{0,4},{4,8},{8,12},{1,5},{5,9},{9,13},{2,6},{6,10},{10,14},{3,7},{... | collective-permute-start | bytes 98312 | tf_op jit(solution)/shard_map/ppermute | solution.py:24
  244.6 0.8 copy-start.13
  251.9 10.1 %collective-permute-start.19 = (f32[1,32,2,128]{3,2,1,0:T(2,128)S(1)}, f32[1,32,2,128]{3,2,1,0:T(2,128)S(1)}, u32[]{:S(2)}, u32[]{:S(2)}) collective-permute-start(f32[1,32,2,128]{3,2,1,0:T(2,128)S(1)} %bitcast.577), channel_id=1, source_target_pairs={{4,0},{8,4},{12,8},{5,1},{9,5},{13,9},{6,2},{10,6},{14,10},{7,3},{... | collective-permute-start | bytes 98312 | tf_op jit(solution)/shard_map/ppermute | solution.py:25
  253.1 8.8 %collective-permute-start.18 = (f32[1,32,2,128]{3,2,1,0:T(2,128)S(1)}, f32[1,32,2,128]{3,2,1,0:T(2,128)S(1)}, u32[]{:S(2)}, u32[]{:S(2)}) collective-permute-start(f32[1,32,2,128]{3,2,1,0:T(2,128)S(1)} %bitcast.578), channel_id=1, source_target_pairs={{0,4},{4,8},{8,12},{1,5},{5,9},{9,13},{2,6},{6,10},{10,14},{3,7},{... | collective-permute-start | bytes 98312 | tf_op jit(solution)/shard_map/ppermute | solution.py:24
  267.6 0.8 copy-start.2
  274.0 6.1 %collective-permute-start.21 = (f32[1,32,2,128]{3,2,1,0:T(2,128)S(1)}, f32[1,32,2,128]{3,2,1,0:T(2,128)S(1)}, u32[]{:S(2)}, u32[]{:S(2)}) collective-permute-start(f32[1,32,2,128]{3,2,1,0:T(2,128)S(1)} %bitcast.586), channel_id=1, source_target_pairs={{4,0},{8,4},{12,8},{5,1},{9,5},{13,9},{6,2},{10,6},{14,10},{7,3},{... | collective-permute-start | bytes 98312 | tf_op jit(solution)/shard_map/ppermute | solution.py:25
  275.3 6.1 %collective-permute-start.20 = (f32[1,32,2,128]{3,2,1,0:T(2,128)S(1)}, f32[1,32,2,128]{3,2,1,0:T(2,128)S(1)}, u32[]{:S(2)}, u32[]{:S(2)}) collective-permute-start(f32[1,32,2,128]{3,2,1,0:T(2,128)S(1)} %bitcast.587), channel_id=1, source_target_pairs={{0,4},{4,8},{8,12},{1,5},{5,9},{9,13},{2,6},{6,10},{10,14},{3,7},{... | collective-permute-start | bytes 98312 | tf_op jit(solution)/shard_map/ppermute | solution.py:24
  286.5 0.8 copy-start.11
  293.7 10.1 %collective-permute-start.23 = (f32[1,32,2,128]{3,2,1,0:T(2,128)S(1)}, f32[1,32,2,128]{3,2,1,0:T(2,128)S(1)}, u32[]{:S(2)}, u32[]{:S(2)}) collective-permute-start(f32[1,32,2,128]{3,2,1,0:T(2,128)S(1)} %bitcast.580), channel_id=1, source_target_pairs={{4,0},{8,4},{12,8},{5,1},{9,5},{13,9},{6,2},{10,6},{14,10},{7,3},{... | collective-permute-start | bytes 98312 | tf_op jit(solution)/shard_map/ppermute | solution.py:25
  295.0 8.8 %collective-permute-start.22 = (f32[1,32,2,128]{3,2,1,0:T(2,128)S(1)}, f32[1,32,2,128]{3,2,1,0:T(2,128)S(1)}, u32[]{:S(2)}, u32[]{:S(2)}) collective-permute-start(f32[1,32,2,128]{3,2,1,0:T(2,128)S(1)} %bitcast.581), channel_id=1, source_target_pairs={{0,4},{4,8},{8,12},{1,5},{5,9},{9,13},{2,6},{6,10},{10,14},{3,7},{... | collective-permute-start | bytes 98312 | tf_op jit(solution)/shard_map/ppermute | solution.py:24
  309.3 0.8 copy-start.4
  309.3 1.2 copy-start.7
  315.7 5.8 %collective-permute-start.25 = (f32[1,32,2,128]{3,2,1,0:T(2,128)S(1)}, f32[1,32,2,128]{3,2,1,0:T(2,128)S(1)}, u32[]{:S(2)}, u32[]{:S(2)}) collective-permute-start(f32[1,32,2,128]{3,2,1,0:T(2,128)S(1)} %bitcast.589), channel_id=1, source_target_pairs={{4,0},{8,4},{12,8},{5,1},{9,5},{13,9},{6,2},{10,6},{14,10},{7,3},{... | collective-permute-start | bytes 98312 | tf_op jit(solution)/shard_map/ppermute | solution.py:25
  317.0 6.1 %collective-permute-start.24 = (f32[1,32,2,128]{3,2,1,0:T(2,128)S(1)}, f32[1,32,2,128]{3,2,1,0:T(2,128)S(1)}, u32[]{:S(2)}, u32[]{:S(2)}) collective-permute-start(f32[1,32,2,128]{3,2,1,0:T(2,128)S(1)} %bitcast.590), channel_id=1, source_target_pairs={{0,4},{4,8},{8,12},{1,5},{5,9},{9,13},{2,6},{6,10},{10,14},{3,7},{... | collective-permute-start | bytes 98312 | tf_op jit(solution)/shard_map/ppermute | solution.py:24
Sparse Core Ops, SparseCore 0:
  151.6 43.7 all-gather.15
where the time goes:
time: 336 us; the launch traced here: 334 us
  local copies, waits for them, and re-layouts  91.3 us (27%)
  starting transfers between devices  77.5 us (23%)
  blocking collectives  68.5 us (20%)
  waiting for transfers between devices  42.9 us (13%)
  other arithmetic  39.1 us (12%)
  between operations  15.1 us (4%)
    all_gather x13, blocking collectives, share_edges(): lax.all_gather(edge_rows[None], ('col', 'sub'), axis=1, tiled=True)  68.5 us
    ppermute x13, starting transfers between devices, padded(): before = lax.ppermute(last, axis, up)  60.8 us
    all_gather x1, waiting for transfers between devices, shards(): lax.all_gather(stacked[chosen_slots], ('col', 'sub'), axis=0, tiled=True)  33.9 us
    select_n x6, other arithmetic, shards(): flow_x = jnp.where(wet_cells, jnp.where(open_x, updated_x, 0.0), flow_x)  20.1 us
    ppermute x13, starting transfers between devices, padded(): after = lax.ppermute(first, axis, down)  16.6 us
    unnamed x41, local copies, waits for them, and re-layouts  11.5 us
    ppermute x13, waiting for transfers between devices, padded(): before = lax.ppermute(last, axis, up)  8.97 us
    slice x6, local copies, waits for them, and re-layouts, shards(): surface[:, :, 1:]  8.08 us
  transfers between devices with their start and end apart: 27, of which 7 were waited for; matrix products, arithmetic and copies ran while one was open for 14% of the time, Pallas kernels for 0%

commit v1 on v0

v1 whole, which is shorter than its diff:
```python
import functools
import math

import jax
import jax.numpy as jnp
from jax import lax
from jax.experimental import pallas as pl
from jax.experimental.pallas import tpu as pltpu
from jax.sharding import PartitionSpec as P

STEPS = 6
GRAV = 9.81
STEP_TIME = 0.5
SPACING = 5.0
RATE = 0.1
DEPTH_FLOOR = 0.3

FIELDS = 5
HALO = STEPS
PAIR = 2 * HALO
PACK_ROWS = 32
SIDE = 128
TOP = 16
ROWS = SIDE + 32
LO = 8
HI = SIDE + 24
CHUNK = 24
NT = 4
GROUP = SIDE // NT
CLOSED = 1e30
POWER = -(7.0 / 3.0) / math.log(2.0)

ENTRY = 32
NEAR = {"w": 0, "e": 1, "n": 2, "s": 3, "nw": 4, "ne": 5, "sw": 6, "se": 7}
STEP_TO = ((0, -1), (0, 1), (-1, 0), (1, 0), (-1, -1), (-1, 1), (1, -1), (1, 1))
LEAVE, STAY, RECEIVE = 0, NT * ENTRY, 2 * NT * ENTRY

SMEM = pltpu.SMEM
ANY = pl.ANY


def lane_index():
    return lax.broadcasted_iota(jnp.int32, (1, SIDE), 1)


def index_kernel(
    shape, pos_ref, before_ref, after_ref, wet_ref, table, inv_before, inv_after, count
):
    cols, subs, tile_count, total = shape
    lanes = cols * subs
    row_tiles = lanes * tile_count
    tile_rows = total // row_tiles
    my_row, my_col, my_sub = pos_ref[0], pos_ref[1], pos_ref[2]
    me = my_row * lanes + my_col * subs + my_sub

    def invert(s, carry):
        for u in range(8):
            inv_before[before_ref[s * 8 + u]] = s * 8 + u
            inv_after[after_ref[s * 8 + u]] = s * 8 + u
        return carry

    lax.fori_loop(0, total // 8, invert, 0)
    for i in range(2 * NT):
        table[i * ENTRY] = 0
    for i in range(lanes * 2):
        table[RECEIVE + i] = -1
    for i in range(lanes + 1):
        count[i] = 0

    def modulo(value, size):
        return lax.rem(value + size, size)

    def entry(base, tile, source, target):
        table[base] = 1
        table[base + 1] = jnp.where(wet_ref[tile] == 1, 1, 0)
        table[base + 2] = source
        table[base + 3] = target
        row, col = lax.div(tile, row_tiles), lax.rem(tile, row_tiles)
        for n, (dr, dc) in enumerate(STEP_TO):
            r, c = row + dr, col + dc
            there = (r >= 0) & (r < tile_rows) & (c >= 0) & (c < row_tiles)
            near = jnp.where(there, tile + (dr * row_tiles + dc), tile)
            at = inv_before[near]
            lane = lax.rem(lax.div(at, tile_count), lanes)
            rel = modulo(my_col - lax.div(lane, subs), cols) * subs + modulo(
                my_sub - lax.rem(lane, subs), subs
            )
            table[base + 4 + 3 * n] = jnp.where(there & (wet_ref[near] == 1), 1, 0)
            table[base + 5 + 3 * n] = rel
            table[base + 6 + 3 * n] = lax.rem(at, tile_count)

    def own(s, carry):
        tile = before_ref[me * tile_count + s]
        device = lax.div(inv_after[tile], tile_count)
        stays = device == me

        @pl.when(stays)
        def _():
            at = jnp.minimum(count[0], NT - 1)
            count[0] = at + 1
            entry(STAY + at * ENTRY, tile, s, s)

        @pl.when(jnp.logical_not(stays))
        def _():
            lane = lax.rem(device, lanes)
            rel = modulo(lax.div(lane, subs) - my_col, cols) * subs + modulo(
                lax.rem(lane, subs) - my_sub, subs
            )
            place = jnp.minimum(count[rel], 1)
            count[rel] = place + 1
            at = jnp.minimum(count[lanes], NT - 1)
            count[lanes] = at + 1
            entry(LEAVE + at * ENTRY, tile, s, rel * 2 + place)

        return carry

    lax.fori_loop(0, tile_count, own, 0)

    for rel in range(1, lanes):
        col = modulo(my_col - rel // subs, cols)
        sub = modulo(my_sub - rel % subs, subs)
        device = my_row * lanes + col * subs + sub

        def arriving(s, found):
            at = inv_after[before_ref[device * tile_count + s]]
            mine = lax.div(at, tile_count) == me

            @pl.when(mine)
            def _():
                table[RECEIVE + rel * 2 + jnp.minimum(found, 1)] = lax.rem(at, tile_count)

            return found + jnp.where(mine, 1, 0)

        lax.fori_loop(0, tile_count, arriving, jnp.int32(0))


def make_table(shape, position, before, after, wet):
    cols, subs, _, total = shape
    size = RECEIVE + 2 * cols * subs
    return pl.pallas_call(
        functools.partial(index_kernel, shape),
        name="index_table",
        out_shape=jax.ShapeDtypeStruct((size,), jnp.int32),
        in_specs=[pl.BlockSpec(memory_space=SMEM)] * 4,
        out_specs=pl.BlockSpec(memory_space=SMEM),
        scratch_shapes=[
            SMEM((total,), jnp.int32),
            SMEM((total,), jnp.int32),
            SMEM((cols * subs + 1,), jnp.int32),
        ],
    )(position, before, after, wet)


def pack_kernel(*refs):
    fields = refs[:FIELDS]
    columns, first, last = refs[FIELDS:]
    lane = lane_index()
    packed = jnp.zeros((SIDE, SIDE), jnp.float32)
    for t in range(2):
        for f in range(FIELDS):
            at = PAIR * (t * FIELDS + f)
            moved = pltpu.roll(fields[f][t], at + HALO, 1)
            packed = jnp.where((lane >= at) & (lane < at + PAIR), moved, packed)
            first[t, HALO * f : HALO * (f + 1), :] = fields[f][t, :HALO, :]
            last[t, 2 + HALO * f : 2 + HALO * (f + 1), :] = fields[f][t, SIDE - HALO :, :]
        first[t, FIELDS * HALO :, :] = jnp.zeros((2, SIDE), jnp.float32)
        last[t, :2, :] = jnp.zeros((2, SIDE), jnp.float32)
    columns[0] = packed


def pack_edges(fields, tile_count):
    rows = jax.ShapeDtypeStruct((tile_count, PACK_ROWS, SIDE), jnp.float32)
    return pl.pallas_call(
        pack_kernel,
        name="pack_edges",
        grid=(tile_count // 2,),
        out_shape=(jax.ShapeDtypeStruct((tile_count // 2, SIDE, SIDE), jnp.float32), rows, rows),
        in_specs=[pl.BlockSpec((2, SIDE, SIDE), lambda i: (i, 0, 0))] * FIELDS,
        out_specs=(
            pl.BlockSpec((1, SIDE, SIDE), lambda i: (i, 0, 0)),
            pl.BlockSpec((2, PACK_ROWS, SIDE), lambda i: (i, 0, 0)),
            pl.BlockSpec((2, PACK_ROWS, SIDE), lambda i: (i, 0, 0)),
        ),
    )(*fields)


def face(flow, level, level_next, ground, friction):
    wetted = jnp.maximum(level, level_next) - ground
    drive = (GRAV * STEP_TIME / SPACING) * jnp.maximum(wetted, 0.0) * (level_next - level)
    power = jnp.exp2(POWER * jnp.log(jnp.maximum(wetted, DEPTH_FLOOR)))
    return (flow - drive) / (1.0 + friction * jnp.abs(flow) * power)


def chunks():
    for r in range(LO, HI, CHUNK):
        yield r, min(CHUNK, HI - r)


def assemble(table, base, i, halo_cols, halo_above, halo_below, block, strip):
    lane = lane_index()
    at = GROUP * i

    def near(name):
        place = base + 5 + 3 * NEAR[name]
        return table[place], table[place + 1]

    def inside(lo, hi):
        return (lane >= at + lo) & (lane < at + hi)

    west, east = near("w"), near("e")
    for f in range(FIELDS):
        rows = pl.ds(HALO * f, 8)

        def ends(halo, middle, left, right, out):
            mid = halo[middle[0], middle[1], rows, :]
            block[f][i, out : out + 8, :] = mid
            lower = jnp.where(lane < SIDE // 2, mid, halo[left[0], left[1], rows, :])
            upper = jnp.where(lane < SIDE // 2, halo[right[0], right[1], rows, :], mid)
            value = jnp.where(
                inside(0, 16),
                pltpu.roll(lower, (at + 8) % SIDE, 1),
                pltpu.roll(upper, (at + 24) % SIDE, 1),
            )
            strip[f][out : out + 8, :] = jnp.where(
                inside(0, GROUP), value, strip[f][out : out + 8, :]
            )

        ends(halo_above, near("n"), near("nw"), near("ne"), LO)
        ends(halo_below, near("s"), near("sw"), near("se"), TOP + SIDE)

        def shifted(place, goal):
            source = PAIR * (lax.rem(place[1], 2) * FIELDS + f)
            shift = lax.rem(goal - source + 2 * SIDE, SIDE)
            return pltpu.roll(halo_cols[place[0], lax.div(place[1], 2)], shift, 1)

        core = block[f][i, TOP : TOP + SIDE, :]
        value = strip[f][TOP : TOP + SIDE, :]
        value = jnp.where(inside(0, 8), shifted(west, at + 2), value)
        value = jnp.where(inside(8, 16), pltpu.roll(core, (at + 8) % SIDE, 1), value)
        value = jnp.where(inside(16, 24), pltpu.roll(core, (at + 24) % SIDE, 1), value)
        value = jnp.where(inside(24, GROUP), shifted(east, at + 24 - HALO), value)
        strip[f][TOP : TOP + SIDE, :] = value


def advance_kernel(lanes, base, leaving, *refs):
    table = refs[0]
    inputs = refs[1 : 1 + FIELDS]
    halos = refs[1 + FIELDS : 1 + FIELDS + 3 * lanes]
    n_out = lanes - 1 if leaving else 3
    outs = refs[1 + FIELDS + 3 * lanes : 1 + FIELDS + 3 * lanes + n_out]
    (
        halo_cols, halo_above, halo_below,
        level, flow_x, flow_y, ground, friction, ground_x, ground_y,
        s_level, s_flow_x, s_flow_y, s_ground, s_friction, s_ground_x, s_ground_y,
        hist_level, hist_flow, sem_halo, sem_in, sem_out,
    ) = refs[1 + FIELDS + 3 * lanes + n_out :]
    block = (level, flow_x, flow_y, ground, friction)
    strip = (s_level, s_flow_x, s_flow_y, s_ground, s_friction)
    lane = lane_index()
    core = pl.ds(TOP, SIDE)

    halo_copies = []
    for k in range(lanes):
        for n, target in enumerate((halo_cols, halo_above, halo_below)):
            copy = pltpu.make_async_copy(halos[3 * k + n], target.at[k], sem_halo.at[3 * k + n])
            copy.start()
            halo_copies.append(copy)

    def entry(i):
        at = base + i * ENTRY
        return table[at] == 1, table[at + 1] == 1, table[at + 2], table[at + 3]

    def near_wet(i, name):
        return table[base + i * ENTRY + 4 + 3 * NEAR[name]] == 1

    def loads(i, slot):
        return [
            pltpu.make_async_copy(inputs[f].at[slot], block[f].at[i, core, :], sem_in.at[i, f])
            for f in range(FIELDS)
        ]

    for i in range(NT):
        valid, _, slot, _ = entry(i)

        @pl.when(valid)
        def _():
            for copy in loads(i, slot):
                copy.start()

    for copy in halo_copies:
        copy.wait()
    for i in range(NT):
        valid, wet, slot, _ = entry(i)

        @pl.when(valid)
        def _():
            for copy in loads(i, slot):
                copy.wait()

        @pl.when(valid & wet)
        def _():
            assemble(
                table, base + i * ENTRY, i, halo_cols, halo_above, halo_below, block, strip
            )

    def lane_wet(center, left, right):
        value = jnp.zeros((1, SIDE), jnp.int32)
        for i in range(NT):
            at = GROUP * i
            mid = jnp.where(jnp.bool_(True) if center == "c" else near_wet(i, center), 1, 0)
            sides = jnp.where(
                lane < at + 8,
                jnp.where(near_wet(i, left), 1, 0),
                jnp.where(lane < at + 24, mid, jnp.where(near_wet(i, right), 1, 0)),
            )
            value = jnp.where((lane >= at) & (lane < at + GROUP), sides, value)
        return value

    wet_above = lane_wet("n", "nw", "ne")
    wet_core = lane_wet("c", "w", "e")
    wet_below = lane_wet("s", "sw", "se")

    def row_bands(r, rows, above, core_value, below):
        row = r + lax.broadcasted_iota(jnp.int32, (rows, 1), 0)
        return jnp.where(row < TOP, above, jnp.where(row < TOP + SIDE, core_value, below))

    for r, rows in chunks():
        at, south = pl.ds(r, rows), pl.ds(r + 1, rows)
        z = s_ground[at, :]
        here = row_bands(r, rows, wet_above, wet_core, wet_below)
        next_row = row_bands(r + 1, rows, wet_above, wet_core, wet_below)
        open_x = (here == 1) & (pltpu.roll(here, SIDE - 1, 1) == 1)
        open_y = (here == 1) & (next_row == 1)
        s_ground_x[at, :] = jnp.where(
            open_x, jnp.maximum(z, pltpu.roll(z, SIDE - 1, 1)), CLOSED
        )
        s_ground_y[at, :] = jnp.where(open_y, jnp.maximum(z, s_ground[south, :]), CLOSED)
        hist_flow[0, at, :] = jnp.where(open_x, s_flow_x[at, :], 0.0)
        s_flow_y[at, :] = jnp.where(open_y, s_flow_y[at, :], 0.0)
        m = s_friction[at, :]
        s_friction[at, :] = (GRAV * STEP_TIME) * m * m
        hist_level[0, at, :] = s_level[at, :] + z

    def strip_step(step, carry):
        for r, rows in chunks():
            at, south = pl.ds(r, rows), pl.ds(r + 1, rows)
            e = hist_level[step, at, :]
            c = s_friction[at, :]
            hist_flow[step + 1, at, :] = face(
                hist_flow[step, at, :], e, pltpu.roll(e, SIDE - 1, 1), s_ground_x[at, :], c
            )
            s_flow_y[at, :] = face(
                s_flow_y[at, :], e, hist_level[step, south, :], s_ground_y[at, :], c
            )
        for r, rows in chunks():
            at, north = pl.ds(r, rows), pl.ds(r - 1, rows)
            qx = hist_flow[step + 1, at, :]
            hist_level[step + 1, at, :] = hist_level[step, at, :] + RATE * (
                (pltpu.roll(qx, 1, 1) - qx) + (s_flow_y[north, :] - s_flow_y[at, :])
            )
        return carry

    lax.fori_loop(0, STEPS, strip_step, 0)

    def stores(i, target):
        pieces = (level, flow_x, flow_y)
        if not leaving:
            return [
                (
                    None,
                    [
                        pltpu.make_async_copy(
                            pieces[f].at[i, core, :], outs[f].at[target], sem_out.at[i, f]
                        )
                        for f in range(3)
                    ],
                )
            ]
        return [
            (
                lax.div(target, 2) == k,
                [
                    pltpu.make_async_copy(
                        pieces[f].at[i, core, :],
                        outs[k - 1].at[lax.rem(target, 2), f],
                        sem_out.at[i, f],
                    )
                    for f in range(3)
                ],
            )
            for k in range(1, lanes)
        ]

    def each_store(i, valid, target, act):
        for chosen, copies in stores(i, target):
            @pl.when(valid if chosen is None else valid & chosen)
            def _():
                for copy in copies:
                    act(copy)

    for i in range(NT):
        valid, wet, _, target = entry(i)
        to_east = (SIDE - 1 - GROUP * i - 24) % SIDE
        to_west = (SIDE - GROUP * i - 7) % SIDE
        at_east, at_west = lane == SIDE - 1, lane == 0

        @pl.when(valid & wet)
        def _():
            flag = {name: jnp.where(near_wet(i, name), 1, 0) for name in NEAR}
            above = jnp.where(at_east, flag["n"] * flag["ne"], flag["n"])
            middle = jnp.where(at_east, flag["e"], 1)
            below = jnp.where(at_east, flag["s"] * flag["se"], flag["s"])
            for r, rows in chunks():
                at, south = pl.ds(r, rows), pl.ds(r + 1, rows)
                z = ground[i, at, :]
                z_east = jnp.where(
                    at_east, pltpu.roll(s_ground[at, :], to_east, 1), pltpu.roll(z, SIDE - 1, 1)
                )
                open_x = row_bands(r, rows, above, middle, below) == 1
                open_y = row_bands(r + 1, rows, flag["n"], 1, flag["s"]) * row_bands(
                    r, rows, flag["n"], 1, flag["s"]
                )
                open_y = open_y == 1
                ground_x[i, at, :] = jnp.where(open_x, jnp.maximum(z, z_east), CLOSED)
                ground_y[i, at, :] = jnp.where(
                    open_y, jnp.maximum(z, ground[i, south, :]), CLOSED
                )
                flow_x[i, at, :] = jnp.where(open_x, flow_x[i, at, :], 0.0)
                flow_y[i, at, :] = jnp.where(open_y, flow_y[i, at, :], 0.0)
                m = friction[i, at, :]
                friction[i, at, :] = (GRAV * STEP_TIME) * m * m
                level[i, at, :] = level[i, at, :] + z

            def tile_step(step, carry):
                for r, rows in chunks():
                    at, south = pl.ds(r, rows), pl.ds(r + 1, rows)
                    e = level[i, at, :]
                    c = friction[i, at, :]
                    e_east = jnp.where(
                        at_east,
                        pltpu.roll(hist_level[step, at, :], to_east, 1),
                        pltpu.roll(e, SIDE - 1, 1),
                    )
                    flow_x[i, at, :] = face(flow_x[i, at, :], e, e_east, ground_x[i, at, :], c)
                    flow_y[i, at, :] = face(
                        flow_y[i, at, :], e, level[i, south, :], ground_y[i, at, :], c
                    )
                for r, rows in chunks():
                    at, north = pl.ds(r, rows), pl.ds(r - 1, rows)
                    qx = flow_x[i, at, :]
                    qx_west = jnp.where(
                        at_west,
                        pltpu.roll(hist_flow[step + 1, at, :], to_west, 1),
                        pltpu.roll(qx, 1, 1),
                    )
                    level[i, at, :] = level[i, at, :] + RATE * (
                        (qx_west - qx) + (flow_y[i, north, :] - flow_y[i, at, :])
                    )
                return carry

            lax.fori_loop(0, STEPS, tile_step, 0)
            level[i, core, :] = level[i, core, :] - ground[i, core, :]

        each_store(i, valid, target, lambda copy: copy.start())

    for i in range(NT):
        valid, _, _, target = entry(i)
        each_store(i, valid, target, lambda copy: copy.wait())


def advance(table, fields, halos, base, leaving):
    lanes = len(halos)
    tile_count = fields[0].shape[0]
    if leaving:
        outs = tuple(
            jax.ShapeDtypeStruct((2, 3, SIDE, SIDE), jnp.float32) for _ in range(lanes - 1)
        )
    else:
        outs = (jax.ShapeDtypeStruct((tile_count, SIDE, SIDE), jnp.float32),) * 3
    flat = [array for group in halos for array in group]
    block = pltpu.VMEM((NT, ROWS, SIDE), jnp.float32)
    strip = pltpu.VMEM((ROWS, SIDE), jnp.float32)
    history = pltpu.VMEM((STEPS + 1, ROWS, SIDE), jnp.float32)
    cells = (NT + 1) * ROWS * SIDE * STEPS
    return pl.pallas_call(
        functools.partial(advance_kernel, lanes, base, leaving),
        name="advance_leaving" if leaving else "advance_staying",
        out_shape=outs,
        in_specs=[pl.BlockSpec(memory_space=SMEM)]
        + [pl.BlockSpec(memory_space=ANY)] * (FIELDS + 3 * lanes),
        out_specs=tuple(pl.BlockSpec(memory_space=ANY) for _ in outs),
        scratch_shapes=[
            pltpu.VMEM((lanes,) + halos[0][0].shape, jnp.float32),
            pltpu.VMEM((lanes,) + halos[0][1].shape, jnp.float32),
            pltpu.VMEM((lanes,) + halos[0][2].shape, jnp.float32),
        ]
        + [block] * 7
        + [strip] * 7
        + [history] * 2
        + [
            pltpu.SemaphoreType.DMA((3 * lanes,)),
            pltpu.SemaphoreType.DMA((NT, FIELDS)),
            pltpu.SemaphoreType.DMA((NT, 3)),
        ],
        compiler_params=pltpu.CompilerParams(vmem_limit_bytes=32 * 1024 * 1024),
        cost_estimate=pl.CostEstimate(
            flops=60 * cells, bytes_accessed=8 * NT * SIDE * SIDE * 4, transcendentals=6 * cells
        ),
    )(table, *fields, *flat)


def place_kernel(lanes, *refs):
    table = refs[0]
    received = refs[1:lanes]
    outs = refs[lanes + 3 : lanes + 6]
    sem = refs[lanes + 6]

    def each(act):
        for k in range(1, lanes):
            for j in range(2):
                slot = table[RECEIVE + 2 * k + j]

                @pl.when(slot >= 0)
                def _():
                    for f in range(3):
                        act(
                            pltpu.make_async_copy(
                                received[k - 1].at[j, f], outs[f].at[slot], sem.at[k, j, f]
                            )
                        )

    each(lambda copy: copy.start())
    each(lambda copy: copy.wait())


def place(table, received, partial_outs):
    lanes = len(received) + 1
    return pl.pallas_call(
        functools.partial(place_kernel, lanes),
        name="place_arrivals",
        out_shape=tuple(jax.ShapeDtypeStruct(o.shape, o.dtype) for o in partial_outs),
        in_specs=[pl.BlockSpec(memory_space=SMEM)] + [pl.BlockSpec(memory_space=ANY)] * (lanes + 2),
        out_specs=tuple(pl.BlockSpec(memory_space=ANY) for _ in partial_outs),
        scratch_shapes=[pltpu.SemaphoreType.DMA((lanes, 2, 3))],
        input_output_aliases={lanes: 0, lanes + 1: 1, lanes + 2: 2},
    )(table, *received, *partial_outs)


def shift_lanes(array, col_shift, sub_shift):
    cols, subs = lax.axis_size("col"), lax.axis_size("sub")
    pairs = [
        (c * subs + s, ((c + col_shift) % cols) * subs + (s + sub_shift) % subs)
        for c in range(cols)
        for s in range(subs)
    ]
    return lax.ppermute(array, ("col", "sub"), pairs)


def spread(array):
    cols, subs = lax.axis_size("col"), lax.axis_size("sub")
    out = []
    for c in range(cols):
        part = array if c == 0 else shift_lanes(array, c, 0)
        out.append(part)
        for s in range(1, subs):
            out.append(shift_lanes(part, 0, s))
    return out


def shards(
    water_depth, flow_east, flow_south, bed_level, manning_n, placed_before, placed_after, wet_tiles
):
    cols, subs, rows = lax.axis_size("col"), lax.axis_size("sub"), lax.axis_size("row")
    tile_count = water_depth.shape[0]
    fields = (water_depth, flow_east, flow_south, bed_level, manning_n)
    position = jnp.stack([lax.axis_index("row"), lax.axis_index("col"), lax.axis_index("sub")])
    table = make_table(
        (cols, subs, tile_count, placed_before.shape[0]),
        position.astype(jnp.int32),
        placed_before,
        placed_after,
        wet_tiles,
    )
    columns, first, last = pack_edges(fields, tile_count)
    above = lax.ppermute(last, "row", [(i, i + 1) for i in range(rows - 1)])
    below = lax.ppermute(first, "row", [(i + 1, i) for i in range(rows - 1)])
    halos = list(zip(spread(columns), spread(above), spread(below)))
    leaving = advance(table, fields, halos, LEAVE, True)
    received = [
        shift_lanes(leaving[k - 1], k // subs, k % subs) for k in range(1, cols * subs)
    ]
    staying = advance(table, fields, halos, STAY, False)
    return place(table, received, staying)


def solution(mesh):
    tiles = P(("basin", "row", "col", "sub"), None, None)
    return jax.shard_map(
        shards,
        mesh=mesh,
        in_specs=(tiles,) * FIELDS + (P("basin"),) * 3,
        out_specs=(tiles,) * 3,
        check_vma=False,
    )
```

time: 336 us -> 89.9 us (0.27)
  local copies, waits for them, and re-layouts: 91.3 us -> 5.51 us
  blocking collectives: 68.5 us -> 0 us
  starting transfers between devices: 77.5 us -> 12.5 us
  Pallas kernels: 0 us -> 59.1 us
  other arithmetic: 39.1 us -> 0.61 us
  waiting for transfers between devices: 42.9 us -> 11.3 us
  between operations: 15.1 us -> 0.87 us
    all_gather x13 -> x0, blocking collectives: 68.5 us -> none  [share_edges(): lax.all_gather(edge_rows[None], ('col', 'sub'), axis=1, tiled=True)]
    ppermute x26 -> x14, starting transfers between devices: 77.4 us -> 12.5 us  [the longest x12 6.68 us: shift_lanes(): return lax.ppermute(array, ('col', 'sub'), pairs)]
    pallas_call x0 -> x5, Pallas kernels: none -> 59.1 us  [the longest x1 25.8 us: place(): pl.pallas_call(functools.partial(place_kernel, lanes), name='place_arriva...]
    gather x59 -> x0, local copies, waits for them, and re-layouts: 45.3 us -> none  [the longest x1 4.77 us: shards(): chosen = block_piece[jnp.clip(position, 0, piece_rows - 1)]]
    all_gather x1 -> x0, waiting for transfers between devices: 33.9 us -> none  [shards(): lax.all_gather(stacked[chosen_slots], ('col', 'sub'), axis=0, tiled=True)]
    select_n x27 -> x0, other arithmetic: 27.5 us -> none  [the longest x6 20.1 us: shards(): flow_x = jnp.where(wet_cells, jnp.where(open_x, updated_x, 0.0), flow_x)]
    slice x35 -> x0, local copies, waits for them, and re-layouts: 21.7 us -> none  [the longest x6 8.08 us: shards(): surface[:, :, 1:]]
    add x18 -> x0, other arithmetic: 8.06 us -> none  [the longest x6 8 us: shards(): surface = depth_now + ground]
  transfers between devices with their start and end apart: 27 -> 14, of which waited for: 7 -> 5; matrix products, arithmetic and copies ran while one was open for 14% -> 1% of each run, Pallas kernels for 0% -> 18%
where the time goes in v1:
time: 89.9 us; the launch traced here: 89.8 us
  Pallas kernels  59.1 us (66%)
  starting transfers between devices  12.5 us (14%)
  waiting for transfers between devices  11.3 us (13%)
  local copies, waits for them, and re-layouts  5.51 us (6%)
    pallas_call x1, Pallas kernels, place(): pl.pallas_call(functools.partial(place_kernel, lanes), name='place_arriva...  25.8 us
    pallas_call x2, Pallas kernels, advance(): pl.pallas_call(functools.partial(advance_kernel, lanes, base, leaving), n...  25.7 us
    ppermute x12, waiting for transfers between devices, shift_lanes(): return lax.ppermute(array, ('col', 'sub'), pairs)  8.82 us
    ppermute x12, starting transfers between devices, shift_lanes(): return lax.ppermute(array, ('col', 'sub'), pairs)  6.68 us
    unnamed x28, local copies, waits for them, and re-layouts  5.51 us
    ppermute x1, starting transfers between devices, shards(): above = lax.ppermute(last, 'row', [(i, i + 1) for i in range(rows - 1)])  4.55 us
    pallas_call x1, Pallas kernels, pack_edges(): pl.pallas_call(pack_kernel, name='pack_edges', grid=(tile_count // 2,), o...  4.19 us
    pallas_call x1, Pallas kernels, make_table(): pl.pallas_call(functools.partial(index_kernel, shape), name='index_table'...  3.4 us
  transfers between devices with their start and end apart: 14, of which 5 were waited for; matrix products, arithmetic and copies ran while one was open for 1% of the time, Pallas kernels for 18%

profile of v1, /device:TPU:0, one launch (start us, length us, event | category | flops | bytes accessed | tf_op | source)
XLA Modules:
  0.0 89.8 jit_solution(2169361148927845423)
XLA Ops:
  0.6 0.0 copy-start.2
  0.6 0.0 copy-start.3
  0.7 0.0 copy-start.4
  0.7 0.0 copy-start
  0.7 0.0 copy-start.1
  0.7 4.2 %pack_edges.1 = (f32[4,128,128]{2,1,0:T(8,128)}, f32[8,32,128]{2,1,0:T(8,128)}, f32[8,32,128]{2,1,0:T(8,128)}) custom-call(f32[8,128,128]{2,1,0:T(8,128)} %refs_1_.5, f32[8,128,128]{2,1,0:T(8,128)} %refs_2_.5, f32[8,128,128]{2,1,0:T(8,128)} %refs_3_.5, f32[8,128,128]{2,1,0:T(8,128)} %refs_4_.5, f32[8,128,128]{2,1,0:T(8,128)} %refs_5_.3), custom_call_target="tpu_custom_call" | custom-call | tf_op jit(solution)/shard_map/pack_edges/pallas_call | solution.py:173
  4.9 2.9 %collective-permute-start.5 = (f32[4,128,128]{2,1,0:T(8,128)}, f32[4,128,128]{2,1,0:T(8,128)S(1)}, u32[]{:S(2)}, u32[]{:S(2)}) collective-permute-start(f32[4,128,128]{2,1,0:T(8,128)} %get-tuple-element.12.refs_6_), channel_id=1, source_target_pairs={{0,2},{1,3},{2,0},{3,1},{4,6},{5,7},{6,4},{7,5},{8,10},{9,11},{10,... | collective-permute-start | bytes 786440 | tf_op jit(solution)/shard_map/ppermute | solution.py:556
  7.8 1.3 %collective-permute-start.1 = (f32[8,32,128]{2,1,0:T(8,128)}, f32[8,32,128]{2,1,0:T(8,128)S(1)}, u32[]{:S(2)}, u32[]{:S(2)}) collective-permute-start(f32[8,32,128]{2,1,0:T(8,128)} %get-tuple-element.14), channel_id=1, source_target_pairs={{4,0},{8,4},{12,8},{5,1},{9,5},{13,9},{6,2},{10,6},{14,10},{7,3},{... | collective-permute-start | bytes 393224 | tf_op jit(solution)/shard_map/ppermute | solution.py:586
  9.1 4.6 %collective-permute-start = (f32[8,32,128]{2,1,0:T(8,128)}, f32[8,32,128]{2,1,0:T(8,128)S(1)}, u32[]{:S(2)}, u32[]{:S(2)}) collective-permute-start(f32[8,32,128]{2,1,0:T(8,128)} %get-tuple-element.13), channel_id=1, source_target_pairs={{0,4},{4,8},{8,12},{1,5},{5,9},{9,13},{2,6},{6,10},{10,14},{3,7},{... | collective-permute-start | bytes 393224 | tf_op jit(solution)/shard_map/ppermute | solution.py:585
  13.7 1.2 %collective-permute-done.1.refs_8_ = f32[8,32,128]{2,1,0:T(8,128)S(1)} collective-permute-done((f32[8,32,128]{2,1,0:T(8,128)}, f32[8,32,128]{2,1,0:T(8,128)S(1)}, u32[]{:S(2)}, u32[]{:S(2)}) %collective-permute-start.1) | collective-permute-done | bytes 131104 | tf_op jit(solution)/shard_map/ppermute | solution.py:586
  14.9 0.4 collective-permute-start.7
  15.2 1.2 %collective-permute-done.refs_7_ = f32[8,32,128]{2,1,0:T(8,128)S(1)} collective-permute-done((f32[8,32,128]{2,1,0:T(8,128)}, f32[8,32,128]{2,1,0:T(8,128)S(1)}, u32[]{:S(2)}, u32[]{:S(2)}) %collective-permute-start) | collective-permute-done | bytes 131104 | tf_op jit(solution)/shard_map/ppermute | solution.py:585
  16.5 0.4 collective-permute-start.6
  16.9 0.0 collective-permute-start.2
  16.9 0.5 collective-permute-start.3
  17.4 0.0 copy-start.7
  17.4 0.7 copy-done.7
  18.1 0.0 collective-permute-done.5.refs_12_
  18.1 0.0 collective-permute-start.8
  18.1 2.4 %collective-permute-done.7.refs_14_ = f32[8,32,128]{2,1,0:T(8,128)} collective-permute-done((f32[8,32,128]{2,1,0:T(8,128)S(1)}, f32[8,32,128]{2,1,0:T(8,128)}, u32[]{:S(2)}, u32[]{:S(2)}) %collective-permute-start.7) | collective-permute-done | bytes 131104 | tf_op jit(solution)/shard_map/ppermute | solution.py:556
  20.5 0.0 collective-permute-start.4
  20.5 1.4 %collective-permute-done.6.refs_13_ = f32[8,32,128]{2,1,0:T(8,128)} collective-permute-done((f32[8,32,128]{2,1,0:T(8,128)S(1)}, f32[8,32,128]{2,1,0:T(8,128)}, u32[]{:S(2)}, u32[]{:S(2)}) %collective-permute-start.6) | collective-permute-done | bytes 131104 | tf_op jit(solution)/shard_map/ppermute | solution.py:556
  21.9 0.0 collective-permute-start.10
  21.9 0.0 collective-permute-done.3.refs_10_
  21.9 0.0 copy-start.9
  21.9 0.7 copy-done.9
  22.6 0.5 collective-permute-start.9
  23.1 0.6 pad_add_fusion.pos_ref
  23.7 3.4 %index_table.1.refs_0_ = s32[264]{0:T(512)} custom-call(s32[3]{0:T(128)} %pad_add_fusion.pos_ref, s32[128]{0:T(128)} %before_ref.1, s32[128]{0:T(128)} %after_ref.1, s32[128]{0:T(128)} %wet_ref.1), custom_call_target="tpu_custom_call" | custom-call | tf_op jit(solution)/shard_map/index_table/pallas_call | solution.py:140
  27.1 0.0 collective-permute-done.4.refs_11_
  27.1 0.0 collective-permute-done.2.refs_9_
  27.1 0.0 collective-permute-done.10.refs_17_
  27.1 0.0 collective-permute-done.9.refs_16_
  27.1 0.0 collective-permute-done.8.refs_15_
  27.1 0.0 copy-done.2
  27.1 0.0 copy-done.3
  27.2 0.0 copy-done.4
  27.2 0.0 copy-done
  27.2 0.0 copy-done.1
  27.2 0.0 copy-start.5
  27.2 0.7 copy-done.5
  27.9 0.0 copy-start.6
  27.9 0.9 %copy-done.6 = f32[4,128,128]{2,1,0:T(8,128)S(1)} copy-done((f32[4,128,128]{2,1,0:T(8,128)S(1)}, f32[4,128,128]{2,1,0:T(8,128)}, u32[]{:S(2)}) %copy-start.6) | copy-done | bytes 262168
  28.8 0.0 copy-start.8
  28.8 0.9 %copy-done.8 = f32[8,32,128]{2,1,0:T(8,128)S(1)} copy-done((f32[8,32,128]{2,1,0:T(8,128)S(1)}, f32[8,32,128]{2,1,0:T(8,128)}, u32[]{:S(2)}) %copy-start.8) | copy-done | bytes 131096
  29.7 0.0 copy-start.10
  29.7 0.9 %copy-done.10 = f32[8,32,128]{2,1,0:T(8,128)S(1)} copy-done((f32[8,32,128]{2,1,0:T(8,128)S(1)}, f32[8,32,128]{2,1,0:T(8,128)}, u32[]{:S(2)}) %copy-start.10) | copy-done | bytes 131096
  30.6 13.1 %advance_leaving.1 = (f32[2,3,128,128]{3,2,1,0:T(8,128)S(1)}, f32[2,3,128,128]{3,2,1,0:T(8,128)S(1)}, f32[2,3,128,128]{3,2,1,0:T(8,128)S(1)}) custom-call(s32[264]{0:T(512)S(1)} %copy-done.5, f32[8,128,128]{2,1,0:T(8,128)S(1)} %copy-done, f32[8,128,128]{2,1,0:T(8,128)S(1)} %copy-done.1, f32[8,128,128]{2,1,0:T(8,128)S(1)} %copy-done.2, ...), custom_call_target="tpu_custom_call" | custom-call | flops 36864000 | bytes 2097152 | tf_op jit(solution)/shard_map/advance_leaving/pallas_call | solution.py:485
  43.7 0.1 collective-permute-start.11
  43.8 0.1 collective-permute-start.12
  43.8 1.8 %collective-permute-start.13 = (f32[2,3,128,128]{3,2,1,0:T(8,128)S(1)}, f32[2,3,128,128]{3,2,1,0:T(8,128)S(1)}, u32[]{:S(2)}, u32[]{:S(2)}) collective-permute-start(f32[2,3,128,128]{3,2,1,0:T(8,128)S(1)} %get-tuple-element.17), channel_id=1, source_target_pairs={{0,3},{1,2},{2,1},{3,0},{4,7},{5,6},{6,5},{7,4},{8,11},{9,10},{10,... | collective-permute-start | bytes 1179656 | tf_op jit(solution)/shard_map/ppermute | solution.py:556
  45.6 12.6 %advance_staying.1 = (f32[8,128,128]{2,1,0:T(8,128)}, f32[8,128,128]{2,1,0:T(8,128)}, f32[8,128,128]{2,1,0:T(8,128)}) custom-call(s32[264]{0:T(512)S(1)} %copy-done.5, f32[8,128,128]{2,1,0:T(8,128)S(1)} %copy-done, f32[8,128,128]{2,1,0:T(8,128)S(1)} %copy-done.1, f32[8,128,128]{2,1,0:T(8,128)S(1)} %copy-done.2, f32[8,128,128]{2,1,0:T(8,128)S(1)} %copy-done.3, ...), custom_call_target="tpu_custom_call" | custom-call | flops 36864000 | bytes 2097152 | tf_op jit(solution)/shard_map/advance_staying/pallas_call | solution.py:485
  58.2 0.0 collective-permute-done.11.refs_1_
  58.2 0.0 copy-start.11
  58.3 0.0 collective-permute-done.12.refs_2_
  58.3 0.0 copy-start.12
  58.3 5.0 %collective-permute-done.13.refs_3_ = f32[2,3,128,128]{3,2,1,0:T(8,128)S(1)} collective-permute-done((f32[2,3,128,128]{3,2,1,0:T(8,128)S(1)}, f32[2,3,128,128]{3,2,1,0:T(8,128)S(1)}, u32[]{:S(2)}, u32[]{:S(2)}) %collective-permute-start.13) | collective-permute-done | bytes 393248 | tf_op jit(solution)/shard_map/ppermute | solution.py:556
  63.3 0.0 copy-done.11
  63.3 0.0 copy-start.13
  63.3 0.0 copy-done.12
  63.3 0.8 copy-done.13
  64.0 25.8 %place_arrivals.1 = (f32[8,128,128]{2,1,0:T(8,128)}, f32[8,128,128]{2,1,0:T(8,128)}, f32[8,128,128]{2,1,0:T(8,128)}) custom-call(s32[264]{0:T(512)} %index_table.1.refs_0_, f32[2,3,128,128]{3,2,1,0:T(8,128)} %copy-done.11, f32[2,3,128,128]{3,2,1,0:T(8,128)} %copy-done.12, ...), custom_call_target="tpu_custom_call", output_to_operand_aliasing={{0}: (4, {}), {1}: (5, {}), {2}: (6, {})} | custom-call | tf_op jit(solution)/shard_map/place_arrivals/pallas_call | solution.py:538
Async XLA Ops:
  0.6 26.5 %copy-start.2 = (f32[8,128,128]{2,1,0:T(8,128)S(1)}, f32[8,128,128]{2,1,0:T(8,128)}, u32[]{:S(2)}) copy-start(f32[8,128,128]{2,1,0:T(8,128)} %refs_3_.5) | copy-start | bytes 1572868
  0.6 26.5 %copy-start.3 = (f32[8,128,128]{2,1,0:T(8,128)S(1)}, f32[8,128,128]{2,1,0:T(8,128)}, u32[]{:S(2)}) copy-start(f32[8,128,128]{2,1,0:T(8,128)} %refs_4_.5) | copy-start | bytes 1572868
  0.7 26.5 %copy-start.4 = (f32[8,128,128]{2,1,0:T(8,128)S(1)}, f32[8,128,128]{2,1,0:T(8,128)}, u32[]{:S(2)}) copy-start(f32[8,128,128]{2,1,0:T(8,128)} %refs_5_.3) | copy-start | bytes 1572868
  0.7 26.5 %copy-start = (f32[8,128,128]{2,1,0:T(8,128)S(1)}, f32[8,128,128]{2,1,0:T(8,128)}, u32[]{:S(2)}) copy-start(f32[8,128,128]{2,1,0:T(8,128)} %refs_1_.5) | copy-start | bytes 1572868
  0.7 26.5 %copy-start.1 = (f32[8,128,128]{2,1,0:T(8,128)S(1)}, f32[8,128,128]{2,1,0:T(8,128)}, u32[]{:S(2)}) copy-start(f32[8,128,128]{2,1,0:T(8,128)} %refs_2_.5) | copy-start | bytes 1572868
  4.9 13.2 %collective-permute-start.5 = (f32[4,128,128]{2,1,0:T(8,128)}, f32[4,128,128]{2,1,0:T(8,128)S(1)}, u32[]{:S(2)}, u32[]{:S(2)}) collective-permute-start(f32[4,128,128]{2,1,0:T(8,128)} %get-tuple-element.12.refs_6_), channel_id=1, source_target_pairs={{0,2},{1,3},{2,0},{3,1},{4,6},{5,7},{6,4},{7,5},{8,10},{9,11},{10,... | collective-permute-start | bytes 786440 | tf_op jit(solution)/shard_map/ppermute | solution.py:556
  7.8 7.1 %collective-permute-start.1 = (f32[8,32,128]{2,1,0:T(8,128)}, f32[8,32,128]{2,1,0:T(8,128)S(1)}, u32[]{:S(2)}, u32[]{:S(2)}) collective-permute-start(f32[8,32,128]{2,1,0:T(8,128)} %get-tuple-element.14), channel_id=1, source_target_pairs={{4,0},{8,4},{12,8},{5,1},{9,5},{13,9},{6,2},{10,6},{14,10},{7,3},{... | collective-permute-start | bytes 393224 | tf_op jit(solution)/shard_map/ppermute | solution.py:586
  9.1 7.4 %collective-permute-start = (f32[8,32,128]{2,1,0:T(8,128)}, f32[8,32,128]{2,1,0:T(8,128)S(1)}, u32[]{:S(2)}, u32[]{:S(2)}) collective-permute-start(f32[8,32,128]{2,1,0:T(8,128)} %get-tuple-element.13), channel_id=1, source_target_pairs={{0,4},{4,8},{8,12},{1,5},{5,9},{9,13},{2,6},{6,10},{10,14},{3,7},{... | collective-permute-start | bytes 393224 | tf_op jit(solution)/shard_map/ppermute | solution.py:585
  14.9 5.6 %collective-permute-start.7 = (f32[8,32,128]{2,1,0:T(8,128)S(1)}, f32[8,32,128]{2,1,0:T(8,128)}, u32[]{:S(2)}, u32[]{:S(2)}) collective-permute-start(f32[8,32,128]{2,1,0:T(8,128)S(1)} %collective-permute-done.1.refs_8_), channel_id=1, source_target_pairs={{0,2},{1,3},{2,0},{3,1},{4,6},{5,7},{6,4},{7,5},{8,10},{9,11},{10,... | collective-permute-start | bytes 393224 | tf_op jit(solution)/shard_map/ppermute | solution.py:556
  16.5 5.4 %collective-permute-start.6 = (f32[8,32,128]{2,1,0:T(8,128)S(1)}, f32[8,32,128]{2,1,0:T(8,128)}, u32[]{:S(2)}, u32[]{:S(2)}) collective-permute-start(f32[8,32,128]{2,1,0:T(8,128)S(1)} %collective-permute-done.refs_7_), channel_id=1, source_target_pairs={{0,2},{1,3},{2,0},{3,1},{4,6},{5,7},{6,4},{7,5},{8,10},{9,11},{10,... | collective-permute-start | bytes 393224 | tf_op jit(solution)/shard_map/ppermute | solution.py:556
  16.9 10.2 %collective-permute-start.2 = (f32[4,128,128]{2,1,0:T(8,128)}, f32[4,128,128]{2,1,0:T(8,128)S(1)}, u32[]{:S(2)}, u32[]{:S(2)}) collective-permute-start(f32[4,128,128]{2,1,0:T(8,128)} %get-tuple-element.12.refs_6_), channel_id=1, source_target_pairs={{0,1},{1,0},{2,3},{3,2},{4,5},{5,4},{6,7},{7,6},{8,9},{9,8},{10,11... | collective-permute-start | bytes 786440 | tf_op jit(solution)/shard_map/ppermute | solution.py:556
  16.9 5.0 %collective-permute-start.3 = (f32[8,32,128]{2,1,0:T(8,128)S(1)}, f32[8,32,128]{2,1,0:T(8,128)S(1)}, u32[]{:S(2)}, u32[]{:S(2)}) collective-permute-start(f32[8,32,128]{2,1,0:T(8,128)S(1)} %collective-permute-done.refs_7_), channel_id=1, source_target_pairs={{0,1},{1,0},{2,3},{3,2},{4,5},{5,4},{6,7},{7,6},{8,9},{9,8},{10,11... | collective-permute-start | bytes 393224 | tf_op jit(solution)/shard_map/ppermute | solution.py:556
  17.4 0.7 copy-start.7
  18.1 9.1 %collective-permute-start.8 = (f32[4,128,128]{2,1,0:T(8,128)S(1)}, f32[4,128,128]{2,1,0:T(8,128)S(1)}, u32[]{:S(2)}, u32[]{:S(2)}) collective-permute-start(f32[4,128,128]{2,1,0:T(8,128)S(1)} %collective-permute-done.5.refs_12_), channel_id=1, source_target_pairs={{0,1},{1,0},{2,3},{3,2},{4,5},{5,4},{6,7},{7,6},{8,9},{9,8},{10,11... | collective-permute-start | bytes 786440 | tf_op jit(solution)/shard_map/ppermute | solution.py:556
  20.5 6.6 %collective-permute-start.4 = (f32[8,32,128]{2,1,0:T(8,128)S(1)}, f32[8,32,128]{2,1,0:T(8,128)}, u32[]{:S(2)}, u32[]{:S(2)}) collective-permute-start(f32[8,32,128]{2,1,0:T(8,128)S(1)} %collective-permute-done.1.refs_8_), channel_id=1, source_target_pairs={{0,1},{1,0},{2,3},{3,2},{4,5},{5,4},{6,7},{7,6},{8,9},{9,8},{10,11... | collective-permute-start | bytes 393224 | tf_op jit(solution)/shard_map/ppermute | solution.py:556
  21.9 5.2 %collective-permute-start.10 = (f32[8,32,128]{2,1,0:T(8,128)}, f32[8,32,128]{2,1,0:T(8,128)}, u32[]{:S(2)}, u32[]{:S(2)}) collective-permute-start(f32[8,32,128]{2,1,0:T(8,128)} %collective-permute-done.7.refs_14_), channel_id=1, source_target_pairs={{0,1},{1,0},{2,3},{3,2},{4,5},{5,4},{6,7},{7,6},{8,9},{9,8},{10,11... | collective-permute-start | bytes 393224 | tf_op jit(solution)/shard_map/ppermute | solution.py:556
  21.9 0.7 copy-start.9
  22.6 4.6 %collective-permute-start.9 = (f32[8,32,128]{2,1,0:T(8,128)}, f32[8,32,128]{2,1,0:T(8,128)}, u32[]{:S(2)}, u32[]{:S(2)}) collective-permute-start(f32[8,32,128]{2,1,0:T(8,128)} %collective-permute-done.6.refs_13_), channel_id=1, source_target_pairs={{0,1},{1,0},{2,3},{3,2},{4,5},{5,4},{6,7},{7,6},{8,9},{9,8},{10,11... | collective-permute-start | bytes 393224 | tf_op jit(solution)/shard_map/ppermute | solution.py:556
  27.2 0.7 copy-start.5
  27.9 0.9 %copy-start.6 = (f32[4,128,128]{2,1,0:T(8,128)S(1)}, f32[4,128,128]{2,1,0:T(8,128)}, u32[]{:S(2)}) copy-start(f32[4,128,128]{2,1,0:T(8,128)} %get-tuple-element.12.refs_6_) | copy-start | bytes 786436
  28.8 0.9 %copy-start.8 = (f32[8,32,128]{2,1,0:T(8,128)S(1)}, f32[8,32,128]{2,1,0:T(8,128)}, u32[]{:S(2)}) copy-start(f32[8,32,128]{2,1,0:T(8,128)} %copy-done.7) | copy-start | bytes 393220
  29.7 0.9 %copy-start.10 = (f32[8,32,128]{2,1,0:T(8,128)S(1)}, f32[8,32,128]{2,1,0:T(8,128)}, u32[]{:S(2)}) copy-start(f32[8,32,128]{2,1,0:T(8,128)} %copy-done.9) | copy-start | bytes 393220
  43.7 14.6 %collective-permute-start.11 = (f32[2,3,128,128]{3,2,1,0:T(8,128)S(1)}, f32[2,3,128,128]{3,2,1,0:T(8,128)S(1)}, u32[]{:S(2)}, u32[]{:S(2)}) collective-permute-start(f32[2,3,128,128]{3,2,1,0:T(8,128)S(1)} %get-tuple-element.15), channel_id=1, source_target_pairs={{0,1},{1,0},{2,3},{3,2},{4,5},{5,4},{6,7},{7,6},{8,9},{9,8},{10,11... | collective-permute-start | bytes 1179656 | tf_op jit(solution)/shard_map/ppermute | solution.py:556
  43.8 14.5 %collective-permute-start.12 = (f32[2,3,128,128]{3,2,1,0:T(8,128)S(1)}, f32[2,3,128,128]{3,2,1,0:T(8,128)S(1)}, u32[]{:S(2)}, u32[]{:S(2)}) collective-permute-start(f32[2,3,128,128]{3,2,1,0:T(8,128)S(1)} %get-tuple-element.16), channel_id=1, source_target_pairs={{0,2},{1,3},{2,0},{3,1},{4,6},{5,7},{6,4},{7,5},{8,10},{9,11},{10,... | collective-permute-start | bytes 1179656 | tf_op jit(solution)/shard_map/ppermute | solution.py:556
  43.8 19.4 %collective-permute-start.13 = (f32[2,3,128,128]{3,2,1,0:T(8,128)S(1)}, f32[2,3,128,128]{3,2,1,0:T(8,128)S(1)}, u32[]{:S(2)}, u32[]{:S(2)}) collective-permute-start(f32[2,3,128,128]{3,2,1,0:T(8,128)S(1)} %get-tuple-element.17), channel_id=1, source_target_pairs={{0,3},{1,2},{2,1},{3,0},{4,7},{5,6},{6,5},{7,4},{8,11},{9,10},{10,... | collective-permute-start | bytes 1179656 | tf_op jit(solution)/shard_map/ppermute | solution.py:556
  58.2 5.0 %copy-start.11 = (f32[2,3,128,128]{3,2,1,0:T(8,128)}, f32[2,3,128,128]{3,2,1,0:T(8,128)S(1)}, u32[]{:S(2)}) copy-start(f32[2,3,128,128]{3,2,1,0:T(8,128)S(1)} %collective-permute-done.11.refs_1_) | copy-start | bytes 1179652
  58.3 5.0 %copy-start.12 = (f32[2,3,128,128]{3,2,1,0:T(8,128)}, f32[2,3,128,128]{3,2,1,0:T(8,128)S(1)}, u32[]{:S(2)}) copy-start(f32[2,3,128,128]{3,2,1,0:T(8,128)S(1)} %collective-permute-done.12.refs_2_) | copy-start | bytes 1179652
  63.3 0.8 copy-start.13

commit v2 on v1

v2 whole, which is shorter than its diff:
```python
import functools
import math

import jax
import jax.numpy as jnp
from jax import lax
from jax.experimental import pallas as pl
from jax.experimental.pallas import tpu as pltpu
from jax.sharding import PartitionSpec as P

STEPS = 6
GRAV = 9.81
STEP_TIME = 0.5
SPACING = 5.0
RATE = 0.1
DEPTH_FLOOR = 0.3

FIELDS = 5
HALO = STEPS
PAIR = 2 * HALO
PACK_ROWS = 32
SIDE = 128
TOP = 16
ROWS = SIDE + 32
LO = 8
HI = SIDE + 24
CHUNK = 24
NT = 4
GROUP = SIDE // NT
CLOSED = 1e30
POWER = -(7.0 / 3.0) / math.log(2.0)

ENTRY = 32
NEAR = {"w": 0, "e": 1, "n": 2, "s": 3, "nw": 4, "ne": 5, "sw": 6, "se": 7}
STEP_TO = ((0, -1), (0, 1), (-1, 0), (1, 0), (-1, -1), (-1, 1), (1, -1), (1, 1))
LEAVE, STAY, RECEIVE = 0, NT * ENTRY, 2 * NT * ENTRY

SMEM = pltpu.SMEM
VMEM = pltpu.VMEM
ANY = pl.ANY


def lane_index():
    return lax.broadcasted_iota(jnp.int32, (1, SIDE), 1)


def index_kernel(
    shape, pos_ref, before_ref, after_ref, wet_ref, table, inv_before, inv_after, count
):
    cols, subs, tile_count, total = shape
    lanes = cols * subs
    row_tiles = lanes * tile_count
    tile_rows = total // row_tiles
    my_row, my_col, my_sub = pos_ref[0], pos_ref[1], pos_ref[2]
    me = my_row * lanes + my_col * subs + my_sub

    def invert(s, carry):
        for u in range(8):
            inv_before[before_ref[s * 8 + u]] = s * 8 + u
            inv_after[after_ref[s * 8 + u]] = s * 8 + u
        return carry

    lax.fori_loop(0, total // 8, invert, 0)
    for i in range(2 * NT):
        table[i * ENTRY] = 0
    for i in range(lanes * 2):
        table[RECEIVE + i] = -1
    for i in range(lanes + 1):
        count[i] = 0

    def modulo(value, size):
        return lax.rem(value + size, size)

    def entry(base, tile, source, target):
        table[base] = 1
        table[base + 1] = jnp.where(wet_ref[tile] == 1, 1, 0)
        table[base + 2] = source
        table[base + 3] = target
        row, col = lax.div(tile, row_tiles), lax.rem(tile, row_tiles)
        for n, (dr, dc) in enumerate(STEP_TO):
            r, c = row + dr, col + dc
            there = (r >= 0) & (r < tile_rows) & (c >= 0) & (c < row_tiles)
            near = jnp.where(there, tile + (dr * row_tiles + dc), tile)
            at = inv_before[near]
            lane = lax.rem(lax.div(at, tile_count), lanes)
            rel = modulo(my_col - lax.div(lane, subs), cols) * subs + modulo(
                my_sub - lax.rem(lane, subs), subs
            )
            table[base + 4 + 3 * n] = jnp.where(there & (wet_ref[near] == 1), 1, 0)
            table[base + 5 + 3 * n] = rel
            table[base + 6 + 3 * n] = lax.rem(at, tile_count)

    def own(s, carry):
        tile = before_ref[me * tile_count + s]
        device = lax.div(inv_after[tile], tile_count)
        stays = device == me

        @pl.when(stays)
        def _():
            at = jnp.minimum(count[0], NT - 1)
            count[0] = at + 1
            entry(STAY + at * ENTRY, tile, s, s)

        @pl.when(jnp.logical_not(stays))
        def _():
            lane = lax.rem(device, lanes)
            rel = modulo(lax.div(lane, subs) - my_col, cols) * subs + modulo(
                lax.rem(lane, subs) - my_sub, subs
            )
            place = jnp.minimum(count[rel], 1)
            count[rel] = place + 1
            at = jnp.minimum(count[lanes], NT - 1)
            count[lanes] = at + 1
            entry(LEAVE + at * ENTRY, tile, s, rel * 2 + place)

        return carry

    lax.fori_loop(0, tile_count, own, 0)

    for rel in range(1, lanes):
        col = modulo(my_col - rel // subs, cols)
        sub = modulo(my_sub - rel % subs, subs)
        device = my_row * lanes + col * subs + sub

        def arriving(s, found):
            at = inv_after[before_ref[device * tile_count + s]]
            mine = lax.div(at, tile_count) == me

            @pl.when(mine)
            def _():
                table[RECEIVE + rel * 2 + jnp.minimum(found, 1)] = lax.rem(at, tile_count)

            return found + jnp.where(mine, 1, 0)

        lax.fori_loop(0, tile_count, arriving, jnp.int32(0))


def make_table(shape, position, before, after, wet):
    cols, subs, _, total = shape
    size = RECEIVE + 2 * cols * subs
    return pl.pallas_call(
        functools.partial(index_kernel, shape),
        name="index_table",
        out_shape=jax.ShapeDtypeStruct((size,), jnp.int32),
        in_specs=[pl.BlockSpec(memory_space=SMEM)] * 4,
        out_specs=pl.BlockSpec(memory_space=SMEM),
        scratch_shapes=[
            SMEM((total,), jnp.int32),
            SMEM((total,), jnp.int32),
            SMEM((cols * subs + 1,), jnp.int32),
        ],
    )(position, before, after, wet)


def in_vmem(array):
    return pltpu.with_memory_space_constraint(array, VMEM)


def vmem_specs(count):
    return [pl.BlockSpec(memory_space=VMEM)] * count


def pack_kernel(*refs):
    fields = refs[:FIELDS]
    columns, first, last = refs[FIELDS:]
    lane = lane_index()
    for t in range(fields[0].shape[0]):
        packed = jnp.zeros((SIDE, SIDE), jnp.float32) if t % 2 == 0 else packed
        for f in range(FIELDS):
            at = PAIR * (t % 2 * FIELDS + f)
            moved = pltpu.roll(fields[f][t], at + HALO, 1)
            packed = jnp.where((lane >= at) & (lane < at + PAIR), moved, packed)
            first[t, HALO * f : HALO * (f + 1), :] = fields[f][t, :HALO, :]
            last[t, 2 + HALO * f : 2 + HALO * (f + 1), :] = fields[f][t, SIDE - HALO :, :]
        first[t, FIELDS * HALO :, :] = jnp.zeros((2, SIDE), jnp.float32)
        last[t, :2, :] = jnp.zeros((2, SIDE), jnp.float32)
        if t % 2:
            columns[t // 2] = packed


def pack_edges(fields, tile_count):
    rows = VMEM((tile_count, PACK_ROWS, SIDE), jnp.float32)
    return pl.pallas_call(
        pack_kernel,
        name="pack_edges",
        out_shape=(VMEM((tile_count // 2, SIDE, SIDE), jnp.float32), rows, rows),
        in_specs=vmem_specs(FIELDS),
        out_specs=tuple(vmem_specs(3)),
    )(*fields)


def face(flow, level, level_next, ground, friction):
    wetted = jnp.maximum(level, level_next) - ground
    drive = (GRAV * STEP_TIME / SPACING) * jnp.maximum(wetted, 0.0) * (level_next - level)
    power = jnp.exp2(POWER * jnp.log(jnp.maximum(wetted, DEPTH_FLOOR)))
    return (flow - drive) / (1.0 + friction * jnp.abs(flow) * power)


def chunks():
    for r in range(LO, HI, CHUNK):
        yield r, min(CHUNK, HI - r)


def row_bands(r, rows, above, middle, below):
    row = r + lax.broadcasted_iota(jnp.int32, (rows, 1), 0)
    return jnp.where(row < TOP, above, jnp.where(row < TOP + SIDE, middle, below))


def assemble(table, base, i, slot, fields, stacks, block, strip):
    halo_cols, halo_above, halo_below = stacks
    lane = lane_index()
    at = GROUP * i

    def near(name):
        place = base + 5 + 3 * NEAR[name]
        return table[place], table[place + 1]

    def inside(lo, hi):
        return (lane >= at + lo) & (lane < at + hi)

    west, east = near("w"), near("e")
    for f in range(FIELDS):
        rows = pl.ds(HALO * f, 8)

        def ends(halo, middle, left, right, out):
            mid = halo[middle[0], middle[1], rows, :]
            block[f][i, out : out + 8, :] = mid
            lower = jnp.where(lane < SIDE // 2, mid, halo[left[0], left[1], rows, :])
            upper = jnp.where(lane < SIDE // 2, halo[right[0], right[1], rows, :], mid)
            value = jnp.where(
                inside(0, 16),
                pltpu.roll(lower, (at + 8) % SIDE, 1),
                pltpu.roll(upper, (at + 24) % SIDE, 1),
            )
            if i:
                value = jnp.where(inside(0, GROUP), value, strip[f][out : out + 8, :])
            strip[f][out : out + 8, :] = value

        ends(halo_above, near("n"), near("nw"), near("ne"), LO)
        ends(halo_below, near("s"), near("sw"), near("se"), TOP + SIDE)

        def shifted(place, goal):
            source = PAIR * (lax.rem(place[1], 2) * FIELDS + f)
            shift = lax.rem(goal - source + 2 * SIDE, SIDE)
            return pltpu.roll(halo_cols[place[0], lax.div(place[1], 2)], shift, 1)

        core = fields[f][slot]
        block[f][i, TOP : TOP + SIDE, :] = core
        value = shifted(west, at + 2)
        if i:
            value = jnp.where(inside(0, 8), value, strip[f][TOP : TOP + SIDE, :])
        value = jnp.where(inside(8, 16), pltpu.roll(core, (at + 8) % SIDE, 1), value)
        value = jnp.where(inside(16, 24), pltpu.roll(core, (at + 24) % SIDE, 1), value)
        value = jnp.where(inside(24, GROUP), shifted(east, at + 24 - HALO), value)
        strip[f][TOP : TOP + SIDE, :] = value


def prepare_strip(near_wet, strip, ground_x, ground_y):
    level, flow_x, flow_y, ground, friction = strip
    lane = lane_index()

    def lane_wet(center, left, right):
        value = jnp.zeros((1, SIDE), jnp.int32)
        for i in range(NT):
            at = GROUP * i
            middle = near_wet(i, center) if center else 1
            sides = jnp.where(
                lane < at + 8,
                near_wet(i, left),
                jnp.where(lane < at + 24, middle, near_wet(i, right)),
            )
            value = jnp.where((lane >= at) & (lane < at + GROUP), sides, value)
        return value

    bands = (lane_wet("n", "nw", "ne"), lane_wet(None, "w", "e"), lane_wet("s", "sw", "se"))
    for r, rows in chunks():
        at, south = pl.ds(r, rows), pl.ds(r + 1, rows)
        z = ground[at, :]
        here, next_row = row_bands(r, rows, *bands), row_bands(r + 1, rows, *bands)
        open_x = (here == 1) & (pltpu.roll(here, SIDE - 1, 1) == 1)
        open_y = (here == 1) & (next_row == 1)
        z_east = pltpu.roll(z, SIDE - 1, 1)
        ground_x[at, :] = jnp.where(open_x, jnp.maximum(z, z_east), CLOSED)
        ground_y[at, :] = jnp.where(open_y, jnp.maximum(z, ground[south, :]), CLOSED)
        flow_x[at, :] = jnp.where(open_x, flow_x[at, :], 0.0)
        flow_y[at, :] = jnp.where(open_y, flow_y[at, :], 0.0)
        friction[at, :] = (GRAV * STEP_TIME) * friction[at, :] * friction[at, :]
        level[at, :] = level[at, :] + z


def prepare_tile(near_wet, i, block, ground_x, ground_y, strip_ground):
    level, flow_x, flow_y, ground, friction = block
    lane = lane_index()
    last = lane == SIDE - 1
    n, e, s = near_wet(i, "n"), near_wet(i, "e"), near_wet(i, "s")
    bands = (
        jnp.where(last, n * near_wet(i, "ne"), n),
        jnp.where(last, e, 1),
        jnp.where(last, s * near_wet(i, "se"), s),
    )
    for r, rows in chunks():
        at, south = pl.ds(r, rows), pl.ds(r + 1, rows)
        z = ground[i, at, :]
        z_east = jnp.where(
            last, pltpu.roll(strip_ground[at, :], to_east(i), 1), pltpu.roll(z, SIDE - 1, 1)
        )
        open_x = row_bands(r, rows, *bands) == 1
        open_y = (row_bands(r + 1, rows, n, 1, s) == 1) & (row_bands(r, rows, n, 1, s) == 1)
        ground_x[i, at, :] = jnp.where(open_x, jnp.maximum(z, z_east), CLOSED)
        ground_y[i, at, :] = jnp.where(open_y, jnp.maximum(z, ground[i, south, :]), CLOSED)
        flow_x[i, at, :] = jnp.where(open_x, flow_x[i, at, :], 0.0)
        flow_y[i, at, :] = jnp.where(open_y, flow_y[i, at, :], 0.0)
        friction[i, at, :] = (GRAV * STEP_TIME) * friction[i, at, :] * friction[i, at, :]
        level[i, at, :] = level[i, at, :] + z


def to_east(i):
    return (SIDE - 1 - GROUP * i - 24) % SIDE


def to_west(i):
    return (SIDE - GROUP * i - 7) % SIDE


def advance_kernel(lanes, base, leaving, *refs):
    table = refs[0]
    fields = refs[1 : 1 + FIELDS]
    halos = refs[1 + FIELDS : 1 + FIELDS + 3 * lanes]
    n_out = lanes - 1 if leaving else 3
    outs = refs[1 + FIELDS + 3 * lanes : 1 + FIELDS + 3 * lanes + n_out]
    (
        halo_cols, halo_above, halo_below,
        level, flow_x, flow_y, ground, friction, ground_x, ground_y,
        s_level, s_flow_x, s_flow_y, s_ground, s_friction, s_ground_x, s_ground_y,
        sem_out,
    ) = refs[1 + FIELDS + 3 * lanes + n_out :]
    block = (level, flow_x, flow_y, ground, friction)
    strip = (s_level, s_flow_x, s_flow_y, s_ground, s_friction)
    stacks = (halo_cols, halo_above, halo_below)
    lane = lane_index()
    last, first = lane == SIDE - 1, lane == 0
    core = pl.ds(TOP, SIDE)

    def entry(i):
        at = base + i * ENTRY
        return table[at + 1], table[at + 2], table[at + 3]

    def near_wet(i, name):
        return table[base + i * ENTRY + 4 + 3 * NEAR[name]]

    for k in range(lanes):
        for n in range(3):
            stacks[n][k] = halos[3 * k + n][...]
    for i in range(NT):
        assemble(table, base + i * ENTRY, i, entry(i)[1], fields, stacks, block, strip)
    prepare_strip(near_wet, strip, s_ground_x, s_ground_y)
    for i in range(NT):
        prepare_tile(near_wet, i, block, ground_x, ground_y, s_ground)

    def step(_, carry):
        for r, rows in chunks():
            at, south = pl.ds(r, rows), pl.ds(r + 1, rows)
            e, c = s_level[at, :], s_friction[at, :]
            e_east = pltpu.roll(e, SIDE - 1, 1)
            s_flow_x[at, :] = face(s_flow_x[at, :], e, e_east, s_ground_x[at, :], c)
            s_flow_y[at, :] = face(s_flow_y[at, :], e, s_level[south, :], s_ground_y[at, :], c)
        for i in range(NT):
            for r, rows in chunks():
                at, south = pl.ds(r, rows), pl.ds(r + 1, rows)
                e, c = level[i, at, :], friction[i, at, :]
                e_east = jnp.where(
                    last, pltpu.roll(s_level[at, :], to_east(i), 1), pltpu.roll(e, SIDE - 1, 1)
                )
                flow_x[i, at, :] = face(flow_x[i, at, :], e, e_east, ground_x[i, at, :], c)
                flow_y[i, at, :] = face(
                    flow_y[i, at, :], e, level[i, south, :], ground_y[i, at, :], c
                )
        for r, rows in chunks():
            at, north = pl.ds(r, rows), pl.ds(r - 1, rows)
            qx = s_flow_x[at, :]
            s_level[at, :] = s_level[at, :] + RATE * (
                (pltpu.roll(qx, 1, 1) - qx) + (s_flow_y[north, :] - s_flow_y[at, :])
            )
        for i in range(NT):
            for r, rows in chunks():
                at, north = pl.ds(r, rows), pl.ds(r - 1, rows)
                qx = flow_x[i, at, :]
                qx_west = jnp.where(
                    first, pltpu.roll(s_flow_x[at, :], to_west(i), 1), pltpu.roll(qx, 1, 1)
                )
                level[i, at, :] = level[i, at, :] + RATE * (
                    (qx_west - qx) + (flow_y[i, north, :] - flow_y[i, at, :])
                )
        return carry

    lax.fori_loop(0, STEPS, step, 0)

    for i in range(NT):
        wet, slot, _ = entry(i)
        depth = level[i, core, :] - ground[i, core, :]
        level[i, core, :] = jnp.where(wet == 1, depth, fields[0][slot])
        flow_x[i, core, :] = jnp.where(wet == 1, flow_x[i, core, :], fields[1][slot])
        flow_y[i, core, :] = jnp.where(wet == 1, flow_y[i, core, :], fields[2][slot])

    results = (level, flow_x, flow_y)
    if leaving:
        for i in range(NT):
            target = entry(i)[2]
            for k in range(1, lanes):
                @pl.when(lax.div(target, 2) == k)
                def _():
                    for f in range(3):
                        outs[k - 1][lax.rem(target, 2), f] = results[f][i, core, :]

    else:
        copies = [
            pltpu.make_async_copy(
                results[f].at[i, core, :], outs[f].at[entry(i)[2]], sem_out.at[i, f]
            )
            for i in range(NT)
            for f in range(3)
        ]
        for copy in copies:
            copy.start()
        for copy in copies:
            copy.wait()


def advance(table, fields, halos, base, leaving):
    lanes = len(halos)
    if leaving:
        outs = (VMEM((2, 3, SIDE, SIDE), jnp.float32),) * (lanes - 1)
        out_specs = vmem_specs(lanes - 1)
    else:
        outs = (jax.ShapeDtypeStruct(fields[0].shape, jnp.float32),) * 3
        out_specs = [pl.BlockSpec(memory_space=ANY)] * 3
    flat = [array for group in halos for array in group]
    block = VMEM((NT, ROWS, SIDE), jnp.float32)
    strip = VMEM((ROWS, SIDE), jnp.float32)
    cells = (NT + 1) * ROWS * SIDE * STEPS
    return pl.pallas_call(
        functools.partial(advance_kernel, lanes, base, leaving),
        name="advance_leaving" if leaving else "advance_staying",
        out_shape=outs,
        in_specs=[pl.BlockSpec(memory_space=SMEM)] + vmem_specs(FIELDS + 3 * lanes),
        out_specs=tuple(out_specs),
        scratch_shapes=[VMEM((lanes,) + halos[0][n].shape, jnp.float32) for n in range(3)]
        + [block] * 7
        + [strip] * 7
        + [pltpu.SemaphoreType.DMA((NT, 3))],
        compiler_params=pltpu.CompilerParams(vmem_limit_bytes=16 * 1024 * 1024),
        cost_estimate=pl.CostEstimate(
            flops=60 * cells, bytes_accessed=8 * NT * SIDE * SIDE * 4, transcendentals=6 * cells
        ),
    )(table, *fields, *flat)


def place_kernel(lanes, *refs):
    table = refs[0]
    received = refs[1:lanes]
    outs = refs[lanes + 3 : lanes + 6]
    sem = refs[lanes + 6]

    def each(act):
        for k in range(1, lanes):
            for j in range(2):
                slot = table[RECEIVE + 2 * k + j]

                @pl.when(slot >= 0)
                def _():
                    for f in range(3):
                        act(
                            pltpu.make_async_copy(
                                received[k - 1].at[j, f], outs[f].at[slot], sem.at[k, j, f]
                            )
                        )

    each(lambda copy: copy.start())
    each(lambda copy: copy.wait())


def place(table, received, partial_outs):
    lanes = len(received) + 1
    return pl.pallas_call(
        functools.partial(place_kernel, lanes),
        name="place_arrivals",
        out_shape=tuple(jax.ShapeDtypeStruct(o.shape, o.dtype) for o in partial_outs),
        in_specs=[pl.BlockSpec(memory_space=SMEM)]
        + vmem_specs(lanes - 1)
        + [pl.BlockSpec(memory_space=ANY)] * 3,
        out_specs=tuple(pl.BlockSpec(memory_space=ANY) for _ in partial_outs),
        scratch_shapes=[pltpu.SemaphoreType.DMA((lanes, 2, 3))],
        input_output_aliases={lanes: 0, lanes + 1: 1, lanes + 2: 2},
    )(table, *received, *partial_outs)


def shift_lanes(array, col_shift, sub_shift):
    cols, subs = lax.axis_size("col"), lax.axis_size("sub")
    pairs = [
        (c * subs + s, ((c + col_shift) % cols) * subs + (s + sub_shift) % subs)
        for c in range(cols)
        for s in range(subs)
    ]
    return lax.ppermute(array, ("col", "sub"), pairs)


def spread(array):
    cols, subs = lax.axis_size("col"), lax.axis_size("sub")
    out = []
    for c in range(cols):
        part = array if c == 0 else shift_lanes(array, c, 0)
        out.append(part)
        for s in range(1, subs):
            out.append(shift_lanes(part, 0, s))
    return out


def shards(
    water_depth, flow_east, flow_south, bed_level, manning_n, placed_before, placed_after, wet_tiles
):
    cols, subs, rows = lax.axis_size("col"), lax.axis_size("sub"), lax.axis_size("row")
    tile_count = water_depth.shape[0]
    fields = [
        in_vmem(field) for field in (water_depth, flow_east, flow_south, bed_level, manning_n)
    ]
    position = jnp.stack([lax.axis_index("row"), lax.axis_index("col"), lax.axis_index("sub")])
    columns, first, last = pack_edges(fields, tile_count)
    above = lax.ppermute(last, "row", [(i, i + 1) for i in range(rows - 1)])
    below = lax.ppermute(first, "row", [(i + 1, i) for i in range(rows - 1)])
    table = make_table(
        (cols, subs, tile_count, placed_before.shape[0]),
        position.astype(jnp.int32),
        placed_before,
        placed_after,
        wet_tiles,
    )
    above, below, table = lax.optimization_barrier((above, below, table))
    halos = [
        tuple(in_vmem(part) for part in group)
        for group in zip(spread(columns), spread(above), spread(below))
    ]
    leaving = advance(table, fields, halos, LEAVE, True)
    received = [
        in_vmem(shift_lanes(leaving[k - 1], k // subs, k % subs)) for k in range(1, cols * subs)
    ]
    staying = advance(table, fields, halos, STAY, False)
    return place(table, received, staying)


def solution(mesh):
    tiles = P(("basin", "row", "col", "sub"), None, None)
    return jax.shard_map(
        shards,
        mesh=mesh,
        in_specs=(tiles,) * FIELDS + (P("basin"),) * 3,
        out_specs=(tiles,) * 3,
        check_vma=False,
    )
```

time: 89.9 us -> 58.8 us (0.65)
  Pallas kernels: 59.1 us -> 19.6 us
  local copies, waits for them, and re-layouts: 5.51 us -> 10.4 us
  waiting for transfers between devices: 11.3 us -> 13.9 us
    pallas_call x1, Pallas kernels: 25.8 us -> 1.77 us  [place(): pl.pallas_call(functools.partial(place_kernel, lanes), name='place_arriva...]
    pallas_call x2, Pallas kernels: 25.7 us -> 13.1 us  [advance(): pl.pallas_call(functools.partial(advance_kernel, lanes, base, leaving), n...]
    unnamed x28, local copies, waits for them, and re-layouts: 5.51 us -> 10.4 us
    ppermute x12, waiting for transfers between devices: 8.82 us -> 12.4 us  [shift_lanes(): return lax.ppermute(array, ('col', 'sub'), pairs)]
    pallas_call x1, Pallas kernels: 4.19 us -> 1.35 us  [pack_edges(): pl.pallas_call(pack_kernel, name='pack_edges', out_shape=(VMEM((tile_coun...]
    ppermute x12, starting transfers between devices: 6.68 us -> 7.98 us  [shift_lanes(): return lax.ppermute(array, ('col', 'sub'), pairs)]
    ppermute x1, waiting for transfers between devices: 1.23 us -> 0.01 us  [shards(): above = lax.ppermute(last, 'row', [(i, i + 1) for i in range(rows - 1)])]
    ppermute x1, starting transfers between devices: 4.55 us -> 3.48 us  [shards(): above = lax.ppermute(last, 'row', [(i, i + 1) for i in range(rows - 1)])]
  transfers between devices with their start and end apart: 14 -> 14, of which waited for: 5 -> 7; matrix products, arithmetic and copies ran while one was open for 1% -> 1% of each run, Pallas kernels for 18% -> 18%
where the time goes in v2:
time: 58.8 us; the launch traced here: 58.1 us
  Pallas kernels  19.6 us (33%)
  waiting for transfers between devices  13.9 us (24%)
  starting transfers between devices  12.8 us (22%)
  local copies, waits for them, and re-layouts  10.4 us (18%)
  between operations  0.75 us (1%)
  other arithmetic  0.62 us (1%)
    pallas_call x2, Pallas kernels, advance(): pl.pallas_call(functools.partial(advance_kernel, lanes, base, leaving), n...  13.1 us
    ppermute x12, waiting for transfers between devices, shift_lanes(): return lax.ppermute(array, ('col', 'sub'), pairs)  12.4 us
    unnamed x28, local copies, waits for them, and re-layouts  10.4 us
    ppermute x12, starting transfers between devices, shift_lanes(): return lax.ppermute(array, ('col', 'sub'), pairs)  7.98 us
    ppermute x1, starting transfers between devices, shards(): above = lax.ppermute(last, 'row', [(i, i + 1) for i in range(rows - 1)])  3.48 us
    pallas_call x1, Pallas kernels, make_table(): pl.pallas_call(functools.partial(index_kernel, shape), name='index_table'...  3.4 us
    pallas_call x1, Pallas kernels, place(): pl.pallas_call(functools.partial(place_kernel, lanes), name='place_arriva...  1.77 us
    ppermute x1, waiting for transfers between devices, shards(): below = lax.ppermute(first, 'row', [(i + 1, i) for i in range(rows - 1)])  1.51 us
  transfers between devices with their start and end apart: 14, of which 7 were waited for; matrix products, arithmetic and copies ran while one was open for 1% of the time, Pallas kernels for 18%

profile of v2, /device:TPU:0, one launch (start us, length us, event | category | flops | bytes accessed | tf_op | source)
XLA Modules:
  0.0 58.1 jit_solution(5617183185798663302)
XLA Ops:
  0.6 0.0 copy-start
  0.6 1.0 %copy-done = f32[8,128,128]{2,1,0:T(8,128)S(1)} copy-done((f32[8,128,128]{2,1,0:T(8,128)S(1)}, f32[8,128,128]{2,1,0:T(8,128)}, u32[]{:S(2)}) %copy-start) | copy-done | bytes 524312
  1.7 0.0 copy-start.1
  1.7 1.0 %copy-done.1 = f32[8,128,128]{2,1,0:T(8,128)S(1)} copy-done((f32[8,128,128]{2,1,0:T(8,128)S(1)}, f32[8,128,128]{2,1,0:T(8,128)}, u32[]{:S(2)}) %copy-start.1) | copy-done | bytes 524312
  2.7 0.0 copy-start.2
  2.7 1.0 %copy-done.2 = f32[8,128,128]{2,1,0:T(8,128)S(1)} copy-done((f32[8,128,128]{2,1,0:T(8,128)S(1)}, f32[8,128,128]{2,1,0:T(8,128)}, u32[]{:S(2)}) %copy-start.2) | copy-done | bytes 524312
  3.8 0.0 copy-start.3
  3.8 1.0 %copy-done.3 = f32[8,128,128]{2,1,0:T(8,128)S(1)} copy-done((f32[8,128,128]{2,1,0:T(8,128)S(1)}, f32[8,128,128]{2,1,0:T(8,128)}, u32[]{:S(2)}) %copy-start.3) | copy-done | bytes 524312
  4.8 0.0 copy-start.4
  4.8 1.0 %copy-done.4 = f32[8,128,128]{2,1,0:T(8,128)S(1)} copy-done((f32[8,128,128]{2,1,0:T(8,128)S(1)}, f32[8,128,128]{2,1,0:T(8,128)}, u32[]{:S(2)}) %copy-start.4) | copy-done | bytes 524312
  5.8 1.3 %pack_edges.1 = (f32[4,128,128]{2,1,0:T(8,128)S(1)}, f32[8,32,128]{2,1,0:T(8,128)S(1)}, f32[8,32,128]{2,1,0:T(8,128)}) custom-call(f32[8,128,128]{2,1,0:T(8,128)S(1)} %copy-done, f32[8,128,128]{2,1,0:T(8,128)S(1)} %copy-done.1, f32[8,128,128]{2,1,0:T(8,128)S(1)} %copy-done.2, f32[8,128,128]{2,1,0:T(8,128)S(1)} %copy-done.3, f32[8,128,128]{2,1,0:T(8,128)S(1)} %copy-done.4), custom_call_target="tpu_custom_call" | custom-call | tf_op jit(solution)/shard_map/pack_edges/pallas_call | solution.py:183
  7.2 0.0 copy-start.8
  7.2 2.9 %collective-permute-start.5 = (f32[4,128,128]{2,1,0:T(8,128)S(1)}, f32[4,128,128]{2,1,0:T(8,128)S(1)}, u32[]{:S(2)}, u32[]{:S(2)}) collective-permute-start(f32[4,128,128]{2,1,0:T(8,128)S(1)} %get-tuple-element.18.refs_6_), channel_id=1, source_target_pairs={{0,2},{1,3},{2,0},{3,1},{4,6},{5,7},{6,4},{7,5},{8,10},{9,11},{10,... | collective-permute-start | bytes 786440 | tf_op jit(solution)/shard_map/ppermute | solution.py:504
  10.1 3.5 %collective-permute-start = (f32[8,32,128]{2,1,0:T(8,128)}, f32[8,32,128]{2,1,0:T(8,128)S(1)}, u32[]{:S(2)}, u32[]{:S(2)}) collective-permute-start(f32[8,32,128]{2,1,0:T(8,128)} %get-tuple-element.15), channel_id=1, source_target_pairs={{0,4},{4,8},{8,12},{1,5},{5,9},{9,13},{2,6},{6,10},{10,14},{3,7},{... | collective-permute-start | bytes 393224 | tf_op jit(solution)/shard_map/ppermute | solution.py:528
  13.6 1.3 %collective-permute-start.1 = (f32[8,32,128]{2,1,0:T(8,128)S(1)}, f32[8,32,128]{2,1,0:T(8,128)S(1)}, u32[]{:S(2)}, u32[]{:S(2)}) collective-permute-start(f32[8,32,128]{2,1,0:T(8,128)S(1)} %get-tuple-element.16), channel_id=1, source_target_pairs={{4,0},{8,4},{12,8},{5,1},{9,5},{13,9},{6,2},{10,6},{14,10},{7,3},{... | collective-permute-start | bytes 393224 | tf_op jit(solution)/shard_map/ppermute | solution.py:529
  14.9 0.6 %pad_add_fusion.pos_ref = s32[3]{0:T(128)} fusion(s32[1]{0:T(128)} %bitcast.2, s32[1]{0:T(128)} %bitcast.1, s32[1]{0:T(128)} %bitcast), kind=kLoop, calls=%fused_computation | loop fusion | flops 6 | bytes 24 | tf_op jit(solution)/shard_map/stack | solution.py:526
  15.5 3.4 %index_table.1.refs_0_ = s32[264]{0:T(512)} custom-call(s32[3]{0:T(128)} %pad_add_fusion.pos_ref, s32[128]{0:T(128)} %before_ref.1, s32[128]{0:T(128)} %after_ref.1, s32[128]{0:T(128)} %wet_ref.1), custom_call_target="tpu_custom_call" | custom-call | tf_op jit(solution)/shard_map/index_table/pallas_call | solution.py:141
  19.0 0.0 collective-permute-done.refs_7_
  19.0 1.5 %collective-permute-done.1.refs_8_ = f32[8,32,128]{2,1,0:T(8,128)S(1)} collective-permute-done((f32[8,32,128]{2,1,0:T(8,128)S(1)}, f32[8,32,128]{2,1,0:T(8,128)S(1)}, u32[]{:S(2)}, u32[]{:S(2)}) %collective-permute-start.1) | collective-permute-done | bytes 131104 | tf_op jit(solution)/shard_map/ppermute | solution.py:529
  20.5 0.0 copy-start.12
  20.5 0.5 collective-permute-start.7
  21.0 1.5 %collective-permute-start.6 = (f32[8,32,128]{2,1,0:T(8,128)S(1)}, f32[8,32,128]{2,1,0:T(8,128)S(1)}, u32[]{:S(2)}, u32[]{:S(2)}) collective-permute-start(f32[8,32,128]{2,1,0:T(8,128)S(1)} %collective-permute-done.refs_7_), channel_id=1, source_target_pairs={{0,2},{1,3},{2,0},{3,1},{4,6},{5,7},{6,4},{7,5},{8,10},{9,11},{10,... | collective-permute-start | bytes 393224 | tf_op jit(solution)/shard_map/ppermute | solution.py:504
  22.5 0.0 collective-permute-start.2
  22.5 0.5 collective-permute-start.3
  23.0 0.0 collective-permute-done.5.refs_12_
  23.0 0.0 copy-start.10
  23.0 0.1 collective-permute-start.8
  23.1 2.4 %collective-permute-done.7.refs_14_ = f32[8,32,128]{2,1,0:T(8,128)S(1)} collective-permute-done((f32[8,32,128]{2,1,0:T(8,128)S(1)}, f32[8,32,128]{2,1,0:T(8,128)S(1)}, u32[]{:S(2)}, u32[]{:S(2)}) %collective-permute-start.7) | collective-permute-done | bytes 131104 | tf_op jit(solution)/shard_map/ppermute | solution.py:504
  25.4 0.0 collective-permute-start.4
  25.5 1.4 %collective-permute-done.6.refs_13_ = f32[8,32,128]{2,1,0:T(8,128)S(1)} collective-permute-done((f32[8,32,128]{2,1,0:T(8,128)S(1)}, f32[8,32,128]{2,1,0:T(8,128)S(1)}, u32[]{:S(2)}, u32[]{:S(2)}) %collective-permute-start.6) | collective-permute-done | bytes 131104 | tf_op jit(solution)/shard_map/ppermute | solution.py:504
  26.9 0.0 collective-permute-start.10
  26.9 0.0 collective-permute-done.3.refs_10_
  26.9 0.5 collective-permute-start.9
  27.4 0.0 collective-permute-done.4.refs_11_
  27.4 0.0 collective-permute-done.2.refs_9_
  27.4 0.8 %collective-permute-done.10.refs_17_ = f32[8,32,128]{2,1,0:T(8,128)S(1)} collective-permute-done((f32[8,32,128]{2,1,0:T(8,128)S(1)}, f32[8,32,128]{2,1,0:T(8,128)S(1)}, u32[]{:S(2)}, u32[]{:S(2)}) %collective-permute-start.10) | collective-permute-done | bytes 131104 | tf_op jit(solution)/shard_map/ppermute | solution.py:504
  28.2 0.2 collective-permute-done.9.refs_16_
  28.4 0.0 collective-permute-done.8.refs_15_
  28.4 0.0 copy-start.7
  28.4 0.7 %copy-done.7 = s32[264]{0:T(512)S(1)} copy-done((s32[264]{0:T(512)S(1)}, s32[264]{0:T(512)}, u32[]{:S(2)}) %copy-start.7) | copy-done | bytes 1080
  29.1 6.2 %advance_leaving.1 = (f32[2,3,128,128]{3,2,1,0:T(8,128)S(1)}, f32[2,3,128,128]{3,2,1,0:T(8,128)S(1)}, f32[2,3,128,128]{3,2,1,0:T(8,128)S(1)}) custom-call(s32[264]{0:T(512)S(1)} %copy-done.7, f32[8,128,128]{2,1,0:T(8,128)S(1)} %copy-done, f32[8,128,128]{2,1,0:T(8,128)S(1)} %copy-done.1, f32[8,128,128]{2,1,0:T(8,128)S(1)} %copy-done.2, ...), custom_call_target="tpu_custom_call" | custom-call | flops 36864000 | bytes 2097152 | tf_op jit(solution)/shard_map/advance_leaving/pallas_call | solution.py:441
  35.3 0.0 copy-done.8
  35.3 0.0 copy-done.12
  35.3 0.0 copy-done.10
  35.3 0.4 collective-permute-start.11
  35.7 0.6 %collective-permute-start.12 = (f32[2,3,128,128]{3,2,1,0:T(8,128)S(1)}, f32[2,3,128,128]{3,2,1,0:T(8,128)S(1)}, u32[]{:S(2)}, u32[]{:S(2)}) collective-permute-start(f32[2,3,128,128]{3,2,1,0:T(8,128)S(1)} %get-tuple-element.22), channel_id=1, source_target_pairs={{0,2},{1,3},{2,0},{3,1},{4,6},{5,7},{6,4},{7,5},{8,10},{9,11},{10,... | collective-permute-start | bytes 1179656 | tf_op jit(solution)/shard_map/ppermute | solution.py:504
  36.3 0.9 %collective-permute-start.13 = (f32[2,3,128,128]{3,2,1,0:T(8,128)S(1)}, f32[2,3,128,128]{3,2,1,0:T(8,128)S(1)}, u32[]{:S(2)}, u32[]{:S(2)}) collective-permute-start(f32[2,3,128,128]{3,2,1,0:T(8,128)S(1)} %get-tuple-element.23), channel_id=1, source_target_pairs={{0,3},{1,2},{2,1},{3,0},{4,7},{5,6},{6,5},{7,4},{8,11},{9,10},{10,... | collective-permute-start | bytes 1179656 | tf_op jit(solution)/shard_map/ppermute | solution.py:504
  37.2 0.0 copy-start.9
  37.2 0.9 %copy-done.9 = f32[4,128,128]{2,1,0:T(8,128)S(1)} copy-done((f32[4,128,128]{2,1,0:T(8,128)S(1)}, f32[4,128,128]{2,1,0:T(8,128)}, u32[]{:S(2)}) %copy-start.9) | copy-done | bytes 262168
  38.2 0.0 copy-start.11
  38.2 0.9 %copy-done.11 = f32[4,128,128]{2,1,0:T(8,128)S(1)} copy-done((f32[4,128,128]{2,1,0:T(8,128)S(1)}, f32[4,128,128]{2,1,0:T(8,128)}, u32[]{:S(2)}) %copy-start.11) | copy-done | bytes 262168
  39.1 0.0 copy-start.13
  39.1 0.9 %copy-done.13 = f32[8,32,128]{2,1,0:T(8,128)S(1)} copy-done((f32[8,32,128]{2,1,0:T(8,128)S(1)}, f32[8,32,128]{2,1,0:T(8,128)}, u32[]{:S(2)}) %copy-start.13) | copy-done | bytes 131096
  40.0 6.9 %advance_staying.1 = (f32[8,128,128]{2,1,0:T(8,128)}, f32[8,128,128]{2,1,0:T(8,128)}, f32[8,128,128]{2,1,0:T(8,128)}) custom-call(s32[264]{0:T(512)S(1)} %copy-done.7, f32[8,128,128]{2,1,0:T(8,128)S(1)} %copy-done, f32[8,128,128]{2,1,0:T(8,128)S(1)} %copy-done.1, f32[8,128,128]{2,1,0:T(8,128)S(1)} %copy-done.2, f32[8,128,128]{2,1,0:T(8,128)S(1)} %copy-done.3, ...), custom_call_target="tpu_custom_call" | custom-call | flops 36864000 | bytes 2097152 | tf_op jit(solution)/shard_map/advance_staying/pallas_call | solution.py:441
  46.9 0.0 collective-permute-done.11.refs_1_
  46.9 0.7 %collective-permute-done.12.refs_2_ = f32[2,3,128,128]{3,2,1,0:T(8,128)S(1)} collective-permute-done((f32[2,3,128,128]{3,2,1,0:T(8,128)S(1)}, f32[2,3,128,128]{3,2,1,0:T(8,128)S(1)}, u32[]{:S(2)}, u32[]{:S(2)}) %collective-permute-start.12) | collective-permute-done | bytes 393248 | tf_op jit(solution)/shard_map/ppermute | solution.py:504
  47.6 6.9 %collective-permute-done.13.refs_3_ = f32[2,3,128,128]{3,2,1,0:T(8,128)S(1)} collective-permute-done((f32[2,3,128,128]{3,2,1,0:T(8,128)S(1)}, f32[2,3,128,128]{3,2,1,0:T(8,128)S(1)}, u32[]{:S(2)}, u32[]{:S(2)}) %collective-permute-start.13) | collective-permute-done | bytes 393248 | tf_op jit(solution)/shard_map/ppermute | solution.py:504
  54.6 0.0 copy-start.5
  54.6 0.8 %copy-done.5 = f32[2,3,128,128]{3,2,1,0:T(8,128)} copy-done((f32[2,3,128,128]{3,2,1,0:T(8,128)}, f32[2,3,128,128]{3,2,1,0:T(8,128)S(1)}, u32[]{:S(2)}) %copy-start.5) | copy-done | bytes 393240
  55.3 0.0 copy-start.6
  55.3 1.0 %copy-done.6 = f32[2,3,128,128]{3,2,1,0:T(8,128)S(1)} copy-done((f32[2,3,128,128]{3,2,1,0:T(8,128)S(1)}, f32[2,3,128,128]{3,2,1,0:T(8,128)}, u32[]{:S(2)}) %copy-start.6) | copy-done | bytes 393240
  56.3 1.8 %place_arrivals.1 = (f32[8,128,128]{2,1,0:T(8,128)}, f32[8,128,128]{2,1,0:T(8,128)}, f32[8,128,128]{2,1,0:T(8,128)}) custom-call(s32[264]{0:T(512)} %index_table.1.refs_0_, f32[2,3,128,128]{3,2,1,0:T(8,128)S(1)} %collective-permute-done.11.refs_1_, ...), custom_call_target="tpu_custom_call", output_to_operand_aliasing={{0}: (4, {}), {1}: (5, {}), {2}: (6, {})} | custom-call | tf_op jit(solution)/shard_map/place_arrivals/pallas_call | solution.py:484
Async XLA Ops:
  0.6 1.0 %copy-start = (f32[8,128,128]{2,1,0:T(8,128)S(1)}, f32[8,128,128]{2,1,0:T(8,128)}, u32[]{:S(2)}) copy-start(f32[8,128,128]{2,1,0:T(8,128)} %refs_1_.5) | copy-start | bytes 1572868
  1.7 1.0 %copy-start.1 = (f32[8,128,128]{2,1,0:T(8,128)S(1)}, f32[8,128,128]{2,1,0:T(8,128)}, u32[]{:S(2)}) copy-start(f32[8,128,128]{2,1,0:T(8,128)} %refs_2_.5) | copy-start | bytes 1572868
  2.7 1.0 %copy-start.2 = (f32[8,128,128]{2,1,0:T(8,128)S(1)}, f32[8,128,128]{2,1,0:T(8,128)}, u32[]{:S(2)}) copy-start(f32[8,128,128]{2,1,0:T(8,128)} %refs_3_.5) | copy-start | bytes 1572868
  3.8 1.0 %copy-start.3 = (f32[8,128,128]{2,1,0:T(8,128)S(1)}, f32[8,128,128]{2,1,0:T(8,128)}, u32[]{:S(2)}) copy-start(f32[8,128,128]{2,1,0:T(8,128)} %refs_4_.5) | copy-start | bytes 1572868
  4.8 1.0 %copy-start.4 = (f32[8,128,128]{2,1,0:T(8,128)S(1)}, f32[8,128,128]{2,1,0:T(8,128)}, u32[]{:S(2)}) copy-start(f32[8,128,128]{2,1,0:T(8,128)} %refs_5_.3) | copy-start | bytes 1572868
  7.2 28.1 %copy-start.8 = (f32[4,128,128]{2,1,0:T(8,128)}, f32[4,128,128]{2,1,0:T(8,128)S(1)}, u32[]{:S(2)}) copy-start(f32[4,128,128]{2,1,0:T(8,128)S(1)} %get-tuple-element.18.refs_6_) | copy-start | bytes 786436
  7.2 15.8 %collective-permute-start.5 = (f32[4,128,128]{2,1,0:T(8,128)S(1)}, f32[4,128,128]{2,1,0:T(8,128)S(1)}, u32[]{:S(2)}, u32[]{:S(2)}) collective-permute-start(f32[4,128,128]{2,1,0:T(8,128)S(1)} %get-tuple-element.18.refs_6_), channel_id=1, source_target_pairs={{0,2},{1,3},{2,0},{3,1},{4,6},{5,7},{6,4},{7,5},{8,10},{9,11},{10,... | collective-permute-start | bytes 786440 | tf_op jit(solution)/shard_map/ppermute | solution.py:504
  10.1 8.8 %collective-permute-start = (f32[8,32,128]{2,1,0:T(8,128)}, f32[8,32,128]{2,1,0:T(8,128)S(1)}, u32[]{:S(2)}, u32[]{:S(2)}) collective-permute-start(f32[8,32,128]{2,1,0:T(8,128)} %get-tuple-element.15), channel_id=1, source_target_pairs={{0,4},{4,8},{8,12},{1,5},{5,9},{9,13},{2,6},{6,10},{10,14},{3,7},{... | collective-permute-start | bytes 393224 | tf_op jit(solution)/shard_map/ppermute | solution.py:528
  13.6 6.9 %collective-permute-start.1 = (f32[8,32,128]{2,1,0:T(8,128)S(1)}, f32[8,32,128]{2,1,0:T(8,128)S(1)}, u32[]{:S(2)}, u32[]{:S(2)}) collective-permute-start(f32[8,32,128]{2,1,0:T(8,128)S(1)} %get-tuple-element.16), channel_id=1, source_target_pairs={{4,0},{8,4},{12,8},{5,1},{9,5},{13,9},{6,2},{10,6},{14,10},{7,3},{... | collective-permute-start | bytes 393224 | tf_op jit(solution)/shard_map/ppermute | solution.py:529
  20.5 14.8 %copy-start.12 = (f32[8,32,128]{2,1,0:T(8,128)}, f32[8,32,128]{2,1,0:T(8,128)S(1)}, u32[]{:S(2)}) copy-start(f32[8,32,128]{2,1,0:T(8,128)S(1)} %collective-permute-done.1.refs_8_) | copy-start | bytes 393220
  20.5 5.0 %collective-permute-start.7 = (f32[8,32,128]{2,1,0:T(8,128)S(1)}, f32[8,32,128]{2,1,0:T(8,128)S(1)}, u32[]{:S(2)}, u32[]{:S(2)}) collective-permute-start(f32[8,32,128]{2,1,0:T(8,128)S(1)} %collective-permute-done.1.refs_8_), channel_id=1, source_target_pairs={{0,2},{1,3},{2,0},{3,1},{4,6},{5,7},{6,4},{7,5},{8,10},{9,11},{10,... | collective-permute-start | bytes 393224 | tf_op jit(solution)/shard_map/ppermute | solution.py:504
  21.0 5.8 %collective-permute-start.6 = (f32[8,32,128]{2,1,0:T(8,128)S(1)}, f32[8,32,128]{2,1,0:T(8,128)S(1)}, u32[]{:S(2)}, u32[]{:S(2)}) collective-permute-start(f32[8,32,128]{2,1,0:T(8,128)S(1)} %collective-permute-done.refs_7_), channel_id=1, source_target_pairs={{0,2},{1,3},{2,0},{3,1},{4,6},{5,7},{6,4},{7,5},{8,10},{9,11},{10,... | collective-permute-start | bytes 393224 | tf_op jit(solution)/shard_map/ppermute | solution.py:504
  22.5 4.9 %collective-permute-start.2 = (f32[4,128,128]{2,1,0:T(8,128)S(1)}, f32[4,128,128]{2,1,0:T(8,128)S(1)}, u32[]{:S(2)}, u32[]{:S(2)}) collective-permute-start(f32[4,128,128]{2,1,0:T(8,128)S(1)} %get-tuple-element.18.refs_6_), channel_id=1, source_target_pairs={{0,1},{1,0},{2,3},{3,2},{4,5},{5,4},{6,7},{7,6},{8,9},{9,8},{10,11... | collective-permute-start | bytes 786440 | tf_op jit(solution)/shard_map/ppermute | solution.py:504
  22.5 4.3 %collective-permute-start.3 = (f32[8,32,128]{2,1,0:T(8,128)S(1)}, f32[8,32,128]{2,1,0:T(8,128)S(1)}, u32[]{:S(2)}, u32[]{:S(2)}) collective-permute-start(f32[8,32,128]{2,1,0:T(8,128)S(1)} %collective-permute-done.refs_7_), channel_id=1, source_target_pairs={{0,1},{1,0},{2,3},{3,2},{4,5},{5,4},{6,7},{7,6},{8,9},{9,8},{10,11... | collective-permute-start | bytes 393224 | tf_op jit(solution)/shard_map/ppermute | solution.py:504
  23.0 12.3 %copy-start.10 = (f32[4,128,128]{2,1,0:T(8,128)}, f32[4,128,128]{2,1,0:T(8,128)S(1)}, u32[]{:S(2)}) copy-start(f32[4,128,128]{2,1,0:T(8,128)S(1)} %collective-permute-done.5.refs_12_) | copy-start | bytes 786436
  23.0 5.4 %collective-permute-start.8 = (f32[4,128,128]{2,1,0:T(8,128)S(1)}, f32[4,128,128]{2,1,0:T(8,128)S(1)}, u32[]{:S(2)}, u32[]{:S(2)}) collective-permute-start(f32[4,128,128]{2,1,0:T(8,128)S(1)} %collective-permute-done.5.refs_12_), channel_id=1, source_target_pairs={{0,1},{1,0},{2,3},{3,2},{4,5},{5,4},{6,7},{7,6},{8,9},{9,8},{10,11... | collective-permute-start | bytes 786440 | tf_op jit(solution)/shard_map/ppermute | solution.py:504
  25.4 1.9 %collective-permute-start.4 = (f32[8,32,128]{2,1,0:T(8,128)S(1)}, f32[8,32,128]{2,1,0:T(8,128)S(1)}, u32[]{:S(2)}, u32[]{:S(2)}) collective-permute-start(f32[8,32,128]{2,1,0:T(8,128)S(1)} %collective-permute-done.1.refs_8_), channel_id=1, source_target_pairs={{0,1},{1,0},{2,3},{3,2},{4,5},{5,4},{6,7},{7,6},{8,9},{9,8},{10,11... | collective-permute-start | bytes 393224 | tf_op jit(solution)/shard_map/ppermute | solution.py:504
  26.9 1.3 %collective-permute-start.10 = (f32[8,32,128]{2,1,0:T(8,128)S(1)}, f32[8,32,128]{2,1,0:T(8,128)S(1)}, u32[]{:S(2)}, u32[]{:S(2)}) collective-permute-start(f32[8,32,128]{2,1,0:T(8,128)S(1)} %collective-permute-done.7.refs_14_), channel_id=1, source_target_pairs={{0,1},{1,0},{2,3},{3,2},{4,5},{5,4},{6,7},{7,6},{8,9},{9,8},{10,11... | collective-permute-start | bytes 393224 | tf_op jit(solution)/shard_map/ppermute | solution.py:504
  26.9 1.5 %collective-permute-start.9 = (f32[8,32,128]{2,1,0:T(8,128)S(1)}, f32[8,32,128]{2,1,0:T(8,128)S(1)}, u32[]{:S(2)}, u32[]{:S(2)}) collective-permute-start(f32[8,32,128]{2,1,0:T(8,128)S(1)} %collective-permute-done.6.refs_13_), channel_id=1, source_target_pairs={{0,1},{1,0},{2,3},{3,2},{4,5},{5,4},{6,7},{7,6},{8,9},{9,8},{10,11... | collective-permute-start | bytes 393224 | tf_op jit(solution)/shard_map/ppermute | solution.py:504
  28.4 0.7 %copy-start.7 = (s32[264]{0:T(512)S(1)}, s32[264]{0:T(512)}, u32[]{:S(2)}) copy-start(s32[264]{0:T(512)} %index_table.1.refs_0_) | copy-start | bytes 3172
  35.3 11.6 %collective-permute-start.11 = (f32[2,3,128,128]{3,2,1,0:T(8,128)S(1)}, f32[2,3,128,128]{3,2,1,0:T(8,128)S(1)}, u32[]{:S(2)}, u32[]{:S(2)}) collective-permute-start(f32[2,3,128,128]{3,2,1,0:T(8,128)S(1)} %get-tuple-element.21), channel_id=1, source_target_pairs={{0,1},{1,0},{2,3},{3,2},{4,5},{5,4},{6,7},{7,6},{8,9},{9,8},{10,11... | collective-permute-start | bytes 1179656 | tf_op jit(solution)/shard_map/ppermute | solution.py:504
  35.7 12.0 %collective-permute-start.12 = (f32[2,3,128,128]{3,2,1,0:T(8,128)S(1)}, f32[2,3,128,128]{3,2,1,0:T(8,128)S(1)}, u32[]{:S(2)}, u32[]{:S(2)}) collective-permute-start(f32[2,3,128,128]{3,2,1,0:T(8,128)S(1)} %get-tuple-element.22), channel_id=1, source_target_pairs={{0,2},{1,3},{2,0},{3,1},{4,6},{5,7},{6,4},{7,5},{8,10},{9,11},{10,... | collective-permute-start | bytes 1179656 | tf_op jit(solution)/shard_map/ppermute | solution.py:504
  36.3 18.2 %collective-permute-start.13 = (f32[2,3,128,128]{3,2,1,0:T(8,128)S(1)}, f32[2,3,128,128]{3,2,1,0:T(8,128)S(1)}, u32[]{:S(2)}, u32[]{:S(2)}) collective-permute-start(f32[2,3,128,128]{3,2,1,0:T(8,128)S(1)} %get-tuple-element.23), channel_id=1, source_target_pairs={{0,3},{1,2},{2,1},{3,0},{4,7},{5,6},{6,5},{7,4},{8,11},{9,10},{10,... | collective-permute-start | bytes 1179656 | tf_op jit(solution)/shard_map/ppermute | solution.py:504
  37.2 0.9 %copy-start.9 = (f32[4,128,128]{2,1,0:T(8,128)S(1)}, f32[4,128,128]{2,1,0:T(8,128)}, u32[]{:S(2)}) copy-start(f32[4,128,128]{2,1,0:T(8,128)} %copy-done.8) | copy-start | bytes 786436
  38.2 0.9 %copy-start.11 = (f32[4,128,128]{2,1,0:T(8,128)S(1)}, f32[4,128,128]{2,1,0:T(8,128)}, u32[]{:S(2)}) copy-start(f32[4,128,128]{2,1,0:T(8,128)} %copy-done.10) | copy-start | bytes 786436
  39.1 0.9 %copy-start.13 = (f32[8,32,128]{2,1,0:T(8,128)S(1)}, f32[8,32,128]{2,1,0:T(8,128)}, u32[]{:S(2)}) copy-start(f32[8,32,128]{2,1,0:T(8,128)} %copy-done.12) | copy-start | bytes 393220
  54.6 0.8 %copy-start.5 = (f32[2,3,128,128]{3,2,1,0:T(8,128)}, f32[2,3,128,128]{3,2,1,0:T(8,128)S(1)}, u32[]{:S(2)}) copy-start(f32[2,3,128,128]{3,2,1,0:T(8,128)S(1)} %collective-permute-done.13.refs_3_) | copy-start | bytes 1179652
  55.3 1.0 %copy-start.6 = (f32[2,3,128,128]{3,2,1,0:T(8,128)S(1)}, f32[2,3,128,128]{3,2,1,0:T(8,128)}, u32[]{:S(2)}) copy-start(f32[2,3,128,128]{3,2,1,0:T(8,128)} %copy-done.5) | copy-start | bytes 1179652

commit v3 on v2

--- a/solution.py
+++ b/solution.py
@@ -38,118 +38,109 @@
 SMEM = pltpu.SMEM
 VMEM = pltpu.VMEM
 ANY = pl.ANY
+SMALL = pltpu.CompilerParams(vmem_limit_bytes=2 * 1024 * 1024)
 
 
 def lane_index():
     return lax.broadcasted_iota(jnp.int32, (1, SIDE), 1)
 
 
-def index_kernel(
-    shape, pos_ref, before_ref, after_ref, wet_ref, table, inv_before, inv_after, count
-):
+def divide(value, size):
+    if size & (size - 1):
+        return lax.div(value, size)
+    return lax.shift_right_logical(value, size.bit_length() - 1)
+
+
+def remainder(value, size):
+    if size & (size - 1):
+        return lax.rem(value, size)
+    return value & (size - 1)
+
+
+def index_kernel(shape, before_ref, after_ref, wet_ref, table, inv_before, inv_after, count):
     cols, subs, tile_count, total = shape
     lanes = cols * subs
     row_tiles = lanes * tile_count
     tile_rows = total // row_tiles
-    my_row, my_col, my_sub = pos_ref[0], pos_ref[1], pos_ref[2]
+    my_row, my_col, my_sub = (lax.axis_index(name) for name in ("row", "col", "sub"))
     me = my_row * lanes + my_col * subs + my_sub
+    spare = RECEIVE + 2 * lanes
 
     def invert(s, carry):
-        for u in range(8):
-            inv_before[before_ref[s * 8 + u]] = s * 8 + u
-            inv_after[after_ref[s * 8 + u]] = s * 8 + u
+        for u in range(16):
+            inv_before[before_ref[s * 16 + u]] = s * 16 + u
+            inv_after[after_ref[s * 16 + u]] = s * 16 + u
         return carry
 
-    lax.fori_loop(0, total // 8, invert, 0)
-    for i in range(2 * NT):
-        table[i * ENTRY] = 0
+    lax.fori_loop(0, total // 16, invert, 0)
     for i in range(lanes * 2):
         table[RECEIVE + i] = -1
     for i in range(lanes + 1):
         count[i] = 0
 
-    def modulo(value, size):
-        return lax.rem(value + size, size)
-
-    def entry(base, tile, source, target):
-        table[base] = 1
-        table[base + 1] = jnp.where(wet_ref[tile] == 1, 1, 0)
-        table[base + 2] = source
-        table[base + 3] = target
-        row, col = lax.div(tile, row_tiles), lax.rem(tile, row_tiles)
+    def relative(lane, sign):
+        col = remainder(sign * (divide(lane, subs) - my_col) + cols, cols)
+        sub = remainder(sign * (remainder(lane, subs) - my_sub) + subs, subs)
+        return col * subs + sub
+
+    def own(s, carry):
+        tile = before_ref[me * tile_count + s]
+        device = divide(inv_after[tile], tile_count)
+        stays = device == me
+        to = relative(remainder(device, lanes), 1)
+        nth = count[to]
+        count[to] = nth + 1
+        left = count[lanes]
+        count[lanes] = left + jnp.where(stays, 0, 1)
+        base = jnp.where(
+            stays,
+            STAY + jnp.minimum(nth, NT - 1) * ENTRY,
+            LEAVE + jnp.minimum(left, NT - 1) * ENTRY,
+        )
+        table[base + 1] = wet_ref[tile]
+        table[base + 2] = s
+        table[base + 3] = jnp.where(stays, s, to * 2 + jnp.minimum(nth, 1))
+        row, col = divide(tile, row_tiles), remainder(tile, row_tiles)
         for n, (dr, dc) in enumerate(STEP_TO):
             r, c = row + dr, col + dc
             there = (r >= 0) & (r < tile_rows) & (c >= 0) & (c < row_tiles)
             near = jnp.where(there, tile + (dr * row_tiles + dc), tile)
             at = inv_before[near]
-            lane = lax.rem(lax.div(at, tile_count), lanes)
-            rel = modulo(my_col - lax.div(lane, subs), cols) * subs + modulo(
-                my_sub - lax.rem(lane, subs), subs
-            )
-            table[base + 4 + 3 * n] = jnp.where(there & (wet_ref[near] == 1), 1, 0)
-            table[base + 5 + 3 * n] = rel
-            table[base + 6 + 3 * n] = lax.rem(at, tile_count)
-
-    def own(s, carry):
-        tile = before_ref[me * tile_count + s]
-        device = lax.div(inv_after[tile], tile_count)
-        stays = device == me
-
-        @pl.when(stays)
-        def _():
-            at = jnp.minimum(count[0], NT - 1)
-            count[0] = at + 1
-            entry(STAY + at * ENTRY, tile, s, s)
-
-        @pl.when(jnp.logical_not(stays))
-        def _():
-            lane = lax.rem(device, lanes)
-            rel = modulo(lax.div(lane, subs) - my_col, cols) * subs + modulo(
-                lax.rem(lane, subs) - my_sub, subs
-            )
-            place = jnp.minimum(count[rel], 1)
-            count[rel] = place + 1
-            at = jnp.minimum(count[lanes], NT - 1)
-            count[lanes] = at + 1
-            entry(LEAVE + at * ENTRY, tile, s, rel * 2 + place)
-
+            table[base + 4 + 3 * n] = jnp.where(there, wet_ref[near], 0)
+            table[base + 5 + 3 * n] = relative(remainder(divide(at, tile_count), lanes), -1)
+            table[base + 6 + 3 * n] = remainder(at, tile_count)
         return carry
 
     lax.fori_loop(0, tile_count, own, 0)
 
     for rel in range(1, lanes):
-        col = modulo(my_col - rel // subs, cols)
-        sub = modulo(my_sub - rel % subs, subs)
+        col = remainder(my_col + (cols - rel // subs), cols)
+        sub = remainder(my_sub + (subs - rel % subs), subs)
         device = my_row * lanes + col * subs + sub
-
-        def arriving(s, found):
+        found = jnp.int32(0)
+        for s in range(tile_count):
             at = inv_after[before_ref[device * tile_count + s]]
-            mine = lax.div(at, tile_count) == me
-
-            @pl.when(mine)
-            def _():
-                table[RECEIVE + rel * 2 + jnp.minimum(found, 1)] = lax.rem(at, tile_count)
-
-            return found + jnp.where(mine, 1, 0)
-
-        lax.fori_loop(0, tile_count, arriving, jnp.int32(0))
-
-
-def make_table(shape, position, before, after, wet):
+            mine = divide(at, tile_count) == me
+            place = RECEIVE + rel * 2 + jnp.minimum(found, 1)
+            table[jnp.where(mine, place, spare)] = remainder(at, tile_count)
+            found = found + jnp.where(mine, 1, 0)
+
+
+def make_table(shape, before, after, wet):
     cols, subs, _, total = shape
-    size = RECEIVE + 2 * cols * subs
     return pl.pallas_call(
         functools.partial(index_kernel, shape),
         name="index_table",
-        out_shape=jax.ShapeDtypeStruct((size,), jnp.int32),
-        in_specs=[pl.BlockSpec(memory_space=SMEM)] * 4,
+        out_shape=SMEM((RECEIVE + 2 * cols * subs + 1,), jnp.int32),
+        in_specs=[pl.BlockSpec(memory_space=SMEM)] * 3,
         out_specs=pl.BlockSpec(memory_space=SMEM),
         scratch_shapes=[
             SMEM((total,), jnp.int32),
             SMEM((total,), jnp.int32),
             SMEM((cols * subs + 1,), jnp.int32),
         ],
-    )(position, before, after, wet)
+        compiler_params=SMALL,
+    )(before, after, wet)
 
 
 def in_vmem(array):
@@ -160,33 +151,47 @@
     return [pl.BlockSpec(memory_space=VMEM)] * count
 
 
-def pack_kernel(*refs):
-    fields = refs[:FIELDS]
-    columns, first, last = refs[FIELDS:]
+def load_kernel(*refs):
+    sources, refs = refs[:FIELDS], refs[FIELDS:]
+    fields, (columns, first, last, sem) = refs[:FIELDS], refs[FIELDS:]
     lane = lane_index()
-    for t in range(fields[0].shape[0]):
-        packed = jnp.zeros((SIDE, SIDE), jnp.float32) if t % 2 == 0 else packed
-        for f in range(FIELDS):
-            at = PAIR * (t % 2 * FIELDS + f)
-            moved = pltpu.roll(fields[f][t], at + HALO, 1)
-            packed = jnp.where((lane >= at) & (lane < at + PAIR), moved, packed)
+    copies = [
+        pltpu.make_async_copy(sources[f], fields[f], sem.at[f]) for f in range(FIELDS)
+    ]
+    for copy in copies:
+        copy.start()
+    tile_count = fields[0].shape[0]
+    for t in range(tile_count):
+        first[t, FIELDS * HALO :, :] = jnp.zeros((2, SIDE), jnp.float32)
+        last[t, :2, :] = jnp.zeros((2, SIDE), jnp.float32)
+    for f in range(FIELDS):
+        copies[f].wait()
+        for t in range(0, tile_count, 2):
+            packed = columns[t // 2] if f else jnp.zeros((SIDE, SIDE), jnp.float32)
+            for u in range(2):
+                at = PAIR * (u * FIELDS + f)
+                moved = pltpu.roll(fields[f][t + u], at + HALO, 1)
+                packed = jnp.where((lane >= at) & (lane < at + PAIR), moved, packed)
+            columns[t // 2] = packed
+        for t in range(tile_count):
             first[t, HALO * f : HALO * (f + 1), :] = fields[f][t, :HALO, :]
             last[t, 2 + HALO * f : 2 + HALO * (f + 1), :] = fields[f][t, SIDE - HALO :, :]
-        first[t, FIELDS * HALO :, :] = jnp.zeros((2, SIDE), jnp.float32)
-        last[t, :2, :] = jnp.zeros((2, SIDE), jnp.float32)
-        if t % 2:
-            columns[t // 2] = packed
-
-
-def pack_edges(fields, tile_count):
+
+
+def load(arrays):
+    tile_count = arrays[0].shape[0]
     rows = VMEM((tile_count, PACK_ROWS, SIDE), jnp.float32)
+    outs = [VMEM(array.shape, array.dtype) for array in arrays]
+    outs += [VMEM((tile_count // 2, SIDE, SIDE), jnp.float32), rows, rows]
     return pl.pallas_call(
-        pack_kernel,
-        name="pack_edges",
-        out_shape=(VMEM((tile_count // 2, SIDE, SIDE), jnp.float32), rows, rows),
-        in_specs=vmem_specs(FIELDS),
-        out_specs=tuple(vmem_specs(3)),
-    )(*fields)
+        load_kernel,
+        name="load_and_pack",
+        out_shape=tuple(outs),
+        in_specs=[pl.BlockSpec(memory_space=pltpu.HBM)] * FIELDS,
+        out_specs=tuple(vmem_specs(len(outs))),
+        scratch_shapes=[pltpu.SemaphoreType.DMA((FIELDS,))],
+        compiler_params=SMALL,
+    )(*[pltpu.with_memory_space_constraint(array, pltpu.HBM) for array in arrays])
 
 
 def face(flow, level, level_next, ground, friction):
@@ -448,7 +453,7 @@
         + [block] * 7
         + [strip] * 7
         + [pltpu.SemaphoreType.DMA((NT, 3))],
-        compiler_params=pltpu.CompilerParams(vmem_limit_bytes=16 * 1024 * 1024),
+        compiler_params=pltpu.CompilerParams(vmem_limit_bytes=12 * 1024 * 1024),
         cost_estimate=pl.CostEstimate(
             flops=60 * cells, bytes_accessed=8 * NT * SIDE * SIDE * 4, transcendentals=6 * cells
         ),
@@ -491,6 +496,7 @@
         out_specs=tuple(pl.BlockSpec(memory_space=ANY) for _ in partial_outs),
         scratch_shapes=[pltpu.SemaphoreType.DMA((lanes, 2, 3))],
         input_output_aliases={lanes: 0, lanes + 1: 1, lanes + 2: 2},
+        compiler_params=SMALL,
     )(table, *received, *partial_outs)
 
 
@@ -504,15 +510,15 @@
     return lax.ppermute(array, ("col", "sub"), pairs)
 
 
-def spread(array):
-    cols, subs = lax.axis_size("col"), lax.axis_size("sub")
-    out = []
-    for c in range(cols):
-        part = array if c == 0 else shift_lanes(array, c, 0)
-        out.append(part)
-        for s in range(1, subs):
-            out.append(shift_lanes(part, 0, s))
-    return out
+def over_cols(array):
+    return [array] + [shift_lanes(array, c, 0) for c in range(1, lax.axis_size("col"))]
+
+
+def over_subs(parts):
+    subs = lax.axis_size("sub")
+    return [
+        in_vmem(part if s == 0 else shift_lanes(part, 0, s)) for part in parts for s in range(subs)
+    ]
 
 
 def shards(
@@ -520,25 +526,19 @@
 ):
     cols, subs, rows = lax.axis_size("col"), lax.axis_size("sub"), lax.axis_size("row")
     tile_count = water_depth.shape[0]
-    fields = [
-        in_vmem(field) for field in (water_depth, flow_east, flow_south, bed_level, manning_n)
-    ]
-    position = jnp.stack([lax.axis_index("row"), lax.axis_index("col"), lax.axis_index("sub")])
-    columns, first, last = pack_edges(fields, tile_count)
-    above = lax.ppermute(last, "row", [(i, i + 1) for i in range(rows - 1)])
-    below = lax.ppermute(first, "row", [(i + 1, i) for i in range(rows - 1)])
+    *fields, columns, first, last = load(
+        (water_depth, flow_east, flow_south, bed_level, manning_n)
+    )
+    fields = [in_vmem(field) for field in fields]
+    columns = over_cols(columns)
+    above = over_cols(lax.ppermute(last, "row", [(i, i + 1) for i in range(rows - 1)]))
+    below = over_cols(lax.ppermute(first, "row", [(i + 1, i) for i in range(rows - 1)]))
     table = make_table(
-        (cols, subs, tile_count, placed_before.shape[0]),
-        position.astype(jnp.int32),
-        placed_before,
-        placed_after,
-        wet_tiles,
+        (cols, subs, tile_count, placed_before.shape[0]), placed_before, placed_after, wet_tiles
     )
-    above, below, table = lax.optimization_barrier((above, below, table))
-    halos = [
-        tuple(in_vmem(part) for part in group)
-        for group in zip(spread(columns), spread(above), spread(below))
-    ]
+    above[1:], below[1:], table = lax.optimization_barrier((above[1:], below[1:], table))
+    table = pltpu.with_memory_space_constraint(table, SMEM)
+    halos = list(zip(over_subs(columns), over_subs(above), over_subs(below)))
     leaving = advance(table, fields, halos, LEAVE, True)
     received = [
         in_vmem(shift_lanes(leaving[k - 1], k // subs, k % subs)) for k in range(1, cols * subs)

time: 58.8 us -> 49.1 us (0.84)
  local copies, waits for them, and re-layouts: 10.4 us -> 0.01 us
  waiting for transfers between devices: 13.9 us -> 18.8 us
  Pallas kernels: 19.6 us -> 16.8 us
  other arithmetic: 0.62 us -> 0 us
    unnamed x28 -> x6, local copies, waits for them, and re-layouts: 10.4 us -> 0.01 us
    ppermute x2, waiting for transfers between devices: 1.51 us -> 5.03 us  [the longest x1 3.83 us: shards(): lax.ppermute(first, 'row', [(i + 1, i) for i in range(rows - 1)])]
    pallas_call x1, Pallas kernels: 3.4 us -> 1.65 us  [make_table(): pl.pallas_call(functools.partial(index_kernel, shape), name='index_table'...]
    ppermute x12, waiting for transfers between devices: 12.4 us -> 13.7 us  [shift_lanes(): return lax.ppermute(array, ('col', 'sub'), pairs)]
    pallas_call x2, Pallas kernels: 13.1 us -> 11.9 us  [advance(): pl.pallas_call(functools.partial(advance_kernel, lanes, base, leaving), n...]
    pallas_call x1, Pallas kernels: 1.35 us -> 2.14 us  [load(): pl.pallas_call(load_kernel, name='load_and_pack', out_shape=tuple(outs),...]
    pallas_call x1, Pallas kernels: 1.77 us -> 1.07 us  [place(): pl.pallas_call(functools.partial(place_kernel, lanes), name='place_arriva...]
    another operation x1 -> x0, other arithmetic: 0.62 us -> none  [shards(): jnp.stack([lax.axis_index('row'), lax.axis_index('col'), lax.axis_index('...]
  transfers between devices with their start and end apart: 14 -> 14, of which waited for: 7 -> 7; matrix products, arithmetic and copies ran while one was open for 1% -> 0% of each run, Pallas kernels for 18% -> 16%
where the time goes in v3:
time: 49.1 us; the launch traced here: 48.8 us
  waiting for transfers between devices  18.8 us (38%)
  Pallas kernels  16.8 us (34%)
  starting transfers between devices  12.5 us (25%)
  between operations  0.73 us (1%)
    ppermute x12, waiting for transfers between devices, shift_lanes(): return lax.ppermute(array, ('col', 'sub'), pairs)  13.7 us
    pallas_call x2, Pallas kernels, advance(): pl.pallas_call(functools.partial(advance_kernel, lanes, base, leaving), n...  11.9 us
    ppermute x12, starting transfers between devices, shift_lanes(): return lax.ppermute(array, ('col', 'sub'), pairs)  7.58 us
    ppermute x1, waiting for transfers between devices, shards(): lax.ppermute(first, 'row', [(i + 1, i) for i in range(rows - 1)])  3.83 us
    ppermute x1, starting transfers between devices, shards(): lax.ppermute(last, 'row', [(i, i + 1) for i in range(rows - 1)])  3.61 us
    pallas_call x1, Pallas kernels, load(): pl.pallas_call(load_kernel, name='load_and_pack', out_shape=tuple(outs),...  2.14 us
    pallas_call x1, Pallas kernels, make_table(): pl.pallas_call(functools.partial(index_kernel, shape), name='index_table'...  1.65 us
    ppermute x1, starting transfers between devices, shards(): lax.ppermute(first, 'row', [(i + 1, i) for i in range(rows - 1)])  1.29 us
  transfers between devices with their start and end apart: 14, of which 7 were waited for; matrix products, arithmetic and copies ran while one was open for 0% of the time, Pallas kernels for 16%

profile of v3, /device:TPU:0, one launch (start us, length us, event | category | flops | bytes accessed | tf_op | source)
XLA Modules:
  0.0 48.8 jit_solution(8692913637259570175)
XLA Ops:
  0.6 2.1 %load_and_pack.1 = (f32[8,128,128]{2,1,0:T(8,128)S(1)}, f32[8,128,128]{2,1,0:T(8,128)S(1)}, f32[8,128,128]{2,1,0:T(8,128)S(1)}, f32[8,128,128]{2,1,0:T(8,128)S(1...) custom-call(f32[8,128,128]{2,1,0:T(8,128)} %refs_0_.1, ...), custom_call_target="tpu_custom_call" | custom-call | tf_op jit(solution)/shard_map/load_and_pack/pallas_call | solution.py:186
  2.8 3.0 %collective-permute-start.7 = (f32[4,128,128]{2,1,0:T(8,128)S(1)}, f32[4,128,128]{2,1,0:T(8,128)S(1)}, u32[]{:S(2)}, u32[]{:S(2)}) collective-permute-start(f32[4,128,128]{2,1,0:T(8,128)S(1)} %get-tuple-element.28.refs_6_), channel_id=1, source_target_pairs={{0,2},{1,3},{2,0},{3,1},{4,6},{5,7},{6,4},{7,5},{8,10},{9,11},{10,... | collective-permute-start | bytes 786440 | tf_op jit(solution)/shard_map/ppermute | solution.py:510
  5.8 0.0 copy-start
  5.8 0.0 copy-start.1
  5.8 0.0 copy-start.2
  5.8 3.6 %collective-permute-start = (f32[8,32,128]{2,1,0:T(8,128)S(1)}, f32[8,32,128]{2,1,0:T(8,128)S(1)}, u32[]{:S(2)}, u32[]{:S(2)}) collective-permute-start(f32[8,32,128]{2,1,0:T(8,128)S(1)} %get-tuple-element.20), channel_id=1, source_target_pairs={{0,4},{4,8},{8,12},{1,5},{5,9},{9,13},{2,6},{6,10},{10,14},{3,7},{... | collective-permute-start | bytes 393224 | tf_op jit(solution)/shard_map/ppermute | solution.py:534
  9.4 1.3 %collective-permute-start.2 = (f32[8,32,128]{2,1,0:T(8,128)S(1)}, f32[8,32,128]{2,1,0:T(8,128)S(1)}, u32[]{:S(2)}, u32[]{:S(2)}) collective-permute-start(f32[8,32,128]{2,1,0:T(8,128)S(1)} %get-tuple-element.21), channel_id=1, source_target_pairs={{4,0},{8,4},{12,8},{5,1},{9,5},{13,9},{6,2},{10,6},{14,10},{7,3},{... | collective-permute-start | bytes 393224 | tf_op jit(solution)/shard_map/ppermute | solution.py:535
  10.7 1.2 %collective-permute-done.refs_7_ = f32[8,32,128]{2,1,0:T(8,128)S(1)} collective-permute-done((f32[8,32,128]{2,1,0:T(8,128)S(1)}, f32[8,32,128]{2,1,0:T(8,128)S(1)}, u32[]{:S(2)}, u32[]{:S(2)}) %collective-permute-start) | collective-permute-done | bytes 131104 | tf_op jit(solution)/shard_map/ppermute | solution.py:534
  11.9 0.5 %collective-permute-start.1 = (f32[8,32,128]{2,1,0:T(8,128)S(1)}, f32[8,32,128]{2,1,0:T(8,128)S(1)}, u32[]{:S(2)}, u32[]{:S(2)}) collective-permute-start(f32[8,32,128]{2,1,0:T(8,128)S(1)} %collective-permute-done.refs_7_), channel_id=1, source_target_pairs={{0,2},{1,3},{2,0},{3,1},{4,6},{5,7},{6,4},{7,5},{8,10},{9,11},{10,... | collective-permute-start | bytes 393224 | tf_op jit(solution)/shard_map/ppermute | solution.py:510
  12.4 3.8 %collective-permute-done.2.refs_8_ = f32[8,32,128]{2,1,0:T(8,128)S(1)} collective-permute-done((f32[8,32,128]{2,1,0:T(8,128)S(1)}, f32[8,32,128]{2,1,0:T(8,128)S(1)}, u32[]{:S(2)}, u32[]{:S(2)}) %collective-permute-start.2) | collective-permute-done | bytes 131104 | tf_op jit(solution)/shard_map/ppermute | solution.py:535
  16.3 0.5 %collective-permute-start.3 = (f32[8,32,128]{2,1,0:T(8,128)S(1)}, f32[8,32,128]{2,1,0:T(8,128)S(1)}, u32[]{:S(2)}, u32[]{:S(2)}) collective-permute-start(f32[8,32,128]{2,1,0:T(8,128)S(1)} %collective-permute-done.2.refs_8_), channel_id=1, source_target_pairs={{0,2},{1,3},{2,0},{3,1},{4,6},{5,7},{6,4},{7,5},{8,10},{9,11},{10,... | collective-permute-start | bytes 393224 | tf_op jit(solution)/shard_map/ppermute | solution.py:510
  16.8 0.0 collective-permute-start.4
  16.8 0.5 %collective-permute-start.5 = (f32[8,32,128]{2,1,0:T(8,128)S(1)}, f32[8,32,128]{2,1,0:T(8,128)S(1)}, u32[]{:S(2)}, u32[]{:S(2)}) collective-permute-start(f32[8,32,128]{2,1,0:T(8,128)S(1)} %collective-permute-done.refs_7_), channel_id=1, source_target_pairs={{0,1},{1,0},{2,3},{3,2},{4,5},{5,4},{6,7},{7,6},{8,9},{9,8},{10,11... | collective-permute-start | bytes 393224 | tf_op jit(solution)/shard_map/ppermute | solution.py:510
  17.3 0.0 collective-permute-done.7.refs_12_
  17.3 0.0 collective-permute-start.8
  17.3 0.0 copy-done
  17.3 0.0 copy-done.1
  17.3 0.0 copy-done.2
  17.3 1.6 %index_table.1.refs_0_ = s32[265]{0:T(512)S(4)} custom-call(s32[128]{0:T(128)S(1)} %copy-done, s32[128]{0:T(128)S(1)} %copy-done.1, s32[128]{0:T(128)S(1)} %copy-done.2), custom_call_target="tpu_custom_call" | custom-call | tf_op jit(solution)/shard_map/index_table/pallas_call | solution.py:131
  19.0 0.0 collective-permute-done.1.refs_13_
  19.0 0.6 %collective-permute-start.6 = (f32[8,32,128]{2,1,0:T(8,128)S(1)}, f32[8,32,128]{2,1,0:T(8,128)S(1)}, u32[]{:S(2)}, u32[]{:S(2)}) collective-permute-start(f32[8,32,128]{2,1,0:T(8,128)S(1)} %collective-permute-done.2.refs_8_), channel_id=1, source_target_pairs={{0,1},{1,0},{2,3},{3,2},{4,5},{5,4},{6,7},{7,6},{8,9},{9,8},{10,11... | collective-permute-start | bytes 393224 | tf_op jit(solution)/shard_map/ppermute | solution.py:510
  19.6 1.7 %collective-permute-done.3.refs_14_ = f32[8,32,128]{2,1,0:T(8,128)S(1)} collective-permute-done((f32[8,32,128]{2,1,0:T(8,128)S(1)}, f32[8,32,128]{2,1,0:T(8,128)S(1)}, u32[]{:S(2)}, u32[]{:S(2)}) %collective-permute-start.3) | collective-permute-done | bytes 131104 | tf_op jit(solution)/shard_map/ppermute | solution.py:510
  21.2 0.0 collective-permute-start.10
  21.2 0.0 collective-permute-done.5.refs_10_
  21.2 0.5 %collective-permute-start.9 = (f32[8,32,128]{2,1,0:T(8,128)S(1)}, f32[8,32,128]{2,1,0:T(8,128)S(1)}, u32[]{:S(2)}, u32[]{:S(2)}) collective-permute-start(f32[8,32,128]{2,1,0:T(8,128)S(1)} %collective-permute-done.1.refs_13_), channel_id=1, source_target_pairs={{0,1},{1,0},{2,3},{3,2},{4,5},{5,4},{6,7},{7,6},{8,9},{9,8},{10,11... | collective-permute-start | bytes 393224 | tf_op jit(solution)/shard_map/ppermute | solution.py:510
  21.8 0.0 collective-permute-done.6.refs_11_
  21.8 0.0 collective-permute-done.4.refs_9_
  21.8 0.8 %collective-permute-done.10.refs_17_ = f32[8,32,128]{2,1,0:T(8,128)S(1)} collective-permute-done((f32[8,32,128]{2,1,0:T(8,128)S(1)}, f32[8,32,128]{2,1,0:T(8,128)S(1)}, u32[]{:S(2)}, u32[]{:S(2)}) %collective-permute-start.10) | collective-permute-done | bytes 131104 | tf_op jit(solution)/shard_map/ppermute | solution.py:510
  22.6 0.2 collective-permute-done.9.refs_16_
  22.8 0.0 collective-permute-done.8.refs_15_
  22.8 5.6 %advance_leaving.1 = (f32[2,3,128,128]{3,2,1,0:T(8,128)S(1)}, f32[2,3,128,128]{3,2,1,0:T(8,128)S(1)}, f32[2,3,128,128]{3,2,1,0:T(8,128)S(1)}) custom-call(s32[265]{0:T(512)S(4)} %index_table.1.refs_0_, f32[8,128,128]{2,1,0:T(8,128)S(1)} %get-tuple-element.23.refs_1_, f32[8,128,128]{2,1,0:T(8,128)S(1)} %get-tuple-element.24.refs_2_, ...), custom_call_target="tpu_custom_call" | custom-call | flops 36864000 | bytes 2097152 | tf_op jit(solution)/shard_map/advance_leaving/pallas_call | solution.py:446
  28.4 0.4 collective-permute-start.11
  28.8 0.5 %collective-permute-start.12 = (f32[2,3,128,128]{3,2,1,0:T(8,128)S(1)}, f32[2,3,128,128]{3,2,1,0:T(8,128)S(1)}, u32[]{:S(2)}, u32[]{:S(2)}) collective-permute-start(f32[2,3,128,128]{3,2,1,0:T(8,128)S(1)} %get-tuple-element.32), channel_id=1, source_target_pairs={{0,2},{1,3},{2,0},{3,1},{4,6},{5,7},{6,4},{7,5},{8,10},{9,11},{10,... | collective-permute-start | bytes 1179656 | tf_op jit(solution)/shard_map/ppermute | solution.py:510
  29.3 1.0 %collective-permute-start.13 = (f32[2,3,128,128]{3,2,1,0:T(8,128)S(1)}, f32[2,3,128,128]{3,2,1,0:T(8,128)S(1)}, u32[]{:S(2)}, u32[]{:S(2)}) collective-permute-start(f32[2,3,128,128]{3,2,1,0:T(8,128)S(1)} %get-tuple-element.33), channel_id=1, source_target_pairs={{0,3},{1,2},{2,1},{3,0},{4,7},{5,6},{6,5},{7,4},{8,11},{9,10},{10,... | collective-permute-start | bytes 1179656 | tf_op jit(solution)/shard_map/ppermute | solution.py:510
  30.3 6.3 %advance_staying.1 = (f32[8,128,128]{2,1,0:T(8,128)}, f32[8,128,128]{2,1,0:T(8,128)}, f32[8,128,128]{2,1,0:T(8,128)}) custom-call(s32[265]{0:T(512)S(4)} %index_table.1.refs_0_, f32[8,128,128]{2,1,0:T(8,128)S(1)} %get-tuple-element.23.refs_1_, f32[8,128,128]{2,1,0:T(8,128)S(1)} %get-tuple-element.24.refs_2_, f32[8,128,128]{2,1,0:T(8,128)S(1)} %get-tuple-element.25.refs_3_, ...), custom_call_target="tpu_custom_call" | custom-call | flops 36864000 | bytes 2097152 | tf_op jit(solution)/shard_map/advance_staying/pallas_call | solution.py:446
  36.6 0.0 collective-permute-done.11.refs_1_
  36.7 4.1 %collective-permute-done.12.refs_2_ = f32[2,3,128,128]{3,2,1,0:T(8,128)S(1)} collective-permute-done((f32[2,3,128,128]{3,2,1,0:T(8,128)S(1)}, f32[2,3,128,128]{3,2,1,0:T(8,128)S(1)}, u32[]{:S(2)}, u32[]{:S(2)}) %collective-permute-start.12) | collective-permute-done | bytes 393248 | tf_op jit(solution)/shard_map/ppermute | solution.py:510
  40.8 6.9 %collective-permute-done.13.refs_3_ = f32[2,3,128,128]{3,2,1,0:T(8,128)S(1)} collective-permute-done((f32[2,3,128,128]{3,2,1,0:T(8,128)S(1)}, f32[2,3,128,128]{3,2,1,0:T(8,128)S(1)}, u32[]{:S(2)}, u32[]{:S(2)}) %collective-permute-start.13) | collective-permute-done | bytes 393248 | tf_op jit(solution)/shard_map/ppermute | solution.py:510
  47.7 1.1 %place_arrivals.1 = (f32[8,128,128]{2,1,0:T(8,128)}, f32[8,128,128]{2,1,0:T(8,128)}, f32[8,128,128]{2,1,0:T(8,128)}) custom-call(s32[265]{0:T(512)S(4)} %index_table.1.refs_0_, f32[2,3,128,128]{3,2,1,0:T(8,128)S(1)} %collective-permute-done.11.refs_1_, ...), custom_call_target="tpu_custom_call", output_to_operand_aliasing={{0}: (4, {}), {1}: (5, {}), {2}: (6, {})} | custom-call | tf_op jit(solution)/shard_map/place_arrivals/pallas_call | solution.py:489
Async XLA Ops:
  2.8 14.5 %collective-permute-start.7 = (f32[4,128,128]{2,1,0:T(8,128)S(1)}, f32[4,128,128]{2,1,0:T(8,128)S(1)}, u32[]{:S(2)}, u32[]{:S(2)}) collective-permute-start(f32[4,128,128]{2,1,0:T(8,128)S(1)} %get-tuple-element.28.refs_6_), channel_id=1, source_target_pairs={{0,2},{1,3},{2,0},{3,1},{4,6},{5,7},{6,4},{7,5},{8,10},{9,11},{10,... | collective-permute-start | bytes 786440 | tf_op jit(solution)/shard_map/ppermute | solution.py:510
  5.8 11.5 %copy-start = (s32[128]{0:T(128)S(1)}, s32[128]{0:T(128)}, u32[]{:S(2)}) copy-start(s32[128]{0:T(128)} %before_ref.1) | copy-start | bytes 1540
  5.8 11.5 %copy-start.1 = (s32[128]{0:T(128)S(1)}, s32[128]{0:T(128)}, u32[]{:S(2)}) copy-start(s32[128]{0:T(128)} %after_ref.1) | copy-start | bytes 1540
  5.8 11.5 %copy-start.2 = (s32[128]{0:T(128)S(1)}, s32[128]{0:T(128)}, u32[]{:S(2)}) copy-start(s32[128]{0:T(128)} %wet_ref.1) | copy-start | bytes 1540
  5.8 6.1 %collective-permute-start = (f32[8,32,128]{2,1,0:T(8,128)S(1)}, f32[8,32,128]{2,1,0:T(8,128)S(1)}, u32[]{:S(2)}, u32[]{:S(2)}) collective-permute-start(f32[8,32,128]{2,1,0:T(8,128)S(1)} %get-tuple-element.20), channel_id=1, source_target_pairs={{0,4},{4,8},{8,12},{1,5},{5,9},{9,13},{2,6},{6,10},{10,14},{3,7},{... | collective-permute-start | bytes 393224 | tf_op jit(solution)/shard_map/ppermute | solution.py:534
  9.4 6.9 %collective-permute-start.2 = (f32[8,32,128]{2,1,0:T(8,128)S(1)}, f32[8,32,128]{2,1,0:T(8,128)S(1)}, u32[]{:S(2)}, u32[]{:S(2)}) collective-permute-start(f32[8,32,128]{2,1,0:T(8,128)S(1)} %get-tuple-element.21), channel_id=1, source_target_pairs={{4,0},{8,4},{12,8},{5,1},{9,5},{13,9},{6,2},{10,6},{14,10},{7,3},{... | collective-permute-start | bytes 393224 | tf_op jit(solution)/shard_map/ppermute | solution.py:535
  11.9 7.1 %collective-permute-start.1 = (f32[8,32,128]{2,1,0:T(8,128)S(1)}, f32[8,32,128]{2,1,0:T(8,128)S(1)}, u32[]{:S(2)}, u32[]{:S(2)}) collective-permute-start(f32[8,32,128]{2,1,0:T(8,128)S(1)} %collective-permute-done.refs_7_), channel_id=1, source_target_pairs={{0,2},{1,3},{2,0},{3,1},{4,6},{5,7},{6,4},{7,5},{8,10},{9,11},{10,... | collective-permute-start | bytes 393224 | tf_op jit(solution)/shard_map/ppermute | solution.py:510
  16.3 5.0 %collective-permute-start.3 = (f32[8,32,128]{2,1,0:T(8,128)S(1)}, f32[8,32,128]{2,1,0:T(8,128)S(1)}, u32[]{:S(2)}, u32[]{:S(2)}) collective-permute-start(f32[8,32,128]{2,1,0:T(8,128)S(1)} %collective-permute-done.2.refs_8_), channel_id=1, source_target_pairs={{0,2},{1,3},{2,0},{3,1},{4,6},{5,7},{6,4},{7,5},{8,10},{9,11},{10,... | collective-permute-start | bytes 393224 | tf_op jit(solution)/shard_map/ppermute | solution.py:510
  16.8 5.0 %collective-permute-start.4 = (f32[4,128,128]{2,1,0:T(8,128)S(1)}, f32[4,128,128]{2,1,0:T(8,128)S(1)}, u32[]{:S(2)}, u32[]{:S(2)}) collective-permute-start(f32[4,128,128]{2,1,0:T(8,128)S(1)} %get-tuple-element.28.refs_6_), channel_id=1, source_target_pairs={{0,1},{1,0},{2,3},{3,2},{4,5},{5,4},{6,7},{7,6},{8,9},{9,8},{10,11... | collective-permute-start | bytes 786440 | tf_op jit(solution)/shard_map/ppermute | solution.py:510
  16.8 4.4 %collective-permute-start.5 = (f32[8,32,128]{2,1,0:T(8,128)S(1)}, f32[8,32,128]{2,1,0:T(8,128)S(1)}, u32[]{:S(2)}, u32[]{:S(2)}) collective-permute-start(f32[8,32,128]{2,1,0:T(8,128)S(1)} %collective-permute-done.refs_7_), channel_id=1, source_target_pairs={{0,1},{1,0},{2,3},{3,2},{4,5},{5,4},{6,7},{7,6},{8,9},{9,8},{10,11... | collective-permute-start | bytes 393224 | tf_op jit(solution)/shard_map/ppermute | solution.py:510
  17.3 5.5 %collective-permute-start.8 = (f32[4,128,128]{2,1,0:T(8,128)S(1)}, f32[4,128,128]{2,1,0:T(8,128)S(1)}, u32[]{:S(2)}, u32[]{:S(2)}) collective-permute-start(f32[4,128,128]{2,1,0:T(8,128)S(1)} %collective-permute-done.7.refs_12_), channel_id=1, source_target_pairs={{0,1},{1,0},{2,3},{3,2},{4,5},{5,4},{6,7},{7,6},{8,9},{9,8},{10,11... | collective-permute-start | bytes 786440 | tf_op jit(solution)/shard_map/ppermute | solution.py:510
  19.0 2.7 %collective-permute-start.6 = (f32[8,32,128]{2,1,0:T(8,128)S(1)}, f32[8,32,128]{2,1,0:T(8,128)S(1)}, u32[]{:S(2)}, u32[]{:S(2)}) collective-permute-start(f32[8,32,128]{2,1,0:T(8,128)S(1)} %collective-permute-done.2.refs_8_), channel_id=1, source_target_pairs={{0,1},{1,0},{2,3},{3,2},{4,5},{5,4},{6,7},{7,6},{8,9},{9,8},{10,11... | collective-permute-start | bytes 393224 | tf_op jit(solution)/shard_map/ppermute | solution.py:510
  21.2 1.3 %collective-permute-start.10 = (f32[8,32,128]{2,1,0:T(8,128)S(1)}, f32[8,32,128]{2,1,0:T(8,128)S(1)}, u32[]{:S(2)}, u32[]{:S(2)}) collective-permute-start(f32[8,32,128]{2,1,0:T(8,128)S(1)} %collective-permute-done.3.refs_14_), channel_id=1, source_target_pairs={{0,1},{1,0},{2,3},{3,2},{4,5},{5,4},{6,7},{7,6},{8,9},{9,8},{10,11... | collective-permute-start | bytes 393224 | tf_op jit(solution)/shard_map/ppermute | solution.py:510
  21.2 1.5 %collective-permute-start.9 = (f32[8,32,128]{2,1,0:T(8,128)S(1)}, f32[8,32,128]{2,1,0:T(8,128)S(1)}, u32[]{:S(2)}, u32[]{:S(2)}) collective-permute-start(f32[8,32,128]{2,1,0:T(8,128)S(1)} %collective-permute-done.1.refs_13_), channel_id=1, source_target_pairs={{0,1},{1,0},{2,3},{3,2},{4,5},{5,4},{6,7},{7,6},{8,9},{9,8},{10,11... | collective-permute-start | bytes 393224 | tf_op jit(solution)/shard_map/ppermute | solution.py:510
  28.4 8.2 %collective-permute-start.11 = (f32[2,3,128,128]{3,2,1,0:T(8,128)S(1)}, f32[2,3,128,128]{3,2,1,0:T(8,128)S(1)}, u32[]{:S(2)}, u32[]{:S(2)}) collective-permute-start(f32[2,3,128,128]{3,2,1,0:T(8,128)S(1)} %get-tuple-element.31), channel_id=1, source_target_pairs={{0,1},{1,0},{2,3},{3,2},{4,5},{5,4},{6,7},{7,6},{8,9},{9,8},{10,11... | collective-permute-start | bytes 1179656 | tf_op jit(solution)/shard_map/ppermute | solution.py:510
  28.8 12.0 %collective-permute-start.12 = (f32[2,3,128,128]{3,2,1,0:T(8,128)S(1)}, f32[2,3,128,128]{3,2,1,0:T(8,128)S(1)}, u32[]{:S(2)}, u32[]{:S(2)}) collective-permute-start(f32[2,3,128,128]{3,2,1,0:T(8,128)S(1)} %get-tuple-element.32), channel_id=1, source_target_pairs={{0,2},{1,3},{2,0},{3,1},{4,6},{5,7},{6,4},{7,5},{8,10},{9,11},{10,... | collective-permute-start | bytes 1179656 | tf_op jit(solution)/shard_map/ppermute | solution.py:510
  29.3 18.3 %collective-permute-start.13 = (f32[2,3,128,128]{3,2,1,0:T(8,128)S(1)}, f32[2,3,128,128]{3,2,1,0:T(8,128)S(1)}, u32[]{:S(2)}, u32[]{:S(2)}) collective-permute-start(f32[2,3,128,128]{3,2,1,0:T(8,128)S(1)} %get-tuple-element.33), channel_id=1, source_target_pairs={{0,3},{1,2},{2,1},{3,0},{4,7},{5,6},{6,5},{7,4},{8,11},{9,10},{10,... | collective-permute-start | bytes 1179656 | tf_op jit(solution)/shard_map/ppermute | solution.py:510

commit v4 on v3

--- a/solution.py
+++ b/solution.py
@@ -201,9 +201,37 @@
     return (flow - drive) / (1.0 + friction * jnp.abs(flow) * power)
 
 
-def chunks():
-    for r in range(LO, HI, CHUNK):
-        yield r, min(CHUNK, HI - r)
+class Part:
+    def __init__(self, name, base, computed, own, halo_rows, sent):
+        self.name = name
+        self.base = base
+        self.computed = computed
+        self.own = own
+        self.halo_rows = halo_rows
+        self.sent = sent
+
+    def chunks(self):
+        for start, count in self.computed:
+            for r in range(start, start + count, CHUNK):
+                yield r, min(CHUNK, start + count - r)
+
+
+def row_span(span):
+    return pl.ds(span[0], span[1])
+
+
+EDGE = 8
+BAND = 24
+EARLY = Part("leaving_middle", LEAVE, ((TOP, SIDE),), ((0, SIDE),), False, ((EDGE, SIDE - 2 * EDGE),))
+LATE = Part(
+    "leaving_edges",
+    LEAVE,
+    ((LO, BAND), (HI - BAND, BAND)),
+    ((0, BAND - 8), (SIDE - BAND + 8, BAND - 8)),
+    True,
+    ((0, EDGE), (SIDE - EDGE, EDGE)),
+)
+WHOLE = Part("staying", STAY, ((LO, HI - LO),), ((0, SIDE),), True, ((0, SIDE),))
 
 
 def row_bands(r, rows, above, middle, below):
@@ -211,8 +239,8 @@
     return jnp.where(row < TOP, above, jnp.where(row < TOP + SIDE, middle, below))
 
 
-def assemble(table, base, i, slot, fields, stacks, block, strip):
-    halo_cols, halo_above, halo_below = stacks
+def assemble(part, table, base, i, slot, fields, stacks, block, strip):
+    halo_cols = stacks[0]
     lane = lane_index()
     at = GROUP * i
 
@@ -241,26 +269,30 @@
                 value = jnp.where(inside(0, GROUP), value, strip[f][out : out + 8, :])
             strip[f][out : out + 8, :] = value
 
-        ends(halo_above, near("n"), near("nw"), near("ne"), LO)
-        ends(halo_below, near("s"), near("sw"), near("se"), TOP + SIDE)
-
-        def shifted(place, goal):
-            source = PAIR * (lax.rem(place[1], 2) * FIELDS + f)
-            shift = lax.rem(goal - source + 2 * SIDE, SIDE)
-            return pltpu.roll(halo_cols[place[0], lax.div(place[1], 2)], shift, 1)
-
-        core = fields[f][slot]
-        block[f][i, TOP : TOP + SIDE, :] = core
-        value = shifted(west, at + 2)
-        if i:
-            value = jnp.where(inside(0, 8), value, strip[f][TOP : TOP + SIDE, :])
-        value = jnp.where(inside(8, 16), pltpu.roll(core, (at + 8) % SIDE, 1), value)
-        value = jnp.where(inside(16, 24), pltpu.roll(core, (at + 24) % SIDE, 1), value)
-        value = jnp.where(inside(24, GROUP), shifted(east, at + 24 - HALO), value)
-        strip[f][TOP : TOP + SIDE, :] = value
-
-
-def prepare_strip(near_wet, strip, ground_x, ground_y):
+        if part.halo_rows:
+            ends(stacks[1], near("n"), near("nw"), near("ne"), LO)
+            ends(stacks[2], near("s"), near("sw"), near("se"), TOP + SIDE)
+
+        for start, count in part.own:
+            own, out = pl.ds(start, count), pl.ds(TOP + start, count)
+
+            def shifted(place, goal):
+                source = PAIR * (remainder(place[1], 2) * FIELDS + f)
+                shift = remainder(goal - source + 2 * SIDE, SIDE)
+                return pltpu.roll(halo_cols[place[0], divide(place[1], 2), own, :], shift, 1)
+
+            core = fields[f][slot, own, :]
+            block[f][i, out, :] = core
+            value = shifted(west, at + 2)
+            if i:
+                value = jnp.where(inside(0, 8), value, strip[f][out, :])
+            value = jnp.where(inside(8, 16), pltpu.roll(core, (at + 8) % SIDE, 1), value)
+            value = jnp.where(inside(16, 24), pltpu.roll(core, (at + 24) % SIDE, 1), value)
+            value = jnp.where(inside(24, GROUP), shifted(east, at + 24 - HALO), value)
+            strip[f][out, :] = value
+
+
+def prepare_strip(part, near_wet, strip, ground_x, ground_y):
     level, flow_x, flow_y, ground, friction = strip
     lane = lane_index()
 
@@ -278,7 +310,7 @@
         return value
 
     bands = (lane_wet("n", "nw", "ne"), lane_wet(None, "w", "e"), lane_wet("s", "sw", "se"))
-    for r, rows in chunks():
+    for r, rows in part.chunks():
         at, south = pl.ds(r, rows), pl.ds(r + 1, rows)
         z = ground[at, :]
         here, next_row = row_bands(r, rows, *bands), row_bands(r + 1, rows, *bands)
@@ -293,7 +325,7 @@
         level[at, :] = level[at, :] + z
 
 
-def prepare_tile(near_wet, i, block, ground_x, ground_y, strip_ground):
+def prepare_tile(part, near_wet, i, block, ground_x, ground_y, strip_ground):
     level, flow_x, flow_y, ground, friction = block
     lane = lane_index()
     last = lane == SIDE - 1
@@ -303,7 +335,7 @@
         jnp.where(last, e, 1),
         jnp.where(last, s * near_wet(i, "se"), s),
     )
-    for r, rows in chunks():
+    for r, rows in part.chunks():
         at, south = pl.ds(r, rows), pl.ds(r + 1, rows)
         z = ground[i, at, :]
         z_east = jnp.where(
@@ -327,50 +359,53 @@
     return (SIDE - GROUP * i - 7) % SIDE
 
 
-def advance_kernel(lanes, base, leaving, *refs):
+def advance_kernel(part, lanes, *refs):
     table = refs[0]
     fields = refs[1 : 1 + FIELDS]
-    halos = refs[1 + FIELDS : 1 + FIELDS + 3 * lanes]
-    n_out = lanes - 1 if leaving else 3
-    outs = refs[1 + FIELDS + 3 * lanes : 1 + FIELDS + 3 * lanes + n_out]
+    kinds = 3 if part.halo_rows else 1
+    halos, refs = refs[1 + FIELDS : 1 + FIELDS + kinds * lanes], refs[1 + FIELDS + kinds * lanes :]
+    n_out = 3 if part is WHOLE else lanes - 1
+    outs, stacks, refs = refs[:n_out], refs[n_out : n_out + kinds], refs[n_out + kinds :]
     (
-        halo_cols, halo_above, halo_below,
         level, flow_x, flow_y, ground, friction, ground_x, ground_y,
         s_level, s_flow_x, s_flow_y, s_ground, s_friction, s_ground_x, s_ground_y,
         sem_out,
-    ) = refs[1 + FIELDS + 3 * lanes + n_out :]
+    ) = refs
     block = (level, flow_x, flow_y, ground, friction)
     strip = (s_level, s_flow_x, s_flow_y, s_ground, s_friction)
-    stacks = (halo_cols, halo_above, halo_below)
     lane = lane_index()
     last, first = lane == SIDE - 1, lane == 0
-    core = pl.ds(TOP, SIDE)
 
     def entry(i):
-        at = base + i * ENTRY
+        at = part.base + i * ENTRY
         return table[at + 1], table[at + 2], table[at + 3]
 
     def near_wet(i, name):
-        return table[base + i * ENTRY + 4 + 3 * NEAR[name]]
+        return table[part.base + i * ENTRY + 4 + 3 * NEAR[name]]
 
     for k in range(lanes):
-        for n in range(3):
-            stacks[n][k] = halos[3 * k + n][...]
+        for n in range(kinds):
+            if n:
+                stacks[n][k] = halos[kinds * k + n][...]
+            else:
+                for span in part.own:
+                    stacks[0][k, :, row_span(span), :] = halos[kinds * k][:, row_span(span), :]
     for i in range(NT):
-        assemble(table, base + i * ENTRY, i, entry(i)[1], fields, stacks, block, strip)
-    prepare_strip(near_wet, strip, s_ground_x, s_ground_y)
+        base = part.base + i * ENTRY
+        assemble(part, table, base, i, entry(i)[1], fields, stacks, block, strip)
+    prepare_strip(part, near_wet, strip, s_ground_x, s_ground_y)
     for i in range(NT):
-        prepare_tile(near_wet, i, block, ground_x, ground_y, s_ground)
+        prepare_tile(part, near_wet, i, block, ground_x, ground_y, s_ground)
 
     def step(_, carry):
-        for r, rows in chunks():
+        for r, rows in part.chunks():
             at, south = pl.ds(r, rows), pl.ds(r + 1, rows)
             e, c = s_level[at, :], s_friction[at, :]
             e_east = pltpu.roll(e, SIDE - 1, 1)
             s_flow_x[at, :] = face(s_flow_x[at, :], e, e_east, s_ground_x[at, :], c)
             s_flow_y[at, :] = face(s_flow_y[at, :], e, s_level[south, :], s_ground_y[at, :], c)
         for i in range(NT):
-            for r, rows in chunks():
+            for r, rows in part.chunks():
                 at, south = pl.ds(r, rows), pl.ds(r + 1, rows)
                 e, c = level[i, at, :], friction[i, at, :]
                 e_east = jnp.where(
@@ -380,14 +415,14 @@
                 flow_y[i, at, :] = face(
                     flow_y[i, at, :], e, level[i, south, :], ground_y[i, at, :], c
                 )
-        for r, rows in chunks():
+        for r, rows in part.chunks():
             at, north = pl.ds(r, rows), pl.ds(r - 1, rows)
             qx = s_flow_x[at, :]
             s_level[at, :] = s_level[at, :] + RATE * (
                 (pltpu.roll(qx, 1, 1) - qx) + (s_flow_y[north, :] - s_flow_y[at, :])
             )
         for i in range(NT):
-            for r, rows in chunks():
+            for r, rows in part.chunks():
                 at, north = pl.ds(r, rows), pl.ds(r - 1, rows)
                 qx = flow_x[i, at, :]
                 qx_west = jnp.where(
@@ -400,27 +435,34 @@
 
     lax.fori_loop(0, STEPS, step, 0)
 
+    results = (level, flow_x, flow_y)
     for i in range(NT):
         wet, slot, _ = entry(i)
-        depth = level[i, core, :] - ground[i, core, :]
-        level[i, core, :] = jnp.where(wet == 1, depth, fields[0][slot])
-        flow_x[i, core, :] = jnp.where(wet == 1, flow_x[i, core, :], fields[1][slot])
-        flow_y[i, core, :] = jnp.where(wet == 1, flow_y[i, core, :], fields[2][slot])
-
-    results = (level, flow_x, flow_y)
-    if leaving:
+        for start, count in part.sent:
+            own, at = pl.ds(start, count), pl.ds(TOP + start, count)
+            level[i, at, :] = level[i, at, :] - ground[i, at, :]
+            for f in range(3):
+                results[f][i, at, :] = jnp.where(
+                    wet == 1, results[f][i, at, :], fields[f][slot, own, :]
+                )
+
+    if part is not WHOLE:
         for i in range(NT):
             target = entry(i)[2]
             for k in range(1, lanes):
-                @pl.when(lax.div(target, 2) == k)
+                @pl.when(divide(target, 2) == k)
                 def _():
-                    for f in range(3):
-                        outs[k - 1][lax.rem(target, 2), f] = results[f][i, core, :]
+                    out = 0
+                    for start, count in part.sent:
+                        for f in range(3):
+                            value = results[f][i, pl.ds(TOP + start, count), :]
+                            outs[k - 1][remainder(target, 2), f, out : out + count, :] = value
+                        out += count
 
     else:
         copies = [
             pltpu.make_async_copy(
-                results[f].at[i, core, :], outs[f].at[entry(i)[2]], sem_out.at[i, f]
+                results[f].at[i, pl.ds(TOP, SIDE), :], outs[f].at[entry(i)[2]], sem_out.at[i, f]
             )
             for i in range(NT)
             for f in range(3)
@@ -431,36 +473,39 @@
             copy.wait()
 
 
-def advance(table, fields, halos, base, leaving):
+def advance(part, table, fields, halos):
     lanes = len(halos)
-    if leaving:
-        outs = (VMEM((2, 3, SIDE, SIDE), jnp.float32),) * (lanes - 1)
-        out_specs = vmem_specs(lanes - 1)
-    else:
+    sent = sum(count for _, count in part.sent)
+    if part is WHOLE:
         outs = (jax.ShapeDtypeStruct(fields[0].shape, jnp.float32),) * 3
         out_specs = [pl.BlockSpec(memory_space=ANY)] * 3
+    else:
+        outs = (VMEM((2, 3, sent, SIDE), jnp.float32),) * (lanes - 1)
+        out_specs = vmem_specs(lanes - 1)
+    if not part.halo_rows:
+        halos = [group[:1] for group in halos]
     flat = [array for group in halos for array in group]
     block = VMEM((NT, ROWS, SIDE), jnp.float32)
     strip = VMEM((ROWS, SIDE), jnp.float32)
-    cells = (NT + 1) * ROWS * SIDE * STEPS
+    cells = (NT + 1) * sum(count for _, count in part.computed) * SIDE * STEPS
     return pl.pallas_call(
-        functools.partial(advance_kernel, lanes, base, leaving),
-        name="advance_leaving" if leaving else "advance_staying",
+        functools.partial(advance_kernel, part, lanes),
+        name="advance_" + part.name,
         out_shape=outs,
-        in_specs=[pl.BlockSpec(memory_space=SMEM)] + vmem_specs(FIELDS + 3 * lanes),
+        in_specs=[pl.BlockSpec(memory_space=SMEM)] + vmem_specs(FIELDS + len(flat)),
         out_specs=tuple(out_specs),
-        scratch_shapes=[VMEM((lanes,) + halos[0][n].shape, jnp.float32) for n in range(3)]
+        scratch_shapes=[VMEM((lanes,) + array.shape, jnp.float32) for array in halos[0]]
         + [block] * 7
         + [strip] * 7
         + [pltpu.SemaphoreType.DMA((NT, 3))],
         compiler_params=pltpu.CompilerParams(vmem_limit_bytes=12 * 1024 * 1024),
         cost_estimate=pl.CostEstimate(
-            flops=60 * cells, bytes_accessed=8 * NT * SIDE * SIDE * 4, transcendentals=6 * cells
+            flops=60 * cells, bytes_accessed=8 * NT * sent * SIDE * 4, transcendentals=6 * cells
         ),
     )(table, *fields, *flat)
 
 
-def place_kernel(lanes, *refs):
+def place_kernel(spans, lanes, *refs):
     table = refs[0]
     received = refs[1:lanes]
     outs = refs[lanes + 3 : lanes + 6]
@@ -473,28 +518,33 @@
 
                 @pl.when(slot >= 0)
                 def _():
-                    for f in range(3):
-                        act(
-                            pltpu.make_async_copy(
-                                received[k - 1].at[j, f], outs[f].at[slot], sem.at[k, j, f]
+                    at = 0
+                    for n, (start, count) in enumerate(spans):
+                        for f in range(3):
+                            act(
+                                pltpu.make_async_copy(
+                                    received[k - 1].at[j, f, pl.ds(at, count), :],
+                                    outs[f].at[slot, pl.ds(start, count), :],
+                                    sem.at[k, j, f, n],
+                                )
                             )
-                        )
+                        at += count
 
     each(lambda copy: copy.start())
     each(lambda copy: copy.wait())
 
 
-def place(table, received, partial_outs):
+def place(part, table, received, partial_outs):
     lanes = len(received) + 1
     return pl.pallas_call(
-        functools.partial(place_kernel, lanes),
-        name="place_arrivals",
+        functools.partial(place_kernel, part.sent, lanes),
+        name="place_" + part.name,
         out_shape=tuple(jax.ShapeDtypeStruct(o.shape, o.dtype) for o in partial_outs),
         in_specs=[pl.BlockSpec(memory_space=SMEM)]
         + vmem_specs(lanes - 1)
         + [pl.BlockSpec(memory_space=ANY)] * 3,
         out_specs=tuple(pl.BlockSpec(memory_space=ANY) for _ in partial_outs),
-        scratch_shapes=[pltpu.SemaphoreType.DMA((lanes, 2, 3))],
+        scratch_shapes=[pltpu.SemaphoreType.DMA((lanes, 2, 3, len(part.sent)))],
         input_output_aliases={lanes: 0, lanes + 1: 1, lanes + 2: 2},
         compiler_params=SMALL,
     )(table, *received, *partial_outs)
@@ -536,15 +586,21 @@
     table = make_table(
         (cols, subs, tile_count, placed_before.shape[0]), placed_before, placed_after, wet_tiles
     )
-    above[1:], below[1:], table = lax.optimization_barrier((above[1:], below[1:], table))
+    columns[1:], table = lax.optimization_barrier((columns[1:], table))
     table = pltpu.with_memory_space_constraint(table, SMEM)
-    halos = list(zip(over_subs(columns), over_subs(above), over_subs(below)))
-    leaving = advance(table, fields, halos, LEAVE, True)
-    received = [
-        in_vmem(shift_lanes(leaving[k - 1], k // subs, k % subs)) for k in range(1, cols * subs)
-    ]
-    staying = advance(table, fields, halos, STAY, False)
-    return place(table, received, staying)
+    columns = over_subs(columns)
+
+    def send(parts):
+        return [
+            in_vmem(shift_lanes(parts[k - 1], k // subs, k % subs)) for k in range(1, cols * subs)
+        ]
+
+    middle = send(advance(EARLY, table, fields, [(part,) for part in columns]))
+    halos = list(zip(columns, over_subs(above), over_subs(below)))
+    edges = send(advance(LATE, table, fields, halos))
+    outs = advance(WHOLE, table, fields, halos)
+    outs = place(EARLY, table, middle, outs)
+    return place(LATE, table, edges, outs)
 
 
 def solution(mesh):

time: 49.1 us -> 61.4 us (1.25)
  waiting for transfers between devices: 18.8 us -> 25.6 us
  Pallas kernels: 16.8 us -> 19.6 us
  starting transfers between devices: 12.5 us -> 14.9 us
    ppermute x12 -> x15, waiting for transfers between devices: 13.7 us -> 23.5 us  [shift_lanes(): return lax.ppermute(array, ('col', 'sub'), pairs)]
    ppermute x1, waiting for transfers between devices: 3.83 us -> 0.01 us  [shards(): lax.ppermute(first, 'row', [(i + 1, i) for i in range(rows - 1)])]
    pallas_call x3 -> x5, Pallas kernels: 13 us -> 15.8 us  [the longest x3 13.7 us: advance(): pl.pallas_call(functools.partial(advance_kernel, part, lanes), name='adva...]
    ppermute x12 -> x15, starting transfers between devices: 7.58 us -> 9.9 us  [shift_lanes(): return lax.ppermute(array, ('col', 'sub'), pairs)]
    ppermute x1, waiting for transfers between devices: 1.2 us -> 2.1 us  [shards(): lax.ppermute(last, 'row', [(i, i + 1) for i in range(rows - 1)])]
  transfers between devices with their start and end apart: 14 -> 17, of which waited for: 7 -> 5; matrix products, arithmetic and copies ran while one was open for 0% -> 0% of each run, Pallas kernels for 16% -> 27%
where the time goes in v4:
time: 61.4 us; the launch traced here: 60.9 us
  waiting for transfers between devices  25.6 us (42%)
  Pallas kernels  19.6 us (32%)
  starting transfers between devices  14.9 us (24%)
  between operations  0.79 us (1%)
    ppermute x15, waiting for transfers between devices, shift_lanes(): return lax.ppermute(array, ('col', 'sub'), pairs)  23.5 us
    pallas_call x3, Pallas kernels, advance(): pl.pallas_call(functools.partial(advance_kernel, part, lanes), name='adva...  13.7 us
    ppermute x15, starting transfers between devices, shift_lanes(): return lax.ppermute(array, ('col', 'sub'), pairs)  9.9 us
    ppermute x1, starting transfers between devices, shards(): lax.ppermute(last, 'row', [(i, i + 1) for i in range(rows - 1)])  3.73 us
    pallas_call x2, Pallas kernels, place(): pl.pallas_call(functools.partial(place_kernel, part.sent, lanes), name='p...  2.16 us
    pallas_call x1, Pallas kernels, load(): pl.pallas_call(load_kernel, name='load_and_pack', out_shape=tuple(outs),...  2.14 us
    ppermute x1, waiting for transfers between devices, shards(): lax.ppermute(last, 'row', [(i, i + 1) for i in range(rows - 1)])  2.1 us
    pallas_call x1, Pallas kernels, make_table(): pl.pallas_call(functools.partial(index_kernel, shape), name='index_table'...  1.65 us
  transfers between devices with their start and end apart: 17, of which 5 were waited for; matrix products, arithmetic and copies ran while one was open for 0% of the time, Pallas kernels for 27%

profile of v4, /device:TPU:0, one launch (start us, length us, event | category | flops | bytes accessed | tf_op | source)
XLA Modules:
  0.0 60.9 jit_solution(8747820660686749738)
XLA Ops:
  0.6 2.1 %load_and_pack.1 = (f32[8,128,128]{2,1,0:T(8,128)S(1)}, f32[8,128,128]{2,1,0:T(8,128)S(1)}, f32[8,128,128]{2,1,0:T(8,128)S(1)}, f32[8,128,128]{2,1,0:T(8,128)S(1...) custom-call(f32[8,128,128]{2,1,0:T(8,128)} %refs_0_.1, ...), custom_call_target="tpu_custom_call" | custom-call | tf_op jit(solution)/shard_map/load_and_pack/pallas_call | solution.py:186
  2.8 0.0 copy-start
  2.8 0.0 copy-start.1
  2.8 0.0 copy-start.2
  2.8 3.0 %collective-permute-start = (f32[4,128,128]{2,1,0:T(8,128)S(1)}, f32[4,128,128]{2,1,0:T(8,128)S(1)}, u32[]{:S(2)}, u32[]{:S(2)}) collective-permute-start(f32[4,128,128]{2,1,0:T(8,128)S(1)} %get-tuple-element.25.refs_6_), channel_id=1, source_target_pairs={{0,2},{1,3},{2,0},{3,1},{4,6},{5,7},{6,4},{7,5},{8,10},{9,11},{10,... | collective-permute-start | bytes 786440 | tf_op jit(solution)/shard_map/ppermute | solution.py:560
  5.8 0.0 collective-permute-start.3
  5.8 0.0 copy-done
  5.8 0.0 copy-done.1
  5.8 0.0 copy-done.2
  5.8 1.6 %index_table.1.refs_0_ = s32[265]{0:T(512)S(4)} custom-call(s32[128]{0:T(128)S(1)} %copy-done, s32[128]{0:T(128)S(1)} %copy-done.1, s32[128]{0:T(128)S(1)} %copy-done.2), custom_call_target="tpu_custom_call" | custom-call | tf_op jit(solution)/shard_map/index_table/pallas_call | solution.py:131
  7.5 4.6 %collective-permute-done.refs_12_.refs_8_ = f32[4,128,128]{2,1,0:T(8,128)S(1)} collective-permute-done((f32[4,128,128]{2,1,0:T(8,128)S(1)}, f32[4,128,128]{2,1,0:T(8,128)S(1)}, u32[]{:S(2)}, u32[]{:S(2)}) %collective-permute-start) | collective-permute-done | bytes 262176 | tf_op jit(solution)/shard_map/ppermute | solution.py:560
  12.1 0.0 collective-permute-start.8
  12.1 3.7 %collective-permute-start.1 = (f32[8,32,128]{2,1,0:T(8,128)S(1)}, f32[8,32,128]{2,1,0:T(8,128)S(1)}, u32[]{:S(2)}, u32[]{:S(2)}) collective-permute-start(f32[8,32,128]{2,1,0:T(8,128)S(1)} %get-tuple-element.32), channel_id=1, source_target_pairs={{0,4},{4,8},{8,12},{1,5},{5,9},{9,13},{2,6},{6,10},{10,14},{3,7},{... | collective-permute-start | bytes 393224 | tf_op jit(solution)/shard_map/ppermute | solution.py:584
  15.9 1.3 %collective-permute-start.2 = (f32[8,32,128]{2,1,0:T(8,128)S(1)}, f32[8,32,128]{2,1,0:T(8,128)S(1)}, u32[]{:S(2)}, u32[]{:S(2)}) collective-permute-start(f32[8,32,128]{2,1,0:T(8,128)S(1)} %get-tuple-element.33), channel_id=1, source_target_pairs={{4,0},{8,4},{12,8},{5,1},{9,5},{13,9},{6,2},{10,6},{14,10},{7,3},{... | collective-permute-start | bytes 393224 | tf_op jit(solution)/shard_map/ppermute | solution.py:585
  17.2 2.1 %collective-permute-done.1.refs_7_ = f32[8,32,128]{2,1,0:T(8,128)S(1)} collective-permute-done((f32[8,32,128]{2,1,0:T(8,128)S(1)}, f32[8,32,128]{2,1,0:T(8,128)S(1)}, u32[]{:S(2)}, u32[]{:S(2)}) %collective-permute-start.1) | collective-permute-done | bytes 131104 | tf_op jit(solution)/shard_map/ppermute | solution.py:584
  19.3 1.5 %collective-permute-start.6 = (f32[8,32,128]{2,1,0:T(8,128)S(1)}, f32[8,32,128]{2,1,0:T(8,128)S(1)}, u32[]{:S(2)}, u32[]{:S(2)}) collective-permute-start(f32[8,32,128]{2,1,0:T(8,128)S(1)} %collective-permute-done.1.refs_7_), channel_id=1, source_target_pairs={{0,2},{1,3},{2,0},{3,1},{4,6},{5,7},{6,4},{7,5},{8,10},{9,11},{10,... | collective-permute-start | bytes 393224 | tf_op jit(solution)/shard_map/ppermute | solution.py:560
  20.8 0.0 collective-permute-start.4
  20.8 0.0 collective-permute-done.3.refs_9_.refs_7_
  20.8 0.0 collective-permute-done.8.refs_15_.refs_9_
  20.8 5.0 %advance_leaving_middle.1 = (f32[2,3,112,128]{3,2,1,0:T(8,128)S(1)}, f32[2,3,112,128]{3,2,1,0:T(8,128)S(1)}, f32[2,3,112,128]{3,2,1,0:T(8,128)S(1)}) custom-call(s32[265]{0:T(512)S(4)} %index_table.1.refs_0_, f32[8,128,128]{2,1,0:T(8,128)S(1)} %get-tuple-element.27.refs_1_, f32[8,128,128]{2,1,0:T(8,128)S(1)} %get-tuple-element.28.refs_2_, ...), custom_call_target="tpu_custom_call" | custom-call | flops 29491200 | bytes 1835008 | tf_op jit(solution)/shard_map/advance_leaving_middle/pallas_call | solution.py:491
  25.8 0.6 collective-permute-start.14
  26.4 0.5 collective-permute-start.15
  26.9 0.0 collective-permute-done.2.refs_8_
  26.9 0.9 %collective-permute-start.16 = (f32[2,3,112,128]{3,2,1,0:T(8,128)S(1)}, f32[2,3,112,128]{3,2,1,0:T(8,128)S(1)}, u32[]{:S(2)}, u32[]{:S(2)}) collective-permute-start(f32[2,3,112,128]{3,2,1,0:T(8,128)S(1)} %get-tuple-element.40), channel_id=1, source_target_pairs={{0,3},{1,2},{2,1},{3,0},{4,7},{5,6},{6,5},{7,4},{8,11},{9,10},{10,... | collective-permute-start | bytes 1032200 | tf_op jit(solution)/shard_map/ppermute | solution.py:560
  27.8 0.0 collective-permute-done.6.refs_13_
  27.8 0.7 %collective-permute-start.7 = (f32[8,32,128]{2,1,0:T(8,128)S(1)}, f32[8,32,128]{2,1,0:T(8,128)S(1)}, u32[]{:S(2)}, u32[]{:S(2)}) collective-permute-start(f32[8,32,128]{2,1,0:T(8,128)S(1)} %collective-permute-done.2.refs_8_), channel_id=1, source_target_pairs={{0,2},{1,3},{2,0},{3,1},{4,6},{5,7},{6,4},{7,5},{8,10},{9,11},{10,... | collective-permute-start | bytes 393224 | tf_op jit(solution)/shard_map/ppermute | solution.py:560
  28.5 0.0 collective-permute-done.4.refs_10_
  28.5 0.3 collective-permute-start.5
  28.8 17.8 %collective-permute-done.7.refs_14_ = f32[8,32,128]{2,1,0:T(8,128)S(1)} collective-permute-done((f32[8,32,128]{2,1,0:T(8,128)S(1)}, f32[8,32,128]{2,1,0:T(8,128)S(1)}, u32[]{:S(2)}, u32[]{:S(2)}) %collective-permute-start.7) | collective-permute-done | bytes 131104 | tf_op jit(solution)/shard_map/ppermute | solution.py:560
  46.6 0.0 collective-permute-start.9
  46.6 0.0 collective-permute-done.5.refs_11_
  46.6 0.5 collective-permute-start.10
  47.1 0.8 %collective-permute-done.9.refs_16_ = f32[8,32,128]{2,1,0:T(8,128)S(1)} collective-permute-done((f32[8,32,128]{2,1,0:T(8,128)S(1)}, f32[8,32,128]{2,1,0:T(8,128)S(1)}, u32[]{:S(2)}, u32[]{:S(2)}) %collective-permute-start.9) | collective-permute-done | bytes 131104 | tf_op jit(solution)/shard_map/ppermute | solution.py:560
  47.9 0.2 collective-permute-done.10.refs_17_
  48.1 2.3 %advance_leaving_edges.1 = (f32[2,3,16,128]{3,2,1,0:T(8,128)S(1)}, f32[2,3,16,128]{3,2,1,0:T(8,128)S(1)}, f32[2,3,16,128]{3,2,1,0:T(8,128)S(1)}) custom-call(s32[265]{0:T(512)S(4)} %index_table.1.refs_0_, f32[8,128,128]{2,1,0:T(8,128)S(1)} %get-tuple-element.27.refs_1_, f32[8,128,128]{2,1,0:T(8,128)S(1)} %get-tuple-element.28.refs_2_, ...), custom_call_target="tpu_custom_call" | custom-call | flops 11059200 | bytes 262144 | tf_op jit(solution)/shard_map/advance_leaving_edges/pallas_call | solution.py:491
  50.5 0.4 collective-permute-start.11
  50.8 0.5 collective-permute-start.12
  51.4 0.0 collective-permute-done.14.refs_1_
  51.4 1.0 %collective-permute-start.13 = (f32[2,3,16,128]{3,2,1,0:T(8,128)S(1)}, f32[2,3,16,128]{3,2,1,0:T(8,128)S(1)}, u32[]{:S(2)}, u32[]{:S(2)}) collective-permute-start(f32[2,3,16,128]{3,2,1,0:T(8,128)S(1)} %get-tuple-element.37), channel_id=1, source_target_pairs={{0,3},{1,2},{2,1},{3,0},{4,7},{5,6},{6,5},{7,4},{8,11},{9,10},{10,... | collective-permute-start | bytes 147464 | tf_op jit(solution)/shard_map/ppermute | solution.py:560
  52.4 6.3 %advance_staying.1 = (f32[8,128,128]{2,1,0:T(8,128)}, f32[8,128,128]{2,1,0:T(8,128)}, f32[8,128,128]{2,1,0:T(8,128)}) custom-call(s32[265]{0:T(512)S(4)} %index_table.1.refs_0_, f32[8,128,128]{2,1,0:T(8,128)S(1)} %get-tuple-element.27.refs_1_, f32[8,128,128]{2,1,0:T(8,128)S(1)} %get-tuple-element.28.refs_2_, f32[8,128,128]{2,1,0:T(8,128)S(1)} %get-tuple-element.29.refs_3_, ...), custom_call_target="tpu_custom_call" | custom-call | flops 33177600 | bytes 2097152 | tf_op jit(solution)/shard_map/advance_staying/pallas_call | solution.py:491
  58.7 0.0 collective-permute-done.15.refs_2_
  58.7 0.0 collective-permute-done.16.refs_3_
  58.7 1.0 %place_leaving_middle.1 = (f32[8,128,128]{2,1,0:T(8,128)}, f32[8,128,128]{2,1,0:T(8,128)}, f32[8,128,128]{2,1,0:T(8,128)}) custom-call(s32[265]{0:T(512)S(4)} %index_table.1.refs_0_, f32[2,3,112,128]{3,2,1,0:T(8,128)S(1)} %collective-permute-done.14.refs_1_, ...), custom_call_target="tpu_custom_call", output_to_operand_aliasing={{0}: (4, {}), {1}: (5, {}), {2}: (6, {})} | custom-call | tf_op jit(solution)/shard_map/place_leaving_middle/pallas_call | solution.py:539
  59.8 0.0 collective-permute-done.11.refs_1_
  59.8 0.0 collective-permute-done.12.refs_2_
  59.8 0.0 collective-permute-done.13.refs_3_
  59.8 1.1 %place_leaving_edges.1 = (f32[8,128,128]{2,1,0:T(8,128)}, f32[8,128,128]{2,1,0:T(8,128)}, f32[8,128,128]{2,1,0:T(8,128)}) custom-call(s32[265]{0:T(512)S(4)} %index_table.1.refs_0_, f32[2,3,16,128]{3,2,1,0:T(8,128)S(1)} %collective-permute-done.11.refs_1_, ...), custom_call_target="tpu_custom_call", output_to_operand_aliasing={{0}: (4, {}), {1}: (5, {}), {2}: (6, {})} | custom-call | tf_op jit(solution)/shard_map/place_leaving_edges/pallas_call | solution.py:539
Async XLA Ops:
  2.8 3.0 %copy-start = (s32[128]{0:T(128)S(1)}, s32[128]{0:T(128)}, u32[]{:S(2)}) copy-start(s32[128]{0:T(128)} %before_ref.1) | copy-start | bytes 1540
  2.8 3.0 %copy-start.1 = (s32[128]{0:T(128)S(1)}, s32[128]{0:T(128)}, u32[]{:S(2)}) copy-start(s32[128]{0:T(128)} %after_ref.1) | copy-start | bytes 1540
  2.8 3.0 %copy-start.2 = (s32[128]{0:T(128)S(1)}, s32[128]{0:T(128)}, u32[]{:S(2)}) copy-start(s32[128]{0:T(128)} %wet_ref.1) | copy-start | bytes 1540
  2.8 9.3 %collective-permute-start = (f32[4,128,128]{2,1,0:T(8,128)S(1)}, f32[4,128,128]{2,1,0:T(8,128)S(1)}, u32[]{:S(2)}, u32[]{:S(2)}) collective-permute-start(f32[4,128,128]{2,1,0:T(8,128)S(1)} %get-tuple-element.25.refs_6_), channel_id=1, source_target_pairs={{0,2},{1,3},{2,0},{3,1},{4,6},{5,7},{6,4},{7,5},{8,10},{9,11},{10,... | collective-permute-start | bytes 786440 | tf_op jit(solution)/shard_map/ppermute | solution.py:560
  5.8 14.9 %collective-permute-start.3 = (f32[4,128,128]{2,1,0:T(8,128)S(1)}, f32[4,128,128]{2,1,0:T(8,128)S(1)}, u32[]{:S(2)}, u32[]{:S(2)}) collective-permute-start(f32[4,128,128]{2,1,0:T(8,128)S(1)} %get-tuple-element.25.refs_6_), channel_id=1, source_target_pairs={{0,1},{1,0},{2,3},{3,2},{4,5},{5,4},{6,7},{7,6},{8,9},{9,8},{10,11... | collective-permute-start | bytes 786440 | tf_op jit(solution)/shard_map/ppermute | solution.py:560
  12.1 8.6 %collective-permute-start.8 = (f32[4,128,128]{2,1,0:T(8,128)S(1)}, f32[4,128,128]{2,1,0:T(8,128)S(1)}, u32[]{:S(2)}, u32[]{:S(2)}) collective-permute-start(f32[4,128,128]{2,1,0:T(8,128)S(1)} %collective-permute-done.refs_12_.refs_8_), channel_id=1, source_target_pairs={{0,1},{1,0},{2,3},{3,2},{4,5},{5,4},{6,7},{7,6},{8,9},{9,8},{10,11... | collective-permute-start | bytes 786440 | tf_op jit(solution)/shard_map/ppermute | solution.py:560
  12.1 7.1 %collective-permute-start.1 = (f32[8,32,128]{2,1,0:T(8,128)S(1)}, f32[8,32,128]{2,1,0:T(8,128)S(1)}, u32[]{:S(2)}, u32[]{:S(2)}) collective-permute-start(f32[8,32,128]{2,1,0:T(8,128)S(1)} %get-tuple-element.32), channel_id=1, source_target_pairs={{0,4},{4,8},{8,12},{1,5},{5,9},{9,13},{2,6},{6,10},{10,14},{3,7},{... | collective-permute-start | bytes 393224 | tf_op jit(solution)/shard_map/ppermute | solution.py:584
  15.9 11.0 %collective-permute-start.2 = (f32[8,32,128]{2,1,0:T(8,128)S(1)}, f32[8,32,128]{2,1,0:T(8,128)S(1)}, u32[]{:S(2)}, u32[]{:S(2)}) collective-permute-start(f32[8,32,128]{2,1,0:T(8,128)S(1)} %get-tuple-element.33), channel_id=1, source_target_pairs={{4,0},{8,4},{12,8},{5,1},{9,5},{13,9},{6,2},{10,6},{14,10},{7,3},{... | collective-permute-start | bytes 393224 | tf_op jit(solution)/shard_map/ppermute | solution.py:585
  19.3 8.5 %collective-permute-start.6 = (f32[8,32,128]{2,1,0:T(8,128)S(1)}, f32[8,32,128]{2,1,0:T(8,128)S(1)}, u32[]{:S(2)}, u32[]{:S(2)}) collective-permute-start(f32[8,32,128]{2,1,0:T(8,128)S(1)} %collective-permute-done.1.refs_7_), channel_id=1, source_target_pairs={{0,2},{1,3},{2,0},{3,1},{4,6},{5,7},{6,4},{7,5},{8,10},{9,11},{10,... | collective-permute-start | bytes 393224 | tf_op jit(solution)/shard_map/ppermute | solution.py:560
  20.8 7.7 %collective-permute-start.4 = (f32[8,32,128]{2,1,0:T(8,128)S(1)}, f32[8,32,128]{2,1,0:T(8,128)S(1)}, u32[]{:S(2)}, u32[]{:S(2)}) collective-permute-start(f32[8,32,128]{2,1,0:T(8,128)S(1)} %collective-permute-done.1.refs_7_), channel_id=1, source_target_pairs={{0,1},{1,0},{2,3},{3,2},{4,5},{5,4},{6,7},{7,6},{8,9},{9,8},{10,11... | collective-permute-start | bytes 393224 | tf_op jit(solution)/shard_map/ppermute | solution.py:560
  25.8 25.6 %collective-permute-start.14 = (f32[2,3,112,128]{3,2,1,0:T(8,128)S(1)}, f32[2,3,112,128]{3,2,1,0:T(8,128)S(1)}, u32[]{:S(2)}, u32[]{:S(2)}) collective-permute-start(f32[2,3,112,128]{3,2,1,0:T(8,128)S(1)} %get-tuple-element.38), channel_id=1, source_target_pairs={{0,1},{1,0},{2,3},{3,2},{4,5},{5,4},{6,7},{7,6},{8,9},{9,8},{10,11... | collective-permute-start | bytes 1032200 | tf_op jit(solution)/shard_map/ppermute | solution.py:560
  26.4 32.4 %collective-permute-start.15 = (f32[2,3,112,128]{3,2,1,0:T(8,128)S(1)}, f32[2,3,112,128]{3,2,1,0:T(8,128)S(1)}, u32[]{:S(2)}, u32[]{:S(2)}) collective-permute-start(f32[2,3,112,128]{3,2,1,0:T(8,128)S(1)} %get-tuple-element.39), channel_id=1, source_target_pairs={{0,2},{1,3},{2,0},{3,1},{4,6},{5,7},{6,4},{7,5},{8,10},{9,11},{10,... | collective-permute-start | bytes 1032200 | tf_op jit(solution)/shard_map/ppermute | solution.py:560
  26.9 31.8 %collective-permute-start.16 = (f32[2,3,112,128]{3,2,1,0:T(8,128)S(1)}, f32[2,3,112,128]{3,2,1,0:T(8,128)S(1)}, u32[]{:S(2)}, u32[]{:S(2)}) collective-permute-start(f32[2,3,112,128]{3,2,1,0:T(8,128)S(1)} %get-tuple-element.40), channel_id=1, source_target_pairs={{0,3},{1,2},{2,1},{3,0},{4,7},{5,6},{6,5},{7,4},{8,11},{9,10},{10,... | collective-permute-start | bytes 1032200 | tf_op jit(solution)/shard_map/ppermute | solution.py:560
  27.8 18.8 %collective-permute-start.7 = (f32[8,32,128]{2,1,0:T(8,128)S(1)}, f32[8,32,128]{2,1,0:T(8,128)S(1)}, u32[]{:S(2)}, u32[]{:S(2)}) collective-permute-start(f32[8,32,128]{2,1,0:T(8,128)S(1)} %collective-permute-done.2.refs_8_), channel_id=1, source_target_pairs={{0,2},{1,3},{2,0},{3,1},{4,6},{5,7},{6,4},{7,5},{8,10},{9,11},{10,... | collective-permute-start | bytes 393224 | tf_op jit(solution)/shard_map/ppermute | solution.py:560
  28.5 18.1 %collective-permute-start.5 = (f32[8,32,128]{2,1,0:T(8,128)S(1)}, f32[8,32,128]{2,1,0:T(8,128)S(1)}, u32[]{:S(2)}, u32[]{:S(2)}) collective-permute-start(f32[8,32,128]{2,1,0:T(8,128)S(1)} %collective-permute-done.2.refs_8_), channel_id=1, source_target_pairs={{0,1},{1,0},{2,3},{3,2},{4,5},{5,4},{6,7},{7,6},{8,9},{9,8},{10,11... | collective-permute-start | bytes 393224 | tf_op jit(solution)/shard_map/ppermute | solution.py:560
  46.6 1.3 %collective-permute-start.9 = (f32[8,32,128]{2,1,0:T(8,128)S(1)}, f32[8,32,128]{2,1,0:T(8,128)S(1)}, u32[]{:S(2)}, u32[]{:S(2)}) collective-permute-start(f32[8,32,128]{2,1,0:T(8,128)S(1)} %collective-permute-done.6.refs_13_), channel_id=1, source_target_pairs={{0,1},{1,0},{2,3},{3,2},{4,5},{5,4},{6,7},{7,6},{8,9},{9,8},{10,11... | collective-permute-start | bytes 393224 | tf_op jit(solution)/shard_map/ppermute | solution.py:560
  46.6 1.5 %collective-permute-start.10 = (f32[8,32,128]{2,1,0:T(8,128)S(1)}, f32[8,32,128]{2,1,0:T(8,128)S(1)}, u32[]{:S(2)}, u32[]{:S(2)}) collective-permute-start(f32[8,32,128]{2,1,0:T(8,128)S(1)} %collective-permute-done.7.refs_14_), channel_id=1, source_target_pairs={{0,1},{1,0},{2,3},{3,2},{4,5},{5,4},{6,7},{7,6},{8,9},{9,8},{10,11... | collective-permute-start | bytes 393224 | tf_op jit(solution)/shard_map/ppermute | solution.py:560
  50.5 9.3 %collective-permute-start.11 = (f32[2,3,16,128]{3,2,1,0:T(8,128)S(1)}, f32[2,3,16,128]{3,2,1,0:T(8,128)S(1)}, u32[]{:S(2)}, u32[]{:S(2)}) collective-permute-start(f32[2,3,16,128]{3,2,1,0:T(8,128)S(1)} %get-tuple-element.35), channel_id=1, source_target_pairs={{0,1},{1,0},{2,3},{3,2},{4,5},{5,4},{6,7},{7,6},{8,9},{9,8},{10,11... | collective-permute-start | bytes 147464 | tf_op jit(solution)/shard_map/ppermute | solution.py:560
  50.8 9.0 %collective-permute-start.12 = (f32[2,3,16,128]{3,2,1,0:T(8,128)S(1)}, f32[2,3,16,128]{3,2,1,0:T(8,128)S(1)}, u32[]{:S(2)}, u32[]{:S(2)}) collective-permute-start(f32[2,3,16,128]{3,2,1,0:T(8,128)S(1)} %get-tuple-element.36), channel_id=1, source_target_pairs={{0,2},{1,3},{2,0},{3,1},{4,6},{5,7},{6,4},{7,5},{8,10},{9,11},{10,... | collective-permute-start | bytes 147464 | tf_op jit(solution)/shard_map/ppermute | solution.py:560
  51.4 8.4 %collective-permute-start.13 = (f32[2,3,16,128]{3,2,1,0:T(8,128)S(1)}, f32[2,3,16,128]{3,2,1,0:T(8,128)S(1)}, u32[]{:S(2)}, u32[]{:S(2)}) collective-permute-start(f32[2,3,16,128]{3,2,1,0:T(8,128)S(1)} %get-tuple-element.37), channel_id=1, source_target_pairs={{0,3},{1,2},{2,1},{3,0},{4,7},{5,6},{6,5},{7,4},{8,11},{9,10},{10,... | collective-permute-start | bytes 147464 | tf_op jit(solution)/shard_map/ppermute | solution.py:560

commit v5 on v4

--- a/solution.py
+++ b/solution.py
@@ -153,8 +153,9 @@
 
 def load_kernel(*refs):
     sources, refs = refs[:FIELDS], refs[FIELDS:]
-    fields, (columns, first, last, sem) = refs[:FIELDS], refs[FIELDS:]
+    fields, (columns, pair_even, pair_odd, first, last, sem) = refs[:FIELDS], refs[FIELDS:]
     lane = lane_index()
+    odd = remainder(lax.axis_index("row"), 2) == 1
     copies = [
         pltpu.make_async_copy(sources[f], fields[f], sem.at[f]) for f in range(FIELDS)
     ]
@@ -176,6 +177,8 @@
         for t in range(tile_count):
             first[t, HALO * f : HALO * (f + 1), :] = fields[f][t, :HALO, :]
             last[t, 2 + HALO * f : 2 + HALO * (f + 1), :] = fields[f][t, SIDE - HALO :, :]
+    pair_even[...] = jnp.where(odd, first[...], last[...])
+    pair_odd[...] = jnp.where(odd, last[...], first[...])
 
 
 def load(arrays):
@@ -189,9 +192,26 @@
         out_shape=tuple(outs),
         in_specs=[pl.BlockSpec(memory_space=pltpu.HBM)] * FIELDS,
         out_specs=tuple(vmem_specs(len(outs))),
-        scratch_shapes=[pltpu.SemaphoreType.DMA((FIELDS,))],
+        scratch_shapes=[rows, rows, pltpu.SemaphoreType.DMA((FIELDS,))],
         compiler_params=SMALL,
     )(*[pltpu.with_memory_space_constraint(array, pltpu.HBM) for array in arrays])
+
+
+def join_kernel(met_even, met_odd, joined):
+    odd = remainder(lax.axis_index("row"), 2) == 1
+    joined[0] = jnp.where(odd, met_even[...], met_odd[...])
+    joined[1] = jnp.where(odd, met_odd[...], met_even[...])
+
+
+def join(met_even, met_odd):
+    return pl.pallas_call(
+        join_kernel,
+        name="join_row_halos",
+        out_shape=VMEM((2,) + met_even.shape, met_even.dtype),
+        in_specs=vmem_specs(2),
+        out_specs=pl.BlockSpec(memory_space=VMEM),
+        compiler_params=SMALL,
+    )(in_vmem(met_even), in_vmem(met_odd))
 
 
 def face(flow, level, level_next, ground, friction):
@@ -255,11 +275,13 @@
     for f in range(FIELDS):
         rows = pl.ds(HALO * f, 8)
 
-        def ends(halo, middle, left, right, out):
-            mid = halo[middle[0], middle[1], rows, :]
+        def ends(side, middle, left, right, out):
+            mid, left_end, right_end = (
+                stacks[1][place[0], side, place[1], rows, :] for place in (middle, left, right)
+            )
             block[f][i, out : out + 8, :] = mid
-            lower = jnp.where(lane < SIDE // 2, mid, halo[left[0], left[1], rows, :])
-            upper = jnp.where(lane < SIDE // 2, halo[right[0], right[1], rows, :], mid)
+            lower = jnp.where(lane < SIDE // 2, mid, left_end)
+            upper = jnp.where(lane < SIDE // 2, right_end, mid)
             value = jnp.where(
                 inside(0, 16),
                 pltpu.roll(lower, (at + 8) % SIDE, 1),
@@ -270,8 +292,8 @@
             strip[f][out : out + 8, :] = value
 
         if part.halo_rows:
-            ends(stacks[1], near("n"), near("nw"), near("ne"), LO)
-            ends(stacks[2], near("s"), near("sw"), near("se"), TOP + SIDE)
+            ends(0, near("n"), near("nw"), near("ne"), LO)
+            ends(1, near("s"), near("sw"), near("se"), TOP + SIDE)
 
         for start, count in part.own:
             own, out = pl.ds(start, count), pl.ds(TOP + start, count)
@@ -362,7 +384,7 @@
 def advance_kernel(part, lanes, *refs):
     table = refs[0]
     fields = refs[1 : 1 + FIELDS]
-    kinds = 3 if part.halo_rows else 1
+    kinds = 2 if part.halo_rows else 1
     halos, refs = refs[1 + FIELDS : 1 + FIELDS + kinds * lanes], refs[1 + FIELDS + kinds * lanes :]
     n_out = 3 if part is WHOLE else lanes - 1
     outs, stacks, refs = refs[:n_out], refs[n_out : n_out + kinds], refs[n_out + kinds :]
@@ -571,23 +593,38 @@
     ]
 
 
+def meet_rows(array, parity):
+    rows, subs = lax.axis_size("row"), lax.axis_size("sub")
+    pairs = []
+    for r in range(rows):
+        other = r + 1 if r % 2 == parity else r - 1
+        for s in range(subs):
+            if 0 <= other < rows:
+                pairs.append((r * subs + s, other * subs + s))
+            else:
+                pairs.append((r * subs + s, r * subs + (s + 1) % subs))
+    return lax.ppermute(array, ("row", "sub"), pairs)
+
+
 def shards(
     water_depth, flow_east, flow_south, bed_level, manning_n, placed_before, placed_after, wet_tiles
 ):
-    cols, subs, rows = lax.axis_size("col"), lax.axis_size("sub"), lax.axis_size("row")
+    cols, subs = lax.axis_size("col"), lax.axis_size("sub")
     tile_count = water_depth.shape[0]
-    *fields, columns, first, last = load(
+    *fields, columns, pair_even, pair_odd = load(
         (water_depth, flow_east, flow_south, bed_level, manning_n)
     )
     fields = [in_vmem(field) for field in fields]
     columns = over_cols(columns)
-    above = over_cols(lax.ppermute(last, "row", [(i, i + 1) for i in range(rows - 1)]))
-    below = over_cols(lax.ppermute(first, "row", [(i + 1, i) for i in range(rows - 1)]))
+    met_even, met_odd = meet_rows(pair_even, 0), meet_rows(pair_odd, 1)
     table = make_table(
         (cols, subs, tile_count, placed_before.shape[0]), placed_before, placed_after, wet_tiles
     )
-    columns[1:], table = lax.optimization_barrier((columns[1:], table))
+    columns[1:], met_even, met_odd, table = lax.optimization_barrier(
+        (columns[1:], met_even, met_odd, table)
+    )
     table = pltpu.with_memory_space_constraint(table, SMEM)
+    near_rows = over_subs(over_cols(join(met_even, met_odd)))
     columns = over_subs(columns)
 
     def send(parts):
@@ -596,7 +633,7 @@
         ]
 
     middle = send(advance(EARLY, table, fields, [(part,) for part in columns]))
-    halos = list(zip(columns, over_subs(above), over_subs(below)))
+    halos = list(zip(columns, near_rows))
     edges = send(advance(LATE, table, fields, halos))
     outs = advance(WHOLE, table, fields, halos)
     outs = place(EARLY, table, middle, outs)

time: 61.4 us -> 39.7 us (0.65)
  waiting for transfers between devices: 25.6 us -> 7.96 us
  starting transfers between devices: 14.9 us -> 11.3 us
    ppermute x15 -> x12, waiting for transfers between devices: 23.5 us -> 6.74 us  [shift_lanes(): return lax.ppermute(array, ('col', 'sub'), pairs)]
    ppermute x2, starting transfers between devices: 5.02 us -> 1.58 us  [meet_rows(): return lax.ppermute(array, ('row', 'sub'), pairs)]
    ppermute x2, waiting for transfers between devices: 2.1 us -> 1.22 us  [meet_rows(): return lax.ppermute(array, ('row', 'sub'), pairs)]
    ppermute x15 -> x12, starting transfers between devices: 9.9 us -> 9.68 us  [shift_lanes(): return lax.ppermute(array, ('col', 'sub'), pairs)]
  transfers between devices with their start and end apart: 17 -> 14, of which waited for: 5 -> 6; matrix products, arithmetic and copies ran while one was open for 0% -> 0% of each run, Pallas kernels for 27% -> 41%
where the time goes in v5:
time: 39.7 us; the launch traced here: 39.6 us
  Pallas kernels  19.6 us (49%)
  starting transfers between devices  11.3 us (28%)
  waiting for transfers between devices  7.96 us (20%)
  between operations  0.72 us (2%)
    pallas_call x3, Pallas kernels, advance(): pl.pallas_call(functools.partial(advance_kernel, part, lanes), name='adva...  13.7 us
    ppermute x12, starting transfers between devices, shift_lanes(): return lax.ppermute(array, ('col', 'sub'), pairs)  9.68 us
    ppermute x12, waiting for transfers between devices, shift_lanes(): return lax.ppermute(array, ('col', 'sub'), pairs)  6.74 us
    pallas_call x1, Pallas kernels, load(): pl.pallas_call(load_kernel, name='load_and_pack', out_shape=tuple(outs),...  2.16 us
    pallas_call x2, Pallas kernels, place(): pl.pallas_call(functools.partial(place_kernel, part.sent, lanes), name='p...  2.14 us
    pallas_call x1, Pallas kernels, make_table(): pl.pallas_call(functools.partial(index_kernel, shape), name='index_table'...  1.65 us
    ppermute x2, starting transfers between devices, meet_rows(): return lax.ppermute(array, ('row', 'sub'), pairs)  1.58 us
    ppermute x2, waiting for transfers between devices, meet_rows(): return lax.ppermute(array, ('row', 'sub'), pairs)  1.22 us
  transfers between devices with their start and end apart: 14, of which 6 were waited for; matrix products, arithmetic and copies ran while one was open for 0% of the time, Pallas kernels for 41%

profile of v5, /device:TPU:0, one launch (start us, length us, event | category | flops | bytes accessed | tf_op | source)
XLA Modules:
  0.0 39.6 jit_solution(6994208560513292874)
XLA Ops:
  0.6 2.2 %load_and_pack.1 = (f32[8,128,128]{2,1,0:T(8,128)S(1)}, f32[8,128,128]{2,1,0:T(8,128)S(1)}, f32[8,128,128]{2,1,0:T(8,128)S(1)}, f32[8,128,128]{2,1,0:T(8,128)S(1...) custom-call(f32[8,128,128]{2,1,0:T(8,128)} %refs_0_.1, ...), custom_call_target="tpu_custom_call" | custom-call | tf_op jit(solution)/shard_map/load_and_pack/pallas_call | solution.py:189
  2.8 3.0 %collective-permute-start = (f32[4,128,128]{2,1,0:T(8,128)S(1)}, f32[4,128,128]{2,1,0:T(8,128)S(1)}, u32[]{:S(2)}, u32[]{:S(2)}) collective-permute-start(f32[4,128,128]{2,1,0:T(8,128)S(1)} %get-tuple-element.27.refs_6_), channel_id=1, source_target_pairs={{0,2},{1,3},{2,0},{3,1},{4,6},{5,7},{6,4},{7,5},{8,10},{9,11},{10,... | collective-permute-start | bytes 786440 | tf_op jit(solution)/shard_map/ppermute | solution.py:582
  5.8 0.0 copy-start
  5.8 0.0 copy-start.1
  5.8 0.0 copy-start.2
  5.8 1.6 %collective-permute-start.1 = (f32[8,32,128]{2,1,0:T(8,128)S(1)}, f32[8,32,128]{2,1,0:T(8,128)S(1)}, u32[]{:S(2)}, u32[]{:S(2)}) collective-permute-start(f32[8,32,128]{2,1,0:T(8,128)S(1)} %get-tuple-element.28), channel_id=1, source_target_pairs={{0,4},{1,5},{4,0},{5,1},{8,12},{9,13},{12,8},{13,9},{2,6},{3,7},{6... | collective-permute-start | bytes 393224 | tf_op jit(solution)/shard_map/ppermute | solution.py:606
  7.4 0.0 collective-permute-start.2
  7.4 0.5 %collective-permute-start.3 = (f32[4,128,128]{2,1,0:T(8,128)S(1)}, f32[4,128,128]{2,1,0:T(8,128)S(1)}, u32[]{:S(2)}, u32[]{:S(2)}) collective-permute-start(f32[4,128,128]{2,1,0:T(8,128)S(1)} %get-tuple-element.27.refs_6_), channel_id=1, source_target_pairs={{0,1},{1,0},{2,3},{3,2},{4,5},{5,4},{6,7},{7,6},{8,9},{9,8},{10,11... | collective-permute-start | bytes 786440 | tf_op jit(solution)/shard_map/ppermute | solution.py:582
  7.9 0.0 copy-done
  7.9 0.0 copy-done.1
  7.9 0.0 copy-done.2
  7.9 1.6 %index_table.1.refs_0_ = s32[265]{0:T(512)S(4)} custom-call(s32[128]{0:T(128)S(1)} %copy-done, s32[128]{0:T(128)S(1)} %copy-done.1, s32[128]{0:T(128)S(1)} %copy-done.2), custom_call_target="tpu_custom_call" | custom-call | tf_op jit(solution)/shard_map/index_table/pallas_call | solution.py:131
  9.6 1.2 %collective-permute-done.1.met_even = f32[8,32,128]{2,1,0:T(8,128)S(1)} collective-permute-done((f32[8,32,128]{2,1,0:T(8,128)S(1)}, f32[8,32,128]{2,1,0:T(8,128)S(1)}, u32[]{:S(2)}, u32[]{:S(2)}) %collective-permute-start.1) | collective-permute-done | bytes 131104 | tf_op jit(solution)/shard_map/ppermute | solution.py:606
  10.8 0.0 collective-permute-done.2.met_odd
  10.8 1.3 %collective-permute-done.refs_10_.refs_8_ = f32[4,128,128]{2,1,0:T(8,128)S(1)} collective-permute-done((f32[4,128,128]{2,1,0:T(8,128)S(1)}, f32[4,128,128]{2,1,0:T(8,128)S(1)}, u32[]{:S(2)}, u32[]{:S(2)}) %collective-permute-start) | collective-permute-done | bytes 262176 | tf_op jit(solution)/shard_map/ppermute | solution.py:582
  12.1 0.0 collective-permute-start.6
  12.1 1.8 %collective-permute-start.5 = (f32[2,8,32,128]{3,2,1,0:T(8,128)S(1)}, f32[2,8,32,128]{3,2,1,0:T(8,128)S(1)}, u32[]{:S(2)}, u32[]{:S(2)}) collective-permute-start(f32[2,8,32,128]{3,2,1,0:T(8,128)S(1)} %join_row_halos.1.refs_7_), channel_id=1, source_target_pairs={{0,2},{1,3},{2,0},{3,1},{4,6},{5,7},{6,4},{7,5},{8,10},{9,11},{10,... | collective-permute-start | bytes 786440 | tf_op jit(solution)/shard_map/ppermute | solution.py:582
  13.9 0.0 collective-permute-done.3.refs_8_.refs_7_
  13.9 0.0 collective-permute-done.6.refs_12_.refs_9_
  14.0 5.0 %advance_leaving_middle.1 = (f32[2,3,112,128]{3,2,1,0:T(8,128)S(1)}, f32[2,3,112,128]{3,2,1,0:T(8,128)S(1)}, f32[2,3,112,128]{3,2,1,0:T(8,128)S(1)}) custom-call(s32[265]{0:T(512)S(4)} %index_table.1.refs_0_, f32[8,128,128]{2,1,0:T(8,128)S(1)} %get-tuple-element.31.refs_1_, f32[8,128,128]{2,1,0:T(8,128)S(1)} %get-tuple-element.32.refs_2_, ...), custom_call_target="tpu_custom_call" | custom-call | flops 29491200 | bytes 1835008 | tf_op jit(solution)/shard_map/advance_leaving_middle/pallas_call | solution.py:513
  19.0 0.3 collective-permute-start.11
  19.3 1.4 %collective-permute-start.12 = (f32[2,3,112,128]{3,2,1,0:T(8,128)S(1)}, f32[2,3,112,128]{3,2,1,0:T(8,128)S(1)}, u32[]{:S(2)}, u32[]{:S(2)}) collective-permute-start(f32[2,3,112,128]{3,2,1,0:T(8,128)S(1)} %get-tuple-element.43), channel_id=1, source_target_pairs={{0,2},{1,3},{2,0},{3,1},{4,6},{5,7},{6,4},{7,5},{8,10},{9,11},{10,... | collective-permute-start | bytes 1032200 | tf_op jit(solution)/shard_map/ppermute | solution.py:582
  20.6 0.3 collective-permute-start.13
  20.9 0.5 %collective-permute-start.4 = (f32[2,8,32,128]{3,2,1,0:T(8,128)S(1)}, f32[2,8,32,128]{3,2,1,0:T(8,128)S(1)}, u32[]{:S(2)}, u32[]{:S(2)}) collective-permute-start(f32[2,8,32,128]{3,2,1,0:T(8,128)S(1)} %join_row_halos.1.refs_7_), channel_id=1, source_target_pairs={{0,1},{1,0},{2,3},{3,2},{4,5},{5,4},{6,7},{7,6},{8,9},{9,8},{10,11... | collective-permute-start | bytes 786440 | tf_op jit(solution)/shard_map/ppermute | solution.py:582
  21.4 0.0 collective-permute-done.5.refs_11_
  21.4 0.0 collective-permute-start.7
  21.4 1.2 %collective-permute-done.4.refs_9_ = f32[2,8,32,128]{3,2,1,0:T(8,128)S(1)} collective-permute-done((f32[2,8,32,128]{3,2,1,0:T(8,128)S(1)}, f32[2,8,32,128]{3,2,1,0:T(8,128)S(1)}, u32[]{:S(2)}, u32[]{:S(2)}) %collective-permute-start.4) | collective-permute-done | bytes 262176 | tf_op jit(solution)/shard_map/ppermute | solution.py:582
  22.6 0.4 collective-permute-done.7.refs_13_
  22.9 2.3 %advance_leaving_edges.1 = (f32[2,3,16,128]{3,2,1,0:T(8,128)S(1)}, f32[2,3,16,128]{3,2,1,0:T(8,128)S(1)}, f32[2,3,16,128]{3,2,1,0:T(8,128)S(1)}) custom-call(s32[265]{0:T(512)S(4)} %index_table.1.refs_0_, f32[8,128,128]{2,1,0:T(8,128)S(1)} %get-tuple-element.31.refs_1_, f32[8,128,128]{2,1,0:T(8,128)S(1)} %get-tuple-element.32.refs_2_, ...), custom_call_target="tpu_custom_call" | custom-call | flops 11059200 | bytes 262144 | tf_op jit(solution)/shard_map/advance_leaving_edges/pallas_call | solution.py:513
  25.3 0.4 %collective-permute-start.8 = (f32[2,3,16,128]{3,2,1,0:T(8,128)S(1)}, f32[2,3,16,128]{3,2,1,0:T(8,128)S(1)}, u32[]{:S(2)}, u32[]{:S(2)}) collective-permute-start(f32[2,3,16,128]{3,2,1,0:T(8,128)S(1)} %get-tuple-element.39), channel_id=1, source_target_pairs={{0,1},{1,0},{2,3},{3,2},{4,5},{5,4},{6,7},{7,6},{8,9},{9,8},{10,11... | collective-permute-start | bytes 147464 | tf_op jit(solution)/shard_map/ppermute | solution.py:582
  25.7 1.4 %collective-permute-start.9 = (f32[2,3,16,128]{3,2,1,0:T(8,128)S(1)}, f32[2,3,16,128]{3,2,1,0:T(8,128)S(1)}, u32[]{:S(2)}, u32[]{:S(2)}) collective-permute-start(f32[2,3,16,128]{3,2,1,0:T(8,128)S(1)} %get-tuple-element.40), channel_id=1, source_target_pairs={{0,2},{1,3},{2,0},{3,1},{4,6},{5,7},{6,4},{7,5},{8,10},{9,11},{10,... | collective-permute-start | bytes 147464 | tf_op jit(solution)/shard_map/ppermute | solution.py:582
  27.1 0.0 collective-permute-done.11.refs_1_
  27.1 0.1 collective-permute-start.10
  27.2 6.3 %advance_staying.1 = (f32[8,128,128]{2,1,0:T(8,128)}, f32[8,128,128]{2,1,0:T(8,128)}, f32[8,128,128]{2,1,0:T(8,128)}) custom-call(s32[265]{0:T(512)S(4)} %index_table.1.refs_0_, f32[8,128,128]{2,1,0:T(8,128)S(1)} %get-tuple-element.31.refs_1_, f32[8,128,128]{2,1,0:T(8,128)S(1)} %get-tuple-element.32.refs_2_, f32[8,128,128]{2,1,0:T(8,128)S(1)} %get-tuple-element.33.refs_3_, ...), custom_call_target="tpu_custom_call" | custom-call | flops 33177600 | bytes 2097152 | tf_op jit(solution)/shard_map/advance_staying/pallas_call | solution.py:513
  33.5 0.0 collective-permute-done.12.refs_2_
  33.5 2.8 %collective-permute-done.13.refs_3_ = f32[2,3,112,128]{3,2,1,0:T(8,128)S(1)} collective-permute-done((f32[2,3,112,128]{3,2,1,0:T(8,128)S(1)}, f32[2,3,112,128]{3,2,1,0:T(8,128)S(1)}, u32[]{:S(2)}, u32[]{:S(2)}) %collective-permute-start.13) | collective-permute-done | bytes 344096 | tf_op jit(solution)/shard_map/ppermute | solution.py:582
  36.4 1.0 %place_leaving_middle.1 = (f32[8,128,128]{2,1,0:T(8,128)}, f32[8,128,128]{2,1,0:T(8,128)}, f32[8,128,128]{2,1,0:T(8,128)}) custom-call(s32[265]{0:T(512)S(4)} %index_table.1.refs_0_, f32[2,3,112,128]{3,2,1,0:T(8,128)S(1)} %collective-permute-done.11.refs_1_, ...), custom_call_target="tpu_custom_call", output_to_operand_aliasing={{0}: (4, {}), {1}: (5, {}), {2}: (6, {})} | custom-call | tf_op jit(solution)/shard_map/place_leaving_middle/pallas_call | solution.py:561
  37.4 0.0 collective-permute-done.8.refs_1_
  37.4 1.0 %collective-permute-done.9.refs_2_ = f32[2,3,16,128]{3,2,1,0:T(8,128)S(1)} collective-permute-done((f32[2,3,16,128]{3,2,1,0:T(8,128)S(1)}, f32[2,3,16,128]{3,2,1,0:T(8,128)S(1)}, u32[]{:S(2)}, u32[]{:S(2)}) %collective-permute-start.9) | collective-permute-done | bytes 49184 | tf_op jit(solution)/shard_map/ppermute | solution.py:582
  38.5 0.0 collective-permute-done.10.refs_3_
  38.5 1.1 %place_leaving_edges.1 = (f32[8,128,128]{2,1,0:T(8,128)}, f32[8,128,128]{2,1,0:T(8,128)}, f32[8,128,128]{2,1,0:T(8,128)}) custom-call(s32[265]{0:T(512)S(4)} %index_table.1.refs_0_, f32[2,3,16,128]{3,2,1,0:T(8,128)S(1)} %collective-permute-done.8.refs_1_, ...), custom_call_target="tpu_custom_call", output_to_operand_aliasing={{0}: (4, {}), {1}: (5, {}), {2}: (6, {})} | custom-call | tf_op jit(solution)/shard_map/place_leaving_edges/pallas_call | solution.py:561
  (1 shorter events, 0.0 us)
Async XLA Ops:
  2.8 9.3 %collective-permute-start = (f32[4,128,128]{2,1,0:T(8,128)S(1)}, f32[4,128,128]{2,1,0:T(8,128)S(1)}, u32[]{:S(2)}, u32[]{:S(2)}) collective-permute-start(f32[4,128,128]{2,1,0:T(8,128)S(1)} %get-tuple-element.27.refs_6_), channel_id=1, source_target_pairs={{0,2},{1,3},{2,0},{3,1},{4,6},{5,7},{6,4},{7,5},{8,10},{9,11},{10,... | collective-permute-start | bytes 786440 | tf_op jit(solution)/shard_map/ppermute | solution.py:582
  5.8 2.1 %copy-start = (s32[128]{0:T(128)S(1)}, s32[128]{0:T(128)}, u32[]{:S(2)}) copy-start(s32[128]{0:T(128)} %before_ref.1) | copy-start | bytes 1540
  5.8 2.1 %copy-start.1 = (s32[128]{0:T(128)S(1)}, s32[128]{0:T(128)}, u32[]{:S(2)}) copy-start(s32[128]{0:T(128)} %after_ref.1) | copy-start | bytes 1540
  5.8 2.1 %copy-start.2 = (s32[128]{0:T(128)S(1)}, s32[128]{0:T(128)}, u32[]{:S(2)}) copy-start(s32[128]{0:T(128)} %wet_ref.1) | copy-start | bytes 1540
  5.8 5.0 %collective-permute-start.1 = (f32[8,32,128]{2,1,0:T(8,128)S(1)}, f32[8,32,128]{2,1,0:T(8,128)S(1)}, u32[]{:S(2)}, u32[]{:S(2)}) collective-permute-start(f32[8,32,128]{2,1,0:T(8,128)S(1)} %get-tuple-element.28), channel_id=1, source_target_pairs={{0,4},{1,5},{4,0},{5,1},{8,12},{9,13},{12,8},{13,9},{2,6},{3,7},{6... | collective-permute-start | bytes 393224 | tf_op jit(solution)/shard_map/ppermute | solution.py:606
  7.4 3.4 %collective-permute-start.2 = (f32[8,32,128]{2,1,0:T(8,128)S(1)}, f32[8,32,128]{2,1,0:T(8,128)S(1)}, u32[]{:S(2)}, u32[]{:S(2)}) collective-permute-start(f32[8,32,128]{2,1,0:T(8,128)S(1)} %get-tuple-element.29), channel_id=1, source_target_pairs={{0,1},{1,0},{4,8},{5,9},{8,4},{9,5},{12,13},{13,12},{2,3},{3,2},{6... | collective-permute-start | bytes 393224 | tf_op jit(solution)/shard_map/ppermute | solution.py:606
  7.4 6.6 %collective-permute-start.3 = (f32[4,128,128]{2,1,0:T(8,128)S(1)}, f32[4,128,128]{2,1,0:T(8,128)S(1)}, u32[]{:S(2)}, u32[]{:S(2)}) collective-permute-start(f32[4,128,128]{2,1,0:T(8,128)S(1)} %get-tuple-element.27.refs_6_), channel_id=1, source_target_pairs={{0,1},{1,0},{2,3},{3,2},{4,5},{5,4},{6,7},{7,6},{8,9},{9,8},{10,11... | collective-permute-start | bytes 786440 | tf_op jit(solution)/shard_map/ppermute | solution.py:582
  12.1 1.8 %collective-permute-start.6 = (f32[4,128,128]{2,1,0:T(8,128)S(1)}, f32[4,128,128]{2,1,0:T(8,128)S(1)}, u32[]{:S(2)}, u32[]{:S(2)}) collective-permute-start(f32[4,128,128]{2,1,0:T(8,128)S(1)} %collective-permute-done.refs_10_.refs_8_), channel_id=1, source_target_pairs={{0,1},{1,0},{2,3},{3,2},{4,5},{5,4},{6,7},{7,6},{8,9},{9,8},{10,11... | collective-permute-start | bytes 786440 | tf_op jit(solution)/shard_map/ppermute | solution.py:582
  12.1 9.3 %collective-permute-start.5 = (f32[2,8,32,128]{3,2,1,0:T(8,128)S(1)}, f32[2,8,32,128]{3,2,1,0:T(8,128)S(1)}, u32[]{:S(2)}, u32[]{:S(2)}) collective-permute-start(f32[2,8,32,128]{3,2,1,0:T(8,128)S(1)} %join_row_halos.1.refs_7_), channel_id=1, source_target_pairs={{0,2},{1,3},{2,0},{3,1},{4,6},{5,7},{6,4},{7,5},{8,10},{9,11},{10,... | collective-permute-start | bytes 786440 | tf_op jit(solution)/shard_map/ppermute | solution.py:582
  19.0 8.1 %collective-permute-start.11 = (f32[2,3,112,128]{3,2,1,0:T(8,128)S(1)}, f32[2,3,112,128]{3,2,1,0:T(8,128)S(1)}, u32[]{:S(2)}, u32[]{:S(2)}) collective-permute-start(f32[2,3,112,128]{3,2,1,0:T(8,128)S(1)} %get-tuple-element.42), channel_id=1, source_target_pairs={{0,1},{1,0},{2,3},{3,2},{4,5},{5,4},{6,7},{7,6},{8,9},{9,8},{10,11... | collective-permute-start | bytes 1032200 | tf_op jit(solution)/shard_map/ppermute | solution.py:582
  19.3 14.3 %collective-permute-start.12 = (f32[2,3,112,128]{3,2,1,0:T(8,128)S(1)}, f32[2,3,112,128]{3,2,1,0:T(8,128)S(1)}, u32[]{:S(2)}, u32[]{:S(2)}) collective-permute-start(f32[2,3,112,128]{3,2,1,0:T(8,128)S(1)} %get-tuple-element.43), channel_id=1, source_target_pairs={{0,2},{1,3},{2,0},{3,1},{4,6},{5,7},{6,4},{7,5},{8,10},{9,11},{10,... | collective-permute-start | bytes 1032200 | tf_op jit(solution)/shard_map/ppermute | solution.py:582
  20.6 15.8 %collective-permute-start.13 = (f32[2,3,112,128]{3,2,1,0:T(8,128)S(1)}, f32[2,3,112,128]{3,2,1,0:T(8,128)S(1)}, u32[]{:S(2)}, u32[]{:S(2)}) collective-permute-start(f32[2,3,112,128]{3,2,1,0:T(8,128)S(1)} %get-tuple-element.44), channel_id=1, source_target_pairs={{0,3},{1,2},{2,1},{3,0},{4,7},{5,6},{6,5},{7,4},{8,11},{9,10},{10,... | collective-permute-start | bytes 1032200 | tf_op jit(solution)/shard_map/ppermute | solution.py:582
  20.9 1.7 %collective-permute-start.4 = (f32[2,8,32,128]{3,2,1,0:T(8,128)S(1)}, f32[2,8,32,128]{3,2,1,0:T(8,128)S(1)}, u32[]{:S(2)}, u32[]{:S(2)}) collective-permute-start(f32[2,8,32,128]{3,2,1,0:T(8,128)S(1)} %join_row_halos.1.refs_7_), channel_id=1, source_target_pairs={{0,1},{1,0},{2,3},{3,2},{4,5},{5,4},{6,7},{7,6},{8,9},{9,8},{10,11... | collective-permute-start | bytes 786440 | tf_op jit(solution)/shard_map/ppermute | solution.py:582
  21.4 1.5 %collective-permute-start.7 = (f32[2,8,32,128]{3,2,1,0:T(8,128)S(1)}, f32[2,8,32,128]{3,2,1,0:T(8,128)S(1)}, u32[]{:S(2)}, u32[]{:S(2)}) collective-permute-start(f32[2,8,32,128]{3,2,1,0:T(8,128)S(1)} %collective-permute-done.5.refs_11_), channel_id=1, source_target_pairs={{0,1},{1,0},{2,3},{3,2},{4,5},{5,4},{6,7},{7,6},{8,9},{9,8},{10,11... | collective-permute-start | bytes 786440 | tf_op jit(solution)/shard_map/ppermute | solution.py:582
  25.3 12.2 %collective-permute-start.8 = (f32[2,3,16,128]{3,2,1,0:T(8,128)S(1)}, f32[2,3,16,128]{3,2,1,0:T(8,128)S(1)}, u32[]{:S(2)}, u32[]{:S(2)}) collective-permute-start(f32[2,3,16,128]{3,2,1,0:T(8,128)S(1)} %get-tuple-element.39), channel_id=1, source_target_pairs={{0,1},{1,0},{2,3},{3,2},{4,5},{5,4},{6,7},{7,6},{8,9},{9,8},{10,11... | collective-permute-start | bytes 147464 | tf_op jit(solution)/shard_map/ppermute | solution.py:582
  25.7 12.8 %collective-permute-start.9 = (f32[2,3,16,128]{3,2,1,0:T(8,128)S(1)}, f32[2,3,16,128]{3,2,1,0:T(8,128)S(1)}, u32[]{:S(2)}, u32[]{:S(2)}) collective-permute-start(f32[2,3,16,128]{3,2,1,0:T(8,128)S(1)} %get-tuple-element.40), channel_id=1, source_target_pairs={{0,2},{1,3},{2,0},{3,1},{4,6},{5,7},{6,4},{7,5},{8,10},{9,11},{10,... | collective-permute-start | bytes 147464 | tf_op jit(solution)/shard_map/ppermute | solution.py:582
  27.1 11.4 %collective-permute-start.10 = (f32[2,3,16,128]{3,2,1,0:T(8,128)S(1)}, f32[2,3,16,128]{3,2,1,0:T(8,128)S(1)}, u32[]{:S(2)}, u32[]{:S(2)}) collective-permute-start(f32[2,3,16,128]{3,2,1,0:T(8,128)S(1)} %get-tuple-element.41), channel_id=1, source_target_pairs={{0,3},{1,2},{2,1},{3,0},{4,7},{5,6},{6,5},{7,4},{8,11},{9,10},{10,... | collective-permute-start | bytes 147464 | tf_op jit(solution)/shard_map/ppermute | solution.py:582

commit v6 on v5

--- a/solution.py
+++ b/solution.py
@@ -17,14 +17,27 @@
 
 FIELDS = 5
 HALO = STEPS
-PAIR = 2 * HALO
-PACK_ROWS = 32
+LAST_COLS = (HALO, HALO, HALO - 1, HALO, HALO)
+FIRST_COLS = (HALO, HALO - 1, HALO - 1, HALO, HALO - 1)
+LAST_ROWS = (HALO, HALO - 1, HALO, HALO, HALO)
+FIRST_ROWS = (HALO, HALO - 1, HALO - 1, HALO, HALO - 1)
+
+
+def starts(counts):
+    return [sum(counts[:f]) for f in range(len(counts))]
+
+
+BOTH_COLS = tuple(a + b for a, b in zip(LAST_COLS, FIRST_COLS))
+TILE_LANES = sum(BOTH_COLS)
+TILE_ROWS = max(sum(LAST_ROWS), sum(FIRST_ROWS))
+COL_AT, LAST_AT, FIRST_AT = starts(BOTH_COLS), starts(LAST_ROWS), starts(FIRST_ROWS)
 SIDE = 128
 TOP = 16
 ROWS = SIDE + 32
 LO = 8
 HI = SIDE + 24
 CHUNK = 24
+SPARE = 2
 NT = 4
 GROUP = SIDE // NT
 CLOSED = 1e30
@@ -153,7 +166,8 @@
 
 def load_kernel(*refs):
     sources, refs = refs[:FIELDS], refs[FIELDS:]
-    fields, (columns, pair_even, pair_odd, first, last, sem) = refs[:FIELDS], refs[FIELDS:]
+    fields, (columns, pair_even, pair_odd, first, last, sem, _) = refs[:FIELDS], refs[FIELDS:]
+    spill = refs[-1]
     lane = lane_index()
     odd = remainder(lax.axis_index("row"), 2) == 1
     copies = [
@@ -162,37 +176,48 @@
     for copy in copies:
         copy.start()
     tile_count = fields[0].shape[0]
-    for t in range(tile_count):
-        first[t, FIELDS * HALO :, :] = jnp.zeros((2, SIDE), jnp.float32)
-        last[t, :2, :] = jnp.zeros((2, SIDE), jnp.float32)
+    blocks = tile_count * TILE_LANES // SIDE
     for f in range(FIELDS):
         copies[f].wait()
-        for t in range(0, tile_count, 2):
-            packed = columns[t // 2] if f else jnp.zeros((SIDE, SIDE), jnp.float32)
-            for u in range(2):
-                at = PAIR * (u * FIELDS + f)
-                moved = pltpu.roll(fields[f][t + u], at + HALO, 1)
-                packed = jnp.where((lane >= at) & (lane < at + PAIR), moved, packed)
-            columns[t // 2] = packed
+        for b in range(blocks + 1):
+            target, place = (columns, pl.ds(b * SIDE, SIDE)) if b < blocks else (spill, slice(None))
+            packed = target[place, :]
+            for t in range(tile_count):
+                at = TILE_LANES * t + COL_AT[f] - b * SIDE
+                if at < SIDE and at + BOTH_COLS[f] > 0:
+                    moved = pltpu.roll(fields[f][t], (at + LAST_COLS[f]) % SIDE, 1)
+                    packed = jnp.where((lane >= at) & (lane < at + BOTH_COLS[f]), moved, packed)
+            target[place, :] = packed
         for t in range(tile_count):
-            first[t, HALO * f : HALO * (f + 1), :] = fields[f][t, :HALO, :]
-            last[t, 2 + HALO * f : 2 + HALO * (f + 1), :] = fields[f][t, SIDE - HALO :, :]
+            at, count = TILE_ROWS * t + FIRST_AT[f], FIRST_ROWS[f]
+            first[at : at + count, :] = fields[f][t, :count, :]
+            at, count = TILE_ROWS * t + LAST_AT[f], LAST_ROWS[f]
+            last[at : at + count, :] = fields[f][t, SIDE - count :, :]
+    half = SIDE // 2
+    columns[blocks * SIDE :, :] = jnp.where(
+        lane < half, spill[:half, :], pltpu.roll(spill[half:, :], half, 1)
+    )
     pair_even[...] = jnp.where(odd, first[...], last[...])
     pair_odd[...] = jnp.where(odd, last[...], first[...])
 
 
 def load(arrays):
     tile_count = arrays[0].shape[0]
-    rows = VMEM((tile_count, PACK_ROWS, SIDE), jnp.float32)
+    rows = VMEM((tile_count * TILE_ROWS, SIDE), jnp.float32)
     outs = [VMEM(array.shape, array.dtype) for array in arrays]
-    outs += [VMEM((tile_count // 2, SIDE, SIDE), jnp.float32), rows, rows]
+    outs += [VMEM((tile_count * TILE_LANES, SIDE), jnp.float32), rows, rows]
     return pl.pallas_call(
         load_kernel,
         name="load_and_pack",
         out_shape=tuple(outs),
         in_specs=[pl.BlockSpec(memory_space=pltpu.HBM)] * FIELDS,
         out_specs=tuple(vmem_specs(len(outs))),
-        scratch_shapes=[rows, rows, pltpu.SemaphoreType.DMA((FIELDS,))],
+        scratch_shapes=[
+            rows,
+            rows,
+            pltpu.SemaphoreType.DMA((FIELDS,)),
+            VMEM((SIDE, SIDE), jnp.float32),
+        ],
         compiler_params=SMALL,
     )(*[pltpu.with_memory_space_constraint(array, pltpu.HBM) for array in arrays])
 
@@ -273,9 +298,9 @@
 
     west, east = near("w"), near("e")
     for f in range(FIELDS):
-        rows = pl.ds(HALO * f, 8)
-
-        def ends(side, middle, left, right, out):
+
+        def ends(side, start, middle, left, right, out):
+            rows = pl.ds(start, 8)
             mid, left_end, right_end = (
                 stacks[1][place[0], side, place[1], rows, :] for place in (middle, left, right)
             )
@@ -292,25 +317,30 @@
             strip[f][out : out + 8, :] = value
 
         if part.halo_rows:
-            ends(0, near("n"), near("nw"), near("ne"), LO)
-            ends(1, near("s"), near("sw"), near("se"), TOP + SIDE)
+            start = SPARE + LAST_AT[f] + LAST_ROWS[f] - 8
+            ends(0, start, near("n"), near("nw"), near("ne"), LO)
+            ends(1, SPARE + FIRST_AT[f], near("s"), near("sw"), near("se"), TOP + SIDE)
 
         for start, count in part.own:
             own, out = pl.ds(start, count), pl.ds(TOP + start, count)
 
-            def shifted(place, goal):
-                source = PAIR * (remainder(place[1], 2) * FIELDS + f)
-                shift = remainder(goal - source + 2 * SIDE, SIDE)
-                return pltpu.roll(halo_cols[place[0], divide(place[1], 2), own, :], shift, 1)
+            def shifted(place, offset, goal):
+                lanes_at = TILE_LANES * place[1] + (COL_AT[f] + offset)
+                b, source = divide(lanes_at, SIDE), remainder(lanes_at, SIDE)
+                beyond = jnp.minimum(b + 1, halo_cols.shape[1] - 1)
+                value = jnp.where(
+                    lane >= source, halo_cols[place[0], b, own, :], halo_cols[place[0], beyond, own, :]
+                )
+                return pltpu.roll(value, remainder(goal - source + SIDE, SIDE), 1)
 
             core = fields[f][slot, own, :]
             block[f][i, out, :] = core
-            value = shifted(west, at + 2)
+            value = shifted(west, 0, at + 8 - LAST_COLS[f])
             if i:
                 value = jnp.where(inside(0, 8), value, strip[f][out, :])
             value = jnp.where(inside(8, 16), pltpu.roll(core, (at + 8) % SIDE, 1), value)
             value = jnp.where(inside(16, 24), pltpu.roll(core, (at + 24) % SIDE, 1), value)
-            value = jnp.where(inside(24, GROUP), shifted(east, at + 24 - HALO), value)
+            value = jnp.where(inside(24, GROUP), shifted(east, LAST_COLS[f], at + 24), value)
             strip[f][out, :] = value
 
 
@@ -381,6 +411,23 @@
     return (SIDE - GROUP * i - 7) % SIDE
 
 
+def unpack_columns(part, packed, out):
+    blocks, half = out.shape[0] - 1, SIDE // 2
+    for start, count in part.own:
+        rows = pl.ds(start, count)
+        for b in range(blocks):
+            out[b, rows, :] = packed[b * SIDE + start : b * SIDE + start + count, :]
+        if start < half:
+            n = min(count, half - start)
+            out[blocks, start : start + n, :] = packed[
+                blocks * SIDE + start : blocks * SIDE + start + n, :
+            ]
+        if start + count > half:
+            low, high = max(start, half), start + count
+            lower = packed[blocks * SIDE + low - half : blocks * SIDE + high - half, :]
+            out[blocks, low:high, :] = pltpu.roll(lower, half, 1)
+
+
 def advance_kernel(part, lanes, *refs):
     table = refs[0]
     fields = refs[1 : 1 + FIELDS]
@@ -408,10 +455,13 @@
     for k in range(lanes):
         for n in range(kinds):
             if n:
-                stacks[n][k] = halos[kinds * k + n][...]
+                for side in range(2):
+                    for t in range(fields[0].shape[0]):
+                        stacks[1][k, side, t, SPARE : SPARE + TILE_ROWS, :] = halos[kinds * k + 1][
+                            side, TILE_ROWS * t : TILE_ROWS * (t + 1), :
+                        ]
             else:
-                for span in part.own:
-                    stacks[0][k, :, row_span(span), :] = halos[kinds * k][:, row_span(span), :]
+                unpack_columns(part, halos[kinds * k], stacks[0].at[k])
     for i in range(NT):
         base = part.base + i * ENTRY
         assemble(part, table, base, i, entry(i)[1], fields, stacks, block, strip)
@@ -507,6 +557,10 @@
     if not part.halo_rows:
         halos = [group[:1] for group in halos]
     flat = [array for group in halos for array in group]
+    tile_count = fields[0].shape[0]
+    stacks = [VMEM((lanes, -(-tile_count * TILE_LANES // SIDE), SIDE, SIDE), jnp.float32)]
+    if part.halo_rows:
+        stacks.append(VMEM((lanes, 2, tile_count, SPARE + TILE_ROWS + 1, SIDE), jnp.float32))
     block = VMEM((NT, ROWS, SIDE), jnp.float32)
     strip = VMEM((ROWS, SIDE), jnp.float32)
     cells = (NT + 1) * sum(count for _, count in part.computed) * SIDE * STEPS
@@ -516,7 +570,7 @@
         out_shape=outs,
         in_specs=[pl.BlockSpec(memory_space=SMEM)] + vmem_specs(FIELDS + len(flat)),
         out_specs=tuple(out_specs),
-        scratch_shapes=[VMEM((lanes,) + array.shape, jnp.float32) for array in halos[0]]
+        scratch_shapes=stacks
         + [block] * 7
         + [strip] * 7
         + [pltpu.SemaphoreType.DMA((NT, 3))],
@@ -620,11 +674,12 @@
     table = make_table(
         (cols, subs, tile_count, placed_before.shape[0]), placed_before, placed_after, wet_tiles
     )
-    columns[1:], met_even, met_odd, table = lax.optimization_barrier(
-        (columns[1:], met_even, met_odd, table)
-    )
+    joined = join(met_even, met_odd)
+    near_rows = over_cols(joined)
+    columns[1:], joined, table = lax.optimization_barrier((columns[1:], joined, table))
+    near_rows[0] = joined
     table = pltpu.with_memory_space_constraint(table, SMEM)
-    near_rows = over_subs(over_cols(join(met_even, met_odd)))
+    near_rows = over_subs(near_rows)
     columns = over_subs(columns)
 
     def send(parts):

time: 39.7 us -> 39 us (0.982)
  waiting for transfers between devices: 7.96 us -> 7.22 us
    ppermute x12, waiting for transfers between devices: 6.74 us -> 6.13 us  [shift_lanes(): return lax.ppermute(array, ('col', 'sub'), pairs)]
  transfers between devices with their start and end apart: 14 -> 14, of which waited for: 6 -> 6; matrix products, arithmetic and copies ran while one was open for 0% -> 0% of each run, Pallas kernels for 41% -> 42%
where the time goes in v6:
time: 39 us; the launch traced here: 38.8 us
  Pallas kernels  19.7 us (51%)
  starting transfers between devices  11.2 us (29%)
  waiting for transfers between devices  7.22 us (19%)
  between operations  0.72 us (2%)
    pallas_call x3, Pallas kernels, advance(): pl.pallas_call(functools.partial(advance_kernel, part, lanes), name='adva...  13.7 us
    ppermute x12, starting transfers between devices, shift_lanes(): return lax.ppermute(array, ('col', 'sub'), pairs)  9.62 us
    ppermute x12, waiting for transfers between devices, shift_lanes(): return lax.ppermute(array, ('col', 'sub'), pairs)  6.13 us
    pallas_call x1, Pallas kernels, load(): pl.pallas_call(load_kernel, name='load_and_pack', out_shape=tuple(outs),...  2.21 us
    pallas_call x2, Pallas kernels, place(): pl.pallas_call(functools.partial(place_kernel, part.sent, lanes), name='p...  2.14 us
    pallas_call x1, Pallas kernels, make_table(): pl.pallas_call(functools.partial(index_kernel, shape), name='index_table'...  1.65 us
    ppermute x2, starting transfers between devices, meet_rows(): return lax.ppermute(array, ('row', 'sub'), pairs)  1.58 us
    ppermute x2, waiting for transfers between devices, meet_rows(): return lax.ppermute(array, ('row', 'sub'), pairs)  1.09 us
  transfers between devices with their start and end apart: 14, of which 6 were waited for; matrix products, arithmetic and copies ran while one was open for 0% of the time, Pallas kernels for 42%

profile of v6, /device:TPU:0, one launch (start us, length us, event | category | flops | bytes accessed | tf_op | source)
XLA Modules:
  0.0 38.8 jit_solution(2021140900928661444)
XLA Ops:
  0.6 2.2 %load_and_pack.1 = (f32[8,128,128]{2,1,0:T(8,128)S(1)}, f32[8,128,128]{2,1,0:T(8,128)S(1)}, f32[8,128,128]{2,1,0:T(8,128)S(1)}, f32[8,128,128]{2,1,0:T(8,128)S(1...) custom-call(f32[8,128,128]{2,1,0:T(8,128)} %refs_0_.1, ...), custom_call_target="tpu_custom_call" | custom-call | tf_op jit(solution)/shard_map/load_and_pack/pallas_call | solution.py:209
  2.9 3.0 %collective-permute-start = (f32[448,128]{1,0:T(8,128)S(1)}, f32[448,128]{1,0:T(8,128)S(1)}, u32[]{:S(2)}, u32[]{:S(2)}) collective-permute-start(f32[448,128]{1,0:T(8,128)S(1)} %get-tuple-element.26.refs_6_), channel_id=1, source_target_pairs={{0,2},{1,3},{2,0},{3,1},{4,6},{5,7},{6,4},{7,5},{8,10},{9,11},{10,... | collective-permute-start | bytes 688136 | tf_op jit(solution)/shard_map/ppermute | solution.py:636
  5.9 0.0 copy-start
  5.9 0.0 copy-start.1
  5.9 0.0 copy-start.2
  5.9 1.6 %collective-permute-start.1 = (f32[232,128]{1,0:T(8,128)S(1)}, f32[232,128]{1,0:T(8,128)S(1)}, u32[]{:S(2)}, u32[]{:S(2)}) collective-permute-start(f32[232,128]{1,0:T(8,128)S(1)} %get-tuple-element.27), channel_id=1, source_target_pairs={{0,4},{1,5},{4,0},{5,1},{8,12},{9,13},{12,8},{13,9},{2,6},{3,7},{6... | collective-permute-start | bytes 356360 | tf_op jit(solution)/shard_map/ppermute | solution.py:660
  7.4 0.0 collective-permute-start.2
  7.4 0.5 %collective-permute-start.3 = (f32[448,128]{1,0:T(8,128)S(1)}, f32[448,128]{1,0:T(8,128)S(1)}, u32[]{:S(2)}, u32[]{:S(2)}) collective-permute-start(f32[448,128]{1,0:T(8,128)S(1)} %get-tuple-element.26.refs_6_), channel_id=1, source_target_pairs={{0,1},{1,0},{2,3},{3,2},{4,5},{5,4},{6,7},{7,6},{8,9},{9,8},{10,11... | collective-permute-start | bytes 688136 | tf_op jit(solution)/shard_map/ppermute | solution.py:636
  7.9 0.0 copy-done
  8.0 0.0 copy-done.1
  8.0 0.0 copy-done.2
  8.0 1.6 %index_table.1.refs_0_ = s32[265]{0:T(512)S(4)} custom-call(s32[128]{0:T(128)S(1)} %copy-done, s32[128]{0:T(128)S(1)} %copy-done.1, s32[128]{0:T(128)S(1)} %copy-done.2), custom_call_target="tpu_custom_call" | custom-call | tf_op jit(solution)/shard_map/index_table/pallas_call | solution.py:144
  9.6 1.1 %collective-permute-done.1.met_even = f32[232,128]{1,0:T(8,128)S(1)} collective-permute-done((f32[232,128]{1,0:T(8,128)S(1)}, f32[232,128]{1,0:T(8,128)S(1)}, u32[]{:S(2)}, u32[]{:S(2)}) %collective-permute-start.1) | collective-permute-done | bytes 118816 | tf_op jit(solution)/shard_map/ppermute | solution.py:660
  10.7 0.0 collective-permute-done.2.met_odd
  10.7 0.7 %collective-permute-done.refs_10_.refs_8_ = f32[448,128]{1,0:T(8,128)S(1)} collective-permute-done((f32[448,128]{1,0:T(8,128)S(1)}, f32[448,128]{1,0:T(8,128)S(1)}, u32[]{:S(2)}, u32[]{:S(2)}) %collective-permute-start) | collective-permute-done | bytes 229408 | tf_op jit(solution)/shard_map/ppermute | solution.py:636
  11.5 0.0 collective-permute-start.6
  11.5 1.7 %collective-permute-start.5 = (f32[2,232,128]{2,1,0:T(8,128)S(1)}, f32[2,232,128]{2,1,0:T(8,128)S(1)}, u32[]{:S(2)}, u32[]{:S(2)}) collective-permute-start(f32[2,232,128]{2,1,0:T(8,128)S(1)} %join_row_halos.1.refs_7_), channel_id=1, source_target_pairs={{0,2},{1,3},{2,0},{3,1},{4,6},{5,7},{6,4},{7,5},{8,10},{9,11},{10,... | collective-permute-start | bytes 712712 | tf_op jit(solution)/shard_map/ppermute | solution.py:636
  13.2 0.0 collective-permute-done.3.refs_8_.refs_7_
  13.2 0.0 collective-permute-done.6.refs_12_.refs_9_
  13.2 5.0 %advance_leaving_middle.1 = (f32[2,3,112,128]{3,2,1,0:T(8,128)S(1)}, f32[2,3,112,128]{3,2,1,0:T(8,128)S(1)}, f32[2,3,112,128]{3,2,1,0:T(8,128)S(1)}) custom-call(s32[265]{0:T(512)S(4)} %index_table.1.refs_0_, f32[8,128,128]{2,1,0:T(8,128)S(1)} %get-tuple-element.30.refs_1_, f32[8,128,128]{2,1,0:T(8,128)S(1)} %get-tuple-element.31.refs_2_, ...), custom_call_target="tpu_custom_call" | custom-call | flops 29491200 | bytes 1835008 | tf_op jit(solution)/shard_map/advance_leaving_middle/pallas_call | solution.py:567
  18.2 0.3 collective-permute-start.11
  18.5 1.4 %collective-permute-start.12 = (f32[2,3,112,128]{3,2,1,0:T(8,128)S(1)}, f32[2,3,112,128]{3,2,1,0:T(8,128)S(1)}, u32[]{:S(2)}, u32[]{:S(2)}) collective-permute-start(f32[2,3,112,128]{3,2,1,0:T(8,128)S(1)} %get-tuple-element.41), channel_id=1, source_target_pairs={{0,2},{1,3},{2,0},{3,1},{4,6},{5,7},{6,4},{7,5},{8,10},{9,11},{10,... | collective-permute-start | bytes 1032200 | tf_op jit(solution)/shard_map/ppermute | solution.py:636
  19.9 0.2 collective-permute-start.13
  20.2 0.5 %collective-permute-start.4 = (f32[2,232,128]{2,1,0:T(8,128)S(1)}, f32[2,232,128]{2,1,0:T(8,128)S(1)}, u32[]{:S(2)}, u32[]{:S(2)}) collective-permute-start(f32[2,232,128]{2,1,0:T(8,128)S(1)} %join_row_halos.1.refs_7_), channel_id=1, source_target_pairs={{0,1},{1,0},{2,3},{3,2},{4,5},{5,4},{6,7},{7,6},{8,9},{9,8},{10,11... | collective-permute-start | bytes 712712 | tf_op jit(solution)/shard_map/ppermute | solution.py:636
  20.7 0.0 collective-permute-done.5.refs_11_
  20.7 0.0 collective-permute-start.7
  20.7 1.1 %collective-permute-done.4.refs_9_ = f32[2,232,128]{2,1,0:T(8,128)S(1)} collective-permute-done((f32[2,232,128]{2,1,0:T(8,128)S(1)}, f32[2,232,128]{2,1,0:T(8,128)S(1)}, u32[]{:S(2)}, u32[]{:S(2)}) %collective-permute-start.4) | collective-permute-done | bytes 237600 | tf_op jit(solution)/shard_map/ppermute | solution.py:636
  21.8 0.4 collective-permute-done.7.refs_13_
  22.2 2.3 %advance_leaving_edges.1 = (f32[2,3,16,128]{3,2,1,0:T(8,128)S(1)}, f32[2,3,16,128]{3,2,1,0:T(8,128)S(1)}, f32[2,3,16,128]{3,2,1,0:T(8,128)S(1)}) custom-call(s32[265]{0:T(512)S(4)} %index_table.1.refs_0_, f32[8,128,128]{2,1,0:T(8,128)S(1)} %get-tuple-element.30.refs_1_, f32[8,128,128]{2,1,0:T(8,128)S(1)} %get-tuple-element.31.refs_2_, ...), custom_call_target="tpu_custom_call" | custom-call | flops 11059200 | bytes 262144 | tf_op jit(solution)/shard_map/advance_leaving_edges/pallas_call | solution.py:567
  24.5 0.4 %collective-permute-start.8 = (f32[2,3,16,128]{3,2,1,0:T(8,128)S(1)}, f32[2,3,16,128]{3,2,1,0:T(8,128)S(1)}, u32[]{:S(2)}, u32[]{:S(2)}) collective-permute-start(f32[2,3,16,128]{3,2,1,0:T(8,128)S(1)} %get-tuple-element.37), channel_id=1, source_target_pairs={{0,1},{1,0},{2,3},{3,2},{4,5},{5,4},{6,7},{7,6},{8,9},{9,8},{10,11... | collective-permute-start | bytes 147464 | tf_op jit(solution)/shard_map/ppermute | solution.py:636
  24.9 1.4 %collective-permute-start.9 = (f32[2,3,16,128]{3,2,1,0:T(8,128)S(1)}, f32[2,3,16,128]{3,2,1,0:T(8,128)S(1)}, u32[]{:S(2)}, u32[]{:S(2)}) collective-permute-start(f32[2,3,16,128]{3,2,1,0:T(8,128)S(1)} %get-tuple-element.38), channel_id=1, source_target_pairs={{0,2},{1,3},{2,0},{3,1},{4,6},{5,7},{6,4},{7,5},{8,10},{9,11},{10,... | collective-permute-start | bytes 147464 | tf_op jit(solution)/shard_map/ppermute | solution.py:636
  26.3 0.0 collective-permute-done.11.refs_1_
  26.3 0.1 collective-permute-start.10
  26.5 6.3 %advance_staying.1 = (f32[8,128,128]{2,1,0:T(8,128)}, f32[8,128,128]{2,1,0:T(8,128)}, f32[8,128,128]{2,1,0:T(8,128)}) custom-call(s32[265]{0:T(512)S(4)} %index_table.1.refs_0_, f32[8,128,128]{2,1,0:T(8,128)S(1)} %get-tuple-element.30.refs_1_, f32[8,128,128]{2,1,0:T(8,128)S(1)} %get-tuple-element.31.refs_2_, f32[8,128,128]{2,1,0:T(8,128)S(1)} %get-tuple-element.32.refs_3_, ...), custom_call_target="tpu_custom_call" | custom-call | flops 33177600 | bytes 2097152 | tf_op jit(solution)/shard_map/advance_staying/pallas_call | solution.py:567
  32.8 0.0 collective-permute-done.12.refs_2_
  32.8 2.9 %collective-permute-done.13.refs_3_ = f32[2,3,112,128]{3,2,1,0:T(8,128)S(1)} collective-permute-done((f32[2,3,112,128]{3,2,1,0:T(8,128)S(1)}, f32[2,3,112,128]{3,2,1,0:T(8,128)S(1)}, u32[]{:S(2)}, u32[]{:S(2)}) %collective-permute-start.13) | collective-permute-done | bytes 344096 | tf_op jit(solution)/shard_map/ppermute | solution.py:636
  35.7 1.0 %place_leaving_middle.1 = (f32[8,128,128]{2,1,0:T(8,128)}, f32[8,128,128]{2,1,0:T(8,128)}, f32[8,128,128]{2,1,0:T(8,128)}) custom-call(s32[265]{0:T(512)S(4)} %index_table.1.refs_0_, f32[2,3,112,128]{3,2,1,0:T(8,128)S(1)} %collective-permute-done.11.refs_1_, ...), custom_call_target="tpu_custom_call", output_to_operand_aliasing={{0}: (4, {}), {1}: (5, {}), {2}: (6, {})} | custom-call | tf_op jit(solution)/shard_map/place_leaving_middle/pallas_call | solution.py:615
  36.8 0.0 collective-permute-done.8.refs_1_
  36.8 1.0 %collective-permute-done.9.refs_2_ = f32[2,3,16,128]{3,2,1,0:T(8,128)S(1)} collective-permute-done((f32[2,3,16,128]{3,2,1,0:T(8,128)S(1)}, f32[2,3,16,128]{3,2,1,0:T(8,128)S(1)}, u32[]{:S(2)}, u32[]{:S(2)}) %collective-permute-start.9) | collective-permute-done | bytes 49184 | tf_op jit(solution)/shard_map/ppermute | solution.py:636
  37.7 0.0 collective-permute-done.10.refs_3_
  37.7 1.1 %place_leaving_edges.1 = (f32[8,128,128]{2,1,0:T(8,128)}, f32[8,128,128]{2,1,0:T(8,128)}, f32[8,128,128]{2,1,0:T(8,128)}) custom-call(s32[265]{0:T(512)S(4)} %index_table.1.refs_0_, f32[2,3,16,128]{3,2,1,0:T(8,128)S(1)} %collective-permute-done.8.refs_1_, ...), custom_call_target="tpu_custom_call", output_to_operand_aliasing={{0}: (4, {}), {1}: (5, {}), {2}: (6, {})} | custom-call | tf_op jit(solution)/shard_map/place_leaving_edges/pallas_call | solution.py:615
  (1 shorter events, 0.0 us)
Async XLA Ops:
  2.9 8.6 %collective-permute-start = (f32[448,128]{1,0:T(8,128)S(1)}, f32[448,128]{1,0:T(8,128)S(1)}, u32[]{:S(2)}, u32[]{:S(2)}) collective-permute-start(f32[448,128]{1,0:T(8,128)S(1)} %get-tuple-element.26.refs_6_), channel_id=1, source_target_pairs={{0,2},{1,3},{2,0},{3,1},{4,6},{5,7},{6,4},{7,5},{8,10},{9,11},{10,... | collective-permute-start | bytes 688136 | tf_op jit(solution)/shard_map/ppermute | solution.py:636
  5.9 2.1 %copy-start = (s32[128]{0:T(128)S(1)}, s32[128]{0:T(128)}, u32[]{:S(2)}) copy-start(s32[128]{0:T(128)} %before_ref.1) | copy-start | bytes 1540
  5.9 2.1 %copy-start.1 = (s32[128]{0:T(128)S(1)}, s32[128]{0:T(128)}, u32[]{:S(2)}) copy-start(s32[128]{0:T(128)} %after_ref.1) | copy-start | bytes 1540
  5.9 2.1 %copy-start.2 = (s32[128]{0:T(128)S(1)}, s32[128]{0:T(128)}, u32[]{:S(2)}) copy-start(s32[128]{0:T(128)} %wet_ref.1) | copy-start | bytes 1540
  5.9 4.8 %collective-permute-start.1 = (f32[232,128]{1,0:T(8,128)S(1)}, f32[232,128]{1,0:T(8,128)S(1)}, u32[]{:S(2)}, u32[]{:S(2)}) collective-permute-start(f32[232,128]{1,0:T(8,128)S(1)} %get-tuple-element.27), channel_id=1, source_target_pairs={{0,4},{1,5},{4,0},{5,1},{8,12},{9,13},{12,8},{13,9},{2,6},{3,7},{6... | collective-permute-start | bytes 356360 | tf_op jit(solution)/shard_map/ppermute | solution.py:660
  7.4 3.3 %collective-permute-start.2 = (f32[232,128]{1,0:T(8,128)S(1)}, f32[232,128]{1,0:T(8,128)S(1)}, u32[]{:S(2)}, u32[]{:S(2)}) collective-permute-start(f32[232,128]{1,0:T(8,128)S(1)} %get-tuple-element.28), channel_id=1, source_target_pairs={{0,1},{1,0},{4,8},{5,9},{8,4},{9,5},{12,13},{13,12},{2,3},{3,2},{6... | collective-permute-start | bytes 356360 | tf_op jit(solution)/shard_map/ppermute | solution.py:660
  7.4 5.8 %collective-permute-start.3 = (f32[448,128]{1,0:T(8,128)S(1)}, f32[448,128]{1,0:T(8,128)S(1)}, u32[]{:S(2)}, u32[]{:S(2)}) collective-permute-start(f32[448,128]{1,0:T(8,128)S(1)} %get-tuple-element.26.refs_6_), channel_id=1, source_target_pairs={{0,1},{1,0},{2,3},{3,2},{4,5},{5,4},{6,7},{7,6},{8,9},{9,8},{10,11... | collective-permute-start | bytes 688136 | tf_op jit(solution)/shard_map/ppermute | solution.py:636
  11.5 1.8 %collective-permute-start.6 = (f32[448,128]{1,0:T(8,128)S(1)}, f32[448,128]{1,0:T(8,128)S(1)}, u32[]{:S(2)}, u32[]{:S(2)}) collective-permute-start(f32[448,128]{1,0:T(8,128)S(1)} %collective-permute-done.refs_10_.refs_8_), channel_id=1, source_target_pairs={{0,1},{1,0},{2,3},{3,2},{4,5},{5,4},{6,7},{7,6},{8,9},{9,8},{10,11... | collective-permute-start | bytes 688136 | tf_op jit(solution)/shard_map/ppermute | solution.py:636
  11.5 9.2 %collective-permute-start.5 = (f32[2,232,128]{2,1,0:T(8,128)S(1)}, f32[2,232,128]{2,1,0:T(8,128)S(1)}, u32[]{:S(2)}, u32[]{:S(2)}) collective-permute-start(f32[2,232,128]{2,1,0:T(8,128)S(1)} %join_row_halos.1.refs_7_), channel_id=1, source_target_pairs={{0,2},{1,3},{2,0},{3,1},{4,6},{5,7},{6,4},{7,5},{8,10},{9,11},{10,... | collective-permute-start | bytes 712712 | tf_op jit(solution)/shard_map/ppermute | solution.py:636
  18.2 8.1 %collective-permute-start.11 = (f32[2,3,112,128]{3,2,1,0:T(8,128)S(1)}, f32[2,3,112,128]{3,2,1,0:T(8,128)S(1)}, u32[]{:S(2)}, u32[]{:S(2)}) collective-permute-start(f32[2,3,112,128]{3,2,1,0:T(8,128)S(1)} %get-tuple-element.40), channel_id=1, source_target_pairs={{0,1},{1,0},{2,3},{3,2},{4,5},{5,4},{6,7},{7,6},{8,9},{9,8},{10,11... | collective-permute-start | bytes 1032200 | tf_op jit(solution)/shard_map/ppermute | solution.py:636
  18.5 14.3 %collective-permute-start.12 = (f32[2,3,112,128]{3,2,1,0:T(8,128)S(1)}, f32[2,3,112,128]{3,2,1,0:T(8,128)S(1)}, u32[]{:S(2)}, u32[]{:S(2)}) collective-permute-start(f32[2,3,112,128]{3,2,1,0:T(8,128)S(1)} %get-tuple-element.41), channel_id=1, source_target_pairs={{0,2},{1,3},{2,0},{3,1},{4,6},{5,7},{6,4},{7,5},{8,10},{9,11},{10,... | collective-permute-start | bytes 1032200 | tf_op jit(solution)/shard_map/ppermute | solution.py:636
  19.9 15.8 %collective-permute-start.13 = (f32[2,3,112,128]{3,2,1,0:T(8,128)S(1)}, f32[2,3,112,128]{3,2,1,0:T(8,128)S(1)}, u32[]{:S(2)}, u32[]{:S(2)}) collective-permute-start(f32[2,3,112,128]{3,2,1,0:T(8,128)S(1)} %get-tuple-element.42), channel_id=1, source_target_pairs={{0,3},{1,2},{2,1},{3,0},{4,7},{5,6},{6,5},{7,4},{8,11},{9,10},{10,... | collective-permute-start | bytes 1032200 | tf_op jit(solution)/shard_map/ppermute | solution.py:636
  20.2 1.6 %collective-permute-start.4 = (f32[2,232,128]{2,1,0:T(8,128)S(1)}, f32[2,232,128]{2,1,0:T(8,128)S(1)}, u32[]{:S(2)}, u32[]{:S(2)}) collective-permute-start(f32[2,232,128]{2,1,0:T(8,128)S(1)} %join_row_halos.1.refs_7_), channel_id=1, source_target_pairs={{0,1},{1,0},{2,3},{3,2},{4,5},{5,4},{6,7},{7,6},{8,9},{9,8},{10,11... | collective-permute-start | bytes 712712 | tf_op jit(solution)/shard_map/ppermute | solution.py:636
  20.7 1.5 %collective-permute-start.7 = (f32[2,232,128]{2,1,0:T(8,128)S(1)}, f32[2,232,128]{2,1,0:T(8,128)S(1)}, u32[]{:S(2)}, u32[]{:S(2)}) collective-permute-start(f32[2,232,128]{2,1,0:T(8,128)S(1)} %collective-permute-done.5.refs_11_), channel_id=1, source_target_pairs={{0,1},{1,0},{2,3},{3,2},{4,5},{5,4},{6,7},{7,6},{8,9},{9,8},{10,11... | collective-permute-start | bytes 712712 | tf_op jit(solution)/shard_map/ppermute | solution.py:636
  24.5 12.2 %collective-permute-start.8 = (f32[2,3,16,128]{3,2,1,0:T(8,128)S(1)}, f32[2,3,16,128]{3,2,1,0:T(8,128)S(1)}, u32[]{:S(2)}, u32[]{:S(2)}) collective-permute-start(f32[2,3,16,128]{3,2,1,0:T(8,128)S(1)} %get-tuple-element.37), channel_id=1, source_target_pairs={{0,1},{1,0},{2,3},{3,2},{4,5},{5,4},{6,7},{7,6},{8,9},{9,8},{10,11... | collective-permute-start | bytes 147464 | tf_op jit(solution)/shard_map/ppermute | solution.py:636
  24.9 12.8 %collective-permute-start.9 = (f32[2,3,16,128]{3,2,1,0:T(8,128)S(1)}, f32[2,3,16,128]{3,2,1,0:T(8,128)S(1)}, u32[]{:S(2)}, u32[]{:S(2)}) collective-permute-start(f32[2,3,16,128]{3,2,1,0:T(8,128)S(1)} %get-tuple-element.38), channel_id=1, source_target_pairs={{0,2},{1,3},{2,0},{3,1},{4,6},{5,7},{6,4},{7,5},{8,10},{9,11},{10,... | collective-permute-start | bytes 147464 | tf_op jit(solution)/shard_map/ppermute | solution.py:636
  26.3 11.4 %collective-permute-start.10 = (f32[2,3,16,128]{3,2,1,0:T(8,128)S(1)}, f32[2,3,16,128]{3,2,1,0:T(8,128)S(1)}, u32[]{:S(2)}, u32[]{:S(2)}) collective-permute-start(f32[2,3,16,128]{3,2,1,0:T(8,128)S(1)} %get-tuple-element.39), channel_id=1, source_target_pairs={{0,3},{1,2},{2,1},{3,0},{4,7},{5,6},{6,5},{7,4},{8,11},{9,10},{10,... | collective-permute-start | bytes 147464 | tf_op jit(solution)/shard_map/ppermute | solution.py:636

commit v7 on v6

--- a/solution.py
+++ b/solution.py
@@ -103,13 +103,11 @@
         to = relative(remainder(device, lanes), 1)
         nth = count[to]
         count[to] = nth + 1
+        other = jnp.where(stays | (to == subs), 0, 1)
         left = count[lanes]
-        count[lanes] = left + jnp.where(stays, 0, 1)
-        base = jnp.where(
-            stays,
-            STAY + jnp.minimum(nth, NT - 1) * ENTRY,
-            LEAVE + jnp.minimum(left, NT - 1) * ENTRY,
-        )
+        count[lanes] = left + other
+        place = jnp.minimum(jnp.where(other == 1, NT - 1 - left, nth), NT - 1)
+        base = jnp.where(stays, STAY, LEAVE) + jnp.maximum(place, 0) * ENTRY
         table[base + 1] = wet_ref[tile]
         table[base + 2] = s
         table[base + 3] = jnp.where(stays, s, to * 2 + jnp.minimum(nth, 1))
@@ -247,9 +245,10 @@
 
 
 class Part:
-    def __init__(self, name, base, computed, own, halo_rows, sent):
+    def __init__(self, name, base, tiles, computed, own, halo_rows, sent):
         self.name = name
         self.base = base
+        self.tiles = tiles
         self.computed = computed
         self.own = own
         self.halo_rows = halo_rows
@@ -267,16 +266,21 @@
 
 EDGE = 8
 BAND = 24
-EARLY = Part("leaving_middle", LEAVE, ((TOP, SIDE),), ((0, SIDE),), False, ((EDGE, SIDE - 2 * EDGE),))
+MIDDLE = (EDGE, SIDE - 2 * EDGE)
+EARLY = (
+    Part("leaving_first", LEAVE, 2, ((TOP, SIDE),), ((0, SIDE),), False, (MIDDLE,)),
+    Part("leaving_second", LEAVE + 2 * ENTRY, 2, ((TOP, SIDE),), ((0, SIDE),), False, (MIDDLE,)),
+)
 LATE = Part(
     "leaving_edges",
     LEAVE,
+    NT,
     ((LO, BAND), (HI - BAND, BAND)),
     ((0, BAND - 8), (SIDE - BAND + 8, BAND - 8)),
     True,
     ((0, EDGE), (SIDE - EDGE, EDGE)),
 )
-WHOLE = Part("staying", STAY, ((LO, HI - LO),), ((0, SIDE),), True, ((0, SIDE),))
+WHOLE = Part("staying", STAY, NT, ((LO, HI - LO),), ((0, SIDE),), True, ((0, SIDE),))
 
 
 def row_bands(r, rows, above, middle, below):
@@ -350,7 +354,7 @@
 
     def lane_wet(center, left, right):
         value = jnp.zeros((1, SIDE), jnp.int32)
-        for i in range(NT):
+        for i in range(part.tiles):
             at = GROUP * i
             middle = near_wet(i, center) if center else 1
             sides = jnp.where(
@@ -428,12 +432,13 @@
             out[blocks, low:high, :] = pltpu.roll(lower, half, 1)
 
 
-def advance_kernel(part, lanes, *refs):
+def advance_kernel(part, lanes, units, given, *refs):
     table = refs[0]
     fields = refs[1 : 1 + FIELDS]
     kinds = 2 if part.halo_rows else 1
     halos, refs = refs[1 + FIELDS : 1 + FIELDS + kinds * lanes], refs[1 + FIELDS + kinds * lanes :]
-    n_out = 3 if part is WHOLE else lanes - 1
+    refs = refs[given:]
+    n_out = 3 if part is WHOLE else len(units)
     outs, stacks, refs = refs[:n_out], refs[n_out : n_out + kinds], refs[n_out + kinds :]
     (
         level, flow_x, flow_y, ground, friction, ground_x, ground_y,
@@ -462,11 +467,11 @@
                         ]
             else:
                 unpack_columns(part, halos[kinds * k], stacks[0].at[k])
-    for i in range(NT):
+    for i in range(part.tiles):
         base = part.base + i * ENTRY
         assemble(part, table, base, i, entry(i)[1], fields, stacks, block, strip)
     prepare_strip(part, near_wet, strip, s_ground_x, s_ground_y)
-    for i in range(NT):
+    for i in range(part.tiles):
         prepare_tile(part, near_wet, i, block, ground_x, ground_y, s_ground)
 
     def step(_, carry):
@@ -476,7 +481,7 @@
             e_east = pltpu.roll(e, SIDE - 1, 1)
             s_flow_x[at, :] = face(s_flow_x[at, :], e, e_east, s_ground_x[at, :], c)
             s_flow_y[at, :] = face(s_flow_y[at, :], e, s_level[south, :], s_ground_y[at, :], c)
-        for i in range(NT):
+        for i in range(part.tiles):
             for r, rows in part.chunks():
                 at, south = pl.ds(r, rows), pl.ds(r + 1, rows)
                 e, c = level[i, at, :], friction[i, at, :]
@@ -493,7 +498,7 @@
             s_level[at, :] = s_level[at, :] + RATE * (
                 (pltpu.roll(qx, 1, 1) - qx) + (s_flow_y[north, :] - s_flow_y[at, :])
             )
-        for i in range(NT):
+        for i in range(part.tiles):
             for r, rows in part.chunks():
                 at, north = pl.ds(r, rows), pl.ds(r - 1, rows)
                 qx = flow_x[i, at, :]
@@ -508,7 +513,7 @@
     lax.fori_loop(0, STEPS, step, 0)
 
     results = (level, flow_x, flow_y)
-    for i in range(NT):
+    for i in range(part.tiles):
         wet, slot, _ = entry(i)
         for start, count in part.sent:
             own, at = pl.ds(start, count), pl.ds(TOP + start, count)
@@ -519,16 +524,16 @@
                 )
 
     if part is not WHOLE:
-        for i in range(NT):
+        for i in range(part.tiles):
             target = entry(i)[2]
-            for k in range(1, lanes):
+            for out_ref, k in zip(outs, units):
                 @pl.when(divide(target, 2) == k)
                 def _():
                     out = 0
                     for start, count in part.sent:
                         for f in range(3):
                             value = results[f][i, pl.ds(TOP + start, count), :]
-                            outs[k - 1][remainder(target, 2), f, out : out + count, :] = value
+                            out_ref[remainder(target, 2), f, out : out + count, :] = value
                         out += count
 
     else:
@@ -536,7 +541,7 @@
             pltpu.make_async_copy(
                 results[f].at[i, pl.ds(TOP, SIDE), :], outs[f].at[entry(i)[2]], sem_out.at[i, f]
             )
-            for i in range(NT)
+            for i in range(part.tiles)
             for f in range(3)
         ]
         for copy in copies:
@@ -545,15 +550,15 @@
             copy.wait()
 
 
-def advance(part, table, fields, halos):
+def advance(part, table, fields, halos, units=(), partial=()):
     lanes = len(halos)
     sent = sum(count for _, count in part.sent)
     if part is WHOLE:
         outs = (jax.ShapeDtypeStruct(fields[0].shape, jnp.float32),) * 3
         out_specs = [pl.BlockSpec(memory_space=ANY)] * 3
     else:
-        outs = (VMEM((2, 3, sent, SIDE), jnp.float32),) * (lanes - 1)
-        out_specs = vmem_specs(lanes - 1)
+        outs = (VMEM((2, 3, sent, SIDE), jnp.float32),) * len(units)
+        out_specs = vmem_specs(len(units))
     if not part.halo_rows:
         halos = [group[:1] for group in halos]
     flat = [array for group in halos for array in group]
@@ -561,24 +566,26 @@
     stacks = [VMEM((lanes, -(-tile_count * TILE_LANES // SIDE), SIDE, SIDE), jnp.float32)]
     if part.halo_rows:
         stacks.append(VMEM((lanes, 2, tile_count, SPARE + TILE_ROWS + 1, SIDE), jnp.float32))
-    block = VMEM((NT, ROWS, SIDE), jnp.float32)
+    block = VMEM((part.tiles, ROWS, SIDE), jnp.float32)
     strip = VMEM((ROWS, SIDE), jnp.float32)
-    cells = (NT + 1) * sum(count for _, count in part.computed) * SIDE * STEPS
+    cells = (part.tiles + 1) * sum(count for _, count in part.computed) * SIDE * STEPS
     return pl.pallas_call(
-        functools.partial(advance_kernel, part, lanes),
+        functools.partial(advance_kernel, part, lanes, units, len(partial)),
         name="advance_" + part.name,
         out_shape=outs,
-        in_specs=[pl.BlockSpec(memory_space=SMEM)] + vmem_specs(FIELDS + len(flat)),
+        in_specs=[pl.BlockSpec(memory_space=SMEM)]
+        + vmem_specs(FIELDS + len(flat) + len(partial)),
+        input_output_aliases={1 + FIELDS + len(flat) + n: n for n in range(len(partial))},
         out_specs=tuple(out_specs),
         scratch_shapes=stacks
         + [block] * 7
         + [strip] * 7
-        + [pltpu.SemaphoreType.DMA((NT, 3))],
+        + [pltpu.SemaphoreType.DMA((part.tiles, 3))],
         compiler_params=pltpu.CompilerParams(vmem_limit_bytes=12 * 1024 * 1024),
         cost_estimate=pl.CostEstimate(
-            flops=60 * cells, bytes_accessed=8 * NT * sent * SIDE * 4, transcendentals=6 * cells
+            flops=60 * cells, bytes_accessed=8 * part.tiles * sent * SIDE * 4, transcendentals=6 * cells
         ),
-    )(table, *fields, *flat)
+    )(table, *fields, *flat, *partial)
 
 
 def place_kernel(spans, lanes, *refs):
@@ -610,17 +617,17 @@
     each(lambda copy: copy.wait())
 
 
-def place(part, table, received, partial_outs):
+def place(name, spans, table, received, partial_outs):
     lanes = len(received) + 1
     return pl.pallas_call(
-        functools.partial(place_kernel, part.sent, lanes),
-        name="place_" + part.name,
+        functools.partial(place_kernel, spans, lanes),
+        name="place_" + name,
         out_shape=tuple(jax.ShapeDtypeStruct(o.shape, o.dtype) for o in partial_outs),
         in_specs=[pl.BlockSpec(memory_space=SMEM)]
         + vmem_specs(lanes - 1)
         + [pl.BlockSpec(memory_space=ANY)] * 3,
         out_specs=tuple(pl.BlockSpec(memory_space=ANY) for _ in partial_outs),
-        scratch_shapes=[pltpu.SemaphoreType.DMA((lanes, 2, 3, len(part.sent)))],
+        scratch_shapes=[pltpu.SemaphoreType.DMA((lanes, 2, 3, len(spans)))],
         input_output_aliases={lanes: 0, lanes + 1: 1, lanes + 2: 2},
         compiler_params=SMALL,
     )(table, *received, *partial_outs)
@@ -682,17 +689,24 @@
     near_rows = over_subs(near_rows)
     columns = over_subs(columns)
 
-    def send(parts):
-        return [
-            in_vmem(shift_lanes(parts[k - 1], k // subs, k % subs)) for k in range(1, cols * subs)
-        ]
-
-    middle = send(advance(EARLY, table, fields, [(part,) for part in columns]))
+    def send(part, k):
+        return in_vmem(shift_lanes(part, k // subs, k % subs))
+
+    units = tuple(range(1, cols * subs))
+    ahead, others = subs, tuple(k for k in units if k != subs)
+    alone = [(part,) for part in columns]
+    first, *rest = advance(EARLY[0], table, fields, alone, (ahead,) + others)
+    rest = advance(EARLY[1], table, fields, alone, others, [in_vmem(part) for part in rest])
+    middle = {ahead: send(first, ahead)}
+    middle.update((k, send(part, k)) for k, part in zip(others, rest))
     halos = list(zip(columns, near_rows))
-    edges = send(advance(LATE, table, fields, halos))
+    edges = advance(LATE, table, fields, halos, units)
+    middle[ahead], edges = lax.optimization_barrier((middle[ahead], edges))
+    middle[ahead] = in_vmem(middle[ahead])
+    edges = [send(part, k) for k, part in zip(units, edges)]
     outs = advance(WHOLE, table, fields, halos)
-    outs = place(EARLY, table, middle, outs)
-    return place(LATE, table, edges, outs)
+    outs = place("middle", EARLY[0].sent, table, [middle[k] for k in units], outs)
+    return place("edges", LATE.sent, table, edges, outs)
 
 
 def solution(mesh):

time: 39 us -> 38 us (0.974)
  waiting for transfers between devices: 7.22 us -> 4.47 us
  Pallas kernels: 19.7 us -> 21.1 us
    ppermute x12, waiting for transfers between devices: 6.13 us -> 3.38 us  [shift_lanes(): return lax.ppermute(array, ('col', 'sub'), pairs)]
    pallas_call x5 -> x6, Pallas kernels: 15.8 us -> 17.2 us  [the longest x4 15 us: advance(): pl.pallas_call(functools.partial(advance_kernel, part, lanes, units, len(...]
  transfers between devices with their start and end apart: 14 -> 14, of which waited for: 6 -> 5; matrix products, arithmetic and copies ran while one was open for 0% -> 0% of each run, Pallas kernels for 42% -> 47%
where the time goes in v7:
time: 38 us; the launch traced here: 37.9 us
  Pallas kernels  21.1 us (56%)
  starting transfers between devices  11.5 us (30%)
  waiting for transfers between devices  4.47 us (12%)
  between operations  0.75 us (2%)
    pallas_call x4, Pallas kernels, advance(): pl.pallas_call(functools.partial(advance_kernel, part, lanes, units, len(...  15 us
    ppermute x12, starting transfers between devices, shift_lanes(): return lax.ppermute(array, ('col', 'sub'), pairs)  9.97 us
    ppermute x12, waiting for transfers between devices, shift_lanes(): return lax.ppermute(array, ('col', 'sub'), pairs)  3.38 us
    pallas_call x1, Pallas kernels, load(): pl.pallas_call(load_kernel, name='load_and_pack', out_shape=tuple(outs),...  2.21 us
    pallas_call x2, Pallas kernels, place(): pl.pallas_call(functools.partial(place_kernel, spans, lanes), name='place...  2.16 us
    pallas_call x1, Pallas kernels, make_table(): pl.pallas_call(functools.partial(index_kernel, shape), name='index_table'...  1.64 us
    ppermute x2, starting transfers between devices, meet_rows(): return lax.ppermute(array, ('row', 'sub'), pairs)  1.58 us
    ppermute x2, waiting for transfers between devices, meet_rows(): return lax.ppermute(array, ('row', 'sub'), pairs)  1.09 us
  transfers between devices with their start and end apart: 14, of which 5 were waited for; matrix products, arithmetic and copies ran while one was open for 0% of the time, Pallas kernels for 47%

profile of v7, /device:TPU:0, one launch (start us, length us, event | category | flops | bytes accessed | tf_op | source)
XLA Modules:
  0.0 37.9 jit_solution(8537273725619939009)
XLA Ops:
  0.6 2.2 %load_and_pack.1 = (f32[8,128,128]{2,1,0:T(8,128)S(1)}, f32[8,128,128]{2,1,0:T(8,128)S(1)}, f32[8,128,128]{2,1,0:T(8,128)S(1)}, f32[8,128,128]{2,1,0:T(8,128)S(1...) custom-call(f32[8,128,128]{2,1,0:T(8,128)} %refs_0_.1, ...), custom_call_target="tpu_custom_call" | custom-call | tf_op jit(solution)/shard_map/load_and_pack/pallas_call | solution.py:207
  2.9 3.0 %collective-permute-start = (f32[448,128]{1,0:T(8,128)S(1)}, f32[448,128]{1,0:T(8,128)S(1)}, u32[]{:S(2)}, u32[]{:S(2)}) collective-permute-start(f32[448,128]{1,0:T(8,128)S(1)} %get-tuple-element.32.refs_6_), channel_id=1, source_target_pairs={{0,2},{1,3},{2,0},{3,1},{4,6},{5,7},{6,4},{7,5},{8,10},{9,11},{10,... | collective-permute-start | bytes 688136 | tf_op jit(solution)/shard_map/ppermute | solution.py:643
  5.9 0.0 copy-start
  5.9 0.0 copy-start.1
  5.9 0.0 copy-start.2
  5.9 1.6 %collective-permute-start.1 = (f32[232,128]{1,0:T(8,128)S(1)}, f32[232,128]{1,0:T(8,128)S(1)}, u32[]{:S(2)}, u32[]{:S(2)}) collective-permute-start(f32[232,128]{1,0:T(8,128)S(1)} %get-tuple-element.33), channel_id=1, source_target_pairs={{0,4},{1,5},{4,0},{5,1},{8,12},{9,13},{12,8},{13,9},{2,6},{3,7},{6... | collective-permute-start | bytes 356360 | tf_op jit(solution)/shard_map/ppermute | solution.py:667
  7.4 0.0 collective-permute-start.2
  7.4 0.5 %collective-permute-start.3 = (f32[448,128]{1,0:T(8,128)S(1)}, f32[448,128]{1,0:T(8,128)S(1)}, u32[]{:S(2)}, u32[]{:S(2)}) collective-permute-start(f32[448,128]{1,0:T(8,128)S(1)} %get-tuple-element.32.refs_6_), channel_id=1, source_target_pairs={{0,1},{1,0},{2,3},{3,2},{4,5},{5,4},{6,7},{7,6},{8,9},{9,8},{10,11... | collective-permute-start | bytes 688136 | tf_op jit(solution)/shard_map/ppermute | solution.py:643
  7.9 0.0 copy-done
  8.0 0.0 copy-done.1
  8.0 0.0 copy-done.2
  8.0 1.6 %index_table.1.refs_0_ = s32[265]{0:T(512)S(4)} custom-call(s32[128]{0:T(128)S(1)} %copy-done, s32[128]{0:T(128)S(1)} %copy-done.1, s32[128]{0:T(128)S(1)} %copy-done.2), custom_call_target="tpu_custom_call" | custom-call | tf_op jit(solution)/shard_map/index_table/pallas_call | solution.py:142
  9.6 1.1 %collective-permute-done.1.met_even = f32[232,128]{1,0:T(8,128)S(1)} collective-permute-done((f32[232,128]{1,0:T(8,128)S(1)}, f32[232,128]{1,0:T(8,128)S(1)}, u32[]{:S(2)}, u32[]{:S(2)}) %collective-permute-start.1) | collective-permute-done | bytes 118816 | tf_op jit(solution)/shard_map/ppermute | solution.py:667
  10.7 0.0 collective-permute-done.2.met_odd
  10.7 0.7 %collective-permute-done.refs_8_.refs_10_ = f32[448,128]{1,0:T(8,128)S(1)} collective-permute-done((f32[448,128]{1,0:T(8,128)S(1)}, f32[448,128]{1,0:T(8,128)S(1)}, u32[]{:S(2)}, u32[]{:S(2)}) %collective-permute-start) | collective-permute-done | bytes 229408 | tf_op jit(solution)/shard_map/ppermute | solution.py:643
  11.5 0.0 collective-permute-start.4
  11.5 1.7 %collective-permute-start.7 = (f32[2,232,128]{2,1,0:T(8,128)S(1)}, f32[2,232,128]{2,1,0:T(8,128)S(1)}, u32[]{:S(2)}, u32[]{:S(2)}) collective-permute-start(f32[2,232,128]{2,1,0:T(8,128)S(1)} %join_row_halos.1.refs_7_), channel_id=1, source_target_pairs={{0,2},{1,3},{2,0},{3,1},{4,6},{5,7},{6,4},{7,5},{8,10},{9,11},{10,... | collective-permute-start | bytes 712712 | tf_op jit(solution)/shard_map/ppermute | solution.py:643
  13.2 0.0 collective-permute-done.3.refs_7_.refs_8_
  13.2 0.0 collective-permute-done.4.refs_9_.refs_12_
  13.2 3.2 %advance_leaving_first.1 = (f32[2,3,112,128]{3,2,1,0:T(8,128)S(1)}, f32[2,3,112,128]{3,2,1,0:T(8,128)S(1)}, f32[2,3,112,128]{3,2,1,0:T(8,128)S(1)}) custom-call(s32[265]{0:T(512)S(4)} %index_table.1.refs_0_, f32[8,128,128]{2,1,0:T(8,128)S(1)} %get-tuple-element.36.refs_1_, f32[8,128,128]{2,1,0:T(8,128)S(1)} %get-tuple-element.37.refs_2_, ...), custom_call_target="tpu_custom_call" | custom-call | flops 17694720 | bytes 917504 | tf_op jit(solution)/shard_map/advance_leaving_first/pallas_call | solution.py:572
  16.4 1.5 %collective-permute-start.5 = (f32[2,3,112,128]{3,2,1,0:T(8,128)S(1)}, f32[2,3,112,128]{3,2,1,0:T(8,128)S(1)}, u32[]{:S(2)}, u32[]{:S(2)}) collective-permute-start(f32[2,3,112,128]{3,2,1,0:T(8,128)S(1)} %get-tuple-element.42), channel_id=1, source_target_pairs={{0,2},{1,3},{2,0},{3,1},{4,6},{5,7},{6,4},{7,5},{8,10},{9,11},{10,... | collective-permute-start | bytes 1032200 | tf_op jit(solution)/shard_map/ppermute | solution.py:643
  18.0 3.2 %advance_leaving_second.1 = (f32[2,3,112,128]{3,2,1,0:T(8,128)S(1)}, f32[2,3,112,128]{3,2,1,0:T(8,128)S(1)}) custom-call(s32[265]{0:T(512)S(4)} %index_table.1.refs_0_, f32[8,128,128]{2,1,0:T(8,128)S(1)} %get-tuple-element.36.refs_1_, f32[8,128,128]{2,1,0:T(8,128)S(1)} %get-tuple-element.37.refs_2_, ...), custom_call_target="tpu_custom_call", output_to_operand_aliasing={{0}: (10, {}), {1}: (11, {})} | custom-call | flops 17694720 | bytes 917504 | tf_op jit(solution)/shard_map/advance_leaving_second/pallas_call | solution.py:572
  21.1 0.1 collective-permute-start.12
  21.2 0.7 %collective-permute-start.13 = (f32[2,3,112,128]{3,2,1,0:T(8,128)S(1)}, f32[2,3,112,128]{3,2,1,0:T(8,128)S(1)}, u32[]{:S(2)}, u32[]{:S(2)}) collective-permute-start(f32[2,3,112,128]{3,2,1,0:T(8,128)S(1)} %get-tuple-element.54), channel_id=1, source_target_pairs={{0,3},{1,2},{2,1},{3,0},{4,7},{5,6},{6,5},{7,4},{8,11},{9,10},{10,... | collective-permute-start | bytes 1032200 | tf_op jit(solution)/shard_map/ppermute | solution.py:643
  21.9 0.1 collective-permute-start.6
  22.0 0.0 collective-permute-done.7.refs_11_
  22.0 0.4 %collective-permute-start.8 = (f32[2,232,128]{2,1,0:T(8,128)S(1)}, f32[2,232,128]{2,1,0:T(8,128)S(1)}, u32[]{:S(2)}, u32[]{:S(2)}) collective-permute-start(f32[2,232,128]{2,1,0:T(8,128)S(1)} %collective-permute-done.7.refs_11_), channel_id=1, source_target_pairs={{0,1},{1,0},{2,3},{3,2},{4,5},{5,4},{6,7},{7,6},{8,9},{9,8},{10,11... | collective-permute-start | bytes 712712 | tf_op jit(solution)/shard_map/ppermute | solution.py:643
  22.4 1.0 %collective-permute-done.6.refs_9_ = f32[2,232,128]{2,1,0:T(8,128)S(1)} collective-permute-done((f32[2,232,128]{2,1,0:T(8,128)S(1)}, f32[2,232,128]{2,1,0:T(8,128)S(1)}, u32[]{:S(2)}, u32[]{:S(2)}) %collective-permute-start.6) | collective-permute-done | bytes 237600 | tf_op jit(solution)/shard_map/ppermute | solution.py:643
  23.4 0.3 collective-permute-done.8.refs_13_
  23.7 2.3 %advance_leaving_edges.1 = (f32[2,3,16,128]{3,2,1,0:T(8,128)S(1)}, f32[2,3,16,128]{3,2,1,0:T(8,128)S(1)}, f32[2,3,16,128]{3,2,1,0:T(8,128)S(1)}) custom-call(s32[265]{0:T(512)S(4)} %index_table.1.refs_0_, f32[8,128,128]{2,1,0:T(8,128)S(1)} %get-tuple-element.36.refs_1_, f32[8,128,128]{2,1,0:T(8,128)S(1)} %get-tuple-element.37.refs_2_, ...), custom_call_target="tpu_custom_call" | custom-call | flops 11059200 | bytes 262144 | tf_op jit(solution)/shard_map/advance_leaving_edges/pallas_call | solution.py:572
  26.1 1.3 %collective-permute-done.5.refs_2_ = f32[2,3,112,128]{3,2,1,0:T(8,128)S(1)} collective-permute-done((f32[2,3,112,128]{3,2,1,0:T(8,128)S(1)}, f32[2,3,112,128]{3,2,1,0:T(8,128)S(1)}, u32[]{:S(2)}, u32[]{:S(2)}) %collective-permute-start.5) | collective-permute-done | bytes 344096 | tf_op jit(solution)/shard_map/ppermute | solution.py:643
  27.4 0.0 collective-permute-start.9
  27.4 1.8 %collective-permute-start.10 = (f32[2,3,16,128]{3,2,1,0:T(8,128)S(1)}, f32[2,3,16,128]{3,2,1,0:T(8,128)S(1)}, u32[]{:S(2)}, u32[]{:S(2)}) collective-permute-start(f32[2,3,16,128]{3,2,1,0:T(8,128)S(1)} %get-tuple-element.48), channel_id=1, source_target_pairs={{0,2},{1,3},{2,0},{3,1},{4,6},{5,7},{6,4},{7,5},{8,10},{9,11},{10,... | collective-permute-start | bytes 147464 | tf_op jit(solution)/shard_map/ppermute | solution.py:643
  29.2 0.1 collective-permute-start.11
  29.3 6.3 %advance_staying.1 = (f32[8,128,128]{2,1,0:T(8,128)}, f32[8,128,128]{2,1,0:T(8,128)}, f32[8,128,128]{2,1,0:T(8,128)}) custom-call(s32[265]{0:T(512)S(4)} %index_table.1.refs_0_, f32[8,128,128]{2,1,0:T(8,128)S(1)} %get-tuple-element.36.refs_1_, f32[8,128,128]{2,1,0:T(8,128)S(1)} %get-tuple-element.37.refs_2_, f32[8,128,128]{2,1,0:T(8,128)S(1)} %get-tuple-element.38.refs_3_, ...), custom_call_target="tpu_custom_call" | custom-call | flops 33177600 | bytes 2097152 | tf_op jit(solution)/shard_map/advance_staying/pallas_call | solution.py:572
  35.6 0.0 collective-permute-done.12.refs_1_
  35.6 0.0 collective-permute-done.13.refs_3_
  35.6 1.0 %place_middle.1 = (f32[8,128,128]{2,1,0:T(8,128)}, f32[8,128,128]{2,1,0:T(8,128)}, f32[8,128,128]{2,1,0:T(8,128)}) custom-call(s32[265]{0:T(512)S(4)} %index_table.1.refs_0_, f32[2,3,112,128]{3,2,1,0:T(8,128)S(1)} %collective-permute-done.12.refs_1_, ...), custom_call_target="tpu_custom_call", output_to_operand_aliasing={{0}: (4, {}), {1}: (5, {}), {2}: (6, {})} | custom-call | tf_op jit(solution)/shard_map/place_middle/pallas_call | solution.py:622
  36.7 0.0 collective-permute-done.9.refs_1_
  36.7 0.0 collective-permute-done.10.refs_2_
  36.7 0.0 collective-permute-done.11.refs_3_
  36.7 1.1 %place_edges.1 = (f32[8,128,128]{2,1,0:T(8,128)}, f32[8,128,128]{2,1,0:T(8,128)}, f32[8,128,128]{2,1,0:T(8,128)}) custom-call(s32[265]{0:T(512)S(4)} %index_table.1.refs_0_, f32[2,3,16,128]{3,2,1,0:T(8,128)S(1)} %collective-permute-done.9.refs_1_, ...), custom_call_target="tpu_custom_call", output_to_operand_aliasing={{0}: (4, {}), {1}: (5, {}), {2}: (6, {})} | custom-call | tf_op jit(solution)/shard_map/place_edges/pallas_call | solution.py:622
  (1 shorter events, 0.0 us)
Async XLA Ops:
  2.9 8.6 %collective-permute-start = (f32[448,128]{1,0:T(8,128)S(1)}, f32[448,128]{1,0:T(8,128)S(1)}, u32[]{:S(2)}, u32[]{:S(2)}) collective-permute-start(f32[448,128]{1,0:T(8,128)S(1)} %get-tuple-element.32.refs_6_), channel_id=1, source_target_pairs={{0,2},{1,3},{2,0},{3,1},{4,6},{5,7},{6,4},{7,5},{8,10},{9,11},{10,... | collective-permute-start | bytes 688136 | tf_op jit(solution)/shard_map/ppermute | solution.py:643
  5.9 2.1 %copy-start = (s32[128]{0:T(128)S(1)}, s32[128]{0:T(128)}, u32[]{:S(2)}) copy-start(s32[128]{0:T(128)} %before_ref.1) | copy-start | bytes 1540
  5.9 2.1 %copy-start.1 = (s32[128]{0:T(128)S(1)}, s32[128]{0:T(128)}, u32[]{:S(2)}) copy-start(s32[128]{0:T(128)} %after_ref.1) | copy-start | bytes 1540
  5.9 2.1 %copy-start.2 = (s32[128]{0:T(128)S(1)}, s32[128]{0:T(128)}, u32[]{:S(2)}) copy-start(s32[128]{0:T(128)} %wet_ref.1) | copy-start | bytes 1540
  5.9 4.8 %collective-permute-start.1 = (f32[232,128]{1,0:T(8,128)S(1)}, f32[232,128]{1,0:T(8,128)S(1)}, u32[]{:S(2)}, u32[]{:S(2)}) collective-permute-start(f32[232,128]{1,0:T(8,128)S(1)} %get-tuple-element.33), channel_id=1, source_target_pairs={{0,4},{1,5},{4,0},{5,1},{8,12},{9,13},{12,8},{13,9},{2,6},{3,7},{6... | collective-permute-start | bytes 356360 | tf_op jit(solution)/shard_map/ppermute | solution.py:667
  7.4 3.3 %collective-permute-start.2 = (f32[232,128]{1,0:T(8,128)S(1)}, f32[232,128]{1,0:T(8,128)S(1)}, u32[]{:S(2)}, u32[]{:S(2)}) collective-permute-start(f32[232,128]{1,0:T(8,128)S(1)} %get-tuple-element.34), channel_id=1, source_target_pairs={{0,1},{1,0},{4,8},{5,9},{8,4},{9,5},{12,13},{13,12},{2,3},{3,2},{6... | collective-permute-start | bytes 356360 | tf_op jit(solution)/shard_map/ppermute | solution.py:667
  7.4 5.8 %collective-permute-start.3 = (f32[448,128]{1,0:T(8,128)S(1)}, f32[448,128]{1,0:T(8,128)S(1)}, u32[]{:S(2)}, u32[]{:S(2)}) collective-permute-start(f32[448,128]{1,0:T(8,128)S(1)} %get-tuple-element.32.refs_6_), channel_id=1, source_target_pairs={{0,1},{1,0},{2,3},{3,2},{4,5},{5,4},{6,7},{7,6},{8,9},{9,8},{10,11... | collective-permute-start | bytes 688136 | tf_op jit(solution)/shard_map/ppermute | solution.py:643
  11.5 1.8 %collective-permute-start.4 = (f32[448,128]{1,0:T(8,128)S(1)}, f32[448,128]{1,0:T(8,128)S(1)}, u32[]{:S(2)}, u32[]{:S(2)}) collective-permute-start(f32[448,128]{1,0:T(8,128)S(1)} %collective-permute-done.refs_8_.refs_10_), channel_id=1, source_target_pairs={{0,1},{1,0},{2,3},{3,2},{4,5},{5,4},{6,7},{7,6},{8,9},{9,8},{10,11... | collective-permute-start | bytes 688136 | tf_op jit(solution)/shard_map/ppermute | solution.py:643
  11.5 10.5 %collective-permute-start.7 = (f32[2,232,128]{2,1,0:T(8,128)S(1)}, f32[2,232,128]{2,1,0:T(8,128)S(1)}, u32[]{:S(2)}, u32[]{:S(2)}) collective-permute-start(f32[2,232,128]{2,1,0:T(8,128)S(1)} %join_row_halos.1.refs_7_), channel_id=1, source_target_pairs={{0,2},{1,3},{2,0},{3,1},{4,6},{5,7},{6,4},{7,5},{8,10},{9,11},{10,... | collective-permute-start | bytes 712712 | tf_op jit(solution)/shard_map/ppermute | solution.py:643
  16.4 11.0 %collective-permute-start.5 = (f32[2,3,112,128]{3,2,1,0:T(8,128)S(1)}, f32[2,3,112,128]{3,2,1,0:T(8,128)S(1)}, u32[]{:S(2)}, u32[]{:S(2)}) collective-permute-start(f32[2,3,112,128]{3,2,1,0:T(8,128)S(1)} %get-tuple-element.42), channel_id=1, source_target_pairs={{0,2},{1,3},{2,0},{3,1},{4,6},{5,7},{6,4},{7,5},{8,10},{9,11},{10,... | collective-permute-start | bytes 1032200 | tf_op jit(solution)/shard_map/ppermute | solution.py:643
  21.1 14.5 %collective-permute-start.12 = (f32[2,3,112,128]{3,2,1,0:T(8,128)S(1)}, f32[2,3,112,128]{3,2,1,0:T(8,128)S(1)}, u32[]{:S(2)}, u32[]{:S(2)}) collective-permute-start(f32[2,3,112,128]{3,2,1,0:T(8,128)S(1)} %get-tuple-element.52), channel_id=1, source_target_pairs={{0,1},{1,0},{2,3},{3,2},{4,5},{5,4},{6,7},{7,6},{8,9},{9,8},{10,11... | collective-permute-start | bytes 1032200 | tf_op jit(solution)/shard_map/ppermute | solution.py:643
  21.2 14.4 %collective-permute-start.13 = (f32[2,3,112,128]{3,2,1,0:T(8,128)S(1)}, f32[2,3,112,128]{3,2,1,0:T(8,128)S(1)}, u32[]{:S(2)}, u32[]{:S(2)}) collective-permute-start(f32[2,3,112,128]{3,2,1,0:T(8,128)S(1)} %get-tuple-element.54), channel_id=1, source_target_pairs={{0,3},{1,2},{2,1},{3,0},{4,7},{5,6},{6,5},{7,4},{8,11},{9,10},{10,... | collective-permute-start | bytes 1032200 | tf_op jit(solution)/shard_map/ppermute | solution.py:643
  21.9 1.5 %collective-permute-start.6 = (f32[2,232,128]{2,1,0:T(8,128)S(1)}, f32[2,232,128]{2,1,0:T(8,128)S(1)}, u32[]{:S(2)}, u32[]{:S(2)}) collective-permute-start(f32[2,232,128]{2,1,0:T(8,128)S(1)} %join_row_halos.1.refs_7_), channel_id=1, source_target_pairs={{0,1},{1,0},{2,3},{3,2},{4,5},{5,4},{6,7},{7,6},{8,9},{9,8},{10,11... | collective-permute-start | bytes 712712 | tf_op jit(solution)/shard_map/ppermute | solution.py:643
  22.0 1.8 %collective-permute-start.8 = (f32[2,232,128]{2,1,0:T(8,128)S(1)}, f32[2,232,128]{2,1,0:T(8,128)S(1)}, u32[]{:S(2)}, u32[]{:S(2)}) collective-permute-start(f32[2,232,128]{2,1,0:T(8,128)S(1)} %collective-permute-done.7.refs_11_), channel_id=1, source_target_pairs={{0,1},{1,0},{2,3},{3,2},{4,5},{5,4},{6,7},{7,6},{8,9},{9,8},{10,11... | collective-permute-start | bytes 712712 | tf_op jit(solution)/shard_map/ppermute | solution.py:643
  27.4 9.3 %collective-permute-start.9 = (f32[2,3,16,128]{3,2,1,0:T(8,128)S(1)}, f32[2,3,16,128]{3,2,1,0:T(8,128)S(1)}, u32[]{:S(2)}, u32[]{:S(2)}) collective-permute-start(f32[2,3,16,128]{3,2,1,0:T(8,128)S(1)} %get-tuple-element.47), channel_id=1, source_target_pairs={{0,1},{1,0},{2,3},{3,2},{4,5},{5,4},{6,7},{7,6},{8,9},{9,8},{10,11... | collective-permute-start | bytes 147464 | tf_op jit(solution)/shard_map/ppermute | solution.py:643
  27.4 9.3 %collective-permute-start.10 = (f32[2,3,16,128]{3,2,1,0:T(8,128)S(1)}, f32[2,3,16,128]{3,2,1,0:T(8,128)S(1)}, u32[]{:S(2)}, u32[]{:S(2)}) collective-permute-start(f32[2,3,16,128]{3,2,1,0:T(8,128)S(1)} %get-tuple-element.48), channel_id=1, source_target_pairs={{0,2},{1,3},{2,0},{3,1},{4,6},{5,7},{6,4},{7,5},{8,10},{9,11},{10,... | collective-permute-start | bytes 147464 | tf_op jit(solution)/shard_map/ppermute | solution.py:643
  29.2 7.6 %collective-permute-start.11 = (f32[2,3,16,128]{3,2,1,0:T(8,128)S(1)}, f32[2,3,16,128]{3,2,1,0:T(8,128)S(1)}, u32[]{:S(2)}, u32[]{:S(2)}) collective-permute-start(f32[2,3,16,128]{3,2,1,0:T(8,128)S(1)} %get-tuple-element.49), channel_id=1, source_target_pairs={{0,3},{1,2},{2,1},{3,0},{4,7},{5,6},{6,5},{7,4},{8,11},{9,10},{10,... | collective-permute-start | bytes 147464 | tf_op jit(solution)/shard_map/ppermute | solution.py:643

commit v8 on v7

--- a/solution.py
+++ b/solution.py
@@ -237,6 +237,58 @@
     )(in_vmem(met_even), in_vmem(met_odd))
 
 
+def arrivals(table, units, received, spans, outs, sem):
+    def each(act):
+        for n, k in enumerate(units):
+            for j in range(2):
+                slot = table[RECEIVE + 2 * k + j]
+
+                @pl.when(slot >= 0)
+                def _():
+                    at = 0
+                    for m, (start, count) in enumerate(spans):
+                        for f in range(3):
+                            act(
+                                pltpu.make_async_copy(
+                                    received[n].at[j, f, pl.ds(at, count), :],
+                                    outs[f].at[slot, pl.ds(start, count), :],
+                                    sem.at[n, j, f, m],
+                                )
+                            )
+                        at += count
+
+    return each
+
+
+def place_kernel(groups, *refs):
+    table, received, refs = refs[0], refs[1 : 1 + len(groups)], refs[1 + len(groups) :]
+    outs, sem = refs[3:6], refs[6]
+    copies = [
+        arrivals(table, (k,), (array,), spans, outs, sem.at[pl.ds(n, 1)])
+        for n, ((k, spans), array) in enumerate(zip(groups, received))
+    ]
+    for each in copies:
+        each(lambda copy: copy.start())
+    for each in copies:
+        each(lambda copy: copy.wait())
+
+
+def place(groups, table, received, partial_outs):
+    count = len(received)
+    return pl.pallas_call(
+        functools.partial(place_kernel, groups),
+        name="place_arrivals",
+        out_shape=tuple(jax.ShapeDtypeStruct(o.shape, o.dtype) for o in partial_outs),
+        in_specs=[pl.BlockSpec(memory_space=SMEM)]
+        + vmem_specs(count)
+        + [pl.BlockSpec(memory_space=ANY)] * 3,
+        out_specs=tuple(pl.BlockSpec(memory_space=ANY) for _ in partial_outs),
+        scratch_shapes=[pltpu.SemaphoreType.DMA((count, 2, 3, 2))],
+        input_output_aliases={1 + count + f: f for f in range(3)},
+        compiler_params=SMALL,
+    )(table, *received, *partial_outs)
+
+
 def face(flow, level, level_next, ground, friction):
     wetted = jnp.maximum(level, level_next) - ground
     drive = (GRAV * STEP_TIME / SPACING) * jnp.maximum(wetted, 0.0) * (level_next - level)
@@ -437,14 +489,17 @@
     fields = refs[1 : 1 + FIELDS]
     kinds = 2 if part.halo_rows else 1
     halos, refs = refs[1 + FIELDS : 1 + FIELDS + kinds * lanes], refs[1 + FIELDS + kinds * lanes :]
-    refs = refs[given:]
+    received, refs = refs[:given], refs[given:]
     n_out = 3 if part is WHOLE else len(units)
     outs, stacks, refs = refs[:n_out], refs[n_out : n_out + kinds], refs[n_out + kinds :]
     (
         level, flow_x, flow_y, ground, friction, ground_x, ground_y,
         s_level, s_flow_x, s_flow_y, s_ground, s_friction, s_ground_x, s_ground_y,
-        sem_out,
+        sem_out, sem_in,
     ) = refs
+    if part is WHOLE:
+        placing = arrivals(table, units, received, (MIDDLE,), outs, sem_in)
+        placing(lambda copy: copy.start())
     block = (level, flow_x, flow_y, ground, friction)
     strip = (s_level, s_flow_x, s_flow_y, s_ground, s_friction)
     lane = lane_index()
@@ -546,11 +601,12 @@
         ]
         for copy in copies:
             copy.start()
+        placing(lambda copy: copy.wait())
         for copy in copies:
             copy.wait()
 
 
-def advance(part, table, fields, halos, units=(), partial=()):
+def advance(part, table, fields, halos, units, given=()):
     lanes = len(halos)
     sent = sum(count for _, count in part.sent)
     if part is WHOLE:
@@ -570,67 +626,27 @@
     strip = VMEM((ROWS, SIDE), jnp.float32)
     cells = (part.tiles + 1) * sum(count for _, count in part.computed) * SIDE * STEPS
     return pl.pallas_call(
-        functools.partial(advance_kernel, part, lanes, units, len(partial)),
+        functools.partial(advance_kernel, part, lanes, units, len(given)),
         name="advance_" + part.name,
         out_shape=outs,
         in_specs=[pl.BlockSpec(memory_space=SMEM)]
-        + vmem_specs(FIELDS + len(flat) + len(partial)),
-        input_output_aliases={1 + FIELDS + len(flat) + n: n for n in range(len(partial))},
+        + vmem_specs(FIELDS + len(flat) + len(given)),
+        input_output_aliases={
+            1 + FIELDS + len(flat) + n: n for n in range(0 if part is WHOLE else len(given))
+        },
         out_specs=tuple(out_specs),
         scratch_shapes=stacks
         + [block] * 7
         + [strip] * 7
-        + [pltpu.SemaphoreType.DMA((part.tiles, 3))],
+        + [
+            pltpu.SemaphoreType.DMA((part.tiles, 3)),
+            pltpu.SemaphoreType.DMA((max(len(given), 1), 2, 3, 1)),
+        ],
         compiler_params=pltpu.CompilerParams(vmem_limit_bytes=12 * 1024 * 1024),
         cost_estimate=pl.CostEstimate(
             flops=60 * cells, bytes_accessed=8 * part.tiles * sent * SIDE * 4, transcendentals=6 * cells
         ),
-    )(table, *fields, *flat, *partial)
-
-
-def place_kernel(spans, lanes, *refs):
-    table = refs[0]
-    received = refs[1:lanes]
-    outs = refs[lanes + 3 : lanes + 6]
-    sem = refs[lanes + 6]
-
-    def each(act):
-        for k in range(1, lanes):
-            for j in range(2):
-                slot = table[RECEIVE + 2 * k + j]
-
-                @pl.when(slot >= 0)
-                def _():
-                    at = 0
-                    for n, (start, count) in enumerate(spans):
-                        for f in range(3):
-                            act(
-                                pltpu.make_async_copy(
-                                    received[k - 1].at[j, f, pl.ds(at, count), :],
-                                    outs[f].at[slot, pl.ds(start, count), :],
-                                    sem.at[k, j, f, n],
-                                )
-                            )
-                        at += count
-
-    each(lambda copy: copy.start())
-    each(lambda copy: copy.wait())
-
-
-def place(name, spans, table, received, partial_outs):
-    lanes = len(received) + 1
-    return pl.pallas_call(
-        functools.partial(place_kernel, spans, lanes),
-        name="place_" + name,
-        out_shape=tuple(jax.ShapeDtypeStruct(o.shape, o.dtype) for o in partial_outs),
-        in_specs=[pl.BlockSpec(memory_space=SMEM)]
-        + vmem_specs(lanes - 1)
-        + [pl.BlockSpec(memory_space=ANY)] * 3,
-        out_specs=tuple(pl.BlockSpec(memory_space=ANY) for _ in partial_outs),
-        scratch_shapes=[pltpu.SemaphoreType.DMA((lanes, 2, 3, len(spans)))],
-        input_output_aliases={lanes: 0, lanes + 1: 1, lanes + 2: 2},
-        compiler_params=SMALL,
-    )(table, *received, *partial_outs)
+    )(table, *fields, *flat, *given)
 
 
 def shift_lanes(array, col_shift, sub_shift):
@@ -700,13 +716,15 @@
     middle = {ahead: send(first, ahead)}
     middle.update((k, send(part, k)) for k, part in zip(others, rest))
     halos = list(zip(columns, near_rows))
-    edges = advance(LATE, table, fields, halos, units)
-    middle[ahead], edges = lax.optimization_barrier((middle[ahead], edges))
+    edges = list(advance(LATE, table, fields, halos, units))
+    middle[ahead], edges[0] = lax.optimization_barrier((middle[ahead], edges[0]))
     middle[ahead] = in_vmem(middle[ahead])
     edges = [send(part, k) for k, part in zip(units, edges)]
-    outs = advance(WHOLE, table, fields, halos)
-    outs = place("middle", EARLY[0].sent, table, [middle[k] for k in units], outs)
-    return place("edges", LATE.sent, table, edges, outs)
+    soon = tuple(range(1, subs)) + (ahead,)
+    last = tuple(k for k in units if k not in soon)
+    outs = advance(WHOLE, table, fields, halos, soon, [middle[k] for k in soon])
+    groups = tuple((k, (MIDDLE,)) for k in last) + tuple((k, LATE.sent) for k in units)
+    return place(groups, table, [middle[k] for k in last] + edges, outs)
 
 
 def solution(mesh):

time: 38 us -> 37.4 us (0.984)
  Pallas kernels: 21.1 us -> 20.3 us
    pallas_call x2 -> x1, Pallas kernels: 2.16 us -> 1.11 us  [place(): pl.pallas_call(functools.partial(place_kernel, groups), name='place_arriv...]
  transfers between devices with their start and end apart: 14 -> 14, of which waited for: 5 -> 6; matrix products, arithmetic and copies ran while one was open for 0% -> 0% of each run, Pallas kernels for 47% -> 46%
where the time goes in v8:
time: 37.4 us; the launch traced here: 37.2 us
  Pallas kernels  20.3 us (54%)
  starting transfers between devices  11.8 us (32%)
  waiting for transfers between devices  4.34 us (12%)
  between operations  0.71 us (2%)
    pallas_call x4, Pallas kernels, advance(): pl.pallas_call(functools.partial(advance_kernel, part, lanes, units, len(...  15.3 us
    ppermute x12, starting transfers between devices, shift_lanes(): return lax.ppermute(array, ('col', 'sub'), pairs)  10.3 us
    ppermute x12, waiting for transfers between devices, shift_lanes(): return lax.ppermute(array, ('col', 'sub'), pairs)  3.24 us
    pallas_call x1, Pallas kernels, load(): pl.pallas_call(load_kernel, name='load_and_pack', out_shape=tuple(outs),...  2.21 us
    pallas_call x1, Pallas kernels, make_table(): pl.pallas_call(functools.partial(index_kernel, shape), name='index_table'...  1.64 us
    ppermute x2, starting transfers between devices, meet_rows(): return lax.ppermute(array, ('row', 'sub'), pairs)  1.58 us
    pallas_call x1, Pallas kernels, place(): pl.pallas_call(functools.partial(place_kernel, groups), name='place_arriv...  1.11 us
    ppermute x2, waiting for transfers between devices, meet_rows(): return lax.ppermute(array, ('row', 'sub'), pairs)  1.09 us
  transfers between devices with their start and end apart: 14, of which 6 were waited for; matrix products, arithmetic and copies ran while one was open for 0% of the time, Pallas kernels for 46%

profile of v8, /device:TPU:0, one launch (start us, length us, event | category | flops | bytes accessed | tf_op | source)
XLA Modules:
  0.0 37.2 jit_solution(2804145225332288938)
XLA Ops:
  0.6 2.2 %load_and_pack.1 = (f32[8,128,128]{2,1,0:T(8,128)S(1)}, f32[8,128,128]{2,1,0:T(8,128)S(1)}, f32[8,128,128]{2,1,0:T(8,128)S(1)}, f32[8,128,128]{2,1,0:T(8,128)S(1...) custom-call(f32[8,128,128]{2,1,0:T(8,128)} %refs_0_.1, ...), custom_call_target="tpu_custom_call" | custom-call | tf_op jit(solution)/shard_map/load_and_pack/pallas_call | solution.py:207
  2.9 3.0 %collective-permute-start = (f32[448,128]{1,0:T(8,128)S(1)}, f32[448,128]{1,0:T(8,128)S(1)}, u32[]{:S(2)}, u32[]{:S(2)}) collective-permute-start(f32[448,128]{1,0:T(8,128)S(1)} %get-tuple-element.27.refs_6_), channel_id=1, source_target_pairs={{0,2},{1,3},{2,0},{3,1},{4,6},{5,7},{6,4},{7,5},{8,10},{9,11},{10,... | collective-permute-start | bytes 688136 | tf_op jit(solution)/shard_map/ppermute | solution.py:659
  5.9 0.0 copy-start
  5.9 0.0 copy-start.1
  5.9 0.0 copy-start.2
  5.9 1.6 %collective-permute-start.1 = (f32[232,128]{1,0:T(8,128)S(1)}, f32[232,128]{1,0:T(8,128)S(1)}, u32[]{:S(2)}, u32[]{:S(2)}) collective-permute-start(f32[232,128]{1,0:T(8,128)S(1)} %get-tuple-element.28), channel_id=1, source_target_pairs={{0,4},{1,5},{4,0},{5,1},{8,12},{9,13},{12,8},{13,9},{2,6},{3,7},{6... | collective-permute-start | bytes 356360 | tf_op jit(solution)/shard_map/ppermute | solution.py:683
  7.4 0.0 collective-permute-start.2
  7.4 0.5 %collective-permute-start.3 = (f32[448,128]{1,0:T(8,128)S(1)}, f32[448,128]{1,0:T(8,128)S(1)}, u32[]{:S(2)}, u32[]{:S(2)}) collective-permute-start(f32[448,128]{1,0:T(8,128)S(1)} %get-tuple-element.27.refs_6_), channel_id=1, source_target_pairs={{0,1},{1,0},{2,3},{3,2},{4,5},{5,4},{6,7},{7,6},{8,9},{9,8},{10,11... | collective-permute-start | bytes 688136 | tf_op jit(solution)/shard_map/ppermute | solution.py:659
  7.9 0.0 copy-done
  8.0 0.0 copy-done.1
  8.0 0.0 copy-done.2
  8.0 1.6 %index_table.1.refs_0_ = s32[265]{0:T(512)S(4)} custom-call(s32[128]{0:T(128)S(1)} %copy-done, s32[128]{0:T(128)S(1)} %copy-done.1, s32[128]{0:T(128)S(1)} %copy-done.2), custom_call_target="tpu_custom_call" | custom-call | tf_op jit(solution)/shard_map/index_table/pallas_call | solution.py:142
  9.6 1.1 %collective-permute-done.1.met_even = f32[232,128]{1,0:T(8,128)S(1)} collective-permute-done((f32[232,128]{1,0:T(8,128)S(1)}, f32[232,128]{1,0:T(8,128)S(1)}, u32[]{:S(2)}, u32[]{:S(2)}) %collective-permute-start.1) | collective-permute-done | bytes 118816 | tf_op jit(solution)/shard_map/ppermute | solution.py:683
  10.7 0.0 collective-permute-done.2.met_odd
  10.7 0.7 %collective-permute-done.refs_8_.refs_10_ = f32[448,128]{1,0:T(8,128)S(1)} collective-permute-done((f32[448,128]{1,0:T(8,128)S(1)}, f32[448,128]{1,0:T(8,128)S(1)}, u32[]{:S(2)}, u32[]{:S(2)}) %collective-permute-start) | collective-permute-done | bytes 229408 | tf_op jit(solution)/shard_map/ppermute | solution.py:659
  11.5 0.0 collective-permute-start.4
  11.5 1.7 %collective-permute-start.8 = (f32[2,232,128]{2,1,0:T(8,128)S(1)}, f32[2,232,128]{2,1,0:T(8,128)S(1)}, u32[]{:S(2)}, u32[]{:S(2)}) collective-permute-start(f32[2,232,128]{2,1,0:T(8,128)S(1)} %join_row_halos.1.refs_7_), channel_id=1, source_target_pairs={{0,2},{1,3},{2,0},{3,1},{4,6},{5,7},{6,4},{7,5},{8,10},{9,11},{10,... | collective-permute-start | bytes 712712 | tf_op jit(solution)/shard_map/ppermute | solution.py:659
  13.2 0.0 collective-permute-done.3.refs_7_.refs_8_
  13.2 0.0 collective-permute-done.4.refs_9_.refs_12_
  13.2 3.2 %advance_leaving_first.1 = (f32[2,3,112,128]{3,2,1,0:T(8,128)S(1)}, f32[2,3,112,128]{3,2,1,0:T(8,128)S(1)}, f32[2,3,112,128]{3,2,1,0:T(8,128)S(1)}) custom-call(s32[265]{0:T(512)S(4)} %index_table.1.refs_0_, f32[8,128,128]{2,1,0:T(8,128)S(1)} %get-tuple-element.31.refs_1_, f32[8,128,128]{2,1,0:T(8,128)S(1)} %get-tuple-element.32.refs_2_, ...), custom_call_target="tpu_custom_call" | custom-call | flops 17694720 | bytes 917504 | tf_op jit(solution)/shard_map/advance_leaving_first/pallas_call | solution.py:628
  16.5 1.5 %collective-permute-start.6 = (f32[2,3,112,128]{3,2,1,0:T(8,128)S(1)}, f32[2,3,112,128]{3,2,1,0:T(8,128)S(1)}, u32[]{:S(2)}, u32[]{:S(2)}) collective-permute-start(f32[2,3,112,128]{3,2,1,0:T(8,128)S(1)} %get-tuple-element.40), channel_id=1, source_target_pairs={{0,2},{1,3},{2,0},{3,1},{4,6},{5,7},{6,4},{7,5},{8,10},{9,11},{10,... | collective-permute-start | bytes 1032200 | tf_op jit(solution)/shard_map/ppermute | solution.py:659
  18.0 3.3 %advance_leaving_second.1 = (f32[2,3,112,128]{3,2,1,0:T(8,128)S(1)}, f32[2,3,112,128]{3,2,1,0:T(8,128)S(1)}) custom-call(s32[265]{0:T(512)S(4)} %index_table.1.refs_0_, f32[8,128,128]{2,1,0:T(8,128)S(1)} %get-tuple-element.31.refs_1_, f32[8,128,128]{2,1,0:T(8,128)S(1)} %get-tuple-element.32.refs_2_, ...), custom_call_target="tpu_custom_call", output_to_operand_aliasing={{0}: (10, {}), {1}: (11, {})} | custom-call | flops 17694720 | bytes 917504 | tf_op jit(solution)/shard_map/advance_leaving_second/pallas_call | solution.py:628
  21.3 0.1 collective-permute-start.13
  21.4 0.7 %collective-permute-start.5 = (f32[2,3,112,128]{3,2,1,0:T(8,128)S(1)}, f32[2,3,112,128]{3,2,1,0:T(8,128)S(1)}, u32[]{:S(2)}, u32[]{:S(2)}) collective-permute-start(f32[2,3,112,128]{3,2,1,0:T(8,128)S(1)} %get-tuple-element.39), channel_id=1, source_target_pairs={{0,3},{1,2},{2,1},{3,0},{4,7},{5,6},{6,5},{7,4},{8,11},{9,10},{10,... | collective-permute-start | bytes 1032200 | tf_op jit(solution)/shard_map/ppermute | solution.py:659
  22.0 0.1 collective-permute-start.7
  22.1 0.0 collective-permute-done.8.refs_11_
  22.1 0.4 %collective-permute-start.9 = (f32[2,232,128]{2,1,0:T(8,128)S(1)}, f32[2,232,128]{2,1,0:T(8,128)S(1)}, u32[]{:S(2)}, u32[]{:S(2)}) collective-permute-start(f32[2,232,128]{2,1,0:T(8,128)S(1)} %collective-permute-done.8.refs_11_), channel_id=1, source_target_pairs={{0,1},{1,0},{2,3},{3,2},{4,5},{5,4},{6,7},{7,6},{8,9},{9,8},{10,11... | collective-permute-start | bytes 712712 | tf_op jit(solution)/shard_map/ppermute | solution.py:659
  22.6 1.0 %collective-permute-done.7.refs_9_ = f32[2,232,128]{2,1,0:T(8,128)S(1)} collective-permute-done((f32[2,232,128]{2,1,0:T(8,128)S(1)}, f32[2,232,128]{2,1,0:T(8,128)S(1)}, u32[]{:S(2)}, u32[]{:S(2)}) %collective-permute-start.7) | collective-permute-done | bytes 237600 | tf_op jit(solution)/shard_map/ppermute | solution.py:659
  23.5 0.3 collective-permute-done.9.refs_13_
  23.9 2.4 %advance_leaving_edges.1 = (f32[2,3,16,128]{3,2,1,0:T(8,128)S(1)}, f32[2,3,16,128]{3,2,1,0:T(8,128)S(1)}, f32[2,3,16,128]{3,2,1,0:T(8,128)S(1)}) custom-call(s32[265]{0:T(512)S(4)} %index_table.1.refs_0_, f32[8,128,128]{2,1,0:T(8,128)S(1)} %get-tuple-element.31.refs_1_, f32[8,128,128]{2,1,0:T(8,128)S(1)} %get-tuple-element.32.refs_2_, ...), custom_call_target="tpu_custom_call" | custom-call | flops 11059200 | bytes 262144 | tf_op jit(solution)/shard_map/advance_leaving_edges/pallas_call | solution.py:628
  26.3 1.5 %collective-permute-start.11 = (f32[2,3,16,128]{3,2,1,0:T(8,128)S(1)}, f32[2,3,16,128]{3,2,1,0:T(8,128)S(1)}, u32[]{:S(2)}, u32[]{:S(2)}) collective-permute-start(f32[2,3,16,128]{3,2,1,0:T(8,128)S(1)} %get-tuple-element.44), channel_id=1, source_target_pairs={{0,2},{1,3},{2,0},{3,1},{4,6},{5,7},{6,4},{7,5},{8,10},{9,11},{10,... | collective-permute-start | bytes 147464 | tf_op jit(solution)/shard_map/ppermute | solution.py:659
  27.8 0.0 collective-permute-start.12
  27.9 0.0 collective-permute-done.6.refs_15_
  27.9 0.6 %collective-permute-start.10 = (f32[2,3,16,128]{3,2,1,0:T(8,128)S(1)}, f32[2,3,16,128]{3,2,1,0:T(8,128)S(1)}, u32[]{:S(2)}, u32[]{:S(2)}) collective-permute-start(f32[2,3,16,128]{3,2,1,0:T(8,128)S(1)} %get-tuple-element.43), channel_id=1, source_target_pairs={{0,1},{1,0},{2,3},{3,2},{4,5},{5,4},{6,7},{7,6},{8,9},{9,8},{10,11... | collective-permute-start | bytes 147464 | tf_op jit(solution)/shard_map/ppermute | solution.py:659
  28.5 0.0 collective-permute-done.13.refs_14_
  28.5 6.4 %advance_staying.1 = (f32[8,128,128]{2,1,0:T(8,128)}, f32[8,128,128]{2,1,0:T(8,128)}, f32[8,128,128]{2,1,0:T(8,128)}) custom-call(s32[265]{0:T(512)S(4)} %index_table.1.refs_0_, f32[8,128,128]{2,1,0:T(8,128)S(1)} %get-tuple-element.31.refs_1_, f32[8,128,128]{2,1,0:T(8,128)S(1)} %get-tuple-element.32.refs_2_, f32[8,128,128]{2,1,0:T(8,128)S(1)} %get-tuple-element.33.refs_3_, ...), custom_call_target="tpu_custom_call" | custom-call | flops 33177600 | bytes 2097152 | tf_op jit(solution)/shard_map/advance_staying/pallas_call | solution.py:628
  34.9 0.9 %collective-permute-done.11.refs_3_ = f32[2,3,16,128]{3,2,1,0:T(8,128)S(1)} collective-permute-done((f32[2,3,16,128]{3,2,1,0:T(8,128)S(1)}, f32[2,3,16,128]{3,2,1,0:T(8,128)S(1)}, u32[]{:S(2)}, u32[]{:S(2)}) %collective-permute-start.11) | collective-permute-done | bytes 49184 | tf_op jit(solution)/shard_map/ppermute | solution.py:659
  35.8 0.3 collective-permute-done.12.refs_4_
  36.1 0.0 collective-permute-done.5.refs_1_
  36.1 0.0 collective-permute-done.10.refs_2_
  36.1 1.1 %place_arrivals.1 = (f32[8,128,128]{2,1,0:T(8,128)}, f32[8,128,128]{2,1,0:T(8,128)}, f32[8,128,128]{2,1,0:T(8,128)}) custom-call(s32[265]{0:T(512)S(4)} %index_table.1.refs_0_, f32[2,3,112,128]{3,2,1,0:T(8,128)S(1)} %collective-permute-done.5.refs_1_, ...), custom_call_target="tpu_custom_call", output_to_operand_aliasing={{0}: (5, {}), {1}: (6, {}), {2}: (7, {})} | custom-call | tf_op jit(solution)/shard_map/place_arrivals/pallas_call | solution.py:278
  (1 shorter events, 0.0 us)
Async XLA Ops:
  2.9 8.6 %collective-permute-start = (f32[448,128]{1,0:T(8,128)S(1)}, f32[448,128]{1,0:T(8,128)S(1)}, u32[]{:S(2)}, u32[]{:S(2)}) collective-permute-start(f32[448,128]{1,0:T(8,128)S(1)} %get-tuple-element.27.refs_6_), channel_id=1, source_target_pairs={{0,2},{1,3},{2,0},{3,1},{4,6},{5,7},{6,4},{7,5},{8,10},{9,11},{10,... | collective-permute-start | bytes 688136 | tf_op jit(solution)/shard_map/ppermute | solution.py:659
  5.9 2.1 %copy-start = (s32[128]{0:T(128)S(1)}, s32[128]{0:T(128)}, u32[]{:S(2)}) copy-start(s32[128]{0:T(128)} %before_ref.1) | copy-start | bytes 1540
  5.9 2.1 %copy-start.1 = (s32[128]{0:T(128)S(1)}, s32[128]{0:T(128)}, u32[]{:S(2)}) copy-start(s32[128]{0:T(128)} %after_ref.1) | copy-start | bytes 1540
  5.9 2.1 %copy-start.2 = (s32[128]{0:T(128)S(1)}, s32[128]{0:T(128)}, u32[]{:S(2)}) copy-start(s32[128]{0:T(128)} %wet_ref.1) | copy-start | bytes 1540
  5.9 4.8 %collective-permute-start.1 = (f32[232,128]{1,0:T(8,128)S(1)}, f32[232,128]{1,0:T(8,128)S(1)}, u32[]{:S(2)}, u32[]{:S(2)}) collective-permute-start(f32[232,128]{1,0:T(8,128)S(1)} %get-tuple-element.28), channel_id=1, source_target_pairs={{0,4},{1,5},{4,0},{5,1},{8,12},{9,13},{12,8},{13,9},{2,6},{3,7},{6... | collective-permute-start | bytes 356360 | tf_op jit(solution)/shard_map/ppermute | solution.py:683
  7.4 3.3 %collective-permute-start.2 = (f32[232,128]{1,0:T(8,128)S(1)}, f32[232,128]{1,0:T(8,128)S(1)}, u32[]{:S(2)}, u32[]{:S(2)}) collective-permute-start(f32[232,128]{1,0:T(8,128)S(1)} %get-tuple-element.29), channel_id=1, source_target_pairs={{0,1},{1,0},{4,8},{5,9},{8,4},{9,5},{12,13},{13,12},{2,3},{3,2},{6... | collective-permute-start | bytes 356360 | tf_op jit(solution)/shard_map/ppermute | solution.py:683
  7.4 5.8 %collective-permute-start.3 = (f32[448,128]{1,0:T(8,128)S(1)}, f32[448,128]{1,0:T(8,128)S(1)}, u32[]{:S(2)}, u32[]{:S(2)}) collective-permute-start(f32[448,128]{1,0:T(8,128)S(1)} %get-tuple-element.27.refs_6_), channel_id=1, source_target_pairs={{0,1},{1,0},{2,3},{3,2},{4,5},{5,4},{6,7},{7,6},{8,9},{9,8},{10,11... | collective-permute-start | bytes 688136 | tf_op jit(solution)/shard_map/ppermute | solution.py:659
  11.5 1.8 %collective-permute-start.4 = (f32[448,128]{1,0:T(8,128)S(1)}, f32[448,128]{1,0:T(8,128)S(1)}, u32[]{:S(2)}, u32[]{:S(2)}) collective-permute-start(f32[448,128]{1,0:T(8,128)S(1)} %collective-permute-done.refs_8_.refs_10_), channel_id=1, source_target_pairs={{0,1},{1,0},{2,3},{3,2},{4,5},{5,4},{6,7},{7,6},{8,9},{9,8},{10,11... | collective-permute-start | bytes 688136 | tf_op jit(solution)/shard_map/ppermute | solution.py:659
  11.5 10.7 %collective-permute-start.8 = (f32[2,232,128]{2,1,0:T(8,128)S(1)}, f32[2,232,128]{2,1,0:T(8,128)S(1)}, u32[]{:S(2)}, u32[]{:S(2)}) collective-permute-start(f32[2,232,128]{2,1,0:T(8,128)S(1)} %join_row_halos.1.refs_7_), channel_id=1, source_target_pairs={{0,2},{1,3},{2,0},{3,1},{4,6},{5,7},{6,4},{7,5},{8,10},{9,11},{10,... | collective-permute-start | bytes 712712 | tf_op jit(solution)/shard_map/ppermute | solution.py:659
  16.5 11.4 %collective-permute-start.6 = (f32[2,3,112,128]{3,2,1,0:T(8,128)S(1)}, f32[2,3,112,128]{3,2,1,0:T(8,128)S(1)}, u32[]{:S(2)}, u32[]{:S(2)}) collective-permute-start(f32[2,3,112,128]{3,2,1,0:T(8,128)S(1)} %get-tuple-element.40), channel_id=1, source_target_pairs={{0,2},{1,3},{2,0},{3,1},{4,6},{5,7},{6,4},{7,5},{8,10},{9,11},{10,... | collective-permute-start | bytes 1032200 | tf_op jit(solution)/shard_map/ppermute | solution.py:659
  21.3 7.2 %collective-permute-start.13 = (f32[2,3,112,128]{3,2,1,0:T(8,128)S(1)}, f32[2,3,112,128]{3,2,1,0:T(8,128)S(1)}, u32[]{:S(2)}, u32[]{:S(2)}) collective-permute-start(f32[2,3,112,128]{3,2,1,0:T(8,128)S(1)} %get-tuple-element.46), channel_id=1, source_target_pairs={{0,1},{1,0},{2,3},{3,2},{4,5},{5,4},{6,7},{7,6},{8,9},{9,8},{10,11... | collective-permute-start | bytes 1032200 | tf_op jit(solution)/shard_map/ppermute | solution.py:659
  21.4 14.7 %collective-permute-start.5 = (f32[2,3,112,128]{3,2,1,0:T(8,128)S(1)}, f32[2,3,112,128]{3,2,1,0:T(8,128)S(1)}, u32[]{:S(2)}, u32[]{:S(2)}) collective-permute-start(f32[2,3,112,128]{3,2,1,0:T(8,128)S(1)} %get-tuple-element.39), channel_id=1, source_target_pairs={{0,3},{1,2},{2,1},{3,0},{4,7},{5,6},{6,5},{7,4},{8,11},{9,10},{10,... | collective-permute-start | bytes 1032200 | tf_op jit(solution)/shard_map/ppermute | solution.py:659
  22.0 1.5 %collective-permute-start.7 = (f32[2,232,128]{2,1,0:T(8,128)S(1)}, f32[2,232,128]{2,1,0:T(8,128)S(1)}, u32[]{:S(2)}, u32[]{:S(2)}) collective-permute-start(f32[2,232,128]{2,1,0:T(8,128)S(1)} %join_row_halos.1.refs_7_), channel_id=1, source_target_pairs={{0,1},{1,0},{2,3},{3,2},{4,5},{5,4},{6,7},{7,6},{8,9},{9,8},{10,11... | collective-permute-start | bytes 712712 | tf_op jit(solution)/shard_map/ppermute | solution.py:659
  22.1 1.8 %collective-permute-start.9 = (f32[2,232,128]{2,1,0:T(8,128)S(1)}, f32[2,232,128]{2,1,0:T(8,128)S(1)}, u32[]{:S(2)}, u32[]{:S(2)}) collective-permute-start(f32[2,232,128]{2,1,0:T(8,128)S(1)} %collective-permute-done.8.refs_11_), channel_id=1, source_target_pairs={{0,1},{1,0},{2,3},{3,2},{4,5},{5,4},{6,7},{7,6},{8,9},{9,8},{10,11... | collective-permute-start | bytes 712712 | tf_op jit(solution)/shard_map/ppermute | solution.py:659
  26.3 9.6 %collective-permute-start.11 = (f32[2,3,16,128]{3,2,1,0:T(8,128)S(1)}, f32[2,3,16,128]{3,2,1,0:T(8,128)S(1)}, u32[]{:S(2)}, u32[]{:S(2)}) collective-permute-start(f32[2,3,16,128]{3,2,1,0:T(8,128)S(1)} %get-tuple-element.44), channel_id=1, source_target_pairs={{0,2},{1,3},{2,0},{3,1},{4,6},{5,7},{6,4},{7,5},{8,10},{9,11},{10,... | collective-permute-start | bytes 147464 | tf_op jit(solution)/shard_map/ppermute | solution.py:659
  27.8 8.3 %collective-permute-start.12 = (f32[2,3,16,128]{3,2,1,0:T(8,128)S(1)}, f32[2,3,16,128]{3,2,1,0:T(8,128)S(1)}, u32[]{:S(2)}, u32[]{:S(2)}) collective-permute-start(f32[2,3,16,128]{3,2,1,0:T(8,128)S(1)} %get-tuple-element.45), channel_id=1, source_target_pairs={{0,3},{1,2},{2,1},{3,0},{4,7},{5,6},{6,5},{7,4},{8,11},{9,10},{10,... | collective-permute-start | bytes 147464 | tf_op jit(solution)/shard_map/ppermute | solution.py:659
  27.9 8.2 %collective-permute-start.10 = (f32[2,3,16,128]{3,2,1,0:T(8,128)S(1)}, f32[2,3,16,128]{3,2,1,0:T(8,128)S(1)}, u32[]{:S(2)}, u32[]{:S(2)}) collective-permute-start(f32[2,3,16,128]{3,2,1,0:T(8,128)S(1)} %get-tuple-element.43), channel_id=1, source_target_pairs={{0,1},{1,0},{2,3},{3,2},{4,5},{5,4},{6,7},{7,6},{8,9},{9,8},{10,11... | collective-permute-start | bytes 147464 | tf_op jit(solution)/shard_map/ppermute | solution.py:659

commit v9 on v8

--- a/solution.py
+++ b/solution.py
@@ -19,7 +19,7 @@
 HALO = STEPS
 LAST_COLS = (HALO, HALO, HALO - 1, HALO, HALO)
 FIRST_COLS = (HALO, HALO - 1, HALO - 1, HALO, HALO - 1)
-LAST_ROWS = (HALO, HALO - 1, HALO, HALO, HALO)
+LAST_ROWS = (HALO - 1, HALO - 1, HALO, HALO - 1, HALO - 1)
 FIRST_ROWS = (HALO, HALO - 1, HALO - 1, HALO, HALO - 1)
 
 
@@ -37,7 +37,8 @@
 LO = 8
 HI = SIDE + 24
 CHUNK = 24
-SPARE = 2
+SPARE = 3
+FIXED = TOP - HALO
 NT = 4
 GROUP = SIDE // NT
 CLOSED = 1e30
@@ -191,6 +192,14 @@
             first[at : at + count, :] = fields[f][t, :count, :]
             at, count = TILE_ROWS * t + LAST_AT[f], LAST_ROWS[f]
             last[at : at + count, :] = fields[f][t, SIDE - count :, :]
+    row = SIDE - HALO
+    level = [fields[0][:, r, :] + fields[3][:, r, :] for r in (row, row + 1)]
+    ground = jnp.maximum(fields[3][:, row, :], fields[3][:, row + 1, :])
+    drag = (GRAV * STEP_TIME) * fields[4][:, row, :] * fields[4][:, row, :]
+    flow = face(fields[2][:, row, :], level[0], level[1], ground, drag)
+    for t in range(tile_count):
+        at = TILE_ROWS * t + LAST_AT[2]
+        last[at : at + 1, :] = flow[t : t + 1, :]
     half = SIDE // 2
     columns[blocks * SIDE :, :] = jnp.where(
         lane < half, spill[:half, :], pltpu.roll(spill[half:, :], half, 1)
@@ -340,6 +349,16 @@
     return jnp.where(row < TOP, above, jnp.where(row < TOP + SIDE, middle, below))
 
 
+def fixed_row(r, rows):
+    if not r <= FIXED < r + rows:
+        return None
+    return r + lax.broadcasted_iota(jnp.int32, (rows, 1), 0) == FIXED
+
+
+def unless(where, value, other):
+    return value if where is None else jnp.where(where, other, value)
+
+
 def assemble(part, table, base, i, slot, fields, stacks, block, strip):
     halo_cols = stacks[0]
     lane = lane_index()
@@ -425,11 +444,16 @@
         open_x = (here == 1) & (pltpu.roll(here, SIDE - 1, 1) == 1)
         open_y = (here == 1) & (next_row == 1)
         z_east = pltpu.roll(z, SIDE - 1, 1)
+        fixed = fixed_row(r, rows)
         ground_x[at, :] = jnp.where(open_x, jnp.maximum(z, z_east), CLOSED)
-        ground_y[at, :] = jnp.where(open_y, jnp.maximum(z, ground[south, :]), CLOSED)
+        ground_y[at, :] = unless(
+            fixed, jnp.where(open_y, jnp.maximum(z, ground[south, :]), CLOSED), CLOSED
+        )
         flow_x[at, :] = jnp.where(open_x, flow_x[at, :], 0.0)
         flow_y[at, :] = jnp.where(open_y, flow_y[at, :], 0.0)
-        friction[at, :] = (GRAV * STEP_TIME) * friction[at, :] * friction[at, :]
+        friction[at, :] = unless(
+            fixed, (GRAV * STEP_TIME) * friction[at, :] * friction[at, :], 0.0
+        )
         level[at, :] = level[at, :] + z
 
 
@@ -451,11 +475,16 @@
         )
         open_x = row_bands(r, rows, *bands) == 1
         open_y = (row_bands(r + 1, rows, n, 1, s) == 1) & (row_bands(r, rows, n, 1, s) == 1)
+        fixed = fixed_row(r, rows)
         ground_x[i, at, :] = jnp.where(open_x, jnp.maximum(z, z_east), CLOSED)
-        ground_y[i, at, :] = jnp.where(open_y, jnp.maximum(z, ground[i, south, :]), CLOSED)
+        ground_y[i, at, :] = unless(
+            fixed, jnp.where(open_y, jnp.maximum(z, ground[i, south, :]), CLOSED), CLOSED
+        )
         flow_x[i, at, :] = jnp.where(open_x, flow_x[i, at, :], 0.0)
         flow_y[i, at, :] = jnp.where(open_y, flow_y[i, at, :], 0.0)
-        friction[i, at, :] = (GRAV * STEP_TIME) * friction[i, at, :] * friction[i, at, :]
+        friction[i, at, :] = unless(
+            fixed, (GRAV * STEP_TIME) * friction[i, at, :] * friction[i, at, :], 0.0
+        )
         level[i, at, :] = level[i, at, :] + z
 
 
@@ -517,6 +546,7 @@
             if n:
                 for side in range(2):
                     for t in range(fields[0].shape[0]):
+                        stacks[1][k, side, t, :SPARE, :] = jnp.zeros((SPARE, SIDE), jnp.float32)
                         stacks[1][k, side, t, SPARE : SPARE + TILE_ROWS, :] = halos[kinds * k + 1][
                             side, TILE_ROWS * t : TILE_ROWS * (t + 1), :
                         ]
@@ -565,7 +595,7 @@
                 )
         return carry
 
-    lax.fori_loop(0, STEPS, step, 0)
+    lax.fori_loop(0, STEPS, step, 0, unroll=True)
 
     results = (level, flow_x, flow_y)
     for i in range(part.tiles):
@@ -621,7 +651,7 @@
     tile_count = fields[0].shape[0]
     stacks = [VMEM((lanes, -(-tile_count * TILE_LANES // SIDE), SIDE, SIDE), jnp.float32)]
     if part.halo_rows:
-        stacks.append(VMEM((lanes, 2, tile_count, SPARE + TILE_ROWS + 1, SIDE), jnp.float32))
+        stacks.append(VMEM((lanes, 2, tile_count, SPARE + TILE_ROWS + 10, SIDE), jnp.float32))
     block = VMEM((part.tiles, ROWS, SIDE), jnp.float32)
     strip = VMEM((ROWS, SIDE), jnp.float32)
     cells = (part.tiles + 1) * sum(count for _, count in part.computed) * SIDE * STEPS

time: 37.4 us -> 37.3 us (level)
  waiting for transfers between devices: 4.34 us -> 5.3 us
  Pallas kernels: 20.3 us -> 19.4 us
    pallas_call x4, Pallas kernels: 15.3 us -> 14.3 us  [advance(): pl.pallas_call(functools.partial(advance_kernel, part, lanes, units, len(...]
    ppermute x12, waiting for transfers between devices: 3.24 us -> 4.29 us  [shift_lanes(): return lax.ppermute(array, ('col', 'sub'), pairs)]
  transfers between devices with their start and end apart: 14 -> 14, of which waited for: 6 -> 7; matrix products, arithmetic and copies ran while one was open for 0% -> 0% of each run, Pallas kernels for 46% -> 43%
where the time goes in v9:
time: 37.3 us; the launch traced here: 37.2 us
  Pallas kernels  19.4 us (52%)
  starting transfers between devices  11.6 us (31%)
  waiting for transfers between devices  5.3 us (14%)
  between operations  0.87 us (2%)
    pallas_call x4, Pallas kernels, advance(): pl.pallas_call(functools.partial(advance_kernel, part, lanes, units, len(...  14.3 us
    ppermute x12, starting transfers between devices, shift_lanes(): return lax.ppermute(array, ('col', 'sub'), pairs)  10 us
    ppermute x12, waiting for transfers between devices, shift_lanes(): return lax.ppermute(array, ('col', 'sub'), pairs)  4.29 us
    pallas_call x1, Pallas kernels, load(): pl.pallas_call(load_kernel, name='load_and_pack', out_shape=tuple(outs),...  2.22 us
    pallas_call x1, Pallas kernels, make_table(): pl.pallas_call(functools.partial(index_kernel, shape), name='index_table'...  1.64 us
    ppermute x2, starting transfers between devices, meet_rows(): return lax.ppermute(array, ('row', 'sub'), pairs)  1.58 us
    pallas_call x1, Pallas kernels, place(): pl.pallas_call(functools.partial(place_kernel, groups), name='place_arriv...  1.22 us
    ppermute x2, waiting for transfers between devices, meet_rows(): return lax.ppermute(array, ('row', 'sub'), pairs)  1.01 us
  transfers between devices with their start and end apart: 14, of which 7 were waited for; matrix products, arithmetic and copies ran while one was open for 0% of the time, Pallas kernels for 43%

profile of v9, /device:TPU:0, one launch (start us, length us, event | category | flops | bytes accessed | tf_op | source)
XLA Modules:
  0.0 37.2 jit_solution(15037519104506780796)
XLA Ops:
  0.6 2.2 %load_and_pack.1 = (f32[8,128,128]{2,1,0:T(8,128)S(1)}, f32[8,128,128]{2,1,0:T(8,128)S(1)}, f32[8,128,128]{2,1,0:T(8,128)S(1)}, f32[8,128,128]{2,1,0:T(8,128)S(1...) custom-call(f32[8,128,128]{2,1,0:T(8,128)} %refs_0_.1, ...), custom_call_target="tpu_custom_call" | custom-call | tf_op jit(solution)/shard_map/load_and_pack/pallas_call | solution.py:216
  2.9 3.0 %collective-permute-start = (f32[448,128]{1,0:T(8,128)S(1)}, f32[448,128]{1,0:T(8,128)S(1)}, u32[]{:S(2)}, u32[]{:S(2)}) collective-permute-start(f32[448,128]{1,0:T(8,128)S(1)} %get-tuple-element.27.refs_6_), channel_id=1, source_target_pairs={{0,2},{1,3},{2,0},{3,1},{4,6},{5,7},{6,4},{7,5},{8,10},{9,11},{10,... | collective-permute-start | bytes 688136 | tf_op jit(solution)/shard_map/ppermute | solution.py:689
  5.9 0.0 copy-start
  5.9 0.0 copy-start.1
  5.9 0.0 copy-start.2
  5.9 1.6 %collective-permute-start.1 = (f32[216,128]{1,0:T(8,128)S(1)}, f32[216,128]{1,0:T(8,128)S(1)}, u32[]{:S(2)}, u32[]{:S(2)}) collective-permute-start(f32[216,128]{1,0:T(8,128)S(1)} %get-tuple-element.28), channel_id=1, source_target_pairs={{0,4},{1,5},{4,0},{5,1},{8,12},{9,13},{12,8},{13,9},{2,6},{3,7},{6... | collective-permute-start | bytes 331784 | tf_op jit(solution)/shard_map/ppermute | solution.py:713
  7.5 0.0 collective-permute-start.2
  7.5 0.5 %collective-permute-start.3 = (f32[448,128]{1,0:T(8,128)S(1)}, f32[448,128]{1,0:T(8,128)S(1)}, u32[]{:S(2)}, u32[]{:S(2)}) collective-permute-start(f32[448,128]{1,0:T(8,128)S(1)} %get-tuple-element.27.refs_6_), channel_id=1, source_target_pairs={{0,1},{1,0},{2,3},{3,2},{4,5},{5,4},{6,7},{7,6},{8,9},{9,8},{10,11... | collective-permute-start | bytes 688136 | tf_op jit(solution)/shard_map/ppermute | solution.py:689
  8.0 0.0 copy-done
  8.0 0.0 copy-done.1
  8.0 0.0 copy-done.2
  8.0 1.6 %index_table.1.refs_0_ = s32[265]{0:T(512)S(4)} custom-call(s32[128]{0:T(128)S(1)} %copy-done, s32[128]{0:T(128)S(1)} %copy-done.1, s32[128]{0:T(128)S(1)} %copy-done.2), custom_call_target="tpu_custom_call" | custom-call | tf_op jit(solution)/shard_map/index_table/pallas_call | solution.py:143
  9.6 1.0 %collective-permute-done.1.met_even = f32[216,128]{1,0:T(8,128)S(1)} collective-permute-done((f32[216,128]{1,0:T(8,128)S(1)}, f32[216,128]{1,0:T(8,128)S(1)}, u32[]{:S(2)}, u32[]{:S(2)}) %collective-permute-start.1) | collective-permute-done | bytes 110624 | tf_op jit(solution)/shard_map/ppermute | solution.py:713
  10.6 0.0 collective-permute-done.2.met_odd
  10.7 0.8 %collective-permute-done.refs_8_.refs_10_ = f32[448,128]{1,0:T(8,128)S(1)} collective-permute-done((f32[448,128]{1,0:T(8,128)S(1)}, f32[448,128]{1,0:T(8,128)S(1)}, u32[]{:S(2)}, u32[]{:S(2)}) %collective-permute-start) | collective-permute-done | bytes 229408 | tf_op jit(solution)/shard_map/ppermute | solution.py:689
  11.5 0.0 collective-permute-start.4
  11.5 1.7 %collective-permute-start.8 = (f32[2,216,128]{2,1,0:T(8,128)S(1)}, f32[2,216,128]{2,1,0:T(8,128)S(1)}, u32[]{:S(2)}, u32[]{:S(2)}) collective-permute-start(f32[2,216,128]{2,1,0:T(8,128)S(1)} %join_row_halos.1.refs_7_), channel_id=1, source_target_pairs={{0,2},{1,3},{2,0},{3,1},{4,6},{5,7},{6,4},{7,5},{8,10},{9,11},{10,... | collective-permute-start | bytes 663560 | tf_op jit(solution)/shard_map/ppermute | solution.py:689
  13.2 0.0 collective-permute-done.3.refs_7_.refs_8_
  13.2 0.0 collective-permute-done.4.refs_9_.refs_12_
  13.2 2.7 %advance_leaving_first.1 = (f32[2,3,112,128]{3,2,1,0:T(8,128)S(1)}, f32[2,3,112,128]{3,2,1,0:T(8,128)S(1)}, f32[2,3,112,128]{3,2,1,0:T(8,128)S(1)}) custom-call(s32[265]{0:T(512)S(4)} %index_table.1.refs_0_, f32[8,128,128]{2,1,0:T(8,128)S(1)} %get-tuple-element.31.refs_1_, f32[8,128,128]{2,1,0:T(8,128)S(1)} %get-tuple-element.32.refs_2_, ...), custom_call_target="tpu_custom_call" | custom-call | flops 17694720 | bytes 917504 | tf_op jit(solution)/shard_map/advance_leaving_first/pallas_call | solution.py:658
  15.9 1.5 %collective-permute-start.6 = (f32[2,3,112,128]{3,2,1,0:T(8,128)S(1)}, f32[2,3,112,128]{3,2,1,0:T(8,128)S(1)}, u32[]{:S(2)}, u32[]{:S(2)}) collective-permute-start(f32[2,3,112,128]{3,2,1,0:T(8,128)S(1)} %get-tuple-element.40), channel_id=1, source_target_pairs={{0,2},{1,3},{2,0},{3,1},{4,6},{5,7},{6,4},{7,5},{8,10},{9,11},{10,... | collective-permute-start | bytes 1032200 | tf_op jit(solution)/shard_map/ppermute | solution.py:689
  17.5 2.7 %advance_leaving_second.1 = (f32[2,3,112,128]{3,2,1,0:T(8,128)S(1)}, f32[2,3,112,128]{3,2,1,0:T(8,128)S(1)}) custom-call(s32[265]{0:T(512)S(4)} %index_table.1.refs_0_, f32[8,128,128]{2,1,0:T(8,128)S(1)} %get-tuple-element.31.refs_1_, f32[8,128,128]{2,1,0:T(8,128)S(1)} %get-tuple-element.32.refs_2_, ...), custom_call_target="tpu_custom_call", output_to_operand_aliasing={{0}: (10, {}), {1}: (11, {})} | custom-call | flops 17694720 | bytes 917504 | tf_op jit(solution)/shard_map/advance_leaving_second/pallas_call | solution.py:658
  20.2 0.1 collective-permute-start.13
  20.3 0.7 %collective-permute-start.5 = (f32[2,3,112,128]{3,2,1,0:T(8,128)S(1)}, f32[2,3,112,128]{3,2,1,0:T(8,128)S(1)}, u32[]{:S(2)}, u32[]{:S(2)}) collective-permute-start(f32[2,3,112,128]{3,2,1,0:T(8,128)S(1)} %get-tuple-element.39), channel_id=1, source_target_pairs={{0,3},{1,2},{2,1},{3,0},{4,7},{5,6},{6,5},{7,4},{8,11},{9,10},{10,... | collective-permute-start | bytes 1032200 | tf_op jit(solution)/shard_map/ppermute | solution.py:689
  21.0 0.1 collective-permute-start.7
  21.1 0.0 collective-permute-done.8.refs_11_
  21.1 0.4 %collective-permute-start.9 = (f32[2,216,128]{2,1,0:T(8,128)S(1)}, f32[2,216,128]{2,1,0:T(8,128)S(1)}, u32[]{:S(2)}, u32[]{:S(2)}) collective-permute-start(f32[2,216,128]{2,1,0:T(8,128)S(1)} %collective-permute-done.8.refs_11_), channel_id=1, source_target_pairs={{0,1},{1,0},{2,3},{3,2},{4,5},{5,4},{6,7},{7,6},{8,9},{9,8},{10,11... | collective-permute-start | bytes 663560 | tf_op jit(solution)/shard_map/ppermute | solution.py:689
  21.5 1.0 %collective-permute-done.7.refs_9_ = f32[2,216,128]{2,1,0:T(8,128)S(1)} collective-permute-done((f32[2,216,128]{2,1,0:T(8,128)S(1)}, f32[2,216,128]{2,1,0:T(8,128)S(1)}, u32[]{:S(2)}, u32[]{:S(2)}) %collective-permute-start.7) | collective-permute-done | bytes 221216 | tf_op jit(solution)/shard_map/ppermute | solution.py:689
  22.5 0.3 collective-permute-done.9.refs_13_
  22.8 2.4 %advance_leaving_edges.1 = (f32[2,3,16,128]{3,2,1,0:T(8,128)S(1)}, f32[2,3,16,128]{3,2,1,0:T(8,128)S(1)}, f32[2,3,16,128]{3,2,1,0:T(8,128)S(1)}) custom-call(s32[265]{0:T(512)S(4)} %index_table.1.refs_0_, f32[8,128,128]{2,1,0:T(8,128)S(1)} %get-tuple-element.31.refs_1_, f32[8,128,128]{2,1,0:T(8,128)S(1)} %get-tuple-element.32.refs_2_, ...), custom_call_target="tpu_custom_call" | custom-call | flops 11059200 | bytes 262144 | tf_op jit(solution)/shard_map/advance_leaving_edges/pallas_call | solution.py:658
  25.2 1.5 %collective-permute-start.11 = (f32[2,3,16,128]{3,2,1,0:T(8,128)S(1)}, f32[2,3,16,128]{3,2,1,0:T(8,128)S(1)}, u32[]{:S(2)}, u32[]{:S(2)}) collective-permute-start(f32[2,3,16,128]{3,2,1,0:T(8,128)S(1)} %get-tuple-element.44), channel_id=1, source_target_pairs={{0,2},{1,3},{2,0},{3,1},{4,6},{5,7},{6,4},{7,5},{8,10},{9,11},{10,... | collective-permute-start | bytes 147464 | tf_op jit(solution)/shard_map/ppermute | solution.py:689
  26.8 0.1 collective-permute-start.12
  26.8 0.2 collective-permute-done.6.refs_15_
  27.1 0.4 collective-permute-start.10
  27.4 0.0 collective-permute-done.13.refs_14_
  27.4 6.4 %advance_staying.1 = (f32[8,128,128]{2,1,0:T(8,128)}, f32[8,128,128]{2,1,0:T(8,128)}, f32[8,128,128]{2,1,0:T(8,128)}) custom-call(s32[265]{0:T(512)S(4)} %index_table.1.refs_0_, f32[8,128,128]{2,1,0:T(8,128)S(1)} %get-tuple-element.31.refs_1_, f32[8,128,128]{2,1,0:T(8,128)S(1)} %get-tuple-element.32.refs_2_, f32[8,128,128]{2,1,0:T(8,128)S(1)} %get-tuple-element.33.refs_3_, ...), custom_call_target="tpu_custom_call" | custom-call | flops 33177600 | bytes 2097152 | tf_op jit(solution)/shard_map/advance_staying/pallas_call | solution.py:658
  33.8 1.7 %collective-permute-done.11.refs_3_ = f32[2,3,16,128]{3,2,1,0:T(8,128)S(1)} collective-permute-done((f32[2,3,16,128]{3,2,1,0:T(8,128)S(1)}, f32[2,3,16,128]{3,2,1,0:T(8,128)S(1)}, u32[]{:S(2)}, u32[]{:S(2)}) %collective-permute-start.11) | collective-permute-done | bytes 49184 | tf_op jit(solution)/shard_map/ppermute | solution.py:689
  35.5 0.3 collective-permute-done.12.refs_4_
  35.8 0.0 collective-permute-done.5.refs_1_
  35.8 0.0 collective-permute-done.10.refs_2_
  35.8 1.2 %place_arrivals.1 = (f32[8,128,128]{2,1,0:T(8,128)}, f32[8,128,128]{2,1,0:T(8,128)}, f32[8,128,128]{2,1,0:T(8,128)}) custom-call(s32[265]{0:T(512)S(4)} %index_table.1.refs_0_, f32[2,3,112,128]{3,2,1,0:T(8,128)S(1)} %collective-permute-done.5.refs_1_, ...), custom_call_target="tpu_custom_call", output_to_operand_aliasing={{0}: (5, {}), {1}: (6, {}), {2}: (7, {})} | custom-call | tf_op jit(solution)/shard_map/place_arrivals/pallas_call | solution.py:287
  (1 shorter events, 0.0 us)
Async XLA Ops:
  2.9 8.6 %collective-permute-start = (f32[448,128]{1,0:T(8,128)S(1)}, f32[448,128]{1,0:T(8,128)S(1)}, u32[]{:S(2)}, u32[]{:S(2)}) collective-permute-start(f32[448,128]{1,0:T(8,128)S(1)} %get-tuple-element.27.refs_6_), channel_id=1, source_target_pairs={{0,2},{1,3},{2,0},{3,1},{4,6},{5,7},{6,4},{7,5},{8,10},{9,11},{10,... | collective-permute-start | bytes 688136 | tf_op jit(solution)/shard_map/ppermute | solution.py:689
  5.9 2.1 %copy-start = (s32[128]{0:T(128)S(1)}, s32[128]{0:T(128)}, u32[]{:S(2)}) copy-start(s32[128]{0:T(128)} %before_ref.1) | copy-start | bytes 1540
  5.9 2.1 %copy-start.1 = (s32[128]{0:T(128)S(1)}, s32[128]{0:T(128)}, u32[]{:S(2)}) copy-start(s32[128]{0:T(128)} %after_ref.1) | copy-start | bytes 1540
  5.9 2.1 %copy-start.2 = (s32[128]{0:T(128)S(1)}, s32[128]{0:T(128)}, u32[]{:S(2)}) copy-start(s32[128]{0:T(128)} %wet_ref.1) | copy-start | bytes 1540
  5.9 4.7 %collective-permute-start.1 = (f32[216,128]{1,0:T(8,128)S(1)}, f32[216,128]{1,0:T(8,128)S(1)}, u32[]{:S(2)}, u32[]{:S(2)}) collective-permute-start(f32[216,128]{1,0:T(8,128)S(1)} %get-tuple-element.28), channel_id=1, source_target_pairs={{0,4},{1,5},{4,0},{5,1},{8,12},{9,13},{12,8},{13,9},{2,6},{3,7},{6... | collective-permute-start | bytes 331784 | tf_op jit(solution)/shard_map/ppermute | solution.py:713
  7.5 3.2 %collective-permute-start.2 = (f32[216,128]{1,0:T(8,128)S(1)}, f32[216,128]{1,0:T(8,128)S(1)}, u32[]{:S(2)}, u32[]{:S(2)}) collective-permute-start(f32[216,128]{1,0:T(8,128)S(1)} %get-tuple-element.29), channel_id=1, source_target_pairs={{0,1},{1,0},{4,8},{5,9},{8,4},{9,5},{12,13},{13,12},{2,3},{3,2},{6... | collective-permute-start | bytes 331784 | tf_op jit(solution)/shard_map/ppermute | solution.py:713
  7.5 5.8 %collective-permute-start.3 = (f32[448,128]{1,0:T(8,128)S(1)}, f32[448,128]{1,0:T(8,128)S(1)}, u32[]{:S(2)}, u32[]{:S(2)}) collective-permute-start(f32[448,128]{1,0:T(8,128)S(1)} %get-tuple-element.27.refs_6_), channel_id=1, source_target_pairs={{0,1},{1,0},{2,3},{3,2},{4,5},{5,4},{6,7},{7,6},{8,9},{9,8},{10,11... | collective-permute-start | bytes 688136 | tf_op jit(solution)/shard_map/ppermute | solution.py:689
  11.5 1.8 %collective-permute-start.4 = (f32[448,128]{1,0:T(8,128)S(1)}, f32[448,128]{1,0:T(8,128)S(1)}, u32[]{:S(2)}, u32[]{:S(2)}) collective-permute-start(f32[448,128]{1,0:T(8,128)S(1)} %collective-permute-done.refs_8_.refs_10_), channel_id=1, source_target_pairs={{0,1},{1,0},{2,3},{3,2},{4,5},{5,4},{6,7},{7,6},{8,9},{9,8},{10,11... | collective-permute-start | bytes 688136 | tf_op jit(solution)/shard_map/ppermute | solution.py:689
  11.5 9.6 %collective-permute-start.8 = (f32[2,216,128]{2,1,0:T(8,128)S(1)}, f32[2,216,128]{2,1,0:T(8,128)S(1)}, u32[]{:S(2)}, u32[]{:S(2)}) collective-permute-start(f32[2,216,128]{2,1,0:T(8,128)S(1)} %join_row_halos.1.refs_7_), channel_id=1, source_target_pairs={{0,2},{1,3},{2,0},{3,1},{4,6},{5,7},{6,4},{7,5},{8,10},{9,11},{10,... | collective-permute-start | bytes 663560 | tf_op jit(solution)/shard_map/ppermute | solution.py:689
  15.9 11.1 %collective-permute-start.6 = (f32[2,3,112,128]{3,2,1,0:T(8,128)S(1)}, f32[2,3,112,128]{3,2,1,0:T(8,128)S(1)}, u32[]{:S(2)}, u32[]{:S(2)}) collective-permute-start(f32[2,3,112,128]{3,2,1,0:T(8,128)S(1)} %get-tuple-element.40), channel_id=1, source_target_pairs={{0,2},{1,3},{2,0},{3,1},{4,6},{5,7},{6,4},{7,5},{8,10},{9,11},{10,... | collective-permute-start | bytes 1032200 | tf_op jit(solution)/shard_map/ppermute | solution.py:689
  20.2 7.2 %collective-permute-start.13 = (f32[2,3,112,128]{3,2,1,0:T(8,128)S(1)}, f32[2,3,112,128]{3,2,1,0:T(8,128)S(1)}, u32[]{:S(2)}, u32[]{:S(2)}) collective-permute-start(f32[2,3,112,128]{3,2,1,0:T(8,128)S(1)} %get-tuple-element.46), channel_id=1, source_target_pairs={{0,1},{1,0},{2,3},{3,2},{4,5},{5,4},{6,7},{7,6},{8,9},{9,8},{10,11... | collective-permute-start | bytes 1032200 | tf_op jit(solution)/shard_map/ppermute | solution.py:689
  20.3 15.5 %collective-permute-start.5 = (f32[2,3,112,128]{3,2,1,0:T(8,128)S(1)}, f32[2,3,112,128]{3,2,1,0:T(8,128)S(1)}, u32[]{:S(2)}, u32[]{:S(2)}) collective-permute-start(f32[2,3,112,128]{3,2,1,0:T(8,128)S(1)} %get-tuple-element.39), channel_id=1, source_target_pairs={{0,3},{1,2},{2,1},{3,0},{4,7},{5,6},{6,5},{7,4},{8,11},{9,10},{10,... | collective-permute-start | bytes 1032200 | tf_op jit(solution)/shard_map/ppermute | solution.py:689
  21.0 1.5 %collective-permute-start.7 = (f32[2,216,128]{2,1,0:T(8,128)S(1)}, f32[2,216,128]{2,1,0:T(8,128)S(1)}, u32[]{:S(2)}, u32[]{:S(2)}) collective-permute-start(f32[2,216,128]{2,1,0:T(8,128)S(1)} %join_row_halos.1.refs_7_), channel_id=1, source_target_pairs={{0,1},{1,0},{2,3},{3,2},{4,5},{5,4},{6,7},{7,6},{8,9},{9,8},{10,11... | collective-permute-start | bytes 663560 | tf_op jit(solution)/shard_map/ppermute | solution.py:689
  21.1 1.7 %collective-permute-start.9 = (f32[2,216,128]{2,1,0:T(8,128)S(1)}, f32[2,216,128]{2,1,0:T(8,128)S(1)}, u32[]{:S(2)}, u32[]{:S(2)}) collective-permute-start(f32[2,216,128]{2,1,0:T(8,128)S(1)} %collective-permute-done.8.refs_11_), channel_id=1, source_target_pairs={{0,1},{1,0},{2,3},{3,2},{4,5},{5,4},{6,7},{7,6},{8,9},{9,8},{10,11... | collective-permute-start | bytes 663560 | tf_op jit(solution)/shard_map/ppermute | solution.py:689
  25.2 10.3 %collective-permute-start.11 = (f32[2,3,16,128]{3,2,1,0:T(8,128)S(1)}, f32[2,3,16,128]{3,2,1,0:T(8,128)S(1)}, u32[]{:S(2)}, u32[]{:S(2)}) collective-permute-start(f32[2,3,16,128]{3,2,1,0:T(8,128)S(1)} %get-tuple-element.44), channel_id=1, source_target_pairs={{0,2},{1,3},{2,0},{3,1},{4,6},{5,7},{6,4},{7,5},{8,10},{9,11},{10,... | collective-permute-start | bytes 147464 | tf_op jit(solution)/shard_map/ppermute | solution.py:689
  26.8 9.0 %collective-permute-start.12 = (f32[2,3,16,128]{3,2,1,0:T(8,128)S(1)}, f32[2,3,16,128]{3,2,1,0:T(8,128)S(1)}, u32[]{:S(2)}, u32[]{:S(2)}) collective-permute-start(f32[2,3,16,128]{3,2,1,0:T(8,128)S(1)} %get-tuple-element.45), channel_id=1, source_target_pairs={{0,3},{1,2},{2,1},{3,0},{4,7},{5,6},{6,5},{7,4},{8,11},{9,10},{10,... | collective-permute-start | bytes 147464 | tf_op jit(solution)/shard_map/ppermute | solution.py:689
  27.1 8.7 %collective-permute-start.10 = (f32[2,3,16,128]{3,2,1,0:T(8,128)S(1)}, f32[2,3,16,128]{3,2,1,0:T(8,128)S(1)}, u32[]{:S(2)}, u32[]{:S(2)}) collective-permute-start(f32[2,3,16,128]{3,2,1,0:T(8,128)S(1)} %get-tuple-element.43), channel_id=1, source_target_pairs={{0,1},{1,0},{2,3},{3,2},{4,5},{5,4},{6,7},{7,6},{8,9},{9,8},{10,11... | collective-permute-start | bytes 147464 | tf_op jit(solution)/shard_map/ppermute | solution.py:689

commit v10 on v9

--- a/solution.py
+++ b/solution.py
@@ -753,8 +753,12 @@
     soon = tuple(range(1, subs)) + (ahead,)
     last = tuple(k for k in units if k not in soon)
     outs = advance(WHOLE, table, fields, halos, soon, [middle[k] for k in soon])
-    groups = tuple((k, (MIDDLE,)) for k in last) + tuple((k, LATE.sent) for k in units)
-    return place(groups, table, [middle[k] for k in last] + edges, outs)
+    near = [n for n, k in enumerate(units) if k < subs]
+    far = [n for n, k in enumerate(units) if k >= subs]
+    groups = tuple((k, (MIDDLE,)) for k in last) + tuple((units[n], LATE.sent) for n in near)
+    outs = place(groups, table, [middle[k] for k in last] + [edges[n] for n in near], outs)
+    groups = tuple((units[n], LATE.sent) for n in far)
+    return place(groups, table, [edges[n] for n in far], outs)
 
 
 def solution(mesh):

time: 37.3 us -> 37.5 us (level)
  Pallas kernels: 19.4 us -> 20 us
    pallas_call x1 -> x2, Pallas kernels: 1.22 us -> 1.84 us  [place(): pl.pallas_call(functools.partial(place_kernel, groups), name='place_arriv...]
  transfers between devices with their start and end apart: 14 -> 14, of which waited for: 7 -> 5; matrix products, arithmetic and copies ran while one was open for 0% -> 0% of each run, Pallas kernels for 43% -> 45%
where the time goes in v10:
time: 37.5 us; the launch traced here: 37.4 us
  Pallas kernels  20 us (53%)
  starting transfers between devices  11.5 us (31%)
  waiting for transfers between devices  4.98 us (13%)
  between operations  0.91 us (2%)
    pallas_call x4, Pallas kernels, advance(): pl.pallas_call(functools.partial(advance_kernel, part, lanes, units, len(...  14.2 us
    ppermute x12, starting transfers between devices, shift_lanes(): return lax.ppermute(array, ('col', 'sub'), pairs)  9.93 us
    ppermute x12, waiting for transfers between devices, shift_lanes(): return lax.ppermute(array, ('col', 'sub'), pairs)  3.98 us
    pallas_call x1, Pallas kernels, load(): pl.pallas_call(load_kernel, name='load_and_pack', out_shape=tuple(outs),...  2.22 us
    pallas_call x2, Pallas kernels, place(): pl.pallas_call(functools.partial(place_kernel, groups), name='place_arriv...  1.84 us
    pallas_call x1, Pallas kernels, make_table(): pl.pallas_call(functools.partial(index_kernel, shape), name='index_table'...  1.64 us
    ppermute x2, starting transfers between devices, meet_rows(): return lax.ppermute(array, ('row', 'sub'), pairs)  1.58 us
    ppermute x2, waiting for transfers between devices, meet_rows(): return lax.ppermute(array, ('row', 'sub'), pairs)  1.01 us
  transfers between devices with their start and end apart: 14, of which 5 were waited for; matrix products, arithmetic and copies ran while one was open for 0% of the time, Pallas kernels for 45%

profile of v10, /device:TPU:0, one launch (start us, length us, event | category | flops | bytes accessed | tf_op | source)
XLA Modules:
  0.0 37.4 jit_solution(3145877502455467897)
XLA Ops:
  0.6 2.2 %load_and_pack.1 = (f32[8,128,128]{2,1,0:T(8,128)S(1)}, f32[8,128,128]{2,1,0:T(8,128)S(1)}, f32[8,128,128]{2,1,0:T(8,128)S(1)}, f32[8,128,128]{2,1,0:T(8,128)S(1...) custom-call(f32[8,128,128]{2,1,0:T(8,128)} %refs_0_.1, ...), custom_call_target="tpu_custom_call" | custom-call | tf_op jit(solution)/shard_map/load_and_pack/pallas_call | solution.py:216
  2.9 3.0 %collective-permute-start = (f32[448,128]{1,0:T(8,128)S(1)}, f32[448,128]{1,0:T(8,128)S(1)}, u32[]{:S(2)}, u32[]{:S(2)}) collective-permute-start(f32[448,128]{1,0:T(8,128)S(1)} %get-tuple-element.30.refs_6_), channel_id=1, source_target_pairs={{0,2},{1,3},{2,0},{3,1},{4,6},{5,7},{6,4},{7,5},{8,10},{9,11},{10,... | collective-permute-start | bytes 688136 | tf_op jit(solution)/shard_map/ppermute | solution.py:689
  5.9 0.0 copy-start
  5.9 0.0 copy-start.1
  5.9 0.0 copy-start.2
  5.9 1.6 %collective-permute-start.1 = (f32[216,128]{1,0:T(8,128)S(1)}, f32[216,128]{1,0:T(8,128)S(1)}, u32[]{:S(2)}, u32[]{:S(2)}) collective-permute-start(f32[216,128]{1,0:T(8,128)S(1)} %get-tuple-element.31), channel_id=1, source_target_pairs={{0,4},{1,5},{4,0},{5,1},{8,12},{9,13},{12,8},{13,9},{2,6},{3,7},{6... | collective-permute-start | bytes 331784 | tf_op jit(solution)/shard_map/ppermute | solution.py:713
  7.5 0.0 collective-permute-start.2
  7.5 0.5 %collective-permute-start.3 = (f32[448,128]{1,0:T(8,128)S(1)}, f32[448,128]{1,0:T(8,128)S(1)}, u32[]{:S(2)}, u32[]{:S(2)}) collective-permute-start(f32[448,128]{1,0:T(8,128)S(1)} %get-tuple-element.30.refs_6_), channel_id=1, source_target_pairs={{0,1},{1,0},{2,3},{3,2},{4,5},{5,4},{6,7},{7,6},{8,9},{9,8},{10,11... | collective-permute-start | bytes 688136 | tf_op jit(solution)/shard_map/ppermute | solution.py:689
  8.0 0.0 copy-done
  8.0 0.0 copy-done.1
  8.0 0.0 copy-done.2
  8.0 1.6 %index_table.1.refs_0_ = s32[265]{0:T(512)S(4)} custom-call(s32[128]{0:T(128)S(1)} %copy-done, s32[128]{0:T(128)S(1)} %copy-done.1, s32[128]{0:T(128)S(1)} %copy-done.2), custom_call_target="tpu_custom_call" | custom-call | tf_op jit(solution)/shard_map/index_table/pallas_call | solution.py:143
  9.6 1.0 %collective-permute-done.1.met_even = f32[216,128]{1,0:T(8,128)S(1)} collective-permute-done((f32[216,128]{1,0:T(8,128)S(1)}, f32[216,128]{1,0:T(8,128)S(1)}, u32[]{:S(2)}, u32[]{:S(2)}) %collective-permute-start.1) | collective-permute-done | bytes 110624 | tf_op jit(solution)/shard_map/ppermute | solution.py:713
  10.6 0.0 collective-permute-done.2.met_odd
  10.7 0.8 %collective-permute-done.refs_10_.refs_8_ = f32[448,128]{1,0:T(8,128)S(1)} collective-permute-done((f32[448,128]{1,0:T(8,128)S(1)}, f32[448,128]{1,0:T(8,128)S(1)}, u32[]{:S(2)}, u32[]{:S(2)}) %collective-permute-start) | collective-permute-done | bytes 229408 | tf_op jit(solution)/shard_map/ppermute | solution.py:689
  11.5 0.0 collective-permute-start.6
  11.5 1.7 %collective-permute-start.5 = (f32[2,216,128]{2,1,0:T(8,128)S(1)}, f32[2,216,128]{2,1,0:T(8,128)S(1)}, u32[]{:S(2)}, u32[]{:S(2)}) collective-permute-start(f32[2,216,128]{2,1,0:T(8,128)S(1)} %join_row_halos.1.refs_7_), channel_id=1, source_target_pairs={{0,2},{1,3},{2,0},{3,1},{4,6},{5,7},{6,4},{7,5},{8,10},{9,11},{10,... | collective-permute-start | bytes 663560 | tf_op jit(solution)/shard_map/ppermute | solution.py:689
  13.2 0.0 collective-permute-done.3.refs_8_.refs_7_
  13.2 0.0 collective-permute-done.6.refs_12_.refs_9_
  13.2 2.7 %advance_leaving_first.1 = (f32[2,3,112,128]{3,2,1,0:T(8,128)S(1)}, f32[2,3,112,128]{3,2,1,0:T(8,128)S(1)}, f32[2,3,112,128]{3,2,1,0:T(8,128)S(1)}) custom-call(s32[265]{0:T(512)S(4)} %index_table.1.refs_0_, f32[8,128,128]{2,1,0:T(8,128)S(1)} %get-tuple-element.34.refs_1_, f32[8,128,128]{2,1,0:T(8,128)S(1)} %get-tuple-element.35.refs_2_, ...), custom_call_target="tpu_custom_call" | custom-call | flops 17694720 | bytes 917504 | tf_op jit(solution)/shard_map/advance_leaving_first/pallas_call | solution.py:658
  15.9 1.6 %collective-permute-start.11 = (f32[2,3,112,128]{3,2,1,0:T(8,128)S(1)}, f32[2,3,112,128]{3,2,1,0:T(8,128)S(1)}, u32[]{:S(2)}, u32[]{:S(2)}) collective-permute-start(f32[2,3,112,128]{3,2,1,0:T(8,128)S(1)} %get-tuple-element.46), channel_id=1, source_target_pairs={{0,2},{1,3},{2,0},{3,1},{4,6},{5,7},{6,4},{7,5},{8,10},{9,11},{10,... | collective-permute-start | bytes 1032200 | tf_op jit(solution)/shard_map/ppermute | solution.py:689
  17.5 2.7 %advance_leaving_second.1 = (f32[2,3,112,128]{3,2,1,0:T(8,128)S(1)}, f32[2,3,112,128]{3,2,1,0:T(8,128)S(1)}) custom-call(s32[265]{0:T(512)S(4)} %index_table.1.refs_0_, f32[8,128,128]{2,1,0:T(8,128)S(1)} %get-tuple-element.34.refs_1_, f32[8,128,128]{2,1,0:T(8,128)S(1)} %get-tuple-element.35.refs_2_, ...), custom_call_target="tpu_custom_call", output_to_operand_aliasing={{0}: (10, {}), {1}: (11, {})} | custom-call | flops 17694720 | bytes 917504 | tf_op jit(solution)/shard_map/advance_leaving_second/pallas_call | solution.py:658
  20.2 0.1 collective-permute-start.13
  20.3 0.7 %collective-permute-start.10 = (f32[2,3,112,128]{3,2,1,0:T(8,128)S(1)}, f32[2,3,112,128]{3,2,1,0:T(8,128)S(1)}, u32[]{:S(2)}, u32[]{:S(2)}) collective-permute-start(f32[2,3,112,128]{3,2,1,0:T(8,128)S(1)} %get-tuple-element.45), channel_id=1, source_target_pairs={{0,3},{1,2},{2,1},{3,0},{4,7},{5,6},{6,5},{7,4},{8,11},{9,10},{10,... | collective-permute-start | bytes 1032200 | tf_op jit(solution)/shard_map/ppermute | solution.py:689
  21.0 0.1 collective-permute-start.4
  21.0 0.0 collective-permute-done.5.refs_11_
  21.0 0.4 %collective-permute-start.7 = (f32[2,216,128]{2,1,0:T(8,128)S(1)}, f32[2,216,128]{2,1,0:T(8,128)S(1)}, u32[]{:S(2)}, u32[]{:S(2)}) collective-permute-start(f32[2,216,128]{2,1,0:T(8,128)S(1)} %collective-permute-done.5.refs_11_), channel_id=1, source_target_pairs={{0,1},{1,0},{2,3},{3,2},{4,5},{5,4},{6,7},{7,6},{8,9},{9,8},{10,11... | collective-permute-start | bytes 663560 | tf_op jit(solution)/shard_map/ppermute | solution.py:689
  21.5 1.0 %collective-permute-done.4.refs_9_ = f32[2,216,128]{2,1,0:T(8,128)S(1)} collective-permute-done((f32[2,216,128]{2,1,0:T(8,128)S(1)}, f32[2,216,128]{2,1,0:T(8,128)S(1)}, u32[]{:S(2)}, u32[]{:S(2)}) %collective-permute-start.4) | collective-permute-done | bytes 221216 | tf_op jit(solution)/shard_map/ppermute | solution.py:689
  22.5 0.3 collective-permute-done.7.refs_13_
  22.8 2.4 %advance_leaving_edges.1 = (f32[2,3,16,128]{3,2,1,0:T(8,128)S(1)}, f32[2,3,16,128]{3,2,1,0:T(8,128)S(1)}, f32[2,3,16,128]{3,2,1,0:T(8,128)S(1)}) custom-call(s32[265]{0:T(512)S(4)} %index_table.1.refs_0_, f32[8,128,128]{2,1,0:T(8,128)S(1)} %get-tuple-element.34.refs_1_, f32[8,128,128]{2,1,0:T(8,128)S(1)} %get-tuple-element.35.refs_2_, ...), custom_call_target="tpu_custom_call" | custom-call | flops 11059200 | bytes 262144 | tf_op jit(solution)/shard_map/advance_leaving_edges/pallas_call | solution.py:658
  25.2 1.9 %collective-permute-done.11.refs_15_ = f32[2,3,112,128]{3,2,1,0:T(8,128)S(1)} collective-permute-done((f32[2,3,112,128]{3,2,1,0:T(8,128)S(1)}, f32[2,3,112,128]{3,2,1,0:T(8,128)S(1)}, u32[]{:S(2)}, u32[]{:S(2)}) %collective-permute-start.11) | collective-permute-done | bytes 344096 | tf_op jit(solution)/shard_map/ppermute | solution.py:689
  27.1 0.0 collective-permute-start.12
  27.1 1.7 %collective-permute-start.8 = (f32[2,3,16,128]{3,2,1,0:T(8,128)S(1)}, f32[2,3,16,128]{3,2,1,0:T(8,128)S(1)}, u32[]{:S(2)}, u32[]{:S(2)}) collective-permute-start(f32[2,3,16,128]{3,2,1,0:T(8,128)S(1)} %get-tuple-element.41), channel_id=1, source_target_pairs={{0,2},{1,3},{2,0},{3,1},{4,6},{5,7},{6,4},{7,5},{8,10},{9,11},{10,... | collective-permute-start | bytes 147464 | tf_op jit(solution)/shard_map/ppermute | solution.py:689
  28.8 0.1 collective-permute-start.9
  29.0 0.0 collective-permute-done.13.refs_14_
  29.0 6.4 %advance_staying.1 = (f32[8,128,128]{2,1,0:T(8,128)}, f32[8,128,128]{2,1,0:T(8,128)}, f32[8,128,128]{2,1,0:T(8,128)}) custom-call(s32[265]{0:T(512)S(4)} %index_table.1.refs_0_, f32[8,128,128]{2,1,0:T(8,128)S(1)} %get-tuple-element.34.refs_1_, f32[8,128,128]{2,1,0:T(8,128)S(1)} %get-tuple-element.35.refs_2_, f32[8,128,128]{2,1,0:T(8,128)S(1)} %get-tuple-element.36.refs_3_, ...), custom_call_target="tpu_custom_call" | custom-call | flops 33177600 | bytes 2097152 | tf_op jit(solution)/shard_map/advance_staying/pallas_call | solution.py:658
  35.3 0.0 collective-permute-done.10.refs_1_
  35.3 0.0 collective-permute-done.12.refs_2_
  35.4 1.0 %place_arrivals.2 = (f32[8,128,128]{2,1,0:T(8,128)}, f32[8,128,128]{2,1,0:T(8,128)}, f32[8,128,128]{2,1,0:T(8,128)}) custom-call(s32[265]{0:T(512)S(4)} %index_table.1.refs_0_, f32[2,3,112,128]{3,2,1,0:T(8,128)S(1)} %collective-permute-done.10.refs_1_, ...), custom_call_target="tpu_custom_call", output_to_operand_aliasing={{0}: (3, {}), {1}: (4, {}), {2}: (5, {})} | custom-call | tf_op jit(solution)/shard_map/place_arrivals/pallas_call | solution.py:287
  36.3 0.0 collective-permute-done.8.refs_1_
  36.3 0.0 collective-permute-done.9.refs_2_
  36.4 0.9 %place_arrivals.3 = (f32[8,128,128]{2,1,0:T(8,128)}, f32[8,128,128]{2,1,0:T(8,128)}, f32[8,128,128]{2,1,0:T(8,128)}) custom-call(s32[265]{0:T(512)S(4)} %index_table.1.refs_0_, f32[2,3,16,128]{3,2,1,0:T(8,128)S(1)} %collective-permute-done.8.refs_1_, ...), custom_call_target="tpu_custom_call", output_to_operand_aliasing={{0}: (3, {}), {1}: (4, {}), {2}: (5, {})} | custom-call | tf_op jit(solution)/shard_map/place_arrivals/pallas_call | solution.py:287
  (1 shorter events, 0.0 us)
Async XLA Ops:
  2.9 8.6 %collective-permute-start = (f32[448,128]{1,0:T(8,128)S(1)}, f32[448,128]{1,0:T(8,128)S(1)}, u32[]{:S(2)}, u32[]{:S(2)}) collective-permute-start(f32[448,128]{1,0:T(8,128)S(1)} %get-tuple-element.30.refs_6_), channel_id=1, source_target_pairs={{0,2},{1,3},{2,0},{3,1},{4,6},{5,7},{6,4},{7,5},{8,10},{9,11},{10,... | collective-permute-start | bytes 688136 | tf_op jit(solution)/shard_map/ppermute | solution.py:689
  5.9 2.1 %copy-start = (s32[128]{0:T(128)S(1)}, s32[128]{0:T(128)}, u32[]{:S(2)}) copy-start(s32[128]{0:T(128)} %before_ref.1) | copy-start | bytes 1540
  5.9 2.1 %copy-start.1 = (s32[128]{0:T(128)S(1)}, s32[128]{0:T(128)}, u32[]{:S(2)}) copy-start(s32[128]{0:T(128)} %after_ref.1) | copy-start | bytes 1540
  5.9 2.1 %copy-start.2 = (s32[128]{0:T(128)S(1)}, s32[128]{0:T(128)}, u32[]{:S(2)}) copy-start(s32[128]{0:T(128)} %wet_ref.1) | copy-start | bytes 1540
  5.9 4.7 %collective-permute-start.1 = (f32[216,128]{1,0:T(8,128)S(1)}, f32[216,128]{1,0:T(8,128)S(1)}, u32[]{:S(2)}, u32[]{:S(2)}) collective-permute-start(f32[216,128]{1,0:T(8,128)S(1)} %get-tuple-element.31), channel_id=1, source_target_pairs={{0,4},{1,5},{4,0},{5,1},{8,12},{9,13},{12,8},{13,9},{2,6},{3,7},{6... | collective-permute-start | bytes 331784 | tf_op jit(solution)/shard_map/ppermute | solution.py:713
  7.5 3.2 %collective-permute-start.2 = (f32[216,128]{1,0:T(8,128)S(1)}, f32[216,128]{1,0:T(8,128)S(1)}, u32[]{:S(2)}, u32[]{:S(2)}) collective-permute-start(f32[216,128]{1,0:T(8,128)S(1)} %get-tuple-element.32), channel_id=1, source_target_pairs={{0,1},{1,0},{4,8},{5,9},{8,4},{9,5},{12,13},{13,12},{2,3},{3,2},{6... | collective-permute-start | bytes 331784 | tf_op jit(solution)/shard_map/ppermute | solution.py:713
  7.5 5.8 %collective-permute-start.3 = (f32[448,128]{1,0:T(8,128)S(1)}, f32[448,128]{1,0:T(8,128)S(1)}, u32[]{:S(2)}, u32[]{:S(2)}) collective-permute-start(f32[448,128]{1,0:T(8,128)S(1)} %get-tuple-element.30.refs_6_), channel_id=1, source_target_pairs={{0,1},{1,0},{2,3},{3,2},{4,5},{5,4},{6,7},{7,6},{8,9},{9,8},{10,11... | collective-permute-start | bytes 688136 | tf_op jit(solution)/shard_map/ppermute | solution.py:689
  11.5 1.8 %collective-permute-start.6 = (f32[448,128]{1,0:T(8,128)S(1)}, f32[448,128]{1,0:T(8,128)S(1)}, u32[]{:S(2)}, u32[]{:S(2)}) collective-permute-start(f32[448,128]{1,0:T(8,128)S(1)} %collective-permute-done.refs_10_.refs_8_), channel_id=1, source_target_pairs={{0,1},{1,0},{2,3},{3,2},{4,5},{5,4},{6,7},{7,6},{8,9},{9,8},{10,11... | collective-permute-start | bytes 688136 | tf_op jit(solution)/shard_map/ppermute | solution.py:689
  11.5 9.6 %collective-permute-start.5 = (f32[2,216,128]{2,1,0:T(8,128)S(1)}, f32[2,216,128]{2,1,0:T(8,128)S(1)}, u32[]{:S(2)}, u32[]{:S(2)}) collective-permute-start(f32[2,216,128]{2,1,0:T(8,128)S(1)} %join_row_halos.1.refs_7_), channel_id=1, source_target_pairs={{0,2},{1,3},{2,0},{3,1},{4,6},{5,7},{6,4},{7,5},{8,10},{9,11},{10,... | collective-permute-start | bytes 663560 | tf_op jit(solution)/shard_map/ppermute | solution.py:689
  15.9 11.1 %collective-permute-start.11 = (f32[2,3,112,128]{3,2,1,0:T(8,128)S(1)}, f32[2,3,112,128]{3,2,1,0:T(8,128)S(1)}, u32[]{:S(2)}, u32[]{:S(2)}) collective-permute-start(f32[2,3,112,128]{3,2,1,0:T(8,128)S(1)} %get-tuple-element.46), channel_id=1, source_target_pairs={{0,2},{1,3},{2,0},{3,1},{4,6},{5,7},{6,4},{7,5},{8,10},{9,11},{10,... | collective-permute-start | bytes 1032200 | tf_op jit(solution)/shard_map/ppermute | solution.py:689
  20.2 8.7 %collective-permute-start.13 = (f32[2,3,112,128]{3,2,1,0:T(8,128)S(1)}, f32[2,3,112,128]{3,2,1,0:T(8,128)S(1)}, u32[]{:S(2)}, u32[]{:S(2)}) collective-permute-start(f32[2,3,112,128]{3,2,1,0:T(8,128)S(1)} %get-tuple-element.49), channel_id=1, source_target_pairs={{0,1},{1,0},{2,3},{3,2},{4,5},{5,4},{6,7},{7,6},{8,9},{9,8},{10,11... | collective-permute-start | bytes 1032200 | tf_op jit(solution)/shard_map/ppermute | solution.py:689
  20.3 15.0 %collective-permute-start.10 = (f32[2,3,112,128]{3,2,1,0:T(8,128)S(1)}, f32[2,3,112,128]{3,2,1,0:T(8,128)S(1)}, u32[]{:S(2)}, u32[]{:S(2)}) collective-permute-start(f32[2,3,112,128]{3,2,1,0:T(8,128)S(1)} %get-tuple-element.45), channel_id=1, source_target_pairs={{0,3},{1,2},{2,1},{3,0},{4,7},{5,6},{6,5},{7,4},{8,11},{9,10},{10,... | collective-permute-start | bytes 1032200 | tf_op jit(solution)/shard_map/ppermute | solution.py:689
  21.0 1.5 %collective-permute-start.4 = (f32[2,216,128]{2,1,0:T(8,128)S(1)}, f32[2,216,128]{2,1,0:T(8,128)S(1)}, u32[]{:S(2)}, u32[]{:S(2)}) collective-permute-start(f32[2,216,128]{2,1,0:T(8,128)S(1)} %join_row_halos.1.refs_7_), channel_id=1, source_target_pairs={{0,1},{1,0},{2,3},{3,2},{4,5},{5,4},{6,7},{7,6},{8,9},{9,8},{10,11... | collective-permute-start | bytes 663560 | tf_op jit(solution)/shard_map/ppermute | solution.py:689
  21.0 1.7 %collective-permute-start.7 = (f32[2,216,128]{2,1,0:T(8,128)S(1)}, f32[2,216,128]{2,1,0:T(8,128)S(1)}, u32[]{:S(2)}, u32[]{:S(2)}) collective-permute-start(f32[2,216,128]{2,1,0:T(8,128)S(1)} %collective-permute-done.5.refs_11_), channel_id=1, source_target_pairs={{0,1},{1,0},{2,3},{3,2},{4,5},{5,4},{6,7},{7,6},{8,9},{9,8},{10,11... | collective-permute-start | bytes 663560 | tf_op jit(solution)/shard_map/ppermute | solution.py:689
  27.1 8.3 %collective-permute-start.12 = (f32[2,3,16,128]{3,2,1,0:T(8,128)S(1)}, f32[2,3,16,128]{3,2,1,0:T(8,128)S(1)}, u32[]{:S(2)}, u32[]{:S(2)}) collective-permute-start(f32[2,3,16,128]{3,2,1,0:T(8,128)S(1)} %get-tuple-element.48), channel_id=1, source_target_pairs={{0,1},{1,0},{2,3},{3,2},{4,5},{5,4},{6,7},{7,6},{8,9},{9,8},{10,11... | collective-permute-start | bytes 147464 | tf_op jit(solution)/shard_map/ppermute | solution.py:689
  27.1 9.3 %collective-permute-start.8 = (f32[2,3,16,128]{3,2,1,0:T(8,128)S(1)}, f32[2,3,16,128]{3,2,1,0:T(8,128)S(1)}, u32[]{:S(2)}, u32[]{:S(2)}) collective-permute-start(f32[2,3,16,128]{3,2,1,0:T(8,128)S(1)} %get-tuple-element.41), channel_id=1, source_target_pairs={{0,2},{1,3},{2,0},{3,1},{4,6},{5,7},{6,4},{7,5},{8,10},{9,11},{10,... | collective-permute-start | bytes 147464 | tf_op jit(solution)/shard_map/ppermute | solution.py:689
  28.8 7.5 %collective-permute-start.9 = (f32[2,3,16,128]{3,2,1,0:T(8,128)S(1)}, f32[2,3,16,128]{3,2,1,0:T(8,128)S(1)}, u32[]{:S(2)}, u32[]{:S(2)}) collective-permute-start(f32[2,3,16,128]{3,2,1,0:T(8,128)S(1)} %get-tuple-element.42), channel_id=1, source_target_pairs={{0,3},{1,2},{2,1},{3,0},{4,7},{5,6},{6,5},{7,4},{8,11},{9,10},{10,... | collective-permute-start | bytes 147464 | tf_op jit(solution)/shard_map/ppermute | solution.py:689

commit v11 on v9

--- a/solution.py
+++ b/solution.py
@@ -254,19 +254,24 @@
 
                 @pl.when(slot >= 0)
                 def _():
-                    at = 0
-                    for m, (start, count) in enumerate(spans):
-                        for f in range(3):
-                            act(
-                                pltpu.make_async_copy(
-                                    received[n].at[j, f, pl.ds(at, count), :],
-                                    outs[f].at[slot, pl.ds(start, count), :],
-                                    sem.at[n, j, f, m],
-                                )
-                            )
-                        at += count
-
-    return each
+                    act(n, j, slot)
+
+    def start(n, j, slot):
+        at = 0
+        for begin, count in spans:
+            for f in range(3):
+                pltpu.make_async_copy(
+                    received[n].at[j, f, pl.ds(at, count), :],
+                    outs[f].at[slot, pl.ds(begin, count), :],
+                    sem.at[n, j],
+                ).start()
+            at += count
+
+    def wait(n, j, slot):
+        tile = received[n].at[j]
+        pltpu.make_async_copy(tile, tile, sem.at[n, j]).wait()
+
+    return lambda: each(start), lambda: each(wait)
 
 
 def place_kernel(groups, *refs):
@@ -276,10 +281,10 @@
         arrivals(table, (k,), (array,), spans, outs, sem.at[pl.ds(n, 1)])
         for n, ((k, spans), array) in enumerate(zip(groups, received))
     ]
-    for each in copies:
-        each(lambda copy: copy.start())
-    for each in copies:
-        each(lambda copy: copy.wait())
+    for start, _ in copies:
+        start()
+    for _, wait in copies:
+        wait()
 
 
 def place(groups, table, received, partial_outs):
@@ -292,7 +297,7 @@
         + vmem_specs(count)
         + [pl.BlockSpec(memory_space=ANY)] * 3,
         out_specs=tuple(pl.BlockSpec(memory_space=ANY) for _ in partial_outs),
-        scratch_shapes=[pltpu.SemaphoreType.DMA((count, 2, 3, 2))],
+        scratch_shapes=[pltpu.SemaphoreType.DMA((count, 2))],
         input_output_aliases={1 + count + f: f for f in range(3)},
         compiler_params=SMALL,
     )(table, *received, *partial_outs)
@@ -527,8 +532,8 @@
         sem_out, sem_in,
     ) = refs
     if part is WHOLE:
-        placing = arrivals(table, units, received, (MIDDLE,), outs, sem_in)
-        placing(lambda copy: copy.start())
+        start_placing, wait_placing = arrivals(table, units, received, (MIDDLE,), outs, sem_in)
+        start_placing()
     block = (level, flow_x, flow_y, ground, friction)
     strip = (s_level, s_flow_x, s_flow_y, s_ground, s_friction)
     lane = lane_index()
@@ -631,7 +636,7 @@
         ]
         for copy in copies:
             copy.start()
-        placing(lambda copy: copy.wait())
+        wait_placing()
         for copy in copies:
             copy.wait()
 
@@ -670,7 +675,7 @@
         + [strip] * 7
         + [
             pltpu.SemaphoreType.DMA((part.tiles, 3)),
-            pltpu.SemaphoreType.DMA((max(len(given), 1), 2, 3, 1)),
+            pltpu.SemaphoreType.DMA((max(len(given), 1), 2)),
         ],
         compiler_params=pltpu.CompilerParams(vmem_limit_bytes=12 * 1024 * 1024),
         cost_estimate=pl.CostEstimate(
@@ -753,8 +758,8 @@
     soon = tuple(range(1, subs)) + (ahead,)
     last = tuple(k for k in units if k not in soon)
     outs = advance(WHOLE, table, fields, halos, soon, [middle[k] for k in soon])
-    groups = tuple((k, (MIDDLE,)) for k in last) + tuple((k, LATE.sent) for k in units)
-    return place(groups, table, [middle[k] for k in last] + edges, outs)
+    outs = place(tuple((k, (MIDDLE,)) for k in last), table, [middle[k] for k in last], outs)
+    return place(tuple((k, LATE.sent) for k in units), table, edges, outs)
 
 
 def solution(mesh):

time: 37.3 us -> 36.8 us (0.987)
    ppermute x12, waiting for transfers between devices: 4.29 us -> 3.92 us  [shift_lanes(): return lax.ppermute(array, ('col', 'sub'), pairs)]
    pallas_call x1 -> x2, Pallas kernels: 1.22 us -> 1.46 us  [place(): pl.pallas_call(functools.partial(place_kernel, groups), name='place_arriv...]
  transfers between devices with their start and end apart: 14 -> 14, of which waited for: 7 -> 8; matrix products, arithmetic and copies ran while one was open for 0% -> 0% of each run, Pallas kernels for 43% -> 45%
where the time goes in v11:
time: 36.8 us; the launch traced here: 36.7 us
  Pallas kernels  19.4 us (53%)
  starting transfers between devices  11.5 us (31%)
  waiting for transfers between devices  4.93 us (13%)
  between operations  0.88 us (2%)
    pallas_call x4, Pallas kernels, advance(): pl.pallas_call(functools.partial(advance_kernel, part, lanes, units, len(...  14.1 us
    ppermute x12, starting transfers between devices, shift_lanes(): return lax.ppermute(array, ('col', 'sub'), pairs)  9.87 us
    ppermute x12, waiting for transfers between devices, shift_lanes(): return lax.ppermute(array, ('col', 'sub'), pairs)  3.92 us
    pallas_call x1, Pallas kernels, load(): pl.pallas_call(load_kernel, name='load_and_pack', out_shape=tuple(outs),...  2.22 us
    pallas_call x1, Pallas kernels, make_table(): pl.pallas_call(functools.partial(index_kernel, shape), name='index_table'...  1.64 us
    ppermute x2, starting transfers between devices, meet_rows(): return lax.ppermute(array, ('row', 'sub'), pairs)  1.58 us
    pallas_call x2, Pallas kernels, place(): pl.pallas_call(functools.partial(place_kernel, groups), name='place_arriv...  1.46 us
    ppermute x2, waiting for transfers between devices, meet_rows(): return lax.ppermute(array, ('row', 'sub'), pairs)  1.01 us
  transfers between devices with their start and end apart: 14, of which 8 were waited for; matrix products, arithmetic and copies ran while one was open for 0% of the time, Pallas kernels for 45%

profile of v11, /device:TPU:0, one launch (start us, length us, event | category | flops | bytes accessed | tf_op | source)
XLA Modules:
  0.0 36.7 jit_solution(16318911998244724299)
XLA Ops:
  0.6 2.2 %load_and_pack.1 = (f32[8,128,128]{2,1,0:T(8,128)S(1)}, f32[8,128,128]{2,1,0:T(8,128)S(1)}, f32[8,128,128]{2,1,0:T(8,128)S(1)}, f32[8,128,128]{2,1,0:T(8,128)S(1...) custom-call(f32[8,128,128]{2,1,0:T(8,128)} %refs_0_.1, ...), custom_call_target="tpu_custom_call" | custom-call | tf_op jit(solution)/shard_map/load_and_pack/pallas_call | solution.py:216
  2.9 3.0 %collective-permute-start = (f32[448,128]{1,0:T(8,128)S(1)}, f32[448,128]{1,0:T(8,128)S(1)}, u32[]{:S(2)}, u32[]{:S(2)}) collective-permute-start(f32[448,128]{1,0:T(8,128)S(1)} %get-tuple-element.30.refs_6_), channel_id=1, source_target_pairs={{0,2},{1,3},{2,0},{3,1},{4,6},{5,7},{6,4},{7,5},{8,10},{9,11},{10,... | collective-permute-start | bytes 688136 | tf_op jit(solution)/shard_map/ppermute | solution.py:694
  5.9 0.0 copy-start
  5.9 0.0 copy-start.1
  5.9 0.0 copy-start.2
  5.9 1.6 %collective-permute-start.1 = (f32[216,128]{1,0:T(8,128)S(1)}, f32[216,128]{1,0:T(8,128)S(1)}, u32[]{:S(2)}, u32[]{:S(2)}) collective-permute-start(f32[216,128]{1,0:T(8,128)S(1)} %get-tuple-element.31), channel_id=1, source_target_pairs={{0,4},{1,5},{4,0},{5,1},{8,12},{9,13},{12,8},{13,9},{2,6},{3,7},{6... | collective-permute-start | bytes 331784 | tf_op jit(solution)/shard_map/ppermute | solution.py:718
  7.5 0.0 collective-permute-start.2
  7.5 0.5 %collective-permute-start.3 = (f32[448,128]{1,0:T(8,128)S(1)}, f32[448,128]{1,0:T(8,128)S(1)}, u32[]{:S(2)}, u32[]{:S(2)}) collective-permute-start(f32[448,128]{1,0:T(8,128)S(1)} %get-tuple-element.30.refs_6_), channel_id=1, source_target_pairs={{0,1},{1,0},{2,3},{3,2},{4,5},{5,4},{6,7},{7,6},{8,9},{9,8},{10,11... | collective-permute-start | bytes 688136 | tf_op jit(solution)/shard_map/ppermute | solution.py:694
  8.0 0.0 copy-done
  8.0 0.0 copy-done.1
  8.0 0.0 copy-done.2
  8.0 1.6 %index_table.1.refs_0_ = s32[265]{0:T(512)S(4)} custom-call(s32[128]{0:T(128)S(1)} %copy-done, s32[128]{0:T(128)S(1)} %copy-done.1, s32[128]{0:T(128)S(1)} %copy-done.2), custom_call_target="tpu_custom_call" | custom-call | tf_op jit(solution)/shard_map/index_table/pallas_call | solution.py:143
  9.6 1.0 %collective-permute-done.1.met_even = f32[216,128]{1,0:T(8,128)S(1)} collective-permute-done((f32[216,128]{1,0:T(8,128)S(1)}, f32[216,128]{1,0:T(8,128)S(1)}, u32[]{:S(2)}, u32[]{:S(2)}) %collective-permute-start.1) | collective-permute-done | bytes 110624 | tf_op jit(solution)/shard_map/ppermute | solution.py:718
  10.6 0.0 collective-permute-done.2.met_odd
  10.7 0.8 %collective-permute-done.refs_8_.refs_10_ = f32[448,128]{1,0:T(8,128)S(1)} collective-permute-done((f32[448,128]{1,0:T(8,128)S(1)}, f32[448,128]{1,0:T(8,128)S(1)}, u32[]{:S(2)}, u32[]{:S(2)}) %collective-permute-start) | collective-permute-done | bytes 229408 | tf_op jit(solution)/shard_map/ppermute | solution.py:694
  11.5 0.0 collective-permute-start.4
  11.5 1.7 %collective-permute-start.7 = (f32[2,216,128]{2,1,0:T(8,128)S(1)}, f32[2,216,128]{2,1,0:T(8,128)S(1)}, u32[]{:S(2)}, u32[]{:S(2)}) collective-permute-start(f32[2,216,128]{2,1,0:T(8,128)S(1)} %join_row_halos.1.refs_7_), channel_id=1, source_target_pairs={{0,2},{1,3},{2,0},{3,1},{4,6},{5,7},{6,4},{7,5},{8,10},{9,11},{10,... | collective-permute-start | bytes 663560 | tf_op jit(solution)/shard_map/ppermute | solution.py:694
  13.2 0.0 collective-permute-done.3.refs_7_.refs_8_
  13.2 0.0 collective-permute-done.4.refs_9_.refs_12_
  13.2 2.7 %advance_leaving_first.1 = (f32[2,3,112,128]{3,2,1,0:T(8,128)S(1)}, f32[2,3,112,128]{3,2,1,0:T(8,128)S(1)}, f32[2,3,112,128]{3,2,1,0:T(8,128)S(1)}) custom-call(s32[265]{0:T(512)S(4)} %index_table.1.refs_0_, f32[8,128,128]{2,1,0:T(8,128)S(1)} %get-tuple-element.34.refs_1_, f32[8,128,128]{2,1,0:T(8,128)S(1)} %get-tuple-element.35.refs_2_, ...), custom_call_target="tpu_custom_call" | custom-call | flops 17694720 | bytes 917504 | tf_op jit(solution)/shard_map/advance_leaving_first/pallas_call | solution.py:663
  15.9 1.5 %collective-permute-start.5 = (f32[2,3,112,128]{3,2,1,0:T(8,128)S(1)}, f32[2,3,112,128]{3,2,1,0:T(8,128)S(1)}, u32[]{:S(2)}, u32[]{:S(2)}) collective-permute-start(f32[2,3,112,128]{3,2,1,0:T(8,128)S(1)} %get-tuple-element.40), channel_id=1, source_target_pairs={{0,2},{1,3},{2,0},{3,1},{4,6},{5,7},{6,4},{7,5},{8,10},{9,11},{10,... | collective-permute-start | bytes 1032200 | tf_op jit(solution)/shard_map/ppermute | solution.py:694
  17.4 2.7 %advance_leaving_second.1 = (f32[2,3,112,128]{3,2,1,0:T(8,128)S(1)}, f32[2,3,112,128]{3,2,1,0:T(8,128)S(1)}) custom-call(s32[265]{0:T(512)S(4)} %index_table.1.refs_0_, f32[8,128,128]{2,1,0:T(8,128)S(1)} %get-tuple-element.34.refs_1_, f32[8,128,128]{2,1,0:T(8,128)S(1)} %get-tuple-element.35.refs_2_, ...), custom_call_target="tpu_custom_call", output_to_operand_aliasing={{0}: (10, {}), {1}: (11, {})} | custom-call | flops 17694720 | bytes 917504 | tf_op jit(solution)/shard_map/advance_leaving_second/pallas_call | solution.py:663
  20.1 0.1 collective-permute-start.13
  20.2 0.7 %collective-permute-start.12 = (f32[2,3,112,128]{3,2,1,0:T(8,128)S(1)}, f32[2,3,112,128]{3,2,1,0:T(8,128)S(1)}, u32[]{:S(2)}, u32[]{:S(2)}) collective-permute-start(f32[2,3,112,128]{3,2,1,0:T(8,128)S(1)} %get-tuple-element.48), channel_id=1, source_target_pairs={{0,3},{1,2},{2,1},{3,0},{4,7},{5,6},{6,5},{7,4},{8,11},{9,10},{10,... | collective-permute-start | bytes 1032200 | tf_op jit(solution)/shard_map/ppermute | solution.py:694
  20.9 0.1 collective-permute-start.6
  20.9 0.0 collective-permute-done.7.refs_11_
  20.9 0.4 %collective-permute-start.8 = (f32[2,216,128]{2,1,0:T(8,128)S(1)}, f32[2,216,128]{2,1,0:T(8,128)S(1)}, u32[]{:S(2)}, u32[]{:S(2)}) collective-permute-start(f32[2,216,128]{2,1,0:T(8,128)S(1)} %collective-permute-done.7.refs_11_), channel_id=1, source_target_pairs={{0,1},{1,0},{2,3},{3,2},{4,5},{5,4},{6,7},{7,6},{8,9},{9,8},{10,11... | collective-permute-start | bytes 663560 | tf_op jit(solution)/shard_map/ppermute | solution.py:694
  21.4 1.0 %collective-permute-done.6.refs_9_ = f32[2,216,128]{2,1,0:T(8,128)S(1)} collective-permute-done((f32[2,216,128]{2,1,0:T(8,128)S(1)}, f32[2,216,128]{2,1,0:T(8,128)S(1)}, u32[]{:S(2)}, u32[]{:S(2)}) %collective-permute-start.6) | collective-permute-done | bytes 221216 | tf_op jit(solution)/shard_map/ppermute | solution.py:694
  22.4 0.3 collective-permute-done.8.refs_13_
  22.7 2.4 %advance_leaving_edges.1 = (f32[2,3,16,128]{3,2,1,0:T(8,128)S(1)}, f32[2,3,16,128]{3,2,1,0:T(8,128)S(1)}, f32[2,3,16,128]{3,2,1,0:T(8,128)S(1)}) custom-call(s32[265]{0:T(512)S(4)} %index_table.1.refs_0_, f32[8,128,128]{2,1,0:T(8,128)S(1)} %get-tuple-element.34.refs_1_, f32[8,128,128]{2,1,0:T(8,128)S(1)} %get-tuple-element.35.refs_2_, ...), custom_call_target="tpu_custom_call" | custom-call | flops 11059200 | bytes 262144 | tf_op jit(solution)/shard_map/advance_leaving_edges/pallas_call | solution.py:663
  25.1 1.5 %collective-permute-start.10 = (f32[2,3,16,128]{3,2,1,0:T(8,128)S(1)}, f32[2,3,16,128]{3,2,1,0:T(8,128)S(1)}, u32[]{:S(2)}, u32[]{:S(2)}) collective-permute-start(f32[2,3,16,128]{3,2,1,0:T(8,128)S(1)} %get-tuple-element.44), channel_id=1, source_target_pairs={{0,2},{1,3},{2,0},{3,1},{4,6},{5,7},{6,4},{7,5},{8,10},{9,11},{10,... | collective-permute-start | bytes 147464 | tf_op jit(solution)/shard_map/ppermute | solution.py:694
  26.6 0.1 collective-permute-start.11
  26.7 0.4 %collective-permute-done.5.refs_15_ = f32[2,3,112,128]{3,2,1,0:T(8,128)S(1)} collective-permute-done((f32[2,3,112,128]{3,2,1,0:T(8,128)S(1)}, f32[2,3,112,128]{3,2,1,0:T(8,128)S(1)}, u32[]{:S(2)}, u32[]{:S(2)}) %collective-permute-start.5) | collective-permute-done | bytes 344096 | tf_op jit(solution)/shard_map/ppermute | solution.py:694
  27.1 0.2 collective-permute-start.9
  27.3 0.0 collective-permute-done.13.refs_14_
  27.3 6.3 %advance_staying.1 = (f32[8,128,128]{2,1,0:T(8,128)}, f32[8,128,128]{2,1,0:T(8,128)}, f32[8,128,128]{2,1,0:T(8,128)}) custom-call(s32[265]{0:T(512)S(4)} %index_table.1.refs_0_, f32[8,128,128]{2,1,0:T(8,128)S(1)} %get-tuple-element.34.refs_1_, f32[8,128,128]{2,1,0:T(8,128)S(1)} %get-tuple-element.35.refs_2_, f32[8,128,128]{2,1,0:T(8,128)S(1)} %get-tuple-element.36.refs_3_, ...), custom_call_target="tpu_custom_call" | custom-call | flops 33177600 | bytes 2097152 | tf_op jit(solution)/shard_map/advance_staying/pallas_call | solution.py:663
  33.6 0.1 collective-permute-done.12.refs_1_
  33.7 0.7 %place_arrivals.2 = (f32[8,128,128]{2,1,0:T(8,128)}, f32[8,128,128]{2,1,0:T(8,128)}, f32[8,128,128]{2,1,0:T(8,128)}) custom-call(s32[265]{0:T(512)S(4)} %index_table.1.refs_0_, f32[2,3,112,128]{3,2,1,0:T(8,128)S(1)} %collective-permute-done.12.refs_1_, ...), custom_call_target="tpu_custom_call", output_to_operand_aliasing={{0}: (2, {}), {1}: (3, {}), {2}: (4, {})} | custom-call | tf_op jit(solution)/shard_map/place_arrivals/pallas_call | solution.py:292
  34.4 1.1 %collective-permute-done.10.refs_2_ = f32[2,3,16,128]{3,2,1,0:T(8,128)S(1)} collective-permute-done((f32[2,3,16,128]{3,2,1,0:T(8,128)S(1)}, f32[2,3,16,128]{3,2,1,0:T(8,128)S(1)}, u32[]{:S(2)}, u32[]{:S(2)}) %collective-permute-start.10) | collective-permute-done | bytes 49184 | tf_op jit(solution)/shard_map/ppermute | solution.py:694
  35.5 0.3 collective-permute-done.11.refs_3_
  35.8 0.0 collective-permute-done.9.refs_1_
  35.8 0.7 %place_arrivals.3 = (f32[8,128,128]{2,1,0:T(8,128)}, f32[8,128,128]{2,1,0:T(8,128)}, f32[8,128,128]{2,1,0:T(8,128)}) custom-call(s32[265]{0:T(512)S(4)} %index_table.1.refs_0_, f32[2,3,16,128]{3,2,1,0:T(8,128)S(1)} %collective-permute-done.9.refs_1_, ...), custom_call_target="tpu_custom_call", output_to_operand_aliasing={{0}: (4, {}), {1}: (5, {}), {2}: (6, {})} | custom-call | tf_op jit(solution)/shard_map/place_arrivals/pallas_call | solution.py:292
  (1 shorter events, 0.0 us)
Async XLA Ops:
  2.9 8.6 %collective-permute-start = (f32[448,128]{1,0:T(8,128)S(1)}, f32[448,128]{1,0:T(8,128)S(1)}, u32[]{:S(2)}, u32[]{:S(2)}) collective-permute-start(f32[448,128]{1,0:T(8,128)S(1)} %get-tuple-element.30.refs_6_), channel_id=1, source_target_pairs={{0,2},{1,3},{2,0},{3,1},{4,6},{5,7},{6,4},{7,5},{8,10},{9,11},{10,... | collective-permute-start | bytes 688136 | tf_op jit(solution)/shard_map/ppermute | solution.py:694
  5.9 2.1 %copy-start = (s32[128]{0:T(128)S(1)}, s32[128]{0:T(128)}, u32[]{:S(2)}) copy-start(s32[128]{0:T(128)} %before_ref.1) | copy-start | bytes 1540
  5.9 2.1 %copy-start.1 = (s32[128]{0:T(128)S(1)}, s32[128]{0:T(128)}, u32[]{:S(2)}) copy-start(s32[128]{0:T(128)} %after_ref.1) | copy-start | bytes 1540
  5.9 2.1 %copy-start.2 = (s32[128]{0:T(128)S(1)}, s32[128]{0:T(128)}, u32[]{:S(2)}) copy-start(s32[128]{0:T(128)} %wet_ref.1) | copy-start | bytes 1540
  5.9 4.7 %collective-permute-start.1 = (f32[216,128]{1,0:T(8,128)S(1)}, f32[216,128]{1,0:T(8,128)S(1)}, u32[]{:S(2)}, u32[]{:S(2)}) collective-permute-start(f32[216,128]{1,0:T(8,128)S(1)} %get-tuple-element.31), channel_id=1, source_target_pairs={{0,4},{1,5},{4,0},{5,1},{8,12},{9,13},{12,8},{13,9},{2,6},{3,7},{6... | collective-permute-start | bytes 331784 | tf_op jit(solution)/shard_map/ppermute | solution.py:718
  7.5 3.2 %collective-permute-start.2 = (f32[216,128]{1,0:T(8,128)S(1)}, f32[216,128]{1,0:T(8,128)S(1)}, u32[]{:S(2)}, u32[]{:S(2)}) collective-permute-start(f32[216,128]{1,0:T(8,128)S(1)} %get-tuple-element.32), channel_id=1, source_target_pairs={{0,1},{1,0},{4,8},{5,9},{8,4},{9,5},{12,13},{13,12},{2,3},{3,2},{6... | collective-permute-start | bytes 331784 | tf_op jit(solution)/shard_map/ppermute | solution.py:718
  7.5 5.8 %collective-permute-start.3 = (f32[448,128]{1,0:T(8,128)S(1)}, f32[448,128]{1,0:T(8,128)S(1)}, u32[]{:S(2)}, u32[]{:S(2)}) collective-permute-start(f32[448,128]{1,0:T(8,128)S(1)} %get-tuple-element.30.refs_6_), channel_id=1, source_target_pairs={{0,1},{1,0},{2,3},{3,2},{4,5},{5,4},{6,7},{7,6},{8,9},{9,8},{10,11... | collective-permute-start | bytes 688136 | tf_op jit(solution)/shard_map/ppermute | solution.py:694
  11.5 1.8 %collective-permute-start.4 = (f32[448,128]{1,0:T(8,128)S(1)}, f32[448,128]{1,0:T(8,128)S(1)}, u32[]{:S(2)}, u32[]{:S(2)}) collective-permute-start(f32[448,128]{1,0:T(8,128)S(1)} %collective-permute-done.refs_8_.refs_10_), channel_id=1, source_target_pairs={{0,1},{1,0},{2,3},{3,2},{4,5},{5,4},{6,7},{7,6},{8,9},{9,8},{10,11... | collective-permute-start | bytes 688136 | tf_op jit(solution)/shard_map/ppermute | solution.py:694
  11.5 9.5 %collective-permute-start.7 = (f32[2,216,128]{2,1,0:T(8,128)S(1)}, f32[2,216,128]{2,1,0:T(8,128)S(1)}, u32[]{:S(2)}, u32[]{:S(2)}) collective-permute-start(f32[2,216,128]{2,1,0:T(8,128)S(1)} %join_row_halos.1.refs_7_), channel_id=1, source_target_pairs={{0,2},{1,3},{2,0},{3,1},{4,6},{5,7},{6,4},{7,5},{8,10},{9,11},{10,... | collective-permute-start | bytes 663560 | tf_op jit(solution)/shard_map/ppermute | solution.py:694
  15.9 11.2 %collective-permute-start.5 = (f32[2,3,112,128]{3,2,1,0:T(8,128)S(1)}, f32[2,3,112,128]{3,2,1,0:T(8,128)S(1)}, u32[]{:S(2)}, u32[]{:S(2)}) collective-permute-start(f32[2,3,112,128]{3,2,1,0:T(8,128)S(1)} %get-tuple-element.40), channel_id=1, source_target_pairs={{0,2},{1,3},{2,0},{3,1},{4,6},{5,7},{6,4},{7,5},{8,10},{9,11},{10,... | collective-permute-start | bytes 1032200 | tf_op jit(solution)/shard_map/ppermute | solution.py:694
  20.1 7.1 %collective-permute-start.13 = (f32[2,3,112,128]{3,2,1,0:T(8,128)S(1)}, f32[2,3,112,128]{3,2,1,0:T(8,128)S(1)}, u32[]{:S(2)}, u32[]{:S(2)}) collective-permute-start(f32[2,3,112,128]{3,2,1,0:T(8,128)S(1)} %get-tuple-element.49), channel_id=1, source_target_pairs={{0,1},{1,0},{2,3},{3,2},{4,5},{5,4},{6,7},{7,6},{8,9},{9,8},{10,11... | collective-permute-start | bytes 1032200 | tf_op jit(solution)/shard_map/ppermute | solution.py:694
  20.2 13.5 %collective-permute-start.12 = (f32[2,3,112,128]{3,2,1,0:T(8,128)S(1)}, f32[2,3,112,128]{3,2,1,0:T(8,128)S(1)}, u32[]{:S(2)}, u32[]{:S(2)}) collective-permute-start(f32[2,3,112,128]{3,2,1,0:T(8,128)S(1)} %get-tuple-element.48), channel_id=1, source_target_pairs={{0,3},{1,2},{2,1},{3,0},{4,7},{5,6},{6,5},{7,4},{8,11},{9,10},{10,... | collective-permute-start | bytes 1032200 | tf_op jit(solution)/shard_map/ppermute | solution.py:694
  20.9 1.5 %collective-permute-start.6 = (f32[2,216,128]{2,1,0:T(8,128)S(1)}, f32[2,216,128]{2,1,0:T(8,128)S(1)}, u32[]{:S(2)}, u32[]{:S(2)}) collective-permute-start(f32[2,216,128]{2,1,0:T(8,128)S(1)} %join_row_halos.1.refs_7_), channel_id=1, source_target_pairs={{0,1},{1,0},{2,3},{3,2},{4,5},{5,4},{6,7},{7,6},{8,9},{9,8},{10,11... | collective-permute-start | bytes 663560 | tf_op jit(solution)/shard_map/ppermute | solution.py:694
  20.9 1.7 %collective-permute-start.8 = (f32[2,216,128]{2,1,0:T(8,128)S(1)}, f32[2,216,128]{2,1,0:T(8,128)S(1)}, u32[]{:S(2)}, u32[]{:S(2)}) collective-permute-start(f32[2,216,128]{2,1,0:T(8,128)S(1)} %collective-permute-done.7.refs_11_), channel_id=1, source_target_pairs={{0,1},{1,0},{2,3},{3,2},{4,5},{5,4},{6,7},{7,6},{8,9},{9,8},{10,11... | collective-permute-start | bytes 663560 | tf_op jit(solution)/shard_map/ppermute | solution.py:694
  25.1 10.4 %collective-permute-start.10 = (f32[2,3,16,128]{3,2,1,0:T(8,128)S(1)}, f32[2,3,16,128]{3,2,1,0:T(8,128)S(1)}, u32[]{:S(2)}, u32[]{:S(2)}) collective-permute-start(f32[2,3,16,128]{3,2,1,0:T(8,128)S(1)} %get-tuple-element.44), channel_id=1, source_target_pairs={{0,2},{1,3},{2,0},{3,1},{4,6},{5,7},{6,4},{7,5},{8,10},{9,11},{10,... | collective-permute-start | bytes 147464 | tf_op jit(solution)/shard_map/ppermute | solution.py:694
  26.6 9.2 %collective-permute-start.11 = (f32[2,3,16,128]{3,2,1,0:T(8,128)S(1)}, f32[2,3,16,128]{3,2,1,0:T(8,128)S(1)}, u32[]{:S(2)}, u32[]{:S(2)}) collective-permute-start(f32[2,3,16,128]{3,2,1,0:T(8,128)S(1)} %get-tuple-element.45), channel_id=1, source_target_pairs={{0,3},{1,2},{2,1},{3,0},{4,7},{5,6},{6,5},{7,4},{8,11},{9,10},{10,... | collective-permute-start | bytes 147464 | tf_op jit(solution)/shard_map/ppermute | solution.py:694
  27.1 8.7 %collective-permute-start.9 = (f32[2,3,16,128]{3,2,1,0:T(8,128)S(1)}, f32[2,3,16,128]{3,2,1,0:T(8,128)S(1)}, u32[]{:S(2)}, u32[]{:S(2)}) collective-permute-start(f32[2,3,16,128]{3,2,1,0:T(8,128)S(1)} %get-tuple-element.43), channel_id=1, source_target_pairs={{0,1},{1,0},{2,3},{3,2},{4,5},{5,4},{6,7},{7,6},{8,9},{9,8},{10,11... | collective-permute-start | bytes 147464 | tf_op jit(solution)/shard_map/ppermute | solution.py:694

commit v12 on v11

--- a/solution.py
+++ b/solution.py
@@ -752,14 +752,19 @@
     middle.update((k, send(part, k)) for k, part in zip(others, rest))
     halos = list(zip(columns, near_rows))
     edges = list(advance(LATE, table, fields, halos, units))
-    middle[ahead], edges[0] = lax.optimization_barrier((middle[ahead], edges[0]))
+    own = units.index(ahead)
+    middle[ahead], edges[own] = lax.optimization_barrier((middle[ahead], edges[own]))
     middle[ahead] = in_vmem(middle[ahead])
     edges = [send(part, k) for k, part in zip(units, edges)]
     soon = tuple(range(1, subs)) + (ahead,)
     last = tuple(k for k in units if k not in soon)
     outs = advance(WHOLE, table, fields, halos, soon, [middle[k] for k in soon])
-    outs = place(tuple((k, (MIDDLE,)) for k in last), table, [middle[k] for k in last], outs)
-    return place(tuple((k, LATE.sent) for k in units), table, edges, outs)
+    near = [n for n, k in enumerate(units) if k < subs]
+    far = [n for n, k in enumerate(units) if k >= subs]
+    groups = tuple((k, (MIDDLE,)) for k in last) + tuple((units[n], LATE.sent) for n in near)
+    outs = place(groups, table, [middle[k] for k in last] + [edges[n] for n in near], outs)
+    groups = tuple((units[n], LATE.sent) for n in far)
+    return place(groups, table, [edges[n] for n in far], outs)
 
 
 def solution(mesh):

time: 36.8 us -> 37.2 us (1.011)
  starting transfers between devices: 11.5 us -> 13 us
  waiting for transfers between devices: 4.93 us -> 3.7 us
    ppermute x12, starting transfers between devices: 9.87 us -> 11.4 us  [shift_lanes(): return lax.ppermute(array, ('col', 'sub'), pairs)]
    ppermute x12, waiting for transfers between devices: 3.92 us -> 2.69 us  [shift_lanes(): return lax.ppermute(array, ('col', 'sub'), pairs)]
  transfers between devices with their start and end apart: 14 -> 14, of which waited for: 8 -> 6; matrix products, arithmetic and copies ran while one was open for 0% -> 0% of each run, Pallas kernels for 45% -> 45%
where the time goes in v12:
time: 37.2 us; the launch traced here: 37 us
  Pallas kernels  19.4 us (52%)
  starting transfers between devices  13 us (35%)
  waiting for transfers between devices  3.7 us (10%)
  between operations  0.9 us (2%)
    pallas_call x4, Pallas kernels, advance(): pl.pallas_call(functools.partial(advance_kernel, part, lanes, units, len(...  14.1 us
    ppermute x12, starting transfers between devices, shift_lanes(): return lax.ppermute(array, ('col', 'sub'), pairs)  11.4 us
    ppermute x12, waiting for transfers between devices, shift_lanes(): return lax.ppermute(array, ('col', 'sub'), pairs)  2.69 us
    pallas_call x1, Pallas kernels, load(): pl.pallas_call(load_kernel, name='load_and_pack', out_shape=tuple(outs),...  2.22 us
    pallas_call x1, Pallas kernels, make_table(): pl.pallas_call(functools.partial(index_kernel, shape), name='index_table'...  1.64 us
    ppermute x2, starting transfers between devices, meet_rows(): return lax.ppermute(array, ('row', 'sub'), pairs)  1.58 us
    pallas_call x2, Pallas kernels, place(): pl.pallas_call(functools.partial(place_kernel, groups), name='place_arriv...  1.47 us
    ppermute x2, waiting for transfers between devices, meet_rows(): return lax.ppermute(array, ('row', 'sub'), pairs)  1.01 us
  transfers between devices with their start and end apart: 14, of which 6 were waited for; matrix products, arithmetic and copies ran while one was open for 0% of the time, Pallas kernels for 45%

profile of v12, /device:TPU:0, one launch (start us, length us, event | category | flops | bytes accessed | tf_op | source)
XLA Modules:
  0.0 37.0 jit_solution(694353525725975268)
XLA Ops:
  0.6 2.2 %load_and_pack.1 = (f32[8,128,128]{2,1,0:T(8,128)S(1)}, f32[8,128,128]{2,1,0:T(8,128)S(1)}, f32[8,128,128]{2,1,0:T(8,128)S(1)}, f32[8,128,128]{2,1,0:T(8,128)S(1...) custom-call(f32[8,128,128]{2,1,0:T(8,128)} %refs_0_.1, ...), custom_call_target="tpu_custom_call" | custom-call | tf_op jit(solution)/shard_map/load_and_pack/pallas_call | solution.py:216
  2.9 3.0 %collective-permute-start = (f32[448,128]{1,0:T(8,128)S(1)}, f32[448,128]{1,0:T(8,128)S(1)}, u32[]{:S(2)}, u32[]{:S(2)}) collective-permute-start(f32[448,128]{1,0:T(8,128)S(1)} %get-tuple-element.30.refs_6_), channel_id=1, source_target_pairs={{0,2},{1,3},{2,0},{3,1},{4,6},{5,7},{6,4},{7,5},{8,10},{9,11},{10,... | collective-permute-start | bytes 688136 | tf_op jit(solution)/shard_map/ppermute | solution.py:694
  5.9 0.0 copy-start
  5.9 0.0 copy-start.1
  5.9 0.0 copy-start.2
  5.9 1.6 %collective-permute-start.1 = (f32[216,128]{1,0:T(8,128)S(1)}, f32[216,128]{1,0:T(8,128)S(1)}, u32[]{:S(2)}, u32[]{:S(2)}) collective-permute-start(f32[216,128]{1,0:T(8,128)S(1)} %get-tuple-element.31), channel_id=1, source_target_pairs={{0,4},{1,5},{4,0},{5,1},{8,12},{9,13},{12,8},{13,9},{2,6},{3,7},{6... | collective-permute-start | bytes 331784 | tf_op jit(solution)/shard_map/ppermute | solution.py:718
  7.5 0.0 collective-permute-start.2
  7.5 0.5 %collective-permute-start.3 = (f32[448,128]{1,0:T(8,128)S(1)}, f32[448,128]{1,0:T(8,128)S(1)}, u32[]{:S(2)}, u32[]{:S(2)}) collective-permute-start(f32[448,128]{1,0:T(8,128)S(1)} %get-tuple-element.30.refs_6_), channel_id=1, source_target_pairs={{0,1},{1,0},{2,3},{3,2},{4,5},{5,4},{6,7},{7,6},{8,9},{9,8},{10,11... | collective-permute-start | bytes 688136 | tf_op jit(solution)/shard_map/ppermute | solution.py:694
  8.0 0.0 copy-done
  8.0 0.0 copy-done.1
  8.0 0.0 copy-done.2
  8.0 1.6 %index_table.1.refs_0_ = s32[265]{0:T(512)S(4)} custom-call(s32[128]{0:T(128)S(1)} %copy-done, s32[128]{0:T(128)S(1)} %copy-done.1, s32[128]{0:T(128)S(1)} %copy-done.2), custom_call_target="tpu_custom_call" | custom-call | tf_op jit(solution)/shard_map/index_table/pallas_call | solution.py:143
  9.6 1.0 %collective-permute-done.1.met_even = f32[216,128]{1,0:T(8,128)S(1)} collective-permute-done((f32[216,128]{1,0:T(8,128)S(1)}, f32[216,128]{1,0:T(8,128)S(1)}, u32[]{:S(2)}, u32[]{:S(2)}) %collective-permute-start.1) | collective-permute-done | bytes 110624 | tf_op jit(solution)/shard_map/ppermute | solution.py:718
  10.6 0.0 collective-permute-done.2.met_odd
  10.7 0.8 %collective-permute-done.refs_8_.refs_10_ = f32[448,128]{1,0:T(8,128)S(1)} collective-permute-done((f32[448,128]{1,0:T(8,128)S(1)}, f32[448,128]{1,0:T(8,128)S(1)}, u32[]{:S(2)}, u32[]{:S(2)}) %collective-permute-start) | collective-permute-done | bytes 229408 | tf_op jit(solution)/shard_map/ppermute | solution.py:694
  11.5 0.0 collective-permute-start.4
  11.5 1.7 %collective-permute-start.7 = (f32[2,216,128]{2,1,0:T(8,128)S(1)}, f32[2,216,128]{2,1,0:T(8,128)S(1)}, u32[]{:S(2)}, u32[]{:S(2)}) collective-permute-start(f32[2,216,128]{2,1,0:T(8,128)S(1)} %join_row_halos.1.refs_7_), channel_id=1, source_target_pairs={{0,2},{1,3},{2,0},{3,1},{4,6},{5,7},{6,4},{7,5},{8,10},{9,11},{10,... | collective-permute-start | bytes 663560 | tf_op jit(solution)/shard_map/ppermute | solution.py:694
  13.2 0.0 collective-permute-done.3.refs_7_.refs_8_
  13.2 0.0 collective-permute-done.4.refs_9_.refs_12_
  13.2 2.7 %advance_leaving_first.1 = (f32[2,3,112,128]{3,2,1,0:T(8,128)S(1)}, f32[2,3,112,128]{3,2,1,0:T(8,128)S(1)}, f32[2,3,112,128]{3,2,1,0:T(8,128)S(1)}) custom-call(s32[265]{0:T(512)S(4)} %index_table.1.refs_0_, f32[8,128,128]{2,1,0:T(8,128)S(1)} %get-tuple-element.34.refs_1_, f32[8,128,128]{2,1,0:T(8,128)S(1)} %get-tuple-element.35.refs_2_, ...), custom_call_target="tpu_custom_call" | custom-call | flops 17694720 | bytes 917504 | tf_op jit(solution)/shard_map/advance_leaving_first/pallas_call | solution.py:663
  15.9 1.5 %collective-permute-start.5 = (f32[2,3,112,128]{3,2,1,0:T(8,128)S(1)}, f32[2,3,112,128]{3,2,1,0:T(8,128)S(1)}, u32[]{:S(2)}, u32[]{:S(2)}) collective-permute-start(f32[2,3,112,128]{3,2,1,0:T(8,128)S(1)} %get-tuple-element.40), channel_id=1, source_target_pairs={{0,2},{1,3},{2,0},{3,1},{4,6},{5,7},{6,4},{7,5},{8,10},{9,11},{10,... | collective-permute-start | bytes 1032200 | tf_op jit(solution)/shard_map/ppermute | solution.py:694
  17.4 2.7 %advance_leaving_second.1 = (f32[2,3,112,128]{3,2,1,0:T(8,128)S(1)}, f32[2,3,112,128]{3,2,1,0:T(8,128)S(1)}) custom-call(s32[265]{0:T(512)S(4)} %index_table.1.refs_0_, f32[8,128,128]{2,1,0:T(8,128)S(1)} %get-tuple-element.34.refs_1_, f32[8,128,128]{2,1,0:T(8,128)S(1)} %get-tuple-element.35.refs_2_, ...), custom_call_target="tpu_custom_call", output_to_operand_aliasing={{0}: (10, {}), {1}: (11, {})} | custom-call | flops 17694720 | bytes 917504 | tf_op jit(solution)/shard_map/advance_leaving_second/pallas_call | solution.py:663
  20.1 0.1 collective-permute-start.13
  20.2 0.7 %collective-permute-start.11 = (f32[2,3,112,128]{3,2,1,0:T(8,128)S(1)}, f32[2,3,112,128]{3,2,1,0:T(8,128)S(1)}, u32[]{:S(2)}, u32[]{:S(2)}) collective-permute-start(f32[2,3,112,128]{3,2,1,0:T(8,128)S(1)} %get-tuple-element.47), channel_id=1, source_target_pairs={{0,3},{1,2},{2,1},{3,0},{4,7},{5,6},{6,5},{7,4},{8,11},{9,10},{10,... | collective-permute-start | bytes 1032200 | tf_op jit(solution)/shard_map/ppermute | solution.py:694
  20.9 0.1 collective-permute-start.6
  20.9 0.0 collective-permute-done.7.refs_11_
  20.9 0.4 %collective-permute-start.8 = (f32[2,216,128]{2,1,0:T(8,128)S(1)}, f32[2,216,128]{2,1,0:T(8,128)S(1)}, u32[]{:S(2)}, u32[]{:S(2)}) collective-permute-start(f32[2,216,128]{2,1,0:T(8,128)S(1)} %collective-permute-done.7.refs_11_), channel_id=1, source_target_pairs={{0,1},{1,0},{2,3},{3,2},{4,5},{5,4},{6,7},{7,6},{8,9},{9,8},{10,11... | collective-permute-start | bytes 663560 | tf_op jit(solution)/shard_map/ppermute | solution.py:694
  21.4 1.0 %collective-permute-done.6.refs_9_ = f32[2,216,128]{2,1,0:T(8,128)S(1)} collective-permute-done((f32[2,216,128]{2,1,0:T(8,128)S(1)}, f32[2,216,128]{2,1,0:T(8,128)S(1)}, u32[]{:S(2)}, u32[]{:S(2)}) %collective-permute-start.6) | collective-permute-done | bytes 221216 | tf_op jit(solution)/shard_map/ppermute | solution.py:694
  22.4 0.3 collective-permute-done.8.refs_13_
  22.7 2.4 %advance_leaving_edges.1 = (f32[2,3,16,128]{3,2,1,0:T(8,128)S(1)}, f32[2,3,16,128]{3,2,1,0:T(8,128)S(1)}, f32[2,3,16,128]{3,2,1,0:T(8,128)S(1)}) custom-call(s32[265]{0:T(512)S(4)} %index_table.1.refs_0_, f32[8,128,128]{2,1,0:T(8,128)S(1)} %get-tuple-element.34.refs_1_, f32[8,128,128]{2,1,0:T(8,128)S(1)} %get-tuple-element.35.refs_2_, ...), custom_call_target="tpu_custom_call" | custom-call | flops 11059200 | bytes 262144 | tf_op jit(solution)/shard_map/advance_leaving_edges/pallas_call | solution.py:663
  25.1 0.3 collective-permute-start.12
  25.3 1.4 %collective-permute-start.10 = (f32[2,3,16,128]{3,2,1,0:T(8,128)S(1)}, f32[2,3,16,128]{3,2,1,0:T(8,128)S(1)}, u32[]{:S(2)}, u32[]{:S(2)}) collective-permute-start(f32[2,3,16,128]{3,2,1,0:T(8,128)S(1)} %get-tuple-element.44), channel_id=1, source_target_pairs={{0,3},{1,2},{2,1},{3,0},{4,7},{5,6},{6,5},{7,4},{8,11},{9,10},{10,... | collective-permute-start | bytes 147464 | tf_op jit(solution)/shard_map/ppermute | solution.py:694
  26.7 0.3 collective-permute-done.5.refs_15_
  27.1 1.7 %collective-permute-start.9 = (f32[2,3,16,128]{3,2,1,0:T(8,128)S(1)}, f32[2,3,16,128]{3,2,1,0:T(8,128)S(1)}, u32[]{:S(2)}, u32[]{:S(2)}) collective-permute-start(f32[2,3,16,128]{3,2,1,0:T(8,128)S(1)} %get-tuple-element.43), channel_id=1, source_target_pairs={{0,2},{1,3},{2,0},{3,1},{4,6},{5,7},{6,4},{7,5},{8,10},{9,11},{10,... | collective-permute-start | bytes 147464 | tf_op jit(solution)/shard_map/ppermute | solution.py:694
  28.8 0.0 collective-permute-done.13.refs_14_
  28.8 6.3 %advance_staying.1 = (f32[8,128,128]{2,1,0:T(8,128)}, f32[8,128,128]{2,1,0:T(8,128)}, f32[8,128,128]{2,1,0:T(8,128)}) custom-call(s32[265]{0:T(512)S(4)} %index_table.1.refs_0_, f32[8,128,128]{2,1,0:T(8,128)S(1)} %get-tuple-element.34.refs_1_, f32[8,128,128]{2,1,0:T(8,128)S(1)} %get-tuple-element.35.refs_2_, f32[8,128,128]{2,1,0:T(8,128)S(1)} %get-tuple-element.36.refs_3_, ...), custom_call_target="tpu_custom_call" | custom-call | flops 33177600 | bytes 2097152 | tf_op jit(solution)/shard_map/advance_staying/pallas_call | solution.py:663
  35.1 0.0 collective-permute-done.12.refs_2_
  35.1 0.0 collective-permute-done.11.refs_1_
  35.2 0.8 %place_arrivals.2 = (f32[8,128,128]{2,1,0:T(8,128)}, f32[8,128,128]{2,1,0:T(8,128)}, f32[8,128,128]{2,1,0:T(8,128)}) custom-call(s32[265]{0:T(512)S(4)} %index_table.1.refs_0_, f32[2,3,112,128]{3,2,1,0:T(8,128)S(1)} %collective-permute-done.11.refs_1_, ...), custom_call_target="tpu_custom_call", output_to_operand_aliasing={{0}: (3, {}), {1}: (4, {}), {2}: (5, {})} | custom-call | tf_op jit(solution)/shard_map/place_arrivals/pallas_call | solution.py:292
  35.9 0.0 collective-permute-done.10.refs_2_
  35.9 0.2 collective-permute-done.9.refs_1_
  36.2 0.7 %place_arrivals.3 = (f32[8,128,128]{2,1,0:T(8,128)}, f32[8,128,128]{2,1,0:T(8,128)}, f32[8,128,128]{2,1,0:T(8,128)}) custom-call(s32[265]{0:T(512)S(4)} %index_table.1.refs_0_, f32[2,3,16,128]{3,2,1,0:T(8,128)S(1)} %collective-permute-done.9.refs_1_, ...), custom_call_target="tpu_custom_call", output_to_operand_aliasing={{0}: (3, {}), {1}: (4, {}), {2}: (5, {})} | custom-call | tf_op jit(solution)/shard_map/place_arrivals/pallas_call | solution.py:292
  (1 shorter events, 0.0 us)
Async XLA Ops:
  2.9 8.6 %collective-permute-start = (f32[448,128]{1,0:T(8,128)S(1)}, f32[448,128]{1,0:T(8,128)S(1)}, u32[]{:S(2)}, u32[]{:S(2)}) collective-permute-start(f32[448,128]{1,0:T(8,128)S(1)} %get-tuple-element.30.refs_6_), channel_id=1, source_target_pairs={{0,2},{1,3},{2,0},{3,1},{4,6},{5,7},{6,4},{7,5},{8,10},{9,11},{10,... | collective-permute-start | bytes 688136 | tf_op jit(solution)/shard_map/ppermute | solution.py:694
  5.9 2.1 %copy-start = (s32[128]{0:T(128)S(1)}, s32[128]{0:T(128)}, u32[]{:S(2)}) copy-start(s32[128]{0:T(128)} %before_ref.1) | copy-start | bytes 1540
  5.9 2.1 %copy-start.1 = (s32[128]{0:T(128)S(1)}, s32[128]{0:T(128)}, u32[]{:S(2)}) copy-start(s32[128]{0:T(128)} %after_ref.1) | copy-start | bytes 1540
  5.9 2.1 %copy-start.2 = (s32[128]{0:T(128)S(1)}, s32[128]{0:T(128)}, u32[]{:S(2)}) copy-start(s32[128]{0:T(128)} %wet_ref.1) | copy-start | bytes 1540
  5.9 4.7 %collective-permute-start.1 = (f32[216,128]{1,0:T(8,128)S(1)}, f32[216,128]{1,0:T(8,128)S(1)}, u32[]{:S(2)}, u32[]{:S(2)}) collective-permute-start(f32[216,128]{1,0:T(8,128)S(1)} %get-tuple-element.31), channel_id=1, source_target_pairs={{0,4},{1,5},{4,0},{5,1},{8,12},{9,13},{12,8},{13,9},{2,6},{3,7},{6... | collective-permute-start | bytes 331784 | tf_op jit(solution)/shard_map/ppermute | solution.py:718
  7.5 3.2 %collective-permute-start.2 = (f32[216,128]{1,0:T(8,128)S(1)}, f32[216,128]{1,0:T(8,128)S(1)}, u32[]{:S(2)}, u32[]{:S(2)}) collective-permute-start(f32[216,128]{1,0:T(8,128)S(1)} %get-tuple-element.32), channel_id=1, source_target_pairs={{0,1},{1,0},{4,8},{5,9},{8,4},{9,5},{12,13},{13,12},{2,3},{3,2},{6... | collective-permute-start | bytes 331784 | tf_op jit(solution)/shard_map/ppermute | solution.py:718
  7.5 5.8 %collective-permute-start.3 = (f32[448,128]{1,0:T(8,128)S(1)}, f32[448,128]{1,0:T(8,128)S(1)}, u32[]{:S(2)}, u32[]{:S(2)}) collective-permute-start(f32[448,128]{1,0:T(8,128)S(1)} %get-tuple-element.30.refs_6_), channel_id=1, source_target_pairs={{0,1},{1,0},{2,3},{3,2},{4,5},{5,4},{6,7},{7,6},{8,9},{9,8},{10,11... | collective-permute-start | bytes 688136 | tf_op jit(solution)/shard_map/ppermute | solution.py:694
  11.5 1.8 %collective-permute-start.4 = (f32[448,128]{1,0:T(8,128)S(1)}, f32[448,128]{1,0:T(8,128)S(1)}, u32[]{:S(2)}, u32[]{:S(2)}) collective-permute-start(f32[448,128]{1,0:T(8,128)S(1)} %collective-permute-done.refs_8_.refs_10_), channel_id=1, source_target_pairs={{0,1},{1,0},{2,3},{3,2},{4,5},{5,4},{6,7},{7,6},{8,9},{9,8},{10,11... | collective-permute-start | bytes 688136 | tf_op jit(solution)/shard_map/ppermute | solution.py:694
  11.5 9.5 %collective-permute-start.7 = (f32[2,216,128]{2,1,0:T(8,128)S(1)}, f32[2,216,128]{2,1,0:T(8,128)S(1)}, u32[]{:S(2)}, u32[]{:S(2)}) collective-permute-start(f32[2,216,128]{2,1,0:T(8,128)S(1)} %join_row_halos.1.refs_7_), channel_id=1, source_target_pairs={{0,2},{1,3},{2,0},{3,1},{4,6},{5,7},{6,4},{7,5},{8,10},{9,11},{10,... | collective-permute-start | bytes 663560 | tf_op jit(solution)/shard_map/ppermute | solution.py:694
  15.9 11.2 %collective-permute-start.5 = (f32[2,3,112,128]{3,2,1,0:T(8,128)S(1)}, f32[2,3,112,128]{3,2,1,0:T(8,128)S(1)}, u32[]{:S(2)}, u32[]{:S(2)}) collective-permute-start(f32[2,3,112,128]{3,2,1,0:T(8,128)S(1)} %get-tuple-element.40), channel_id=1, source_target_pairs={{0,2},{1,3},{2,0},{3,1},{4,6},{5,7},{6,4},{7,5},{8,10},{9,11},{10,... | collective-permute-start | bytes 1032200 | tf_op jit(solution)/shard_map/ppermute | solution.py:694
  20.1 8.7 %collective-permute-start.13 = (f32[2,3,112,128]{3,2,1,0:T(8,128)S(1)}, f32[2,3,112,128]{3,2,1,0:T(8,128)S(1)}, u32[]{:S(2)}, u32[]{:S(2)}) collective-permute-start(f32[2,3,112,128]{3,2,1,0:T(8,128)S(1)} %get-tuple-element.49), channel_id=1, source_target_pairs={{0,1},{1,0},{2,3},{3,2},{4,5},{5,4},{6,7},{7,6},{8,9},{9,8},{10,11... | collective-permute-start | bytes 1032200 | tf_op jit(solution)/shard_map/ppermute | solution.py:694
  20.2 14.9 %collective-permute-start.11 = (f32[2,3,112,128]{3,2,1,0:T(8,128)S(1)}, f32[2,3,112,128]{3,2,1,0:T(8,128)S(1)}, u32[]{:S(2)}, u32[]{:S(2)}) collective-permute-start(f32[2,3,112,128]{3,2,1,0:T(8,128)S(1)} %get-tuple-element.47), channel_id=1, source_target_pairs={{0,3},{1,2},{2,1},{3,0},{4,7},{5,6},{6,5},{7,4},{8,11},{9,10},{10,... | collective-permute-start | bytes 1032200 | tf_op jit(solution)/shard_map/ppermute | solution.py:694
  20.9 1.5 %collective-permute-start.6 = (f32[2,216,128]{2,1,0:T(8,128)S(1)}, f32[2,216,128]{2,1,0:T(8,128)S(1)}, u32[]{:S(2)}, u32[]{:S(2)}) collective-permute-start(f32[2,216,128]{2,1,0:T(8,128)S(1)} %join_row_halos.1.refs_7_), channel_id=1, source_target_pairs={{0,1},{1,0},{2,3},{3,2},{4,5},{5,4},{6,7},{7,6},{8,9},{9,8},{10,11... | collective-permute-start | bytes 663560 | tf_op jit(solution)/shard_map/ppermute | solution.py:694
  20.9 1.7 %collective-permute-start.8 = (f32[2,216,128]{2,1,0:T(8,128)S(1)}, f32[2,216,128]{2,1,0:T(8,128)S(1)}, u32[]{:S(2)}, u32[]{:S(2)}) collective-permute-start(f32[2,216,128]{2,1,0:T(8,128)S(1)} %collective-permute-done.7.refs_11_), channel_id=1, source_target_pairs={{0,1},{1,0},{2,3},{3,2},{4,5},{5,4},{6,7},{7,6},{8,9},{9,8},{10,11... | collective-permute-start | bytes 663560 | tf_op jit(solution)/shard_map/ppermute | solution.py:694
  25.1 10.1 %collective-permute-start.12 = (f32[2,3,16,128]{3,2,1,0:T(8,128)S(1)}, f32[2,3,16,128]{3,2,1,0:T(8,128)S(1)}, u32[]{:S(2)}, u32[]{:S(2)}) collective-permute-start(f32[2,3,16,128]{3,2,1,0:T(8,128)S(1)} %get-tuple-element.48), channel_id=1, source_target_pairs={{0,1},{1,0},{2,3},{3,2},{4,5},{5,4},{6,7},{7,6},{8,9},{9,8},{10,11... | collective-permute-start | bytes 147464 | tf_op jit(solution)/shard_map/ppermute | solution.py:694
  25.3 10.6 %collective-permute-start.10 = (f32[2,3,16,128]{3,2,1,0:T(8,128)S(1)}, f32[2,3,16,128]{3,2,1,0:T(8,128)S(1)}, u32[]{:S(2)}, u32[]{:S(2)}) collective-permute-start(f32[2,3,16,128]{3,2,1,0:T(8,128)S(1)} %get-tuple-element.44), channel_id=1, source_target_pairs={{0,3},{1,2},{2,1},{3,0},{4,7},{5,6},{6,5},{7,4},{8,11},{9,10},{10,... | collective-permute-start | bytes 147464 | tf_op jit(solution)/shard_map/ppermute | solution.py:694
  27.1 9.1 %collective-permute-start.9 = (f32[2,3,16,128]{3,2,1,0:T(8,128)S(1)}, f32[2,3,16,128]{3,2,1,0:T(8,128)S(1)}, u32[]{:S(2)}, u32[]{:S(2)}) collective-permute-start(f32[2,3,16,128]{3,2,1,0:T(8,128)S(1)} %get-tuple-element.43), channel_id=1, source_target_pairs={{0,2},{1,3},{2,0},{3,1},{4,6},{5,7},{6,4},{7,5},{8,10},{9,11},{10,... | collective-permute-start | bytes 147464 | tf_op jit(solution)/shard_map/ppermute | solution.py:694
